TPU v7x, 256 devices: a whole 4x4x8 slice. The times are simulated.
256 devices in a mesh: top: 2 (over core), mid: 32 (over z, x), leaf: 4 (over y).
Axes of the slice: x: 4, y: 4, z: 8, core: 2. Of those that a mesh axis runs over, the one named last changes fastest.
Arguments:
- coords: float32 [3, 589824], P(None, ('top', 'mid', 'leaf')), may hold values from 0 to 4
- weights: float32 [589824, 128], P(('top', 'mid', 'leaf')), may hold values from -6 to 6
- labels: int32 [589824, 128], P(('top', 'mid', 'leaf')), may hold values 0 or 1
- order: int32 [256, 2304], P(('top', 'mid', 'leaf')), may hold values from 0 to 2303, each once within a row
- basis: float32 [589824, 64], P(('top', 'mid', 'leaf')), may hold values from -0.125 to 0.125
- transfer_leaf: float32 [256, 64, 64], P(('top', 'mid', 'leaf')), may hold values from -0.75 to 0.75
- transfer_mid: float32 [64, 64, 64], P(('top', 'mid')), may hold values from -0.75 to 0.75
- couple_leaf: float32 [256, 4, 64, 64], P(('top', 'mid', 'leaf')), may hold values from -0.75 to 0.75
- couple_mid: float32 [64, 32, 64, 64], P(('top', 'mid')), may hold values from -0.125 to 0.125
- couple_top: float32 [2, 2, 64, 64], P('top'), may hold values from -0.09375 to 0.09375
Outputs:
- trained: float32 [589824, 128], P(('top', 'mid', 'leaf'))
All inputs are finite; a program needn't handle non-finite values. No bound on the sum of `labels` on one device may be relied on, other than what follows from the above.
Results may differ from a plain program's by a relative error of at most 0.0001.
Values sent between devices are 32-bit elements; how exact they have to be, the bound alone decides.
No kernel may reach another device: no remote copies, remote signals or barrier semaphores. Data moves between devices by JAX's collectives and lax.ppermute only.
A program may use at most 64 MiB of HBM per device.

v0:
```python
import math

import jax
import jax.numpy as jnp
from jax import lax
from jax.sharding import PartitionSpec as P

STEPS = 2


def make_fold(blocks, own_index):

    def fold(total, piece, start):
        count = piece.shape[0]
        keep = (jnp.arange(count) != own_index).astype(jnp.float32)
        return jnp.einsum(
            "jab,jbo->ao", blocks * keep[:, None, None], piece, precision=lax.Precision.HIGHEST
        )

    return fold


def mid_fold(skeleton, fold, init):
    return fold(init, lax.all_gather(skeleton[None], "mid", axis=0, tiled=True), jnp.int32(0))


def on_device(
    coords,
    weights,
    labels,
    order,
    basis,
    transfer_leaf,
    transfer_mid,
    couple_leaf,
    couple_mid,
    couple_top,
):
    hp = lax.Precision.HIGHEST
    leaf_rows = weights.shape[0]
    block = math.gcd(leaf_rows, 384)
    row_blocks = jnp.transpose(coords.reshape(3, leaf_rows // block, block), (1, 0, 2))
    kernel_scale = 4.0 / jnp.sqrt(jnp.float32(leaf_rows))
    targets = jnp.take(labels, order[0], axis=0).astype(jnp.float32)
    own_top = lax.axis_index("top")
    own_mid = lax.axis_index("mid")
    own_leaf = lax.axis_index("leaf")
    leaf_move = transfer_leaf[0]
    mid_move = transfer_mid[0]
    empty = jnp.zeros((basis.shape[1], weights.shape[1]), jnp.float32)
    current = weights
    for step in range(STEPS):
        s0 = jnp.einsum("ia,io->ao", basis, current, precision=hp)
        up0 = jnp.einsum("ba,bo->ao", leaf_move, s0, precision=hp)
        s1 = lax.psum(up0, "leaf")
        s2 = lax.psum(jnp.einsum("ba,bo->ao", mid_move, s1, precision=hp), "mid")
        g1 = mid_fold(s1, make_fold(couple_mid[0], own_mid), empty)
        g2 = make_fold(couple_top[0], own_top)(
            empty, lax.all_gather(s2[None], "top", axis=0, tiled=True), jnp.int32(0)
        )
        g1 = g1 + jnp.dot(mid_move, g2, precision=hp)
        g0 = make_fold(couple_leaf[0], own_leaf)(
            empty, lax.all_gather(s0[None], "leaf", axis=0, tiled=True), jnp.int32(0)
        )
        g0 = g0 + jnp.dot(leaf_move, g1, precision=hp)

        def near(row_points):
            diff_sq = jnp.zeros((row_points.shape[1], leaf_rows), jnp.float32)
            for axis_k in range(3):
                delta = row_points[axis_k][:, None] - coords[axis_k][None, :]
                diff_sq = diff_sq + delta * delta
            kernel_rows = jnp.exp(-jnp.sqrt(diff_sq)) * kernel_scale
            return jnp.dot(kernel_rows, current, precision=hp)

        near_field = lax.map(near, row_blocks).reshape(leaf_rows, current.shape[1])
        field = near_field + jnp.dot(basis, g0, precision=hp)
        current = current - (jax.nn.sigmoid(field) - targets)
    return current


def solution(mesh):
    placed = (
        P(None, ("top", "mid", "leaf")),
        P(("top", "mid", "leaf"), None),
        P(("top", "mid", "leaf"), None),
        P(("top", "mid", "leaf"), None),
        P(("top", "mid", "leaf"), None),
        P(("top", "mid", "leaf"), None, None),
        P(("top", "mid"), None, None),
        P(("top", "mid", "leaf"), None, None, None),
        P(("top", "mid"), None, None, None),
        P("top", None, None, None),
    )
    return jax.shard_map(
        on_device,
        mesh=mesh,
        in_specs=placed,
        out_specs=P(("top", "mid", "leaf"), None),
        check_vma=False,
    )
```

profile of v0, /device:TPU:1, one launch (start us, length us, event | category | flops | bytes accessed | tf_op | source)
XLA Modules:
  0.0 494.8 jit_solution(14005999126944008569)
XLA Ops:
  6.5 2.4 fusion.87
  9.8 15.0 %psum.28 = f32[64,128]{1,0:T(8,128)} all-reduce(f32[64,128]{1,0:T(8,128)S(1)} %convolution_bitcast_fusion.14), channel_id=1, replica_groups=mesh['top'=2,'mid'=32,'leaf'=4] {'leaf'}, use_global_device_ids=true, to_apply=%region_2.3 | all-reduce | flops 8192 | bytes 65536 | tf_op jit(solution)/shard_map/psum | solution.py:55
  25.0 47.5 %while.20 = (s32[]{:T(128)}, f32[6,384,128]{2,1,0:T(8,128)S(1)}, f32[6,3,384]{2,1,0:T(4,128)}, f32[3,2304]{1,0:T(4,128)}, f32[2304,128]{1,0:T(8,128)S(1)}, /*index=5*/s32[]{:T(128)}, s32[]{:T(128)}, s32[]{}, s32[]{}) while((s32[]{:T(128)}, f32[6,384,128]{2,1,0:T(8,128)S(1)}, f32[6,3,384]{2,1,0:T(4,128)}, f32[3,2304]{1,0:T(4,128)}, ...), condition=%wide.region_1.2_spmd, body=%wide.region_0.1_spmd.sunk | while | flops 1367801856 | bytes 1477773 | solution.py:75
  25.0 1.6 slice_reduce_fusion.8
  26.6 0.8 dynamic-slice_reduce_fusion.8
  27.4 5.5 %fusion.121 = f32[6,384,128]{2,1,0:T(8,128)S(1)} fusion(f32[6,384,128]{2,1,0:T(8,128)S(1)} %get-tuple-element.204, s32[]{:T(128)S(6)} %copy.33, f32[2304,128]{1,0:T(8,128)S(1)} %get-tuple-element.216, f32[2304]{0:T(1024)} %get-tuple-element.177, f32[384]{0:T(512)S(1)} %get-tuple-element.178, f32[2304]{0:T(1024)} %get-tuple-element.179, ...), kind=kOutput, calls=%fused_computation.22.clone.1 | convolution fusion | flops 1367801856 | bytes 1413124 | tf_op jit(solution)/shard_map/while/body/eval_jaxpr/dot_general | solution.py:73
  32.9 1.6 slice_reduce_fusion.8
  34.5 0.8 dynamic-slice_reduce_fusion.8
  35.3 5.5 %fusion.121 = f32[6,384,128]{2,1,0:T(8,128)S(1)} fusion(f32[6,384,128]{2,1,0:T(8,128)S(1)} %get-tuple-element.204, s32[]{:T(128)S(6)} %copy.33, f32[2304,128]{1,0:T(8,128)S(1)} %get-tuple-element.216, f32[2304]{0:T(1024)} %get-tuple-element.177, f32[384]{0:T(512)S(1)} %get-tuple-element.178, f32[2304]{0:T(1024)} %get-tuple-element.179, ...), kind=kOutput, calls=%fused_computation.22.clone.1 | convolution fusion | flops 1367801856 | bytes 1413124 | tf_op jit(solution)/shard_map/while/body/eval_jaxpr/dot_general | solution.py:73
  40.8 1.6 slice_reduce_fusion.8
  42.4 0.8 dynamic-slice_reduce_fusion.8
  43.2 5.5 %fusion.121 = f32[6,384,128]{2,1,0:T(8,128)S(1)} fusion(f32[6,384,128]{2,1,0:T(8,128)S(1)} %get-tuple-element.204, s32[]{:T(128)S(6)} %copy.33, f32[2304,128]{1,0:T(8,128)S(1)} %get-tuple-element.216, f32[2304]{0:T(1024)} %get-tuple-element.177, f32[384]{0:T(512)S(1)} %get-tuple-element.178, f32[2304]{0:T(1024)} %get-tuple-element.179, ...), kind=kOutput, calls=%fused_computation.22.clone.1 | convolution fusion | flops 1367801856 | bytes 1413124 | tf_op jit(solution)/shard_map/while/body/eval_jaxpr/dot_general | solution.py:73
  48.7 1.6 slice_reduce_fusion.8
  50.3 0.8 dynamic-slice_reduce_fusion.8
  51.1 5.5 %fusion.121 = f32[6,384,128]{2,1,0:T(8,128)S(1)} fusion(f32[6,384,128]{2,1,0:T(8,128)S(1)} %get-tuple-element.204, s32[]{:T(128)S(6)} %copy.33, f32[2304,128]{1,0:T(8,128)S(1)} %get-tuple-element.216, f32[2304]{0:T(1024)} %get-tuple-element.177, f32[384]{0:T(512)S(1)} %get-tuple-element.178, f32[2304]{0:T(1024)} %get-tuple-element.179, ...), kind=kOutput, calls=%fused_computation.22.clone.1 | convolution fusion | flops 1367801856 | bytes 1413124 | tf_op jit(solution)/shard_map/while/body/eval_jaxpr/dot_general | solution.py:73
  56.6 1.6 slice_reduce_fusion.8
  58.2 0.8 dynamic-slice_reduce_fusion.8
  59.0 5.5 %fusion.121 = f32[6,384,128]{2,1,0:T(8,128)S(1)} fusion(f32[6,384,128]{2,1,0:T(8,128)S(1)} %get-tuple-element.204, s32[]{:T(128)S(6)} %copy.33, f32[2304,128]{1,0:T(8,128)S(1)} %get-tuple-element.216, f32[2304]{0:T(1024)} %get-tuple-element.177, f32[384]{0:T(512)S(1)} %get-tuple-element.178, f32[2304]{0:T(1024)} %get-tuple-element.179, ...), kind=kOutput, calls=%fused_computation.22.clone.1 | convolution fusion | flops 1367801856 | bytes 1413124 | tf_op jit(solution)/shard_map/while/body/eval_jaxpr/dot_general | solution.py:73
  64.5 1.6 slice_reduce_fusion.8
  66.1 0.9 dynamic-slice_reduce_fusion.8
  66.9 5.5 %fusion.121 = f32[6,384,128]{2,1,0:T(8,128)S(1)} fusion(f32[6,384,128]{2,1,0:T(8,128)S(1)} %get-tuple-element.204, s32[]{:T(128)S(6)} %copy.33, f32[2304,128]{1,0:T(8,128)S(1)} %get-tuple-element.216, f32[2304]{0:T(1024)} %get-tuple-element.177, f32[384]{0:T(512)S(1)} %get-tuple-element.178, f32[2304]{0:T(1024)} %get-tuple-element.179, ...), kind=kOutput, calls=%fused_computation.22.clone.1 | convolution fusion | flops 1367801856 | bytes 1413124 | tf_op jit(solution)/shard_map/while/body/eval_jaxpr/dot_general | solution.py:73
  72.5 1.4 copy.25
  73.8 1.4 copy.23
  75.4 3.9 gather_fusion
  79.3 1.4 copy.24
  80.7 1.0 convolution_bitcast_fusion.12
  81.7 118.1 %psum.29 = f32[1,64,128]{2,1,0:T(8,128)S(1)} all-reduce(f32[1,64,128]{2,1,0:T(8,128)S(1)} %convolution_bitcast_fusion.12), channel_id=1, replica_groups=mesh['top'=2,'mid'=32,'leaf'=4] {'mid'}, use_global_device_ids=true, to_apply=%region_3.4 | all-reduce | flops 8192 | bytes 65536 | tf_op jit(solution)/shard_map/psum | solution.py:56
  199.8 33.5 %all_gather.20 = f32[2,64,128]{2,1,0:T(8,128)S(1)} all-gather(f32[1,64,128]{2,1,0:T(8,128)S(1)} %psum.29), channel_id=1, replica_groups=mesh['top'=2,'mid'=32,'leaf'=4] {'top'}, dimensions={0}, use_global_device_ids=true | all-gather | bytes 98304 | tf_op jit(solution)/shard_map/all_gather | solution.py:59
  233.3 9.5 %all-gather = f32[256,128]{1,0:T(8,128)S(1)} all-gather(f32[64,128]{1,0:T(8,128)} %copy-done.14), channel_id=2, replica_groups=mesh['top'=2,'mid'=32,'leaf'=4] {'leaf'}, dimensions={0}, use_global_device_ids=true | all-gather | bytes 163840 | tf_op jit(solution)/shard_map/all_gather | solution.py:63
  242.9 1.1 convolution_bitcast_fusion.11
  244.5 2.5 convolution_bitcast_fusion.13
  247.4 3.0 fusion.61
  250.4 1.4 copy.26
  251.8 1.3 fusion.88
  254.0 11.7 %psum.30 = f32[64,128]{1,0:T(8,128)} all-reduce(f32[64,128]{1,0:T(8,128)S(1)} %convolution_bitcast_fusion.7), channel_id=1, replica_groups=mesh['top'=2,'mid'=32,'leaf'=4] {'leaf'}, use_global_device_ids=true, to_apply=%region_6.7 | all-reduce | flops 8192 | bytes 65536 | tf_op jit(solution)/shard_map/psum | solution.py:55
  265.7 50.9 %while.21 = (s32[]{:T(128)}, f32[6,384,128]{2,1,0:T(8,128)S(1)}, f32[6,3,384]{2,1,0:T(4,128)}, f32[3,2304]{1,0:T(4,128)}, f32[2304,128]{1,0:T(8,128)}, /*index=5*/s32[]{:T(128)}, s32[]{:T(128)}, s32[]{}, s32[]{}) while((s32[]{:T(128)}, f32[6,384,128]{2,1,0:T(8,128)S(1)}, f32[6,3,384]{2,1,0:T(4,128)}, f32[3,2304]{1,0:T(4,128)}, ...), condition=%wide.region_5.6_spmd, body=%wide.region_4.5_spmd.sunk | while | flops 1367801856 | bytes 1477773 | solution.py:75
  265.7 1.6 slice_reduce_fusion.9
  267.3 0.8 dynamic-slice_reduce_fusion.9
  268.1 6.1 %fusion.124 = f32[6,384,128]{2,1,0:T(8,128)S(1)} fusion(f32[6,384,128]{2,1,0:T(8,128)S(1)} %get-tuple-element.231, s32[]{:T(128)S(6)} %copy.39, f32[2304,128]{1,0:T(8,128)} %get-tuple-element.243, f32[2304]{0:T(1024)} %get-tuple-element.188, f32[384]{0:T(512)S(1)} %get-tuple-element.189, f32[2304]{0:T(1024)} %get-tuple-element.190, ...), kind=kOutput, calls=%fused_computation.51.clone.1 | convolution fusion | flops 1367801856 | bytes 1413124 | tf_op jit(solution)/shard_map/while/body/eval_jaxpr/dot_general | solution.py:73
  274.2 1.6 slice_reduce_fusion.9
  275.8 0.8 dynamic-slice_reduce_fusion.9
  276.6 6.1 %fusion.124 = f32[6,384,128]{2,1,0:T(8,128)S(1)} fusion(f32[6,384,128]{2,1,0:T(8,128)S(1)} %get-tuple-element.231, s32[]{:T(128)S(6)} %copy.39, f32[2304,128]{1,0:T(8,128)} %get-tuple-element.243, f32[2304]{0:T(1024)} %get-tuple-element.188, f32[384]{0:T(512)S(1)} %get-tuple-element.189, f32[2304]{0:T(1024)} %get-tuple-element.190, ...), kind=kOutput, calls=%fused_computation.51.clone.1 | convolution fusion | flops 1367801856 | bytes 1413124 | tf_op jit(solution)/shard_map/while/body/eval_jaxpr/dot_general | solution.py:73
  282.7 1.6 slice_reduce_fusion.9
  284.3 0.8 dynamic-slice_reduce_fusion.9
  285.1 6.1 %fusion.124 = f32[6,384,128]{2,1,0:T(8,128)S(1)} fusion(f32[6,384,128]{2,1,0:T(8,128)S(1)} %get-tuple-element.231, s32[]{:T(128)S(6)} %copy.39, f32[2304,128]{1,0:T(8,128)} %get-tuple-element.243, f32[2304]{0:T(1024)} %get-tuple-element.188, f32[384]{0:T(512)S(1)} %get-tuple-element.189, f32[2304]{0:T(1024)} %get-tuple-element.190, ...), kind=kOutput, calls=%fused_computation.51.clone.1 | convolution fusion | flops 1367801856 | bytes 1413124 | tf_op jit(solution)/shard_map/while/body/eval_jaxpr/dot_general | solution.py:73
  291.2 1.6 slice_reduce_fusion.9
  293.6 6.1 %fusion.124 = f32[6,384,128]{2,1,0:T(8,128)S(1)} fusion(f32[6,384,128]{2,1,0:T(8,128)S(1)} %get-tuple-element.231, s32[]{:T(128)S(6)} %copy.39, f32[2304,128]{1,0:T(8,128)} %get-tuple-element.243, f32[2304]{0:T(1024)} %get-tuple-element.188, f32[384]{0:T(512)S(1)} %get-tuple-element.189, f32[2304]{0:T(1024)} %get-tuple-element.190, ...), kind=kOutput, calls=%fused_computation.51.clone.1 | convolution fusion | flops 1367801856 | bytes 1413124 | tf_op jit(solution)/shard_map/while/body/eval_jaxpr/dot_general | solution.py:73
  299.7 1.6 slice_reduce_fusion.9
  302.0 6.1 %fusion.124 = f32[6,384,128]{2,1,0:T(8,128)S(1)} fusion(f32[6,384,128]{2,1,0:T(8,128)S(1)} %get-tuple-element.231, s32[]{:T(128)S(6)} %copy.39, f32[2304,128]{1,0:T(8,128)} %get-tuple-element.243, f32[2304]{0:T(1024)} %get-tuple-element.188, f32[384]{0:T(512)S(1)} %get-tuple-element.189, f32[2304]{0:T(1024)} %get-tuple-element.190, ...), kind=kOutput, calls=%fused_computation.51.clone.1 | convolution fusion | flops 1367801856 | bytes 1413124 | tf_op jit(solution)/shard_map/while/body/eval_jaxpr/dot_general | solution.py:73
  308.1 1.6 slice_reduce_fusion.9
  309.7 0.9 dynamic-slice_reduce_fusion.9
  310.6 6.1 %fusion.124 = f32[6,384,128]{2,1,0:T(8,128)S(1)} fusion(f32[6,384,128]{2,1,0:T(8,128)S(1)} %get-tuple-element.231, s32[]{:T(128)S(6)} %copy.39, f32[2304,128]{1,0:T(8,128)} %get-tuple-element.243, f32[2304]{0:T(1024)} %get-tuple-element.188, f32[384]{0:T(512)S(1)} %get-tuple-element.189, f32[2304]{0:T(1024)} %get-tuple-element.190, ...), kind=kOutput, calls=%fused_computation.51.clone.1 | convolution fusion | flops 1367801856 | bytes 1413124 | tf_op jit(solution)/shard_map/while/body/eval_jaxpr/dot_general | solution.py:73
  316.7 1.4 copy.27
  318.1 1.0 convolution_bitcast_fusion.5
  319.1 110.8 %psum.31 = f32[1,64,128]{2,1,0:T(8,128)S(1)} all-reduce(f32[1,64,128]{2,1,0:T(8,128)S(1)} %convolution_bitcast_fusion.5), channel_id=1, replica_groups=mesh['top'=2,'mid'=32,'leaf'=4] {'mid'}, use_global_device_ids=true, to_apply=%region_7.8 | all-reduce | flops 8192 | bytes 65536 | tf_op jit(solution)/shard_map/psum | solution.py:56
  429.9 35.0 %all_gather.23 = f32[2,64,128]{2,1,0:T(8,128)S(1)} all-gather(f32[1,64,128]{2,1,0:T(8,128)S(1)} %psum.31), channel_id=1, replica_groups=mesh['top'=2,'mid'=32,'leaf'=4] {'top'}, dimensions={0}, use_global_device_ids=true | all-gather | bytes 98304 | tf_op jit(solution)/shard_map/all_gather | solution.py:59
  464.9 9.7 %all-gather.2 = f32[256,128]{1,0:T(8,128)S(1)} all-gather(f32[64,128]{1,0:T(8,128)} %bitcast.166), channel_id=4, replica_groups=mesh['top'=2,'mid'=32,'leaf'=4] {'leaf'}, dimensions={0}, use_global_device_ids=true | all-gather | bytes 163840 | tf_op jit(solution)/shard_map/all_gather | solution.py:63
  474.5 1.7 convolution_bitcast_fusion.4
  476.3 1.9 convolution_bitcast_fusion.8
  478.2 2.8 convolution_bitcast_fusion.6
  481.0 0.9 fusion.69
  482.0 0.9 fusion.68
  482.9 2.4 fusion.67
  485.3 2.7 copy.28
  (68 shorter events, 4.5 us)
Async XLA Ops:
  6.5 68.8 %copy-start = (s32[2304,128]{1,0:T(8,128)S(1)}, s32[2304,128]{1,0:T(8,128)}, u32[]{:S(2)}) copy-start(s32[2304,128]{1,0:T(8,128)} %param.16) | copy-start | bytes 3538948
  6.5 18.4 %copy-start.1 = (f32[2304,128]{1,0:T(8,128)S(1)}, f32[2304,128]{1,0:T(8,128)}, u32[]{:S(2)}) copy-start(f32[2304,128]{1,0:T(8,128)} %param.15) | copy-start | bytes 3538948
  6.5 3.0 copy-start.11
  6.5 237.9 %all-gather.7.cloned.1.call-start = ((), (), s32[]{:S(2)}) async-start(), calls=%async_computation | async-start | bytes 1081344 | tf_op jit(solution)/shard_map/all_gather | solution.py:24
  9.0 0.6 copy-start.14
  24.8 453.3 %all-gather.9.cloned.1.call-start = ((), (), s32[]{:S(2)}) async-start(), calls=%async_computation.1 | async-start | bytes 1081344 | tf_op jit(solution)/shard_map/all_gather | solution.py:24
  73.8 1.4 copy-start.16
  79.3 164.7 %copy-start.8 = (f32[1,4,64,64]{3,2,1,0:T(8,128)S(1)}, f32[1,4,64,64]{3,2,1,0:T(8,128)}, u32[]{:S(2)}) copy-start(f32[1,4,64,64]{3,2,1,0:T(8,128)} %param.21) | copy-start | bytes 196612
  79.3 165.2 %copy-start.2 = (f32[1,32,64,64]{3,2,1,0:T(8,128)S(1)}, f32[1,32,64,64]{3,2,1,0:T(8,128)}, u32[]{:S(2)}) copy-start(f32[1,32,64,64]{3,2,1,0:T(8,128)} %param.22) | copy-start | bytes 1572868
  242.8 4.2 copy-start.19
  242.8 4.2 copy-start.17
  242.8 1.2 copy-start.21
  244.0 3.0 copy-start.9
  244.4 2.8 copy-start.12
  244.5 2.9 copy-start.3
  244.5 2.9 copy-start.5
  253.1 0.6 copy-start.15
  316.7 157.9 %copy-start.22 = (f32[2]{0:T(128)S(1)}, f32[2]{0:T(128)}, u32[]{:S(2)}) copy-start(f32[2]{0:T(128)} %copy-done.21) | copy-start | bytes 28
  316.7 159.6 %copy-start.20 = (f32[4]{0:T(128)S(1)}, f32[4]{0:T(128)}, u32[]{:S(2)}) copy-start(f32[4]{0:T(128)} %copy-done.19) | copy-start | bytes 52
  316.7 161.5 %copy-start.18 = (f32[32]{0:T(128)S(1)}, f32[32]{0:T(128)}, u32[]{:S(2)}) copy-start(f32[32]{0:T(128)} %copy-done.17) | copy-start | bytes 388
  464.9 18.0 %copy-start.7 = (f32[2304,128]{0,1:T(8,128)S(1)}, f32[2304,128]{0,1:T(8,128)}, u32[]{:S(2)}) copy-start(f32[2304,128]{0,1:T(8,128)} %copy.27) | copy-start | bytes 3538948
  478.2 2.9 copy-start.10
  478.2 3.8 copy-start.13
  478.2 4.7 copy-start.4
  478.2 4.7 copy-start.6
Sparse Core Ops, SparseCore 0:
  25.0 76.7 all-gather.6
  265.8 71.1 all-gather.8
where the time goes:
time: 498 us; the launch traced here: 495 us
  blocking collectives  343 us (69%)
  matrix products  93.6 us (19%)
  local copies, waits for them, and re-layouts  43.7 us (9%)
  between operations  13.8 us (3%)
    psum x2, blocking collectives, on_device(): s2 = lax.psum(jnp.einsum('ba,bo->ao', mid_move, s1, precision=hp), 'mid')  229 us
    dot_general x12, matrix products, near(): return jnp.dot(kernel_rows, current, precision=hp)  69.4 us
    all_gather x2, blocking collectives, on_device(): lax.all_gather(s2[None], 'top', axis=0, tiled=True)  68.5 us
    slice x24, local copies, waits for them, and re-layouts, near(): delta = row_points[axis_k][:, None] - coords[axis_k][None, :]  28.7 us
    psum x2, blocking collectives, on_device(): s1 = lax.psum(up0, 'leaf')  26.6 us
    all_gather x2, blocking collectives, on_device(): lax.all_gather(s0[None], 'leaf', axis=0, tiled=True)  19.1 us
    dot_general x6, matrix products, fold(): jnp.einsum('jab,jbo->ao', blocks * keep[:, None, None], piece, precision=...  10.4 us
  transfers between devices with their start and end apart: 2, of which 0 were waited for; matrix products, arithmetic and copies ran while one was open for 23% of the time, Pallas kernels for 0%

commit v1 on v0

v1 whole, which is shorter than its diff:
```python
import functools
import math

import jax
import jax.numpy as jnp
from jax import lax
from jax.experimental import pallas as pl
from jax.experimental.pallas import tpu as pltpu
from jax.sharding import PartitionSpec as P

STEPS = 2
RANK = 64
OUT = 128
N_MID = 32
N_LEAF = 4
QROWS = RANK // N_LEAF
QCOLS = OUT // N_LEAF
HP = lax.Precision.HIGHEST
F32 = jnp.float32
BF16 = jnp.bfloat16
LOG2E = math.log2(math.e)
CHUNKS = 3
BLOCK = 256
TILE = 32
VMEM = pl.BlockSpec(memory_space=pltpu.VMEM)


def split(x):
    hi = x.astype(BF16)
    return hi, (x - hi.astype(F32)).astype(BF16)


def wide(x):
    return jnp.concatenate(split(x), axis=1)


def dot3(tall, wide_rhs):
    d = jnp.dot(tall, wide_rhs, preferred_element_type=F32)
    m, n = d.shape[0] // 2, d.shape[1] // 2
    return d[:m, :n] + (d[:m, n:] + d[m:, :n])


def lane_group():
    return lax.broadcasted_iota(jnp.int32, (QROWS, OUT), 1) // QCOLS


def pack_quarter(full, quarter):
    group = lane_group()
    out = jnp.zeros((QROWS, OUT), F32)
    for k in range(N_LEAF):
        moved = pltpu.roll(
            full[k * QROWS : (k + 1) * QROWS], lax.rem((k - quarter + N_LEAF) * QCOLS, OUT), 1
        )
        out = jnp.where(group == k, moved, out)
    return out


def expand_packed(packed):
    group = lane_group()
    zero = jnp.zeros((QROWS, OUT), F32)
    return jnp.concatenate([jnp.where(group == k, packed, zero) for k in range(N_LEAF)], axis=0)


def fold_and_pack(grouped):
    both = grouped + pltpu.roll(grouped, 2 * QCOLS, 1)
    total = both + pltpu.roll(both, QCOLS, 1)
    group = lane_group()
    out = jnp.zeros((QROWS, OUT), F32)
    for k in range(N_LEAF):
        out = jnp.where(group == k, total[k * QROWS : (k + 1) * QROWS], out)
    return out


def unpack_quarters(packed, quarters):
    group = lane_group()
    rows = []
    for k in range(N_LEAF):
        out = jnp.zeros((QROWS, OUT), F32)
        for block, quarter in zip(packed, quarters):
            moved = pltpu.roll(block, lax.rem((quarter - k + N_LEAF) * QCOLS, OUT), 1)
            out = jnp.where(group == quarter, moved, out)
        rows.append(out)
    return jnp.concatenate(rows, axis=0)


def emit_messages(s0, move, own_ref, message_refs):
    own = lax.axis_index("leaf")
    up0 = lax.dot_general(
        move, s0, (((0,), (0,)), ((), ())), precision=HP, preferred_element_type=F32
    )
    own_ref[...] = pack_quarter(up0, own)
    for k, ref in enumerate(message_refs, 1):
        ref[0:RANK, :] = s0
        ref[RANK : RANK + QROWS, :] = pack_quarter(up0, lax.rem(own + k, N_LEAF))


def first_body(basis_ref, w_ref, move_ref, bcat_ref, bcat_t_ref, whl_ref, own_ref, *message_refs):
    bcat_ref[...] = wide(basis_ref[...])
    whl_ref[...] = wide(w_ref[...])
    bcat_t_ref[...] = bcat_ref[...].T
    s0 = dot3(bcat_t_ref[...], whl_ref[...])
    emit_messages(s0, move_ref[...], own_ref, message_refs)


def near_rows(khi_ref, klo_ref, whl_ref, scale):
    a = jnp.dot(khi_ref[...], whl_ref[...], preferred_element_type=F32)
    b = jnp.dot(klo_ref[...], whl_ref[:, 0:OUT], preferred_element_type=F32)
    return (a[:, :OUT] + (a[:, OUT:] + b)) * scale


def build_body(scale, rows_ref, coords_ref, whl_ref, khi_ref, klo_ref, near_ref):
    points = coords_ref.shape[1]

    def tile(i, carry):
        rows = pl.ds(pl.multiple_of(i * TILE, TILE), TILE)
        own = rows_ref[rows, :]
        own = [jnp.broadcast_to(own[:, k : k + 1], (TILE, BLOCK)) for k in range(3)]
        for j in range(points // BLOCK):
            cols = slice(j * BLOCK, (j + 1) * BLOCK)
            diff_sq = None
            for k in range(3):
                delta = own[k] - coords_ref[k : k + 1, cols]
                diff_sq = delta * delta if diff_sq is None else diff_sq + delta * delta
            dist = diff_sq * lax.rsqrt(jnp.maximum(diff_sq, 1e-37))
            hi, lo = split(jnp.exp2(-dist))
            khi_ref[rows, cols] = hi
            klo_ref[rows, cols] = lo
        return carry

    lax.fori_loop(0, BLOCK // TILE, tile, 0)
    near_ref[...] = near_rows(khi_ref, klo_ref, whl_ref, scale)


def near_body(scale, khi_ref, klo_ref, whl_ref, near_ref):
    near_ref[...] = near_rows(khi_ref, klo_ref, whl_ref, scale)


def middle_body(own_ref, m1_ref, m2_ref, m3_ref, move_ref, out_ref):
    tail = slice(RANK, RANK + QROWS)
    s1 = (own_ref[...] + m1_ref[tail, :]) + (m2_ref[tail, :] + m3_ref[tail, :])
    up1 = lax.dot_general(
        move_ref[...], expand_packed(s1), (((0,), (0,)), ((), ())),
        precision=HP, preferred_element_type=F32,
    )
    message = jnp.concatenate([s1, fold_and_pack(up1)], axis=0)
    out_ref[...] = jnp.broadcast_to(message[None], out_ref.shape)


def couple_body(got_ref, couple_ref, g1_ref, s2_ref, spread_ref):
    s2 = jnp.zeros((QROWS, OUT), F32)
    for m in range(N_MID):
        spread_ref[m * RANK : (m + 1) * RANK, :] = wide(expand_packed(got_ref[m, 0:QROWS, :]))
        s2 = s2 + got_ref[m, QROWS:, :]
    g1_ref[...] = fold_and_pack(dot3(couple_ref[...], spread_ref[...]))
    s2_ref[...] = s2


def update_body(last, near_refs, far, w_ref, targets_ref, bcat_ref, bcat_t_ref, move_ref, outs):
    m1_ref, m2_ref, m3_ref, down_ref, tops = far
    own = lax.axis_index("leaf")
    quarters = [lax.rem(own + N_LEAF - k, N_LEAF) for k in range(N_LEAF)]
    g1 = unpack_quarters([ref[0:QROWS, :] for ref in tops], quarters)
    s2 = unpack_quarters([ref[QROWS:, :] for ref in tops], quarters)
    parts = [ref[0:RANK, :] for ref in (m1_ref, m2_ref, m3_ref)] + [g1, s2]
    g0 = dot3(down_ref[...], wide(jnp.concatenate(parts, axis=0)))
    hi, lo = split(g0)
    rhs = jnp.concatenate(
        [jnp.concatenate([hi, lo], axis=1), jnp.concatenate([hi, jnp.zeros_like(lo)], axis=1)], axis=0
    )
    chunk = near_refs[0].shape[0]
    w_out = outs[0]
    for j in range(w_ref.shape[0] // BLOCK):
        rows = slice(j * BLOCK, (j + 1) * BLOCK)
        at = j * BLOCK % chunk
        f = jnp.dot(bcat_ref[rows, :], rhs, preferred_element_type=F32)
        f = near_refs[j * BLOCK // chunk][at : at + BLOCK, :] + (f[:, :OUT] + f[:, OUT:])
        new = w_ref[rows, :] - ((0.5 * jnp.tanh(0.5 * f) + 0.5) - targets_ref[rows, :])
        w_out[rows, :] = new
        if not last:
            outs[1][rows, :] = wide(new)
    if not last:
        s0 = dot3(bcat_t_ref[...], outs[1][...])
        emit_messages(s0, move_ref[...], outs[2], outs[3:])


def update_mid_body(*refs):
    near, m, (down, *tops), rest = refs[:3], refs[3:6], refs[6:11], refs[11:]
    update_body(False, near, (*m, down, tops), *rest[:5], rest[5:])


def update_last_body(*refs):
    near, m, (down, *tops), rest = refs[:3], refs[3:6], refs[6:11], refs[11:]
    update_body(True, near, (*m, down, tops), rest[0], rest[1], rest[2], None, None, rest[3:])


def params(mib):
    return pltpu.CompilerParams(vmem_limit_bytes=mib << 20)


def shape(*dims, dtype=F32):
    return jax.ShapeDtypeStruct(dims, dtype)


def ring(k):
    return [(i, (i + k) % N_LEAF) for i in range(N_LEAF)]


def tall(x):
    hi = lax.reduce_precision(x, 8, 7)
    return jnp.concatenate([hi, x - hi], axis=0).astype(BF16)


def on_device(
    coords,
    weights,
    labels,
    order,
    basis,
    transfer_leaf,
    transfer_mid,
    couple_leaf,
    couple_mid,
    couple_top,
):
    n = weights.shape[0]
    chunk = n // CHUNKS
    scale = 4.0 / math.sqrt(n)
    own_top = lax.axis_index("top")
    own_mid = lax.axis_index("mid")
    own_leaf = lax.axis_index("leaf")
    leaf_move = transfer_leaf[0]
    mid_move = transfer_mid[0]
    message_shapes = [shape(QROWS, OUT)] + [shape(RANK + QROWS, OUT)] * 3

    bcat, bcat_t, whl, own, *messages = pl.pallas_call(
        first_body,
        out_shape=[
            shape(n, 2 * RANK, dtype=BF16),
            shape(2 * RANK, n, dtype=BF16),
            shape(n, 2 * OUT, dtype=BF16),
            *message_shapes,
        ],
        in_specs=[VMEM] * 3,
        out_specs=[VMEM] * 7,
        compiler_params=params(16),
        name="first",
    )(basis, weights, leaf_move)

    targets = jnp.take(labels, order[0], axis=0).astype(F32)
    keep = (jnp.arange(N_MID) != own_mid).astype(F32)
    couple = tall(
        jnp.transpose(couple_mid[0] * keep[:, None, None], (1, 0, 2)).reshape(RANK, N_MID * RANK)
    )
    from_top = jnp.dot(
        leaf_move, jnp.dot(mid_move, couple_top[0, 1 - own_top], precision=HP), precision=HP
    )
    siblings = [couple_leaf[0, (own_leaf + N_LEAF - k) % N_LEAF] for k in (1, 2, 3)]
    down = tall(jnp.concatenate([*siblings, leaf_move, from_top], axis=1))

    scaled = coords * LOG2E
    scaled_rows = scaled.T
    blocks = chunk // BLOCK
    k_spec = pl.BlockSpec((BLOCK, n), lambda i: (i, 0))
    whl_spec = pl.BlockSpec((n, 2 * OUT), lambda i: (0, 0))
    near_spec = pl.BlockSpec((BLOCK, OUT), lambda i: (i, 0))
    kernels, near = [], []
    for c in range(CHUNKS):
        khi, klo, rows = pl.pallas_call(
            functools.partial(build_body, scale),
            grid=(blocks,),
            out_shape=[shape(chunk, n, dtype=BF16)] * 2 + [shape(chunk, OUT)],
            in_specs=[
                pl.BlockSpec((BLOCK, 3), lambda i, c=c: (c * blocks + i, 0)),
                pl.BlockSpec((3, n), lambda i: (0, 0)),
                whl_spec,
            ],
            out_specs=[k_spec, k_spec, near_spec],
            compiler_params=params(16),
            cost_estimate=pl.CostEstimate(
                flops=chunk * n * 2 * 512, bytes_accessed=chunk * n * 4, transcendentals=2 * chunk * n
            ),
            name="build",
        )(scaled_rows, scaled, whl)
        kernels.append((khi, klo))
        near.append(rows)

    current = weights
    for step in range(STEPS):
        last = step == STEPS - 1
        if step:
            near = [
                pl.pallas_call(
                    functools.partial(near_body, scale),
                    grid=(blocks,),
                    out_shape=shape(chunk, OUT),
                    in_specs=[k_spec, k_spec, whl_spec],
                    out_specs=near_spec,
                    compiler_params=params(16),
                    cost_estimate=pl.CostEstimate(
                        flops=chunk * n * 2 * 512, bytes_accessed=chunk * n * 4, transcendentals=0
                    ),
                    name="near",
                )(khi, klo, whl)
                for khi, klo in kernels
            ]
        messages = [lax.ppermute(m, "leaf", ring(k)) for k, m in enumerate(messages, 1)]
        spread = pl.pallas_call(
            middle_body,
            out_shape=shape(N_MID, 2 * QROWS, OUT),
            in_specs=[VMEM] * 5,
            out_specs=VMEM,
            name="middle",
        )(own, *messages, mid_move)
        got = lax.all_to_all(spread, "mid", 0, 0)
        g1, s2 = pl.pallas_call(
            couple_body,
            out_shape=[shape(QROWS, OUT)] * 2,
            in_specs=[VMEM] * 2,
            out_specs=[VMEM] * 2,
            scratch_shapes=[pltpu.VMEM((N_MID * RANK, 2 * OUT), BF16)],
            compiler_params=params(16),
            name="couple",
        )(got, couple)
        s2 = lax.ppermute(s2, "top", [(0, 1), (1, 0)])
        top = jnp.concatenate([g1, s2], axis=0)
        tops = [top] + [lax.ppermute(top, "leaf", ring(k)) for k in (1, 2, 3)]
        far = (*near, *messages, down, *tops, current, targets, bcat)
        if last:
            current = pl.pallas_call(
                update_last_body,
                out_shape=shape(n, OUT),
                in_specs=[VMEM] * 14,
                out_specs=VMEM,
                compiler_params=params(16),
                name="last",
            )(*far)
        else:
            current, whl, own, *messages = pl.pallas_call(
                update_mid_body,
                out_shape=[shape(n, OUT), shape(n, 2 * OUT, dtype=BF16), *message_shapes],
                in_specs=[VMEM] * 16,
                out_specs=[VMEM] * 6,
                compiler_params=params(16),
                name="update",
            )(*far, bcat_t, leaf_move)
    return current


def solution(mesh):
    placed = (
        P(None, ("top", "mid", "leaf")),
        P(("top", "mid", "leaf"), None),
        P(("top", "mid", "leaf"), None),
        P(("top", "mid", "leaf"), None),
        P(("top", "mid", "leaf"), None),
        P(("top", "mid", "leaf"), None, None),
        P(("top", "mid"), None, None),
        P(("top", "mid", "leaf"), None, None, None),
        P(("top", "mid"), None, None, None),
        P("top", None, None, None),
    )
    return jax.shard_map(
        on_device,
        mesh=mesh,
        in_specs=placed,
        out_specs=P(("top", "mid", "leaf"), None),
        check_vma=False,
    )
```

time: 498 us -> 152 us (0.31)
  blocking collectives: 343 us -> 0 us
  matrix products: 93.6 us -> 0.43 us
  Pallas kernels: 0 us -> 43.3 us
  starting transfers between devices: 0.04 us -> 38.9 us
  waiting for transfers between devices: 0.05 us -> 18.2 us
  between operations: 13.8 us -> 0.58 us
    psum x4 -> x0, blocking collectives: 256 us -> none  [the longest x2 229 us: on_device(): s2 = lax.psum(jnp.einsum('ba,bo->ao', mid_move, s1, precision=hp), 'mid')]
    dot_general x30 -> x2, matrix products: 93.6 us -> 0.43 us  [the longest x1 0.24 us: on_device(): jnp.dot(mid_move, couple_top[0, 1 - own_top], precision=HP)]
    all_gather x4 -> x0, blocking collectives: 87.7 us -> none  [the longest x2 68.5 us: on_device(): lax.all_gather(s2[None], 'top', axis=0, tiled=True)]
    pallas_call x0 -> x13, Pallas kernels: none -> 43.3 us  [the longest x3 24.5 us: on_device(): pl.pallas_call(functools.partial(build_body, scale), grid=(blocks,), out_...]
    unnamed x47 -> x109, local copies, waits for them, and re-layouts: 2.69 us -> 37.9 us
    slice x24 -> x0, local copies, waits for them, and re-layouts: 28.7 us -> none  [near(): delta = row_points[axis_k][:, None] - coords[axis_k][None, :]]
    ppermute x0 -> x14, starting transfers between devices: none -> 23.3 us  [the longest x2 9.76 us: on_device(): s2 = lax.ppermute(s2, 'top', [(0, 1), (1, 0)])]
    all_to_all x0 -> x2, starting transfers between devices: none -> 15.7 us  [on_device(): got = lax.all_to_all(spread, 'mid', 0, 0)]
  transfers between devices with their start and end apart: 2 -> 16, of which waited for: 0 -> 9; matrix products, arithmetic and copies ran while one was open for 23% -> 8% of each run, Pallas kernels for 0% -> 21%
where the time goes in v1:
time: 152 us; the launch traced here: 151 us
  local copies, waits for them, and re-layouts  44.5 us (29%)
  Pallas kernels  43.3 us (28%)
  starting transfers between devices  38.9 us (26%)
  waiting for transfers between devices  18.2 us (12%)
  other arithmetic  4.84 us (3%)
    unnamed x109, local copies, waits for them, and re-layouts  37.9 us
    pallas_call x3, Pallas kernels, on_device(): pl.pallas_call(functools.partial(build_body, scale), grid=(blocks,), out_...  24.5 us
    all_to_all x2, starting transfers between devices, on_device(): got = lax.all_to_all(spread, 'mid', 0, 0)  15.7 us
    all_to_all x2, waiting for transfers between devices, on_device(): got = lax.all_to_all(spread, 'mid', 0, 0)  10.2 us
    ppermute x2, starting transfers between devices, on_device(): s2 = lax.ppermute(s2, 'top', [(0, 1), (1, 0)])  9.76 us
    ppermute x6, starting transfers between devices, on_device(): lax.ppermute(m, 'leaf', ring(k))  8.49 us
    pallas_call x3, Pallas kernels, on_device(): pl.pallas_call(functools.partial(near_body, scale), grid=(blocks,), out_s...  7.06 us
    gather x1, local copies, waits for them, and re-layouts, on_device(): targets = jnp.take(labels, order[0], axis=0).astype(F32)  5.1 us
  transfers between devices with their start and end apart: 16, of which 9 were waited for; matrix products, arithmetic and copies ran while one was open for 8% of the time, Pallas kernels for 21%

profile of v1, /device:TPU:1, one launch (start us, length us, event | category | flops | bytes accessed | tf_op | source)
XLA Modules:
  0.0 150.8 jit_solution(9949139087886517978)
XLA Ops:
  0.0 1.6 %copy.16.basis_ref = f32[2304,64]{1,0:T(8,128)S(1)} copy(f32[2304,64]{0,1:T(8,128)} %param.14) | data formatting | bytes 1179648 | tf_op args[4]
  1.6 0.7 copy-done.30
  2.4 1.6 %first.1 = (bf16[2304,128]{1,0:T(8,128)(2,1)S(1)}, bf16[128,2304]{1,0:T(8,128)(2,1)S(1)}, bf16[2304,256]{1,0:T(8,128)(2,1)S(1)}, f32[16,128]{1,0:T(8,128)S(1)}, ...) custom-call(f32[2304,64]{1,0:T(8,128)S(1)} %copy.16.basis_ref, f32[2304,128]{1,0:T(8,128)S(1)} %copy-done.1, ...), custom_call_target="tpu_custom_call" | custom-call | tf_op jit(solution)/shard_map/first/pallas_call | solution.py:235
  4.0 0.8 copy-done.17
  4.8 0.8 copy-done.28
  6.2 1.0 copy-done.47
  7.2 2.1 %collective-permute-start = (f32[80,128]{1,0:T(8,128)}, f32[80,128]{1,0:T(8,128)S(1)}, u32[]{:S(2)}, u32[]{:S(2)}) collective-permute-start(f32[80,128]{1,0:T(8,128)} %get-tuple-element.37), channel_id=1, source_target_pairs={{0,1},{1,2},{2,3},{3,0},{4,5},{5,6},{6,7},{7,4},{8,9},{9,10},{10,1... | collective-permute-start | bytes 122888 | tf_op jit(solution)/shard_map/ppermute | solution.py:306
  9.3 2.6 %collective-permute-start.1 = (f32[80,128]{1,0:T(8,128)}, f32[80,128]{1,0:T(8,128)S(1)}, u32[]{:S(2)}, u32[]{:S(2)}) collective-permute-start(f32[80,128]{1,0:T(8,128)} %get-tuple-element.38), channel_id=1, source_target_pairs={{0,2},{1,3},{2,0},{3,1},{4,6},{5,7},{6,4},{7,5},{8,10},{9,11},{10,... | collective-permute-start | bytes 122888 | tf_op jit(solution)/shard_map/ppermute | solution.py:306
  12.0 1.1 collective-permute-start.2
  13.0 0.8 broadcast_multiply_fusion
  14.2 1.3 copy-done.48
  15.5 8.2 %build.5 = (bf16[768,2304]{1,0:T(8,128)(2,1)S(1)}, bf16[768,2304]{1,0:T(8,128)(2,1)S(1)}, f32[768,128]{1,0:T(8,128)S(1)}) custom-call(f32[2304,3]{1,0:T(8,128)S(1)} %copy.17.rows_ref, f32[3,2304]{1,0:T(4,128)S(1)} %get-tuple-element.64.coords_ref, bf16[2304,256]{1,0:T(8,128)(2,1)S(1)} %copy-done.48), custom_call_target="tpu_custom_call" | custom-call | flops 1811939328 | bytes 7077888 | tf_op jit(solution)/shard_map/build/pallas_call | solution.py:268
  23.7 1.7 %copy-done.9 = bf16[768,2304]{1,0:T(8,128)(2,1)} copy-done((bf16[768,2304]{1,0:T(8,128)(2,1)}, bf16[768,2304]{1,0:T(8,128)(2,1)S(1)}, u32[]{:S(2)}) %copy-start.9) | copy-done | bytes 3538968
  25.4 1.8 %copy-done.11 = bf16[768,2304]{1,0:T(8,128)(2,1)} copy-done((bf16[768,2304]{1,0:T(8,128)(2,1)}, bf16[768,2304]{1,0:T(8,128)(2,1)S(1)}, u32[]{:S(2)}) %copy-start.11) | copy-done | bytes 3538968
  27.3 8.2 %build.4 = (bf16[768,2304]{1,0:T(8,128)(2,1)S(1)}, bf16[768,2304]{1,0:T(8,128)(2,1)S(1)}, f32[768,128]{1,0:T(8,128)S(1)}) custom-call(f32[2304,3]{1,0:T(8,128)S(1)} %copy.17.rows_ref, f32[3,2304]{1,0:T(4,128)S(1)} %get-tuple-element.64.coords_ref, bf16[2304,256]{1,0:T(8,128)(2,1)S(1)} %copy-done.48), custom_call_target="tpu_custom_call" | custom-call | flops 1811939328 | bytes 7077888 | tf_op jit(solution)/shard_map/build/pallas_call | solution.py:268
  35.5 1.8 %copy-done.13 = bf16[768,2304]{1,0:T(8,128)(2,1)} copy-done((bf16[768,2304]{1,0:T(8,128)(2,1)}, bf16[768,2304]{1,0:T(8,128)(2,1)S(1)}, u32[]{:S(2)}) %copy-start.13) | copy-done | bytes 3538968
  37.3 1.8 %copy-done.15 = bf16[768,2304]{1,0:T(8,128)(2,1)} copy-done((bf16[768,2304]{1,0:T(8,128)(2,1)}, bf16[768,2304]{1,0:T(8,128)(2,1)S(1)}, u32[]{:S(2)}) %copy-start.15) | copy-done | bytes 3538968
  39.1 0.8 copy-done.35
  39.9 8.2 %build.3 = (bf16[768,2304]{1,0:T(8,128)(2,1)S(1)}, bf16[768,2304]{1,0:T(8,128)(2,1)S(1)}, f32[768,128]{1,0:T(8,128)S(1)}) custom-call(f32[2304,3]{1,0:T(8,128)S(1)} %copy.17.rows_ref, f32[3,2304]{1,0:T(4,128)S(1)} %get-tuple-element.64.coords_ref, bf16[2304,256]{1,0:T(8,128)(2,1)S(1)} %copy-done.48), custom_call_target="tpu_custom_call" | custom-call | flops 1811939328 | bytes 7077888 | tf_op jit(solution)/shard_map/build/pallas_call | solution.py:268
  48.1 1.7 %copy-done.5 = bf16[768,2304]{1,0:T(8,128)(2,1)} copy-done((bf16[768,2304]{1,0:T(8,128)(2,1)}, bf16[768,2304]{1,0:T(8,128)(2,1)S(1)}, u32[]{:S(2)}) %copy-start.5) | copy-done | bytes 3538968
  49.9 1.8 %copy-done.7 = bf16[768,2304]{1,0:T(8,128)(2,1)} copy-done((bf16[768,2304]{1,0:T(8,128)(2,1)}, bf16[768,2304]{1,0:T(8,128)(2,1)S(1)}, u32[]{:S(2)}) %copy-start.7) | copy-done | bytes 3538968
  51.7 0.8 copy-done.37
  53.1 1.4 fusion
  54.5 0.6 copy.20
  56.3 2.0 %middle.2 = f32[32,32,128]{2,1,0:T(8,128)} custom-call(f32[16,128]{1,0:T(8,128)} %copy-done.45, f32[80,128]{1,0:T(8,128)} %copy-done.39, f32[80,128]{1,0:T(8,128)} %copy-done.41, f32[80,128]{1,0:T(8,128)} %copy-done.43, f32[64,64]{1,0:T(8,128)} %bitcast.31), custom_call_target="tpu_custom_call" | custom-call | tf_op jit(solution)/shard_map/middle/pallas_call | solution.py:307
  58.3 11.0 %all-to-all-start = ((f32[32,32,128]{2,1,0:T(8,128)}), f32[32,32,128]{2,1,0:T(8,128)S(1)}, u32[]{:S(2)}, u32[]{:S(2)}) async-start(f32[32,32,128]{2,1,0:T(8,128)} %middle.2), calls=%async_computation | async-start | bytes 1048576 | tf_op jit(solution)/shard_map/all_to_all | solution.py:314
  69.4 5.1 %gather_fusion = s32[2304,128]{1,0:T(8,128)} fusion(s32[2304,128]{1,0:T(8,128)S(1)} %copy-done, s32[3072]{0:T(1024)S(1)} %pad_clamp_fusion), kind=kCustom, calls=%fused_computation | custom fusion | bytes 2368512 | tf_op jit(solution)/shard_map/jit(_take)/gather | solution.py:249
  74.5 2.5 %select_convert_fusion.refs_12_ = f32[2304,128]{1,0:T(8,128)S(1)} fusion(s32[2304,128]{1,0:T(8,128)} %gather_fusion, pred[2304]{0:T(1024)(128)(4,1)S(1)} %compare_and_fusion), kind=kLoop, calls=%fused_computation.1 | loop fusion | flops 589824 | bytes 2361600 | tf_op jit(solution)/shard_map/convert_element_type | solution.py:249
  77.0 7.5 %all-to-all-done.got_ref = f32[32,32,128]{2,1,0:T(8,128)S(1)} async-done(((f32[32,32,128]{2,1,0:T(8,128)}), f32[32,32,128]{2,1,0:T(8,128)S(1)}, u32[]{:S(2)}, u32[]{:S(2)}) %all-to-all-start) | async-done | bytes 524320 | tf_op jit(solution)/shard_map/all_to_all | solution.py:314
  85.0 3.7 %collective-permute-start.3 = (f32[16,128]{1,0:T(8,128)S(1)}, f32[16,128]{1,0:T(8,128)S(1)}, u32[]{:S(2)}, u32[]{:S(2)}) collective-permute-start(f32[16,128]{1,0:T(8,128)S(1)} %get-tuple-element.42), channel_id=1, source_target_pairs={{0,128},{128,0},{1,129},{129,1},{2,130},{130,2},{3,131},{131,3},{4... | collective-permute-start | bytes 24584 | tf_op jit(solution)/shard_map/ppermute | solution.py:324
  88.8 0.8 collective-permute-done.3
  89.6 2.2 %collective-permute-start.5 = (f32[32,128]{1,0:T(8,128)S(1)}, f32[32,128]{1,0:T(8,128)S(1)}, u32[]{:S(2)}, u32[]{:S(2)}) collective-permute-start(f32[32,128]{1,0:T(8,128)S(1)} %constant_dynamic-update-slice_fusion.refs_7_), channel_id=1, source_target_pairs={{0,2},{1,3},{2,0},{3,1},{4,6},{5,7},{6,4},{7,5},{8,10},{9,11},{10,... | collective-permute-start | bytes 49160 | tf_op jit(solution)/shard_map/ppermute | solution.py:326
  92.2 1.5 collective-permute-done.5.refs_9_
  93.7 1.9 %collective-permute-done.4.refs_8_ = f32[32,128]{1,0:T(8,128)S(1)} collective-permute-done((f32[32,128]{1,0:T(8,128)S(1)}, f32[32,128]{1,0:T(8,128)S(1)}, u32[]{:S(2)}, u32[]{:S(2)}) %collective-permute-start.4) | collective-permute-done | bytes 16416 | tf_op jit(solution)/shard_map/ppermute | solution.py:326
  95.6 1.1 copy-done.18
  96.7 1.1 copy-done.29
  97.7 1.0 copy-done.34
  98.7 1.0 copy-done.36
  99.7 1.0 copy-done.38
  100.7 0.8 copy-done.44
  101.5 1.5 update.1
  103.0 1.0 copy-done.24
  104.6 1.6 %collective-permute-start.8 = (f32[80,128]{1,0:T(8,128)S(1)}, f32[80,128]{1,0:T(8,128)}, u32[]{:S(2)}, u32[]{:S(2)}) collective-permute-start(f32[80,128]{1,0:T(8,128)S(1)} %get-tuple-element.51), channel_id=1, source_target_pairs={{0,2},{1,3},{2,0},{3,1},{4,6},{5,7},{6,4},{7,5},{8,10},{9,11},{10,... | collective-permute-start | bytes 122888 | tf_op jit(solution)/shard_map/ppermute | solution.py:306
  106.3 1.0 collective-permute-start.9
  107.3 1.9 %collective-permute-done.7.m1_ref.refs_3_ = f32[80,128]{1,0:T(8,128)} collective-permute-done((f32[80,128]{1,0:T(8,128)S(1)}, f32[80,128]{1,0:T(8,128)}, u32[]{:S(2)}, u32[]{:S(2)}) %collective-permute-start.7) | collective-permute-done | bytes 40992 | tf_op jit(solution)/shard_map/ppermute | solution.py:306
  109.8 2.0 %middle.3 = f32[32,32,128]{2,1,0:T(8,128)} custom-call(f32[16,128]{1,0:T(8,128)} %copy-done.46, f32[80,128]{1,0:T(8,128)} %collective-permute-done.7.m1_ref.refs_3_, f32[80,128]{1,0:T(8,128)} %collective-permute-done.8.m2_ref.refs_4_, f32[80,128]{1,0:T(8,128)} %collective-permute-done.9.m3_ref.refs_5_, f32[64,64]{1,0:T(8,128)} %bitcast.32), custom_call_target="tpu_custom_call" | custom-call | tf_op jit(solution)/shard_map/middle/pallas_call | solution.py:307
  111.8 4.6 %all-to-all-start.1 = ((f32[32,32,128]{2,1,0:T(8,128)}), f32[32,32,128]{2,1,0:T(8,128)}, u32[]{:S(2)}, u32[]{:S(2)}) async-start(f32[32,32,128]{2,1,0:T(8,128)} %middle.3), calls=%async_computation.1 | async-start | bytes 1048576 | tf_op jit(solution)/shard_map/all_to_all | solution.py:314
  116.5 2.0 %copy-done.10 = bf16[768,2304]{1,0:T(8,128)(2,1)S(1)} copy-done((bf16[768,2304]{1,0:T(8,128)(2,1)S(1)}, bf16[768,2304]{1,0:T(8,128)(2,1)}, u32[]{:S(2)}) %copy-start.10) | copy-done | bytes 3538968
  118.5 2.0 %copy-done.12 = bf16[768,2304]{1,0:T(8,128)(2,1)S(1)} copy-done((bf16[768,2304]{1,0:T(8,128)(2,1)S(1)}, bf16[768,2304]{1,0:T(8,128)(2,1)}, u32[]{:S(2)}) %copy-start.12) | copy-done | bytes 3538968
  120.5 2.3 %near.5.refs_2_ = f32[768,128]{1,0:T(8,128)S(1)} custom-call(bf16[768,2304]{1,0:T(8,128)(2,1)S(1)} %copy-done.10, bf16[768,2304]{1,0:T(8,128)(2,1)S(1)} %copy-done.12, bf16[2304,256]{1,0:T(8,128)(2,1)S(1)} %get-tuple-element.45.whl_ref), custom_call_target="tpu_custom_call" | custom-call | flops 1811939328 | bytes 7077888 | tf_op jit(solution)/shard_map/near/pallas_call | solution.py:292
  122.8 0.7 copy-done.20
  123.6 2.3 %near.4.refs_1_ = f32[768,128]{1,0:T(8,128)S(1)} custom-call(bf16[768,2304]{1,0:T(8,128)(2,1)S(1)} %copy-done.14, bf16[768,2304]{1,0:T(8,128)(2,1)S(1)} %copy-done.16, bf16[2304,256]{1,0:T(8,128)(2,1)S(1)} %get-tuple-element.45.whl_ref), custom_call_target="tpu_custom_call" | custom-call | flops 1811939328 | bytes 7077888 | tf_op jit(solution)/shard_map/near/pallas_call | solution.py:292
  125.9 0.7 copy-done.22
  126.7 2.7 %all-to-all-done.1.got_ref = f32[32,32,128]{2,1,0:T(8,128)} async-done(((f32[32,32,128]{2,1,0:T(8,128)}), f32[32,32,128]{2,1,0:T(8,128)}, u32[]{:S(2)}, u32[]{:S(2)}) %all-to-all-start.1) | async-done | bytes 524320 | tf_op jit(solution)/shard_map/all_to_all | solution.py:314
  129.4 1.0 copy-done.4
  130.5 1.5 %couple.3 = (f32[16,128]{1,0:T(8,128)S(1)}, f32[16,128]{1,0:T(8,128)S(1)}) custom-call(f32[32,32,128]{2,1,0:T(8,128)} %all-to-all-done.1.got_ref, bf16[128,2048]{1,0:T(8,128)(2,1)S(1)} %copy-done.4), custom_call_target="tpu_custom_call" | custom-call | tf_op jit(solution)/shard_map/couple/pallas_call | solution.py:315
  132.0 6.0 %collective-permute-start.10 = (f32[16,128]{1,0:T(8,128)S(1)}, f32[16,128]{1,0:T(8,128)S(1)}, u32[]{:S(2)}, u32[]{:S(2)}) collective-permute-start(f32[16,128]{1,0:T(8,128)S(1)} %get-tuple-element.55), channel_id=1, source_target_pairs={{0,128},{128,0},{1,129},{129,1},{2,130},{130,2},{3,131},{131,3},{4... | collective-permute-start | bytes 24584 | tf_op jit(solution)/shard_map/ppermute | solution.py:324
  138.0 0.8 collective-permute-done.10
  138.8 2.1 %collective-permute-start.13 = (f32[32,128]{1,0:T(8,128)S(1)}, f32[32,128]{1,0:T(8,128)S(1)}, u32[]{:S(2)}, u32[]{:S(2)}) collective-permute-start(f32[32,128]{1,0:T(8,128)S(1)} %constant_dynamic-update-slice_fusion.2.refs_7_), channel_id=1, source_target_pairs={{0,3},{1,0},{2,1},{3,2},{4,7},{5,4},{6,5},{7,6},{8,11},{9,8},{10,9... | collective-permute-start | bytes 49160 | tf_op jit(solution)/shard_map/ppermute | solution.py:326
  140.9 0.7 collective-permute-start.12
  141.7 2.0 %copy-done.6 = bf16[768,2304]{1,0:T(8,128)(2,1)S(1)} copy-done((bf16[768,2304]{1,0:T(8,128)(2,1)S(1)}, bf16[768,2304]{1,0:T(8,128)(2,1)}, u32[]{:S(2)}) %copy-start.6) | copy-done | bytes 3538968
  143.7 2.0 %copy-done.8 = bf16[768,2304]{1,0:T(8,128)(2,1)S(1)} copy-done((bf16[768,2304]{1,0:T(8,128)(2,1)S(1)}, bf16[768,2304]{1,0:T(8,128)(2,1)}, u32[]{:S(2)}) %copy-start.8) | copy-done | bytes 3538968
  145.7 2.4 %near.3.refs_0_ = f32[768,128]{1,0:T(8,128)S(1)} custom-call(bf16[768,2304]{1,0:T(8,128)(2,1)S(1)} %copy-done.6, bf16[768,2304]{1,0:T(8,128)(2,1)S(1)} %copy-done.8, bf16[2304,256]{1,0:T(8,128)(2,1)S(1)} %get-tuple-element.45.whl_ref), custom_call_target="tpu_custom_call" | custom-call | flops 1811939328 | bytes 7077888 | tf_op jit(solution)/shard_map/near/pallas_call | solution.py:292
  148.1 2.6 %last.1 = f32[2304,128]{1,0:T(8,128)} custom-call(f32[768,128]{1,0:T(8,128)S(1)} %near.3.refs_0_, f32[768,128]{1,0:T(8,128)S(1)} %copy-done.23, f32[768,128]{1,0:T(8,128)S(1)} %copy-done.21, f32[80,128]{1,0:T(8,128)} %collective-permute-done.7.m1_ref.refs_3_, f32[80,128]{1,0:T(8,128)} %collective-permute-done.8.m2_ref.refs_4_, ...), custom_call_target="tpu_custom_call" | custom-call | tf_op jit(solution)/shard_map/last/pallas_call | solution.py:329
  (112 shorter events, 4.9 us)
Async XLA Ops:
  0.0 69.4 %copy-start = (s32[2304,128]{1,0:T(8,128)S(1)}, s32[2304,128]{1,0:T(8,128)}, u32[]{:S(2)}) copy-start(s32[2304,128]{1,0:T(8,128)} %param.12) | copy-start | bytes 3538948
  0.0 1.6 %copy-start.1 = (f32[2304,128]{1,0:T(8,128)S(1)}, f32[2304,128]{1,0:T(8,128)}, u32[]{:S(2)}) copy-start(f32[2304,128]{1,0:T(8,128)} %refs_11_.1) | copy-start | bytes 3538948
  1.6 0.8 copy-start.30
  3.9 0.8 copy-start.17
  4.8 0.8 copy-start.28
  6.2 1.0 copy-start.47
  7.2 48.4 %collective-permute-start = (f32[80,128]{1,0:T(8,128)}, f32[80,128]{1,0:T(8,128)S(1)}, u32[]{:S(2)}, u32[]{:S(2)}) collective-permute-start(f32[80,128]{1,0:T(8,128)} %get-tuple-element.37), channel_id=1, source_target_pairs={{0,1},{1,2},{2,3},{3,0},{4,5},{5,6},{6,7},{7,4},{8,9},{9,10},{10,1... | collective-permute-start | bytes 122888 | tf_op jit(solution)/shard_map/ppermute | solution.py:306
  9.3 46.3 %collective-permute-start.1 = (f32[80,128]{1,0:T(8,128)}, f32[80,128]{1,0:T(8,128)S(1)}, u32[]{:S(2)}, u32[]{:S(2)}) collective-permute-start(f32[80,128]{1,0:T(8,128)} %get-tuple-element.38), channel_id=1, source_target_pairs={{0,2},{1,3},{2,0},{3,1},{4,6},{5,7},{6,4},{7,5},{8,10},{9,11},{10,... | collective-permute-start | bytes 122888 | tf_op jit(solution)/shard_map/ppermute | solution.py:306
  12.0 43.7 %collective-permute-start.2 = (f32[80,128]{1,0:T(8,128)}, f32[80,128]{1,0:T(8,128)S(1)}, u32[]{:S(2)}, u32[]{:S(2)}) collective-permute-start(f32[80,128]{1,0:T(8,128)} %get-tuple-element.39), channel_id=1, source_target_pairs={{0,3},{1,0},{2,1},{3,2},{4,7},{5,4},{6,5},{7,6},{8,11},{9,8},{10,9... | collective-permute-start | bytes 122888 | tf_op jit(solution)/shard_map/ppermute | solution.py:306
  14.2 1.3 copy-start.48
  23.7 1.8 %copy-start.9 = (bf16[768,2304]{1,0:T(8,128)(2,1)}, bf16[768,2304]{1,0:T(8,128)(2,1)S(1)}, u32[]{:S(2)}) copy-start(bf16[768,2304]{1,0:T(8,128)(2,1)S(1)} %get-tuple-element.48.khi_ref) | copy-start | bytes 10616836
  25.4 1.8 %copy-start.11 = (bf16[768,2304]{1,0:T(8,128)(2,1)}, bf16[768,2304]{1,0:T(8,128)(2,1)S(1)}, u32[]{:S(2)}) copy-start(bf16[768,2304]{1,0:T(8,128)(2,1)S(1)} %get-tuple-element.49.klo_ref) | copy-start | bytes 10616836
  27.3 8.2 %copy-start.33 = (f32[768,128]{1,0:T(8,128)}, f32[768,128]{1,0:T(8,128)S(1)}, u32[]{:S(2)}) copy-start(f32[768,128]{1,0:T(8,128)S(1)} %get-tuple-element.36.refs_2_) | copy-start | bytes 1179652
  35.4 1.9 %copy-start.13 = (bf16[768,2304]{1,0:T(8,128)(2,1)}, bf16[768,2304]{1,0:T(8,128)(2,1)S(1)}, u32[]{:S(2)}) copy-start(bf16[768,2304]{1,0:T(8,128)(2,1)S(1)} %get-tuple-element.46.khi_ref) | copy-start | bytes 10616836
  37.3 1.8 %copy-start.15 = (bf16[768,2304]{1,0:T(8,128)(2,1)}, bf16[768,2304]{1,0:T(8,128)(2,1)S(1)}, u32[]{:S(2)}) copy-start(bf16[768,2304]{1,0:T(8,128)(2,1)S(1)} %get-tuple-element.47.klo_ref) | copy-start | bytes 10616836
  39.1 0.8 copy-start.35
  39.9 12.5 %copy-start.51 = (s32[1,2304]{1,0:T(1,128)S(1)}, s32[1,2304]{1,0:T(1,128)}, u32[]{:S(2)}) copy-start(s32[1,2304]{1,0:T(1,128)} %param.13) | copy-start | bytes 27652
  39.9 12.6 %copy-start.49 = (f32[1,64,64]{2,1,0:T(8,128)S(1)}, f32[1,64,64]{2,1,0:T(8,128)}, u32[]{:S(2)}) copy-start(f32[1,64,64]{2,1,0:T(8,128)} %param.16) | copy-start | bytes 49156
  39.9 12.6 %copy-start.52 = (f32[1,2,64,64]{3,2,1,0:T(8,128)S(1)}, f32[1,2,64,64]{3,2,1,0:T(8,128)}, u32[]{:S(2)}) copy-start(f32[1,2,64,64]{3,2,1,0:T(8,128)} %param.19) | copy-start | bytes 98308
  39.9 12.9 %copy-start.31 = (f32[1,64,64]{2,1,0:T(8,128)S(1)}, f32[1,64,64]{2,1,0:T(8,128)}, u32[]{:S(2)}) copy-start(f32[1,64,64]{2,1,0:T(8,128)} %param.15) | copy-start | bytes 49156
  39.9 13.1 %copy-start.50 = (f32[1,4,64,64]{3,2,1,0:T(8,128)S(1)}, f32[1,4,64,64]{3,2,1,0:T(8,128)}, u32[]{:S(2)}) copy-start(f32[1,4,64,64]{3,2,1,0:T(8,128)} %param.17) | copy-start | bytes 196612
  48.1 1.8 %copy-start.5 = (bf16[768,2304]{1,0:T(8,128)(2,1)}, bf16[768,2304]{1,0:T(8,128)(2,1)S(1)}, u32[]{:S(2)}) copy-start(bf16[768,2304]{1,0:T(8,128)(2,1)S(1)} %get-tuple-element.32.khi_ref) | copy-start | bytes 10616836
  49.9 1.8 %copy-start.7 = (bf16[768,2304]{1,0:T(8,128)(2,1)}, bf16[768,2304]{1,0:T(8,128)(2,1)S(1)}, u32[]{:S(2)}) copy-start(bf16[768,2304]{1,0:T(8,128)(2,1)S(1)} %get-tuple-element.33.klo_ref) | copy-start | bytes 10616836
  51.7 0.8 copy-start.37
  58.3 26.2 %all-to-all-start = ((f32[32,32,128]{2,1,0:T(8,128)}), f32[32,32,128]{2,1,0:T(8,128)S(1)}, u32[]{:S(2)}, u32[]{:S(2)}) async-start(f32[32,32,128]{2,1,0:T(8,128)} %middle.2), calls=%async_computation | async-start | bytes 1048576 | tf_op jit(solution)/shard_map/all_to_all | solution.py:314
  74.5 10.0 %copy-start.3 = (bf16[128,2048]{1,0:T(8,128)(2,1)}, bf16[128,2048]{1,0:T(8,128)(2,1)S(1)}, u32[]{:S(2)}) copy-start(bf16[128,2048]{1,0:T(8,128)(2,1)S(1)} %pad_maximum_fusion.couple_ref) | copy-start | bytes 1572868
  84.5 11.1 %copy-start.2 = (f32[2304,128]{1,0:T(8,128)S(1)}, f32[2304,128]{1,0:T(8,128)}, u32[]{:S(2)}) copy-start(f32[2304,128]{1,0:T(8,128)} %refs_11_.1) | copy-start | bytes 3538948
  84.5 11.1 %copy-start.32 = (f32[1,64,64]{2,1,0:T(8,128)S(1)}, f32[1,64,64]{2,1,0:T(8,128)}, u32[]{:S(2)}) copy-start(f32[1,64,64]{2,1,0:T(8,128)} %param.15) | copy-start | bytes 49156
  84.5 11.1 %copy-start.40 = (f32[80,128]{1,0:T(8,128)S(1)}, f32[80,128]{1,0:T(8,128)}, u32[]{:S(2)}) copy-start(f32[80,128]{1,0:T(8,128)} %copy-done.39) | copy-start | bytes 122884
  84.5 11.1 %copy-start.42 = (f32[80,128]{1,0:T(8,128)S(1)}, f32[80,128]{1,0:T(8,128)}, u32[]{:S(2)}) copy-start(f32[80,128]{1,0:T(8,128)} %copy-done.41) | copy-start | bytes 122884
  85.0 4.6 %collective-permute-start.3 = (f32[16,128]{1,0:T(8,128)S(1)}, f32[16,128]{1,0:T(8,128)S(1)}, u32[]{:S(2)}, u32[]{:S(2)}) collective-permute-start(f32[16,128]{1,0:T(8,128)S(1)} %get-tuple-element.42), channel_id=1, source_target_pairs={{0,128},{128,0},{1,129},{129,1},{2,130},{130,2},{3,131},{131,3},{4... | collective-permute-start | bytes 24584 | tf_op jit(solution)/shard_map/ppermute | solution.py:324
  89.6 2.6 %collective-permute-start.6 = (f32[32,128]{1,0:T(8,128)S(1)}, f32[32,128]{1,0:T(8,128)S(1)}, u32[]{:S(2)}, u32[]{:S(2)}) collective-permute-start(f32[32,128]{1,0:T(8,128)S(1)} %constant_dynamic-update-slice_fusion.refs_7_), channel_id=1, source_target_pairs={{0,3},{1,0},{2,1},{3,2},{4,7},{5,4},{6,5},{7,6},{8,11},{9,8},{10,9... | collective-permute-start | bytes 49160 | tf_op jit(solution)/shard_map/ppermute | solution.py:326
  89.6 4.1 %collective-permute-start.5 = (f32[32,128]{1,0:T(8,128)S(1)}, f32[32,128]{1,0:T(8,128)S(1)}, u32[]{:S(2)}, u32[]{:S(2)}) collective-permute-start(f32[32,128]{1,0:T(8,128)S(1)} %constant_dynamic-update-slice_fusion.refs_7_), channel_id=1, source_target_pairs={{0,2},{1,3},{2,0},{3,1},{4,6},{5,7},{6,4},{7,5},{8,10},{9,11},{10,... | collective-permute-start | bytes 49160 | tf_op jit(solution)/shard_map/ppermute | solution.py:326
  91.8 3.8 %collective-permute-start.4 = (f32[32,128]{1,0:T(8,128)S(1)}, f32[32,128]{1,0:T(8,128)S(1)}, u32[]{:S(2)}, u32[]{:S(2)}) collective-permute-start(f32[32,128]{1,0:T(8,128)S(1)} %constant_dynamic-update-slice_fusion.refs_7_), channel_id=1, source_target_pairs={{0,1},{1,2},{2,3},{3,0},{4,5},{5,6},{6,7},{7,4},{8,9},{9,10},{10,1... | collective-permute-start | bytes 49160 | tf_op jit(solution)/shard_map/ppermute | solution.py:326
  91.8 11.2 %copy-start.26 = (bf16[128,320]{1,0:T(8,128)(2,1)}, bf16[128,320]{1,0:T(8,128)(2,1)S(1)}, u32[]{:S(2)}) copy-start(bf16[128,320]{1,0:T(8,128)(2,1)S(1)} %pad_maximum_fusion.1.refs_6_) | copy-start | bytes 245764
  95.6 1.1 copy-start.18
  96.7 1.1 copy-start.29
  97.7 1.0 copy-start.34
  98.7 1.0 copy-start.36
  99.7 1.0 copy-start.38
  100.7 0.8 copy-start.44
  103.0 1.0 copy-start.24
  104.6 4.6 %collective-permute-start.7 = (f32[80,128]{1,0:T(8,128)S(1)}, f32[80,128]{1,0:T(8,128)}, u32[]{:S(2)}, u32[]{:S(2)}) collective-permute-start(f32[80,128]{1,0:T(8,128)S(1)} %get-tuple-element.50), channel_id=1, source_target_pairs={{0,1},{1,2},{2,3},{3,0},{4,5},{5,6},{6,7},{7,4},{8,9},{9,10},{10,1... | collective-permute-start | bytes 122888 | tf_op jit(solution)/shard_map/ppermute | solution.py:306
  104.6 4.6 %collective-permute-start.8 = (f32[80,128]{1,0:T(8,128)S(1)}, f32[80,128]{1,0:T(8,128)}, u32[]{:S(2)}, u32[]{:S(2)}) collective-permute-start(f32[80,128]{1,0:T(8,128)S(1)} %get-tuple-element.51), channel_id=1, source_target_pairs={{0,2},{1,3},{2,0},{3,1},{4,6},{5,7},{6,4},{7,5},{8,10},{9,11},{10,... | collective-permute-start | bytes 122888 | tf_op jit(solution)/shard_map/ppermute | solution.py:306
  106.3 3.5 %collective-permute-start.9 = (f32[80,128]{1,0:T(8,128)S(1)}, f32[80,128]{1,0:T(8,128)}, u32[]{:S(2)}, u32[]{:S(2)}) collective-permute-start(f32[80,128]{1,0:T(8,128)S(1)} %get-tuple-element.52), channel_id=1, source_target_pairs={{0,3},{1,0},{2,1},{3,2},{4,7},{5,4},{6,5},{7,6},{8,11},{9,8},{10,9... | collective-permute-start | bytes 122888 | tf_op jit(solution)/shard_map/ppermute | solution.py:306
  111.8 17.6 %all-to-all-start.1 = ((f32[32,32,128]{2,1,0:T(8,128)}), f32[32,32,128]{2,1,0:T(8,128)}, u32[]{:S(2)}, u32[]{:S(2)}) async-start(f32[32,32,128]{2,1,0:T(8,128)} %middle.3), calls=%async_computation.1 | async-start | bytes 1048576 | tf_op jit(solution)/shard_map/all_to_all | solution.py:314
  116.5 2.0 %copy-start.10 = (bf16[768,2304]{1,0:T(8,128)(2,1)S(1)}, bf16[768,2304]{1,0:T(8,128)(2,1)}, u32[]{:S(2)}) copy-start(bf16[768,2304]{1,0:T(8,128)(2,1)} %copy-done.9) | copy-start | bytes 10616836
  118.5 2.0 %copy-start.12 = (bf16[768,2304]{1,0:T(8,128)(2,1)S(1)}, bf16[768,2304]{1,0:T(8,128)(2,1)}, u32[]{:S(2)}) copy-start(bf16[768,2304]{1,0:T(8,128)(2,1)} %copy-done.11) | copy-start | bytes 10616836
  120.5 3.1 %copy-start.14 = (bf16[768,2304]{1,0:T(8,128)(2,1)S(1)}, bf16[768,2304]{1,0:T(8,128)(2,1)}, u32[]{:S(2)}) copy-start(bf16[768,2304]{1,0:T(8,128)(2,1)} %copy-done.13) | copy-start | bytes 10616836
  120.5 3.1 %copy-start.16 = (bf16[768,2304]{1,0:T(8,128)(2,1)S(1)}, bf16[768,2304]{1,0:T(8,128)(2,1)}, u32[]{:S(2)}) copy-start(bf16[768,2304]{1,0:T(8,128)(2,1)} %copy-done.15) | copy-start | bytes 10616836
  122.8 0.8 copy-start.20
  125.9 0.7 copy-start.22
  129.4 1.0 copy-start.4
  132.0 6.8 %collective-permute-start.10 = (f32[16,128]{1,0:T(8,128)S(1)}, f32[16,128]{1,0:T(8,128)S(1)}, u32[]{:S(2)}, u32[]{:S(2)}) collective-permute-start(f32[16,128]{1,0:T(8,128)S(1)} %get-tuple-element.55), channel_id=1, source_target_pairs={{0,128},{128,0},{1,129},{129,1},{2,130},{130,2},{3,131},{131,3},{4... | collective-permute-start | bytes 24584 | tf_op jit(solution)/shard_map/ppermute | solution.py:324
  138.8 9.2 %collective-permute-start.13 = (f32[32,128]{1,0:T(8,128)S(1)}, f32[32,128]{1,0:T(8,128)S(1)}, u32[]{:S(2)}, u32[]{:S(2)}) collective-permute-start(f32[32,128]{1,0:T(8,128)S(1)} %constant_dynamic-update-slice_fusion.2.refs_7_), channel_id=1, source_target_pairs={{0,3},{1,0},{2,1},{3,2},{4,7},{5,4},{6,5},{7,6},{8,11},{9,8},{10,9... | collective-permute-start | bytes 49160 | tf_op jit(solution)/shard_map/ppermute | solution.py:326
  140.9 7.1 %collective-permute-start.12 = (f32[32,128]{1,0:T(8,128)S(1)}, f32[32,128]{1,0:T(8,128)S(1)}, u32[]{:S(2)}, u32[]{:S(2)}) collective-permute-start(f32[32,128]{1,0:T(8,128)S(1)} %constant_dynamic-update-slice_fusion.2.refs_7_), channel_id=1, source_target_pairs={{0,2},{1,3},{2,0},{3,1},{4,6},{5,7},{6,4},{7,5},{8,10},{9,11},{10,... | collective-permute-start | bytes 49160 | tf_op jit(solution)/shard_map/ppermute | solution.py:326
  141.7 6.4 %collective-permute-start.11 = (f32[32,128]{1,0:T(8,128)S(1)}, f32[32,128]{1,0:T(8,128)S(1)}, u32[]{:S(2)}, u32[]{:S(2)}) collective-permute-start(f32[32,128]{1,0:T(8,128)S(1)} %constant_dynamic-update-slice_fusion.2.refs_7_), channel_id=1, source_target_pairs={{0,1},{1,2},{2,3},{3,0},{4,5},{5,6},{6,7},{7,4},{8,9},{9,10},{10,1... | collective-permute-start | bytes 49160 | tf_op jit(solution)/shard_map/ppermute | solution.py:326
  141.7 2.0 %copy-start.6 = (bf16[768,2304]{1,0:T(8,128)(2,1)S(1)}, bf16[768,2304]{1,0:T(8,128)(2,1)}, u32[]{:S(2)}) copy-start(bf16[768,2304]{1,0:T(8,128)(2,1)} %copy-done.5) | copy-start | bytes 10616836
  143.7 2.0 %copy-start.8 = (bf16[768,2304]{1,0:T(8,128)(2,1)S(1)}, bf16[768,2304]{1,0:T(8,128)(2,1)}, u32[]{:S(2)}) copy-start(bf16[768,2304]{1,0:T(8,128)(2,1)} %copy-done.7) | copy-start | bytes 10616836
  145.7 2.4 %copy-start.19 = (bf16[2304,128]{1,0:T(8,128)(2,1)S(1)}, bf16[2304,128]{1,0:T(8,128)(2,1)}, u32[]{:S(2)}) copy-start(bf16[2304,128]{1,0:T(8,128)(2,1)} %copy-done.17) | copy-start | bytes 1769476
  145.7 2.4 %copy-start.21 = (f32[768,128]{1,0:T(8,128)S(1)}, f32[768,128]{1,0:T(8,128)}, u32[]{:S(2)}) copy-start(f32[768,128]{1,0:T(8,128)} %copy-done.20) | copy-start | bytes 1179652
  145.7 2.4 %copy-start.23 = (f32[768,128]{1,0:T(8,128)S(1)}, f32[768,128]{1,0:T(8,128)}, u32[]{:S(2)}) copy-start(f32[768,128]{1,0:T(8,128)} %copy-done.22) | copy-start | bytes 1179652
  145.7 2.4 %copy-start.25 = (f32[2304,128]{1,0:T(8,128)S(1)}, f32[2304,128]{1,0:T(8,128)}, u32[]{:S(2)}) copy-start(f32[2304,128]{1,0:T(8,128)} %copy-done.24) | copy-start | bytes 3538948
  145.7 2.5 %copy-start.27 = (bf16[128,320]{1,0:T(8,128)(2,1)S(1)}, bf16[128,320]{1,0:T(8,128)(2,1)}, u32[]{:S(2)}) copy-start(bf16[128,320]{1,0:T(8,128)(2,1)} %copy-done.26) | copy-start | bytes 245764
  (5 other events, 3.0 us)

commit v2 on v1

v2 whole, which is shorter than its diff:
```python
import functools
import math

import jax
import jax.numpy as jnp
from jax import lax
from jax.experimental import pallas as pl
from jax.experimental.pallas import tpu as pltpu
from jax.sharding import PartitionSpec as P

STEPS = 2
RANK = 64
OUT = 128
N_MID = 32
N_LEAF = 4
QROWS = RANK // N_LEAF
QCOLS = OUT // N_LEAF
HP = lax.Precision.HIGHEST
F32 = jnp.float32
BF16 = jnp.bfloat16
LOG2E = math.log2(math.e)
CHUNKS = 3
BLOCK = 256
TILE = 32
VMEM = pl.BlockSpec(memory_space=pltpu.VMEM)


def split(x):
    hi = x.astype(BF16)
    return hi, (x - hi.astype(F32)).astype(BF16)


def wide(x):
    return jnp.concatenate(split(x), axis=1)


def dot3(tall, wide_rhs):
    d = jnp.dot(tall, wide_rhs, preferred_element_type=F32)
    m, n = d.shape[0] // 2, d.shape[1] // 2
    return d[:m, :n] + (d[:m, n:] + d[m:, :n])


def lane_group():
    return lax.broadcasted_iota(jnp.int32, (QROWS, OUT), 1) // QCOLS


def pack_quarter(full, quarter):
    group = lane_group()
    out = jnp.zeros((QROWS, OUT), F32)
    for k in range(N_LEAF):
        moved = pltpu.roll(
            full[k * QROWS : (k + 1) * QROWS], lax.rem((k - quarter + N_LEAF) * QCOLS, OUT), 1
        )
        out = jnp.where(group == k, moved, out)
    return out


def expand_packed(packed):
    group = lane_group()
    zero = jnp.zeros((QROWS, OUT), F32)
    return jnp.concatenate([jnp.where(group == k, packed, zero) for k in range(N_LEAF)], axis=0)


def fold_and_pack(grouped):
    both = grouped + pltpu.roll(grouped, 2 * QCOLS, 1)
    total = both + pltpu.roll(both, QCOLS, 1)
    group = lane_group()
    out = jnp.zeros((QROWS, OUT), F32)
    for k in range(N_LEAF):
        out = jnp.where(group == k, total[k * QROWS : (k + 1) * QROWS], out)
    return out


def unpack_quarters(packed, quarters):
    group = lane_group()
    rows = []
    for k in range(N_LEAF):
        out = jnp.zeros((QROWS, OUT), F32)
        for block, quarter in zip(packed, quarters):
            moved = pltpu.roll(block, lax.rem((quarter - k + N_LEAF) * QCOLS, OUT), 1)
            out = jnp.where(group == quarter, moved, out)
        rows.append(out)
    return jnp.concatenate(rows, axis=0)


def tall(x):
    return jnp.concatenate(split(x), axis=0)


def dot_rows(lhs, rhs):
    return lax.dot_general(
        lhs, rhs, (((0,), (0,)), ((), ())), precision=HP, preferred_element_type=F32
    )


def emit_messages(s0, up, own_ref, message_refs):
    own = lax.axis_index("leaf")
    both = dot_rows(up, s0)

    def quarter(q):
        return jnp.concatenate([pack_quarter(both[:RANK], q), pack_quarter(both[RANK:], q)], axis=0)

    own_ref[...] = quarter(own)
    for k, ref in enumerate(message_refs, 1):
        ref[0:RANK, :] = s0
        ref[RANK:, :] = quarter(lax.rem(own + k, N_LEAF))


def first_body(basis_t_ref, w_ref, leaf_ref, mid_ref, up_ref, own_ref, *message_refs):
    through = jnp.dot(leaf_ref[0], mid_ref[0], precision=HP, preferred_element_type=F32)
    up_ref[...] = jnp.concatenate([leaf_ref[0], through], axis=1)
    s0 = dot3(tall(basis_t_ref[...]), wide(w_ref[...]))
    emit_messages(s0, up_ref[...], own_ref, message_refs)


def prepare_body(
    coords_ref, order_ref, basis_t_ref, w_ref, leaf_ref, mid_ref, couple_leaf_ref, couple_mid_ref,
    couple_top_ref, columns_ref, bcat_ref, whl_ref, couple_ref, down_ref,
):
    n = w_ref.shape[0]
    order = order_ref[...].astype(F32)
    rows = jnp.concatenate([coords_ref[...] * LOG2E, order, jnp.zeros((4, n), F32)], axis=0)
    columns_ref[...] = rows.T
    for j in range(n // BLOCK):
        cols = slice(j * BLOCK, (j + 1) * BLOCK)
        bcat_ref[cols, :] = wide(basis_t_ref[:, cols].T)
    whl_ref[...] = wide(w_ref[...])
    own_mid, own_leaf = lax.axis_index("mid"), lax.axis_index("leaf")
    for m in range(N_MID // 2):
        pair = [
            jnp.where(own_mid == i, 0.0, couple_mid_ref[0, i]) for i in (2 * m, 2 * m + 1)
        ]
        couple_ref[:, m * OUT : (m + 1) * OUT] = tall(jnp.concatenate(pair, axis=1))
    other = 1 - lax.axis_index("top")
    from_top = jnp.dot(mid_ref[0], couple_top_ref[0, other], precision=HP, preferred_element_type=F32)
    from_top = jnp.dot(leaf_ref[0], from_top, precision=HP, preferred_element_type=F32)
    siblings = [couple_leaf_ref[0, lax.rem(own_leaf + N_LEAF - k, N_LEAF)] for k in (1, 2, 3)]
    down_ref[...] = tall(jnp.concatenate([*siblings, leaf_ref[0], from_top], axis=1))


def targets_body(columns_ref, labels_ref, out_ref, labels16_ref):
    n = labels_ref.shape[0]
    labels16_ref[...] = labels_ref[...].astype(BF16)
    lane = lax.broadcasted_iota(jnp.int32, (BLOCK, n), 1).astype(F32)

    def rows(i, carry):
        at = pl.ds(pl.multiple_of(i * BLOCK, BLOCK), BLOCK)
        chosen = jnp.where(columns_ref[at, 3:4] == lane, 1.0, 0.0).astype(BF16)
        out_ref[at, :] = jnp.dot(chosen, labels16_ref[...], preferred_element_type=F32)
        return carry

    lax.fori_loop(0, n // BLOCK, rows, 0)


def near_product(khi, klo, whl):
    a = jnp.dot(khi, whl, preferred_element_type=F32)
    b = jnp.dot(klo, whl[:, 0:OUT], preferred_element_type=F32)
    return a[:, :OUT] + (a[:, OUT:] + b)


def build_body(scale, first_row, coords_ref, columns_ref, whl_ref, khi_ref, klo_ref, near_ref, own_ref):
    chunk, points = khi_ref.shape

    def block(i, carry):
        at = pl.multiple_of(i * BLOCK, BLOCK)
        for k in range(3):
            own_ref[k] = jnp.broadcast_to(
                columns_ref[pl.ds(first_row + at, BLOCK), k : k + 1], (BLOCK, OUT)
            )
        total = None
        waiting = None
        for j in range(points // BLOCK):
            for half in range(2):
                cols = slice(j * BLOCK + half * OUT, j * BLOCK + (half + 1) * OUT)
                other = [coords_ref[k : k + 1, cols] * LOG2E for k in range(3)]
                for t in range(BLOCK // TILE):
                    sub = slice(t * TILE, (t + 1) * TILE)
                    diff_sq = None
                    for k in range(3):
                        delta = own_ref[k, sub, :] - other[k]
                        diff_sq = delta * delta if diff_sq is None else diff_sq + delta * delta
                    dist = diff_sq * lax.rsqrt(jnp.maximum(diff_sq, 1e-37))
                    hi, lo = split(jnp.exp2(-dist))
                    rows = pl.ds(at + t * TILE, TILE)
                    khi_ref[rows, cols] = hi
                    klo_ref[rows, cols] = lo
            if j % 3 == 2:
                if waiting is not None:
                    part = near_product(*waiting)
                    total = part if total is None else total + part
                at_cols = slice((j - 2) * BLOCK, (j + 1) * BLOCK)
                rows = pl.ds(at, BLOCK)
                waiting = khi_ref[rows, at_cols], klo_ref[rows, at_cols], whl_ref[at_cols, :]
        near_ref[pl.ds(at, BLOCK), :] = (total + near_product(*waiting)) * scale
        return carry

    lax.fori_loop(0, chunk // BLOCK, block, 0)


def near_body(scale, khi_ref, klo_ref, whl_ref, near_ref):
    def block(i, carry):
        rows = pl.ds(pl.multiple_of(i * BLOCK, BLOCK), BLOCK)
        near_ref[rows, :] = near_product(khi_ref[rows, :], klo_ref[rows, :], whl_ref[...]) * scale
        return carry

    lax.fori_loop(0, khi_ref.shape[0] // BLOCK, block, 0)


def middle_body(own_ref, m1_ref, m2_ref, m3_ref, out_ref):
    tail = slice(RANK, RANK + 2 * QROWS)
    total = (own_ref[...] + m1_ref[tail, :]) + (m2_ref[tail, :] + m3_ref[tail, :])
    out_ref[...] = jnp.broadcast_to(total[None], out_ref.shape)


def couple_body(got_ref, couple_ref, g1_ref, s2_ref, spread_ref):
    s2 = jnp.zeros((QROWS, OUT), F32)
    for m in range(N_MID):
        spread_ref[m * RANK : (m + 1) * RANK, :] = wide(expand_packed(got_ref[m, 0:QROWS, :]))
        s2 = s2 + got_ref[m, QROWS:, :]
    g1_ref[...] = fold_and_pack(dot3(couple_ref[...], spread_ref[...]))
    s2_ref[...] = s2


def update_body(*refs):
    near_refs, messages, down_ref, tops = refs[:3], refs[3:6], refs[6], refs[7:11]
    w_ref, targets_ref, bcat_ref = refs[11:14]
    last = len(refs) == 15
    outs = refs[14:] if last else refs[16:]
    own = lax.axis_index("leaf")
    quarters = [lax.rem(own + N_LEAF - k, N_LEAF) for k in range(N_LEAF)]
    g1 = unpack_quarters([ref[0:QROWS, :] for ref in tops], quarters)
    s2 = unpack_quarters([ref[QROWS:, :] for ref in tops], quarters)
    parts = [ref[0:RANK, :] for ref in messages] + [g1, s2]
    g0 = dot3(down_ref[...], wide(jnp.concatenate(parts, axis=0)))
    hi, lo = split(g0)
    rhs = jnp.concatenate(
        [jnp.concatenate([hi, lo], axis=1), jnp.concatenate([hi, jnp.zeros_like(lo)], axis=1)], axis=0
    )
    chunk = near_refs[0].shape[0]
    w_out = outs[0]
    for j in range(w_ref.shape[0] // BLOCK):
        rows = slice(j * BLOCK, (j + 1) * BLOCK)
        at = j * BLOCK % chunk
        f = jnp.dot(bcat_ref[rows, :], rhs, preferred_element_type=F32)
        f = near_refs[j * BLOCK // chunk][at : at + BLOCK, :] + (f[:, :OUT] + f[:, OUT:])
        new = w_ref[rows, :] - ((0.5 * jnp.tanh(0.5 * f) + 0.5) - targets_ref[rows, :])
        w_out[rows, :] = new
        if not last:
            outs[1][rows, :] = wide(new)
    if not last:
        basis_t_ref, up_ref = refs[14:16]
        s0 = dot3(tall(basis_t_ref[...]), outs[1][...])
        emit_messages(s0, up_ref[...], outs[2], outs[3:])


def params(mib):
    return pltpu.CompilerParams(vmem_limit_bytes=mib << 20)


def shape(*dims, dtype=F32):
    return jax.ShapeDtypeStruct(dims, dtype)


def ring(k):
    return [(i, (i + k) % N_LEAF) for i in range(N_LEAF)]


def call(body, out, operands, mib, name, scratch=(), work=(0, 0, 0)):
    return pl.pallas_call(
        body,
        out_shape=out,
        in_specs=[VMEM] * len(operands),
        out_specs=jax.tree.map(lambda _: VMEM, out),
        scratch_shapes=scratch,
        compiler_params=params(mib),
        cost_estimate=pl.CostEstimate(flops=work[0], bytes_accessed=work[1], transcendentals=work[2]),
        name=name,
    )(*operands)


def on_device(
    coords,
    weights,
    labels,
    order,
    basis,
    transfer_leaf,
    transfer_mid,
    couple_leaf,
    couple_mid,
    couple_top,
):
    n = weights.shape[0]
    chunk = n // CHUNKS
    scale = 4.0 / math.sqrt(n)
    basis_t = basis.T
    message_shapes = [shape(2 * QROWS, OUT)] + [shape(RANK + 2 * QROWS, OUT)] * 3
    near_work = (chunk * n * 2 * 512, chunk * n * 4, 0)

    up, own, *messages = call(
        first_body,
        [shape(RANK, 2 * RANK), *message_shapes],
        (basis_t, weights, transfer_leaf, transfer_mid),
        8,
        "first",
    )
    columns, bcat, whl, couple, down = call(
        prepare_body,
        [
            shape(n, 8),
            shape(n, 2 * RANK, dtype=BF16),
            shape(n, 2 * OUT, dtype=BF16),
            shape(2 * RANK, N_MID * RANK, dtype=BF16),
            shape(2 * RANK, 5 * RANK, dtype=BF16),
        ],
        (coords, order, basis_t, weights, transfer_leaf, transfer_mid, couple_leaf, couple_mid, couple_top),
        12,
        "prepare",
    )
    targets = call(
        targets_body,
        shape(n, OUT),
        (columns, labels),
        12,
        "targets",
        [pltpu.VMEM((n, OUT), BF16)],
        (n * n * 2 * OUT, n * OUT * 8, 0),
    )
    kernels, near = [], []
    for c in range(CHUNKS):
        khi, klo, rows = call(
            functools.partial(build_body, scale, c * chunk),
            [shape(chunk, n, dtype=BF16)] * 2 + [shape(chunk, OUT)],
            (coords, columns, whl),
            12,
            "build",
            [pltpu.VMEM((3, BLOCK, OUT), F32)],
            (*near_work[:2], 2 * chunk * n),
        )
        kernels.append((khi, klo))
        near.append(rows)

    current = weights
    for step in range(STEPS):
        last = step == STEPS - 1
        if step:
            near = [
                call(
                    functools.partial(near_body, scale),
                    shape(chunk, OUT),
                    (khi, klo, whl),
                    8,
                    "near",
                    work=near_work,
                )
                for khi, klo in kernels
            ]
        messages = [lax.ppermute(m, "leaf", ring(k)) for k, m in enumerate(messages, 1)]
        spread = call(middle_body, shape(N_MID, 2 * QROWS, OUT), (own, *messages), 4, "middle")
        got = lax.all_to_all(spread, "mid", 0, 0)
        g1, s2 = call(
            couple_body,
            [shape(QROWS, OUT)] * 2,
            (got, couple),
            8,
            "couple",
            [pltpu.VMEM((N_MID * RANK, 2 * OUT), BF16)],
        )
        s2 = lax.ppermute(s2, "top", [(0, 1), (1, 0)])
        top = jnp.concatenate([g1, s2], axis=0)
        tops = [top] + [lax.ppermute(top, "leaf", ring(k)) for k in (1, 2, 3)]
        far = (*near, *messages, down, *tops, current, targets, bcat)
        if last:
            current = call(update_body, shape(n, OUT), far, 8, "last")
        else:
            current, whl, own, *messages = call(
                update_body,
                [shape(n, OUT), shape(n, 2 * OUT, dtype=BF16), *message_shapes],
                (*far, basis_t, up),
                12,
                "update",
            )
    return current


def solution(mesh):
    placed = (
        P(None, ("top", "mid", "leaf")),
        P(("top", "mid", "leaf"), None),
        P(("top", "mid", "leaf"), None),
        P(("top", "mid", "leaf"), None),
        P(("top", "mid", "leaf"), None),
        P(("top", "mid", "leaf"), None, None),
        P(("top", "mid"), None, None),
        P(("top", "mid", "leaf"), None, None, None),
        P(("top", "mid"), None, None, None),
        P("top", None, None, None),
    )
    return jax.shard_map(
        on_device,
        mesh=mesh,
        in_specs=placed,
        out_specs=P(("top", "mid", "leaf"), None),
        check_vma=False,
    )
```

time: 152 us -> 133 us (0.88)
  waiting for transfers between devices: 18.2 us -> 9.8 us
  local copies, waits for them, and re-layouts: 44.5 us -> 36.4 us
  starting transfers between devices: 38.9 us -> 44.5 us
  other arithmetic: 4.84 us -> 0 us
  Pallas kernels: 43.3 us -> 40.8 us
    all_to_all x2, waiting for transfers between devices: 10.2 us -> 3.78 us  [on_device(): got = lax.all_to_all(spread, 'mid', 0, 0)]
    gather x1 -> x0, local copies, waits for them, and re-layouts: 5.1 us -> none  [on_device(): targets = jnp.take(labels, order[0], axis=0).astype(F32)]
    all_to_all x2, starting transfers between devices: 15.7 us -> 20.5 us  [on_device(): got = lax.all_to_all(spread, 'mid', 0, 0)]
    ppermute x6, waiting for transfers between devices: 3.78 us -> 0.02 us  [on_device(): tops = [top] + [lax.ppermute(top, 'leaf', ring(k)) for k in (1, 2, 3)]]
    pallas_call x13 -> x15, Pallas kernels: 43.3 us -> 40.8 us  [call(): pl.pallas_call(body, out_shape=out, in_specs=[VMEM] * len(operands), out_...]
    convert_element_type x2 -> x0, other arithmetic: 2.48 us -> none  [the longest x1 2.48 us: on_device(): targets = jnp.take(labels, order[0], axis=0).astype(F32)]
    ppermute x2, starting transfers between devices: 9.76 us -> 7.73 us  [on_device(): s2 = lax.ppermute(s2, 'top', [(0, 1), (1, 0)])]
    ppermute x6, waiting for transfers between devices: 2.51 us -> 4.35 us  [on_device(): lax.ppermute(m, 'leaf', ring(k))]
  transfers between devices with their start and end apart: 16 -> 16, of which waited for: 9 -> 6; matrix products, arithmetic and copies ran while one was open for 8% -> 0% of each run, Pallas kernels for 21% -> 26%
where the time goes in v2:
time: 133 us; the launch traced here: 132 us
  starting transfers between devices  44.5 us (33%)
  Pallas kernels  40.8 us (31%)
  local copies, waits for them, and re-layouts  36.4 us (27%)
  waiting for transfers between devices  9.8 us (7%)
    pallas_call x15, Pallas kernels, call(): pl.pallas_call(body, out_shape=out, in_specs=[VMEM] * len(operands), out_...  40.8 us
    unnamed x108, local copies, waits for them, and re-layouts  36.4 us
    all_to_all x2, starting transfers between devices, on_device(): got = lax.all_to_all(spread, 'mid', 0, 0)  20.5 us
    ppermute x6, starting transfers between devices, on_device(): lax.ppermute(m, 'leaf', ring(k))  10.2 us
    ppermute x2, starting transfers between devices, on_device(): s2 = lax.ppermute(s2, 'top', [(0, 1), (1, 0)])  7.73 us
    ppermute x6, starting transfers between devices, on_device(): tops = [top] + [lax.ppermute(top, 'leaf', ring(k)) for k in (1, 2, 3)]  6.08 us
    ppermute x6, waiting for transfers between devices, on_device(): lax.ppermute(m, 'leaf', ring(k))  4.35 us
    all_to_all x2, waiting for transfers between devices, on_device(): got = lax.all_to_all(spread, 'mid', 0, 0)  3.78 us
  transfers between devices with their start and end apart: 16, of which 6 were waited for; matrix products, arithmetic and copies ran while one was open for 0% of the time, Pallas kernels for 26%

profile of v2, /device:TPU:1, one launch (start us, length us, event | category | flops | bytes accessed | tf_op | source)
XLA Modules:
  0.0 132.0 jit_solution(1629811720124039898)
XLA Ops:
  0.0 1.3 copy-done
  1.3 1.1 copy-done.2
  2.3 0.8 copy-done.40
  3.1 0.8 copy-done.42
  3.9 0.8 first.1
  4.6 0.6 copy-done.47
  5.2 2.1 %collective-permute-start = (f32[96,128]{1,0:T(8,128)S(1)}, f32[96,128]{1,0:T(8,128)S(1)}, u32[]{:S(2)}, u32[]{:S(2)}) collective-permute-start(f32[96,128]{1,0:T(8,128)S(1)} %get-tuple-element.41), channel_id=1, source_target_pairs={{0,1},{1,2},{2,3},{3,0},{4,5},{5,6},{6,7},{7,4},{8,9},{9,10},{10,1... | collective-permute-start | bytes 147464 | tf_op jit(solution)/shard_map/ppermute | solution.py:358
  7.4 2.6 %collective-permute-start.1 = (f32[96,128]{1,0:T(8,128)S(1)}, f32[96,128]{1,0:T(8,128)S(1)}, u32[]{:S(2)}, u32[]{:S(2)}) collective-permute-start(f32[96,128]{1,0:T(8,128)S(1)} %get-tuple-element.42), channel_id=1, source_target_pairs={{0,2},{1,3},{2,0},{3,1},{4,6},{5,7},{6,4},{7,5},{8,10},{9,11},{10,... | collective-permute-start | bytes 147464 | tf_op jit(solution)/shard_map/ppermute | solution.py:358
  10.0 1.1 collective-permute-start.2
  11.0 0.9 collective-permute-done.1.m2_ref.refs_4_
  12.0 1.2 collective-permute-done.2.m3_ref.refs_5_
  13.2 0.9 middle.2
  14.1 0.6 copy-done.36
  14.7 0.6 copy-done.38
  15.3 11.0 %all-to-all-start = ((f32[32,32,128]{2,1,0:T(8,128)}), f32[32,32,128]{2,1,0:T(8,128)S(1)}, u32[]{:S(2)}, u32[]{:S(2)}) async-start(f32[32,32,128]{2,1,0:T(8,128)} %middle.2), calls=%async_computation | async-start | bytes 1048576 | tf_op jit(solution)/shard_map/all_to_all | solution.py:360
  26.4 1.2 copy-done.24
  27.6 0.8 copy-done.43
  28.4 0.9 copy-done.44
  29.3 0.8 copy-done.45
  30.1 0.8 copy-done.46
  30.9 1.3 prepare.1
  32.2 7.0 %build.5 = (bf16[768,2304]{1,0:T(8,128)(2,1)S(1)}, bf16[768,2304]{1,0:T(8,128)(2,1)S(1)}, f32[768,128]{1,0:T(8,128)S(1)}) custom-call(f32[3,2304]{1,0:T(4,128)S(1)} %copy-done.46, f32[2304,8]{1,0:T(8,128)S(1)} %get-tuple-element.34.columns_ref, bf16[2304,256]{1,0:T(8,128)(2,1)S(1)} %get-tuple-element.35.whl_ref), custom_call_target="tpu_custom_call" | custom-call | flops 1811939328 | bytes 7077888 | tf_op jit(solution)/shard_map/build/pallas_call | solution.py:269
  39.2 1.8 %copy-done.10 = bf16[768,2304]{1,0:T(8,128)(2,1)} copy-done((bf16[768,2304]{1,0:T(8,128)(2,1)}, bf16[768,2304]{1,0:T(8,128)(2,1)S(1)}, u32[]{:S(2)}) %copy-start.10) | copy-done | bytes 3538968
  41.1 1.8 %copy-done.12 = bf16[768,2304]{1,0:T(8,128)(2,1)} copy-done((bf16[768,2304]{1,0:T(8,128)(2,1)}, bf16[768,2304]{1,0:T(8,128)(2,1)S(1)}, u32[]{:S(2)}) %copy-start.12) | copy-done | bytes 3538968
  42.9 0.8 copy-done.25
  43.7 7.0 %build.4 = (bf16[768,2304]{1,0:T(8,128)(2,1)S(1)}, bf16[768,2304]{1,0:T(8,128)(2,1)S(1)}, f32[768,128]{1,0:T(8,128)S(1)}) custom-call(f32[3,2304]{1,0:T(4,128)S(1)} %copy-done.46, f32[2304,8]{1,0:T(8,128)S(1)} %get-tuple-element.34.columns_ref, bf16[2304,256]{1,0:T(8,128)(2,1)S(1)} %get-tuple-element.35.whl_ref), custom_call_target="tpu_custom_call" | custom-call | flops 1811939328 | bytes 7077888 | tf_op jit(solution)/shard_map/build/pallas_call | solution.py:269
  50.7 1.8 %copy-done.14 = bf16[768,2304]{1,0:T(8,128)(2,1)} copy-done((bf16[768,2304]{1,0:T(8,128)(2,1)}, bf16[768,2304]{1,0:T(8,128)(2,1)S(1)}, u32[]{:S(2)}) %copy-start.14) | copy-done | bytes 3538968
  52.5 1.8 %copy-done.16 = bf16[768,2304]{1,0:T(8,128)(2,1)} copy-done((bf16[768,2304]{1,0:T(8,128)(2,1)}, bf16[768,2304]{1,0:T(8,128)(2,1)S(1)}, u32[]{:S(2)}) %copy-start.16) | copy-done | bytes 3538968
  54.3 0.7 copy-done.27
  55.1 7.0 %build.3 = (bf16[768,2304]{1,0:T(8,128)(2,1)S(1)}, bf16[768,2304]{1,0:T(8,128)(2,1)S(1)}, f32[768,128]{1,0:T(8,128)S(1)}) custom-call(f32[3,2304]{1,0:T(4,128)S(1)} %copy-done.46, f32[2304,8]{1,0:T(8,128)S(1)} %get-tuple-element.34.columns_ref, bf16[2304,256]{1,0:T(8,128)(2,1)S(1)} %get-tuple-element.35.whl_ref), custom_call_target="tpu_custom_call" | custom-call | flops 1811939328 | bytes 7077888 | tf_op jit(solution)/shard_map/build/pallas_call | solution.py:269
  62.1 1.8 %copy-done.6 = bf16[768,2304]{1,0:T(8,128)(2,1)} copy-done((bf16[768,2304]{1,0:T(8,128)(2,1)}, bf16[768,2304]{1,0:T(8,128)(2,1)S(1)}, u32[]{:S(2)}) %copy-start.6) | copy-done | bytes 3538968
  63.8 1.8 %copy-done.8 = bf16[768,2304]{1,0:T(8,128)(2,1)} copy-done((bf16[768,2304]{1,0:T(8,128)(2,1)}, bf16[768,2304]{1,0:T(8,128)(2,1)S(1)}, u32[]{:S(2)}) %copy-start.8) | copy-done | bytes 3538968
  65.6 0.8 copy-done.29
  66.9 2.6 %collective-permute-start.3 = (f32[16,128]{1,0:T(8,128)S(1)}, f32[16,128]{1,0:T(8,128)S(1)}, u32[]{:S(2)}, u32[]{:S(2)}) collective-permute-start(f32[16,128]{1,0:T(8,128)S(1)} %get-tuple-element.48), channel_id=1, source_target_pairs={{0,128},{128,0},{1,129},{129,1},{2,130},{130,2},{3,131},{131,3},{4... | collective-permute-start | bytes 24584 | tf_op jit(solution)/shard_map/ppermute | solution.py:369
  69.5 0.8 collective-permute-done.3
  70.4 2.4 %collective-permute-start.6 = (f32[32,128]{1,0:T(8,128)S(1)}, f32[32,128]{1,0:T(8,128)S(1)}, u32[]{:S(2)}, u32[]{:S(2)}) collective-permute-start(f32[32,128]{1,0:T(8,128)S(1)} %constant_dynamic-update-slice_fusion.refs_7_), channel_id=1, source_target_pairs={{0,3},{1,0},{2,1},{3,2},{4,7},{5,4},{6,5},{7,6},{8,11},{9,8},{10,9... | collective-permute-start | bytes 49160 | tf_op jit(solution)/shard_map/ppermute | solution.py:371
  72.8 0.7 collective-permute-start.4
  73.5 1.3 copy-done.50
  74.7 1.3 copy-done.52
  76.0 4.8 %targets.1.refs_12_ = f32[2304,128]{1,0:T(8,128)S(1)} custom-call(f32[2304,8]{1,0:T(8,128)S(1)} %copy-done.52, s32[2304,128]{1,0:T(8,128)S(1)} %copy-done.50), custom_call_target="tpu_custom_call" | custom-call | flops 1358954496 | bytes 2359296 | tf_op jit(solution)/shard_map/targets/pallas_call | solution.py:269
  80.9 1.5 %update.1 = (f32[2304,128]{1,0:T(8,128)S(1)}, bf16[2304,256]{1,0:T(8,128)(2,1)S(1)}, f32[32,128]{1,0:T(8,128)S(1)}, f32[96,128]{1,0:T(8,128)S(1)}, f32[96,128]{1,0:T(8,128)S(1)}, /*index=5*/f32[96,128]{1,0:T(8,128)S(1)}) custom-call(f32[768,128]{1,0:T(8,128)S(1)} %copy-done.30, f32[768,128]{1,0:T(8,128)S(1)} %copy-done.28, f32[768,128]{1,0:T(8,128)S(1)} %copy-done.26, ...), custom_call_target="tpu_custom_call" | custom-call | tf_op jit(solution)/shard_map/update/pallas_call | solution.py:269
  82.4 1.0 copy-done.22
  83.4 2.0 %collective-permute-start.7 = (f32[96,128]{1,0:T(8,128)S(1)}, f32[96,128]{1,0:T(8,128)S(1)}, u32[]{:S(2)}, u32[]{:S(2)}) collective-permute-start(f32[96,128]{1,0:T(8,128)S(1)} %get-tuple-element.56), channel_id=1, source_target_pairs={{0,1},{1,2},{2,3},{3,0},{4,5},{5,6},{6,7},{7,4},{8,9},{9,10},{10,1... | collective-permute-start | bytes 147464 | tf_op jit(solution)/shard_map/ppermute | solution.py:358
  85.4 1.2 collective-permute-start.8
  86.6 1.2 collective-permute-start.9
  87.8 2.2 %collective-permute-done.8.m2_ref.refs_4_ = f32[96,128]{1,0:T(8,128)S(1)} collective-permute-done((f32[96,128]{1,0:T(8,128)S(1)}, f32[96,128]{1,0:T(8,128)S(1)}, u32[]{:S(2)}, u32[]{:S(2)}) %collective-permute-start.8) | collective-permute-done | bytes 49184 | tf_op jit(solution)/shard_map/ppermute | solution.py:358
  90.0 0.8 middle.3
  90.8 9.5 %all-to-all-start.1 = ((f32[32,32,128]{2,1,0:T(8,128)}), f32[32,32,128]{2,1,0:T(8,128)S(1)}, u32[]{:S(2)}, u32[]{:S(2)}) async-start(f32[32,32,128]{2,1,0:T(8,128)} %middle.3), calls=%async_computation.1 | async-start | bytes 1048576 | tf_op jit(solution)/shard_map/all_to_all | solution.py:360
  100.4 2.0 %copy-done.11 = bf16[768,2304]{1,0:T(8,128)(2,1)S(1)} copy-done((bf16[768,2304]{1,0:T(8,128)(2,1)S(1)}, bf16[768,2304]{1,0:T(8,128)(2,1)}, u32[]{:S(2)}) %copy-start.11) | copy-done | bytes 3538968
  102.4 2.0 %copy-done.13 = bf16[768,2304]{1,0:T(8,128)(2,1)S(1)} copy-done((bf16[768,2304]{1,0:T(8,128)(2,1)S(1)}, bf16[768,2304]{1,0:T(8,128)(2,1)}, u32[]{:S(2)}) %copy-start.13) | copy-done | bytes 3538968
  104.4 2.3 %near.5.refs_2_ = f32[768,128]{1,0:T(8,128)S(1)} custom-call(bf16[768,2304]{1,0:T(8,128)(2,1)S(1)} %copy-done.11, bf16[768,2304]{1,0:T(8,128)(2,1)S(1)} %copy-done.13, bf16[2304,256]{1,0:T(8,128)(2,1)S(1)} %get-tuple-element.51.whl_ref), custom_call_target="tpu_custom_call" | custom-call | flops 1811939328 | bytes 7077888 | tf_op jit(solution)/shard_map/near/pallas_call | solution.py:269
  106.7 0.7 copy-done.17
  107.4 2.3 %near.4.refs_1_ = f32[768,128]{1,0:T(8,128)S(1)} custom-call(bf16[768,2304]{1,0:T(8,128)(2,1)S(1)} %copy-done.15, bf16[768,2304]{1,0:T(8,128)(2,1)S(1)} %copy-done.17, bf16[2304,256]{1,0:T(8,128)(2,1)S(1)} %get-tuple-element.51.whl_ref), custom_call_target="tpu_custom_call" | custom-call | flops 1811939328 | bytes 7077888 | tf_op jit(solution)/shard_map/near/pallas_call | solution.py:269
  109.8 0.8 copy-done.20
  110.6 3.8 %all-to-all-done.1.got_ref = f32[32,32,128]{2,1,0:T(8,128)S(1)} async-done(((f32[32,32,128]{2,1,0:T(8,128)}), f32[32,32,128]{2,1,0:T(8,128)S(1)}, u32[]{:S(2)}, u32[]{:S(2)}) %all-to-all-start.1) | async-done | bytes 524320 | tf_op jit(solution)/shard_map/all_to_all | solution.py:360
  114.3 0.5 couple.3
  114.8 5.1 %collective-permute-start.10 = (f32[16,128]{1,0:T(8,128)S(1)}, f32[16,128]{1,0:T(8,128)S(1)}, u32[]{:S(2)}, u32[]{:S(2)}) collective-permute-start(f32[16,128]{1,0:T(8,128)S(1)} %get-tuple-element.61), channel_id=1, source_target_pairs={{0,128},{128,0},{1,129},{129,1},{2,130},{130,2},{3,131},{131,3},{4... | collective-permute-start | bytes 24584 | tf_op jit(solution)/shard_map/ppermute | solution.py:369
  119.9 0.8 collective-permute-done.10
  120.7 2.5 %collective-permute-start.13 = (f32[32,128]{1,0:T(8,128)S(1)}, f32[32,128]{1,0:T(8,128)S(1)}, u32[]{:S(2)}, u32[]{:S(2)}) collective-permute-start(f32[32,128]{1,0:T(8,128)S(1)} %constant_dynamic-update-slice_fusion.2.refs_7_), channel_id=1, source_target_pairs={{0,3},{1,0},{2,1},{3,2},{4,7},{5,4},{6,5},{7,6},{8,11},{9,8},{10,9... | collective-permute-start | bytes 49160 | tf_op jit(solution)/shard_map/ppermute | solution.py:371
  123.2 0.6 collective-permute-start.11
  123.8 2.0 %copy-done.7 = bf16[768,2304]{1,0:T(8,128)(2,1)S(1)} copy-done((bf16[768,2304]{1,0:T(8,128)(2,1)S(1)}, bf16[768,2304]{1,0:T(8,128)(2,1)}, u32[]{:S(2)}) %copy-start.7) | copy-done | bytes 3538968
  125.8 2.0 %copy-done.9 = bf16[768,2304]{1,0:T(8,128)(2,1)S(1)} copy-done((bf16[768,2304]{1,0:T(8,128)(2,1)S(1)}, bf16[768,2304]{1,0:T(8,128)(2,1)}, u32[]{:S(2)}) %copy-start.9) | copy-done | bytes 3538968
  127.8 2.3 %near.3.refs_0_ = f32[768,128]{1,0:T(8,128)S(1)} custom-call(bf16[768,2304]{1,0:T(8,128)(2,1)S(1)} %copy-done.7, bf16[768,2304]{1,0:T(8,128)(2,1)S(1)} %copy-done.9, bf16[2304,256]{1,0:T(8,128)(2,1)S(1)} %get-tuple-element.51.whl_ref), custom_call_target="tpu_custom_call" | custom-call | flops 1811939328 | bytes 7077888 | tf_op jit(solution)/shard_map/near/pallas_call | solution.py:269
  130.2 1.8 %last.1 = f32[2304,128]{1,0:T(8,128)} custom-call(f32[768,128]{1,0:T(8,128)S(1)} %near.3.refs_0_, f32[768,128]{1,0:T(8,128)S(1)} %copy-done.21, f32[768,128]{1,0:T(8,128)S(1)} %near.5.refs_2_, f32[96,128]{1,0:T(8,128)S(1)} %collective-permute-done.7.m1_ref.refs_3_, f32[96,128]{1,0:T(8,128)S(1)} %collective-permute-done.8.m2_ref.refs_4_, ...), custom_call_target="tpu_custom_call" | custom-call | tf_op jit(solution)/shard_map/last/pallas_call | solution.py:269
  (93 shorter events, 0.7 us)
Async XLA Ops:
  0.0 1.3 copy-start
  1.3 1.1 copy-start.2
  2.3 0.8 copy-start.40
  3.1 0.8 copy-start.42
  3.9 22.5 %copy-start.3 = (f32[2304,64]{0,1:T(8,128)S(1)}, f32[2304,64]{0,1:T(8,128)}, u32[]{:S(2)}) copy-start(f32[2304,64]{0,1:T(8,128)} %param.14) | copy-start | bytes 1769476
  5.2 21.1 %copy-start.1 = (f32[2304,128]{1,0:T(8,128)S(1)}, f32[2304,128]{1,0:T(8,128)}, u32[]{:S(2)}) copy-start(f32[2304,128]{1,0:T(8,128)} %refs_11_.1) | copy-start | bytes 3538948
  5.2 21.2 %copy-start.41 = (f32[1,64,64]{2,1,0:T(8,128)S(1)}, f32[1,64,64]{2,1,0:T(8,128)}, u32[]{:S(2)}) copy-start(f32[1,64,64]{2,1,0:T(8,128)} %leaf_ref.3) | copy-start | bytes 49156
  5.2 21.2 %copy-start.49 = (s32[1,2304]{1,0:T(1,128)S(1)}, s32[1,2304]{1,0:T(1,128)}, u32[]{:S(2)}) copy-start(s32[1,2304]{1,0:T(1,128)} %order_ref.1) | copy-start | bytes 27652
  5.2 5.8 %collective-permute-start = (f32[96,128]{1,0:T(8,128)S(1)}, f32[96,128]{1,0:T(8,128)S(1)}, u32[]{:S(2)}, u32[]{:S(2)}) collective-permute-start(f32[96,128]{1,0:T(8,128)S(1)} %get-tuple-element.41), channel_id=1, source_target_pairs={{0,1},{1,2},{2,3},{3,0},{4,5},{5,6},{6,7},{7,4},{8,9},{9,10},{10,1... | collective-permute-start | bytes 147464 | tf_op jit(solution)/shard_map/ppermute | solution.py:358
  7.4 4.6 %collective-permute-start.1 = (f32[96,128]{1,0:T(8,128)S(1)}, f32[96,128]{1,0:T(8,128)S(1)}, u32[]{:S(2)}, u32[]{:S(2)}) collective-permute-start(f32[96,128]{1,0:T(8,128)S(1)} %get-tuple-element.42), channel_id=1, source_target_pairs={{0,2},{1,3},{2,0},{3,1},{4,6},{5,7},{6,4},{7,5},{8,10},{9,11},{10,... | collective-permute-start | bytes 147464 | tf_op jit(solution)/shard_map/ppermute | solution.py:358
  10.0 3.2 %collective-permute-start.2 = (f32[96,128]{1,0:T(8,128)S(1)}, f32[96,128]{1,0:T(8,128)S(1)}, u32[]{:S(2)}, u32[]{:S(2)}) collective-permute-start(f32[96,128]{1,0:T(8,128)S(1)} %get-tuple-element.43), channel_id=1, source_target_pairs={{0,3},{1,0},{2,1},{3,2},{4,7},{5,4},{6,5},{7,6},{8,11},{9,8},{10,9... | collective-permute-start | bytes 147464 | tf_op jit(solution)/shard_map/ppermute | solution.py:358
  11.0 4.3 %copy-start.34 = (f32[96,128]{1,0:T(8,128)}, f32[96,128]{1,0:T(8,128)S(1)}, u32[]{:S(2)}) copy-start(f32[96,128]{1,0:T(8,128)S(1)} %collective-permute-done.m1_ref.refs_3_) | copy-start | bytes 147460
  15.3 51.1 %all-to-all-start = ((f32[32,32,128]{2,1,0:T(8,128)}), f32[32,32,128]{2,1,0:T(8,128)S(1)}, u32[]{:S(2)}, u32[]{:S(2)}) async-start(f32[32,32,128]{2,1,0:T(8,128)} %middle.2), calls=%async_computation | async-start | bytes 1048576 | tf_op jit(solution)/shard_map/all_to_all | solution.py:360
  26.4 1.2 copy-start.24
  27.6 0.8 copy-start.43
  28.4 0.9 copy-start.44
  29.3 0.8 copy-start.45
  30.1 0.8 copy-start.46
  32.1 7.1 %copy-start.31 = (bf16[128,320]{1,0:T(8,128)(2,1)}, bf16[128,320]{1,0:T(8,128)(2,1)S(1)}, u32[]{:S(2)}) copy-start(bf16[128,320]{1,0:T(8,128)(2,1)S(1)} %get-tuple-element.44.refs_6_) | copy-start | bytes 245764
  32.2 18.5 %copy-start.51 = (f32[2304,8]{1,0:T(8,128)}, f32[2304,8]{1,0:T(8,128)S(1)}, u32[]{:S(2)}) copy-start(f32[2304,8]{1,0:T(8,128)S(1)} %get-tuple-element.34.columns_ref) | copy-start | bytes 221188
  32.2 34.2 %copy-start.18 = (bf16[128,2048]{1,0:T(8,128)(2,1)}, bf16[128,2048]{1,0:T(8,128)(2,1)S(1)}, u32[]{:S(2)}) copy-start(bf16[128,2048]{1,0:T(8,128)(2,1)S(1)} %get-tuple-element.46.couple_ref) | copy-start | bytes 1572868
  39.2 1.8 %copy-start.10 = (bf16[768,2304]{1,0:T(8,128)(2,1)}, bf16[768,2304]{1,0:T(8,128)(2,1)S(1)}, u32[]{:S(2)}) copy-start(bf16[768,2304]{1,0:T(8,128)(2,1)S(1)} %get-tuple-element.54.khi_ref) | copy-start | bytes 10616836
  41.1 1.8 %copy-start.12 = (bf16[768,2304]{1,0:T(8,128)(2,1)}, bf16[768,2304]{1,0:T(8,128)(2,1)S(1)}, u32[]{:S(2)}) copy-start(bf16[768,2304]{1,0:T(8,128)(2,1)S(1)} %get-tuple-element.55.klo_ref) | copy-start | bytes 10616836
  50.7 1.8 %copy-start.14 = (bf16[768,2304]{1,0:T(8,128)(2,1)}, bf16[768,2304]{1,0:T(8,128)(2,1)S(1)}, u32[]{:S(2)}) copy-start(bf16[768,2304]{1,0:T(8,128)(2,1)S(1)} %get-tuple-element.52.khi_ref) | copy-start | bytes 10616836
  52.5 1.8 %copy-start.16 = (bf16[768,2304]{1,0:T(8,128)(2,1)}, bf16[768,2304]{1,0:T(8,128)(2,1)S(1)}, u32[]{:S(2)}) copy-start(bf16[768,2304]{1,0:T(8,128)(2,1)S(1)} %get-tuple-element.53.klo_ref) | copy-start | bytes 10616836
  62.1 1.8 %copy-start.6 = (bf16[768,2304]{1,0:T(8,128)(2,1)}, bf16[768,2304]{1,0:T(8,128)(2,1)S(1)}, u32[]{:S(2)}) copy-start(bf16[768,2304]{1,0:T(8,128)(2,1)S(1)} %get-tuple-element.36.khi_ref) | copy-start | bytes 10616836
  63.8 1.8 %copy-start.8 = (bf16[768,2304]{1,0:T(8,128)(2,1)}, bf16[768,2304]{1,0:T(8,128)(2,1)S(1)}, u32[]{:S(2)}) copy-start(bf16[768,2304]{1,0:T(8,128)(2,1)S(1)} %get-tuple-element.37.klo_ref) | copy-start | bytes 10616836
  65.6 0.8 copy-start.29
  66.9 3.5 %collective-permute-start.3 = (f32[16,128]{1,0:T(8,128)S(1)}, f32[16,128]{1,0:T(8,128)S(1)}, u32[]{:S(2)}, u32[]{:S(2)}) collective-permute-start(f32[16,128]{1,0:T(8,128)S(1)} %get-tuple-element.48), channel_id=1, source_target_pairs={{0,128},{128,0},{1,129},{129,1},{2,130},{130,2},{3,131},{131,3},{4... | collective-permute-start | bytes 24584 | tf_op jit(solution)/shard_map/ppermute | solution.py:369
  70.4 10.4 %copy-start.26 = (f32[768,128]{1,0:T(8,128)S(1)}, f32[768,128]{1,0:T(8,128)}, u32[]{:S(2)}) copy-start(f32[768,128]{1,0:T(8,128)} %copy-done.25) | copy-start | bytes 1179652
  70.4 10.4 %copy-start.28 = (f32[768,128]{1,0:T(8,128)S(1)}, f32[768,128]{1,0:T(8,128)}, u32[]{:S(2)}) copy-start(f32[768,128]{1,0:T(8,128)} %copy-done.27) | copy-start | bytes 1179652
  70.4 10.5 %copy-start.30 = (f32[768,128]{1,0:T(8,128)S(1)}, f32[768,128]{1,0:T(8,128)}, u32[]{:S(2)}) copy-start(f32[768,128]{1,0:T(8,128)} %copy-done.29) | copy-start | bytes 1179652
  70.4 10.5 %copy-start.32 = (bf16[128,320]{1,0:T(8,128)(2,1)S(1)}, bf16[128,320]{1,0:T(8,128)(2,1)}, u32[]{:S(2)}) copy-start(bf16[128,320]{1,0:T(8,128)(2,1)} %copy-done.31) | copy-start | bytes 245764
  70.4 10.5 %copy-start.35 = (f32[96,128]{1,0:T(8,128)S(1)}, f32[96,128]{1,0:T(8,128)}, u32[]{:S(2)}) copy-start(f32[96,128]{1,0:T(8,128)} %copy-done.34) | copy-start | bytes 147460
  70.4 10.5 %copy-start.37 = (f32[96,128]{1,0:T(8,128)S(1)}, f32[96,128]{1,0:T(8,128)}, u32[]{:S(2)}) copy-start(f32[96,128]{1,0:T(8,128)} %copy-done.36) | copy-start | bytes 147460
  70.4 10.5 %copy-start.39 = (f32[96,128]{1,0:T(8,128)S(1)}, f32[96,128]{1,0:T(8,128)}, u32[]{:S(2)}) copy-start(f32[96,128]{1,0:T(8,128)} %copy-done.38) | copy-start | bytes 147460
  70.4 10.5 %copy-start.48 = (f32[64,128]{1,0:T(8,128)S(1)}, f32[64,128]{1,0:T(8,128)}, u32[]{:S(2)}) copy-start(f32[64,128]{1,0:T(8,128)} %copy-done.47) | copy-start | bytes 98308
  70.4 10.4 %collective-permute-start.6 = (f32[32,128]{1,0:T(8,128)S(1)}, f32[32,128]{1,0:T(8,128)S(1)}, u32[]{:S(2)}, u32[]{:S(2)}) collective-permute-start(f32[32,128]{1,0:T(8,128)S(1)} %constant_dynamic-update-slice_fusion.refs_7_), channel_id=1, source_target_pairs={{0,3},{1,0},{2,1},{3,2},{4,7},{5,4},{6,5},{7,6},{8,11},{9,8},{10,9... | collective-permute-start | bytes 49160 | tf_op jit(solution)/shard_map/ppermute | solution.py:371
  72.8 8.0 %collective-permute-start.5 = (f32[32,128]{1,0:T(8,128)S(1)}, f32[32,128]{1,0:T(8,128)S(1)}, u32[]{:S(2)}, u32[]{:S(2)}) collective-permute-start(f32[32,128]{1,0:T(8,128)S(1)} %constant_dynamic-update-slice_fusion.refs_7_), channel_id=1, source_target_pairs={{0,2},{1,3},{2,0},{3,1},{4,6},{5,7},{6,4},{7,5},{8,10},{9,11},{10,... | collective-permute-start | bytes 49160 | tf_op jit(solution)/shard_map/ppermute | solution.py:371
  72.8 8.0 %collective-permute-start.4 = (f32[32,128]{1,0:T(8,128)S(1)}, f32[32,128]{1,0:T(8,128)S(1)}, u32[]{:S(2)}, u32[]{:S(2)}) collective-permute-start(f32[32,128]{1,0:T(8,128)S(1)} %constant_dynamic-update-slice_fusion.refs_7_), channel_id=1, source_target_pairs={{0,1},{1,2},{2,3},{3,0},{4,5},{5,6},{6,7},{7,4},{8,9},{9,10},{10,1... | collective-permute-start | bytes 49160 | tf_op jit(solution)/shard_map/ppermute | solution.py:371
  73.5 1.3 copy-start.50
  74.7 1.3 copy-start.52
  80.8 1.7 %copy-start.4 = (f32[2304,128]{1,0:T(8,128)}, f32[2304,128]{1,0:T(8,128)S(1)}, u32[]{:S(2)}) copy-start(f32[2304,128]{1,0:T(8,128)S(1)} %targets.1.refs_12_) | copy-start | bytes 3538948
  82.4 1.0 copy-start.22
  83.4 4.4 %collective-permute-start.7 = (f32[96,128]{1,0:T(8,128)S(1)}, f32[96,128]{1,0:T(8,128)S(1)}, u32[]{:S(2)}, u32[]{:S(2)}) collective-permute-start(f32[96,128]{1,0:T(8,128)S(1)} %get-tuple-element.56), channel_id=1, source_target_pairs={{0,1},{1,2},{2,3},{3,0},{4,5},{5,6},{6,7},{7,4},{8,9},{9,10},{10,1... | collective-permute-start | bytes 147464 | tf_op jit(solution)/shard_map/ppermute | solution.py:358
  85.4 4.6 %collective-permute-start.8 = (f32[96,128]{1,0:T(8,128)S(1)}, f32[96,128]{1,0:T(8,128)S(1)}, u32[]{:S(2)}, u32[]{:S(2)}) collective-permute-start(f32[96,128]{1,0:T(8,128)S(1)} %get-tuple-element.57), channel_id=1, source_target_pairs={{0,2},{1,3},{2,0},{3,1},{4,6},{5,7},{6,4},{7,5},{8,10},{9,11},{10,... | collective-permute-start | bytes 147464 | tf_op jit(solution)/shard_map/ppermute | solution.py:358
  86.6 3.4 %collective-permute-start.9 = (f32[96,128]{1,0:T(8,128)S(1)}, f32[96,128]{1,0:T(8,128)S(1)}, u32[]{:S(2)}, u32[]{:S(2)}) collective-permute-start(f32[96,128]{1,0:T(8,128)S(1)} %get-tuple-element.58), channel_id=1, source_target_pairs={{0,3},{1,0},{2,1},{3,2},{4,7},{5,4},{6,5},{7,6},{8,11},{9,8},{10,9... | collective-permute-start | bytes 147464 | tf_op jit(solution)/shard_map/ppermute | solution.py:358
  90.8 23.5 %all-to-all-start.1 = ((f32[32,32,128]{2,1,0:T(8,128)}), f32[32,32,128]{2,1,0:T(8,128)S(1)}, u32[]{:S(2)}, u32[]{:S(2)}) async-start(f32[32,32,128]{2,1,0:T(8,128)} %middle.3), calls=%async_computation.1 | async-start | bytes 1048576 | tf_op jit(solution)/shard_map/all_to_all | solution.py:360
  100.3 2.0 %copy-start.11 = (bf16[768,2304]{1,0:T(8,128)(2,1)S(1)}, bf16[768,2304]{1,0:T(8,128)(2,1)}, u32[]{:S(2)}) copy-start(bf16[768,2304]{1,0:T(8,128)(2,1)} %copy-done.10) | copy-start | bytes 10616836
  102.4 2.0 %copy-start.13 = (bf16[768,2304]{1,0:T(8,128)(2,1)S(1)}, bf16[768,2304]{1,0:T(8,128)(2,1)}, u32[]{:S(2)}) copy-start(bf16[768,2304]{1,0:T(8,128)(2,1)} %copy-done.12) | copy-start | bytes 10616836
  104.4 2.3 %copy-start.15 = (bf16[768,2304]{1,0:T(8,128)(2,1)S(1)}, bf16[768,2304]{1,0:T(8,128)(2,1)}, u32[]{:S(2)}) copy-start(bf16[768,2304]{1,0:T(8,128)(2,1)} %copy-done.14) | copy-start | bytes 10616836
  104.4 3.1 %copy-start.17 = (bf16[768,2304]{1,0:T(8,128)(2,1)S(1)}, bf16[768,2304]{1,0:T(8,128)(2,1)}, u32[]{:S(2)}) copy-start(bf16[768,2304]{1,0:T(8,128)(2,1)} %copy-done.16) | copy-start | bytes 10616836
  107.4 6.9 %copy-start.19 = (bf16[128,2048]{1,0:T(8,128)(2,1)S(1)}, bf16[128,2048]{1,0:T(8,128)(2,1)}, u32[]{:S(2)}) copy-start(bf16[128,2048]{1,0:T(8,128)(2,1)} %copy-done.18) | copy-start | bytes 1572868
  109.8 0.8 copy-start.20
  114.8 5.9 %collective-permute-start.10 = (f32[16,128]{1,0:T(8,128)S(1)}, f32[16,128]{1,0:T(8,128)S(1)}, u32[]{:S(2)}, u32[]{:S(2)}) collective-permute-start(f32[16,128]{1,0:T(8,128)S(1)} %get-tuple-element.61), channel_id=1, source_target_pairs={{0,128},{128,0},{1,129},{129,1},{2,130},{130,2},{3,131},{131,3},{4... | collective-permute-start | bytes 24584 | tf_op jit(solution)/shard_map/ppermute | solution.py:369
  120.7 9.4 %collective-permute-start.13 = (f32[32,128]{1,0:T(8,128)S(1)}, f32[32,128]{1,0:T(8,128)S(1)}, u32[]{:S(2)}, u32[]{:S(2)}) collective-permute-start(f32[32,128]{1,0:T(8,128)S(1)} %constant_dynamic-update-slice_fusion.2.refs_7_), channel_id=1, source_target_pairs={{0,3},{1,0},{2,1},{3,2},{4,7},{5,4},{6,5},{7,6},{8,11},{9,8},{10,9... | collective-permute-start | bytes 49160 | tf_op jit(solution)/shard_map/ppermute | solution.py:371
  123.2 6.9 %collective-permute-start.12 = (f32[32,128]{1,0:T(8,128)S(1)}, f32[32,128]{1,0:T(8,128)S(1)}, u32[]{:S(2)}, u32[]{:S(2)}) collective-permute-start(f32[32,128]{1,0:T(8,128)S(1)} %constant_dynamic-update-slice_fusion.2.refs_7_), channel_id=1, source_target_pairs={{0,2},{1,3},{2,0},{3,1},{4,6},{5,7},{6,4},{7,5},{8,10},{9,11},{10,... | collective-permute-start | bytes 49160 | tf_op jit(solution)/shard_map/ppermute | solution.py:371
  123.2 7.0 %collective-permute-start.11 = (f32[32,128]{1,0:T(8,128)S(1)}, f32[32,128]{1,0:T(8,128)S(1)}, u32[]{:S(2)}, u32[]{:S(2)}) collective-permute-start(f32[32,128]{1,0:T(8,128)S(1)} %constant_dynamic-update-slice_fusion.2.refs_7_), channel_id=1, source_target_pairs={{0,1},{1,2},{2,3},{3,0},{4,5},{5,6},{6,7},{7,4},{8,9},{9,10},{10,1... | collective-permute-start | bytes 49160 | tf_op jit(solution)/shard_map/ppermute | solution.py:371
  123.8 2.0 %copy-start.7 = (bf16[768,2304]{1,0:T(8,128)(2,1)S(1)}, bf16[768,2304]{1,0:T(8,128)(2,1)}, u32[]{:S(2)}) copy-start(bf16[768,2304]{1,0:T(8,128)(2,1)} %copy-done.6) | copy-start | bytes 10616836
  125.8 2.0 %copy-start.9 = (bf16[768,2304]{1,0:T(8,128)(2,1)S(1)}, bf16[768,2304]{1,0:T(8,128)(2,1)}, u32[]{:S(2)}) copy-start(bf16[768,2304]{1,0:T(8,128)(2,1)} %copy-done.8) | copy-start | bytes 10616836
  127.8 2.4 %copy-start.5 = (f32[2304,128]{1,0:T(8,128)S(1)}, f32[2304,128]{1,0:T(8,128)}, u32[]{:S(2)}) copy-start(f32[2304,128]{1,0:T(8,128)} %copy-done.4) | copy-start | bytes 3538948
  127.8 2.4 %copy-start.21 = (f32[768,128]{1,0:T(8,128)S(1)}, f32[768,128]{1,0:T(8,128)}, u32[]{:S(2)}) copy-start(f32[768,128]{1,0:T(8,128)} %copy-done.20) | copy-start | bytes 1179652
  127.8 2.4 %copy-start.23 = (f32[2304,128]{1,0:T(8,128)S(1)}, f32[2304,128]{1,0:T(8,128)}, u32[]{:S(2)}) copy-start(f32[2304,128]{1,0:T(8,128)} %copy-done.22) | copy-start | bytes 3538948
  127.8 2.4 %copy-start.33 = (bf16[128,320]{1,0:T(8,128)(2,1)S(1)}, bf16[128,320]{1,0:T(8,128)(2,1)}, u32[]{:S(2)}) copy-start(bf16[128,320]{1,0:T(8,128)(2,1)} %copy-done.31) | copy-start | bytes 245764
  (5 other events, 3.3 us)

commit v3 on v2

--- a/solution.py
+++ b/solution.py
@@ -19,8 +19,8 @@
 F32 = jnp.float32
 BF16 = jnp.bfloat16
 LOG2E = math.log2(math.e)
-CHUNKS = 3
 BLOCK = 256
+REACH = 5
 TILE = 32
 VMEM = pl.BlockSpec(memory_space=pltpu.VMEM)
 
@@ -114,17 +114,16 @@
 
 
 def prepare_body(
-    coords_ref, order_ref, basis_t_ref, w_ref, leaf_ref, mid_ref, couple_leaf_ref, couple_mid_ref,
-    couple_top_ref, columns_ref, bcat_ref, whl_ref, couple_ref, down_ref,
+    coords_ref, order_ref, basis_t_ref, leaf_ref, mid_ref, couple_leaf_ref, couple_mid_ref,
+    couple_top_ref, columns_ref, bcat_ref, couple_ref, down_ref,
 ):
-    n = w_ref.shape[0]
+    n = coords_ref.shape[1]
     order = order_ref[...].astype(F32)
     rows = jnp.concatenate([coords_ref[...] * LOG2E, order, jnp.zeros((4, n), F32)], axis=0)
     columns_ref[...] = rows.T
     for j in range(n // BLOCK):
         cols = slice(j * BLOCK, (j + 1) * BLOCK)
         bcat_ref[cols, :] = wide(basis_t_ref[:, cols].T)
-    whl_ref[...] = wide(w_ref[...])
     own_mid, own_leaf = lax.axis_index("mid"), lax.axis_index("leaf")
     for m in range(N_MID // 2):
         pair = [
@@ -152,58 +151,79 @@
     lax.fori_loop(0, n // BLOCK, rows, 0)
 
 
-def near_product(khi, klo, whl):
-    a = jnp.dot(khi, whl, preferred_element_type=F32)
-    b = jnp.dot(klo, whl[:, 0:OUT], preferred_element_type=F32)
-    return a[:, :OUT] + (a[:, OUT:] + b)
-
-
-def build_body(scale, first_row, coords_ref, columns_ref, whl_ref, khi_ref, klo_ref, near_ref, own_ref):
-    chunk, points = khi_ref.shape
-
-    def block(i, carry):
+def near_body(scale, coords_ref, columns_ref, w_ref, near_ref, k_ref, sum_ref, own_ref, points_ref, wt_ref):
+    n = w_ref.shape[0]
+    blocks = n // BLOCK
+    wrap = (REACH - 1) * BLOCK
+    for j in range(blocks):
+        cols = slice(j * BLOCK, (j + 1) * BLOCK)
+        wt_ref[:, cols] = tall(w_ref[cols, :].T)
+    points_ref[:, 0:n] = coords_ref[...] * LOG2E
+    points_ref[:, n:] = points_ref[:, 0:wrap]
+    wt_ref[:, n:] = wt_ref[:, 0:wrap]
+    sum_ref[...] = jnp.zeros_like(sum_ref)
+
+    def place(i):
         at = pl.multiple_of(i * BLOCK, BLOCK)
         for k in range(3):
-            own_ref[k] = jnp.broadcast_to(
-                columns_ref[pl.ds(first_row + at, BLOCK), k : k + 1], (BLOCK, OUT)
+            own_ref[k] = jnp.broadcast_to(columns_ref[pl.ds(at, BLOCK), k : k + 1], (BLOCK, OUT))
+        return at
+
+    def build(at, slot, d):
+        for cols in (slice(c, c + OUT) for c in range(d * BLOCK, (d + 1) * BLOCK, OUT)):
+            other = [points_ref[k : k + 1, pl.ds(at + cols.start, OUT)] for k in range(3)]
+            for t in range(BLOCK // TILE):
+                sub = slice(t * TILE, (t + 1) * TILE)
+                diff_sq = None
+                for k in range(3):
+                    delta = own_ref[k, sub, :] - other[k]
+                    diff_sq = delta * delta if diff_sq is None else diff_sq + delta * delta
+                dist = diff_sq * lax.rsqrt(jnp.maximum(diff_sq, 1e-37))
+                k_ref[slot, 0, sub, cols], k_ref[slot, 1, sub, cols] = split(jnp.exp2(-dist))
+
+    def product(w, hi, lo, contract):
+        dims = (((1,), (contract,)), ((), ()))
+        a = lax.dot_general(w, hi, dims, preferred_element_type=F32)
+        b = lax.dot_general(w[:OUT], lo, dims, preferred_element_type=F32)
+        return a[:OUT] + (a[OUT:] + b)
+
+    def use(at, slot, d, count):
+        cols = slice(d * BLOCK, (d + count) * BLOCK)
+        where = pl.ds(at + d * BLOCK, count * BLOCK)
+        part = product(wt_ref[:, where], k_ref[slot, 0, :, cols], k_ref[slot, 1, :, cols], 1)
+        if d:
+            sum_ref[:, where] += product(
+                wt_ref[:, pl.ds(at, BLOCK)], k_ref[slot, 0, :, cols], k_ref[slot, 1, :, cols], 0
             )
-        total = None
-        waiting = None
-        for j in range(points // BLOCK):
-            for half in range(2):
-                cols = slice(j * BLOCK + half * OUT, j * BLOCK + (half + 1) * OUT)
-                other = [coords_ref[k : k + 1, cols] * LOG2E for k in range(3)]
-                for t in range(BLOCK // TILE):
-                    sub = slice(t * TILE, (t + 1) * TILE)
-                    diff_sq = None
-                    for k in range(3):
-                        delta = own_ref[k, sub, :] - other[k]
-                        diff_sq = delta * delta if diff_sq is None else diff_sq + delta * delta
-                    dist = diff_sq * lax.rsqrt(jnp.maximum(diff_sq, 1e-37))
-                    hi, lo = split(jnp.exp2(-dist))
-                    rows = pl.ds(at + t * TILE, TILE)
-                    khi_ref[rows, cols] = hi
-                    klo_ref[rows, cols] = lo
-            if j % 3 == 2:
-                if waiting is not None:
-                    part = near_product(*waiting)
-                    total = part if total is None else total + part
-                at_cols = slice((j - 2) * BLOCK, (j + 1) * BLOCK)
-                rows = pl.ds(at, BLOCK)
-                waiting = khi_ref[rows, at_cols], klo_ref[rows, at_cols], whl_ref[at_cols, :]
-        near_ref[pl.ds(at, BLOCK), :] = (total + near_product(*waiting)) * scale
+        return part
+
+    def finish(at, parts):
+        sum_ref[:, pl.ds(at, BLOCK)] += functools.reduce(jnp.add, parts)
+
+    def pair(p, carry):
+        for slot in range(2):
+            prev = pl.multiple_of((2 * p + slot) * BLOCK, BLOCK)
+            at = place(2 * p + slot + 1)
+            total = None
+            for d in range(REACH):
+                part = use(prev, slot, d, 1)
+                total = part if total is None else total + part
+                build(at, 1 - slot, d)
+            finish(prev, [total])
         return carry
 
-    lax.fori_loop(0, chunk // BLOCK, block, 0)
-
-
-def near_body(scale, khi_ref, klo_ref, whl_ref, near_ref):
-    def block(i, carry):
-        rows = pl.ds(pl.multiple_of(i * BLOCK, BLOCK), BLOCK)
-        near_ref[rows, :] = near_product(khi_ref[rows, :], klo_ref[rows, :], whl_ref[...]) * scale
-        return carry
-
-    lax.fori_loop(0, khi_ref.shape[0] // BLOCK, block, 0)
+    first = place(0)
+    for d in range(REACH):
+        build(first, 0, d)
+    lax.fori_loop(0, (blocks - 1) // 2, pair, 0)
+    last = (blocks - 1) * BLOCK
+    finish(last, [use(last, 0, 0, 1), use(last, 0, 1, REACH - 1)])
+    for j in range(blocks):
+        cols = slice(j * BLOCK, (j + 1) * BLOCK)
+        total = sum_ref[:, cols]
+        if j < REACH - 1:
+            total = total + sum_ref[:, n + j * BLOCK : n + (j + 1) * BLOCK]
+        near_ref[cols, :] = total.T * scale
 
 
 def middle_body(own_ref, m1_ref, m2_ref, m3_ref, out_ref):
@@ -222,10 +242,10 @@
 
 
 def update_body(*refs):
-    near_refs, messages, down_ref, tops = refs[:3], refs[3:6], refs[6], refs[7:11]
-    w_ref, targets_ref, bcat_ref = refs[11:14]
-    last = len(refs) == 15
-    outs = refs[14:] if last else refs[16:]
+    near_ref, messages, down_ref, tops = refs[0], refs[1:4], refs[4], refs[5:9]
+    w_ref, targets_ref, bcat_ref = refs[9:12]
+    last = len(refs) == 13
+    outs = refs[12:] if last else refs[14:]
     own = lax.axis_index("leaf")
     quarters = [lax.rem(own + N_LEAF - k, N_LEAF) for k in range(N_LEAF)]
     g1 = unpack_quarters([ref[0:QROWS, :] for ref in tops], quarters)
@@ -236,21 +256,19 @@
     rhs = jnp.concatenate(
         [jnp.concatenate([hi, lo], axis=1), jnp.concatenate([hi, jnp.zeros_like(lo)], axis=1)], axis=0
     )
-    chunk = near_refs[0].shape[0]
     w_out = outs[0]
     for j in range(w_ref.shape[0] // BLOCK):
         rows = slice(j * BLOCK, (j + 1) * BLOCK)
-        at = j * BLOCK % chunk
         f = jnp.dot(bcat_ref[rows, :], rhs, preferred_element_type=F32)
-        f = near_refs[j * BLOCK // chunk][at : at + BLOCK, :] + (f[:, :OUT] + f[:, OUT:])
+        f = near_ref[rows, :] + (f[:, :OUT] + f[:, OUT:])
         new = w_ref[rows, :] - ((0.5 * jnp.tanh(0.5 * f) + 0.5) - targets_ref[rows, :])
         w_out[rows, :] = new
         if not last:
-            outs[1][rows, :] = wide(new)
+            outs[-1][rows, :] = wide(new)
     if not last:
-        basis_t_ref, up_ref = refs[14:16]
-        s0 = dot3(tall(basis_t_ref[...]), outs[1][...])
-        emit_messages(s0, up_ref[...], outs[2], outs[3:])
+        basis_t_ref, up_ref = refs[12:14]
+        s0 = dot3(tall(basis_t_ref[...]), outs[-1][...])
+        emit_messages(s0, up_ref[...], outs[1], outs[2:5])
 
 
 def params(mib):
@@ -291,30 +309,27 @@
     couple_top,
 ):
     n = weights.shape[0]
-    chunk = n // CHUNKS
     scale = 4.0 / math.sqrt(n)
     basis_t = basis.T
     message_shapes = [shape(2 * QROWS, OUT)] + [shape(RANK + 2 * QROWS, OUT)] * 3
-    near_work = (chunk * n * 2 * 512, chunk * n * 4, 0)
 
     up, own, *messages = call(
         first_body,
         [shape(RANK, 2 * RANK), *message_shapes],
         (basis_t, weights, transfer_leaf, transfer_mid),
-        8,
+        58,
         "first",
     )
-    columns, bcat, whl, couple, down = call(
+    columns, bcat, couple, down = call(
         prepare_body,
         [
             shape(n, 8),
             shape(n, 2 * RANK, dtype=BF16),
-            shape(n, 2 * OUT, dtype=BF16),
             shape(2 * RANK, N_MID * RANK, dtype=BF16),
             shape(2 * RANK, 5 * RANK, dtype=BF16),
         ],
-        (coords, order, basis_t, weights, transfer_leaf, transfer_mid, couple_leaf, couple_mid, couple_top),
-        12,
+        (coords, order, basis_t, transfer_leaf, transfer_mid, couple_leaf, couple_mid, couple_top),
+        58,
         "prepare",
     )
     targets = call(
@@ -326,38 +341,30 @@
         [pltpu.VMEM((n, OUT), BF16)],
         (n * n * 2 * OUT, n * OUT * 8, 0),
     )
-    kernels, near = [], []
-    for c in range(CHUNKS):
-        khi, klo, rows = call(
-            functools.partial(build_body, scale, c * chunk),
-            [shape(chunk, n, dtype=BF16)] * 2 + [shape(chunk, OUT)],
-            (coords, columns, whl),
-            12,
-            "build",
-            [pltpu.VMEM((3, BLOCK, OUT), F32)],
-            (*near_work[:2], 2 * chunk * n),
-        )
-        kernels.append((khi, klo))
-        near.append(rows)
+    own, columns = lax.optimization_barrier((own, columns))
 
     current = weights
     for step in range(STEPS):
         last = step == STEPS - 1
-        if step:
-            near = [
-                call(
-                    functools.partial(near_body, scale),
-                    shape(chunk, OUT),
-                    (khi, klo, whl),
-                    8,
-                    "near",
-                    work=near_work,
-                )
-                for khi, klo in kernels
-            ]
+        near = call(
+            functools.partial(near_body, scale),
+            shape(n, OUT),
+            (coords, columns, current),
+            20,
+            "near",
+            [
+                pltpu.VMEM((2, 2, BLOCK, REACH * BLOCK), BF16),
+                pltpu.VMEM((OUT, n + (REACH - 1) * BLOCK), F32),
+                pltpu.VMEM((3, BLOCK, OUT), F32),
+                pltpu.VMEM((3, n + (REACH - 1) * BLOCK), F32),
+                pltpu.VMEM((2 * OUT, n + (REACH - 1) * BLOCK), BF16),
+            ],
+            (6 * n * n * OUT, n * OUT * 12, n * n),
+        )
         messages = [lax.ppermute(m, "leaf", ring(k)) for k, m in enumerate(messages, 1)]
         spread = call(middle_body, shape(N_MID, 2 * QROWS, OUT), (own, *messages), 4, "middle")
         got = lax.all_to_all(spread, "mid", 0, 0)
+        got, near = lax.optimization_barrier((got, near))
         g1, s2 = call(
             couple_body,
             [shape(QROWS, OUT)] * 2,
@@ -369,16 +376,17 @@
         s2 = lax.ppermute(s2, "top", [(0, 1), (1, 0)])
         top = jnp.concatenate([g1, s2], axis=0)
         tops = [top] + [lax.ppermute(top, "leaf", ring(k)) for k in (1, 2, 3)]
-        far = (*near, *messages, down, *tops, current, targets, bcat)
+        far = (near, *messages, down, *tops, current, targets, bcat)
         if last:
             current = call(update_body, shape(n, OUT), far, 8, "last")
         else:
-            current, whl, own, *messages = call(
+            current, own, *messages = call(
                 update_body,
-                [shape(n, OUT), shape(n, 2 * OUT, dtype=BF16), *message_shapes],
+                [shape(n, OUT), *message_shapes],
                 (*far, basis_t, up),
                 12,
                 "update",
+                [pltpu.VMEM((n, 2 * OUT), BF16)],
             )
     return current
 

time: 133 us -> 103 us (0.77)
  local copies, waits for them, and re-layouts: 36.4 us -> 12 us
  starting transfers between devices: 44.5 us -> 40.8 us
    unnamed x108 -> x52, local copies, waits for them, and re-layouts: 36.4 us -> 12 us
    all_to_all x2, starting transfers between devices: 20.5 us -> 16.9 us  [on_device(): got = lax.all_to_all(spread, 'mid', 0, 0)]
    ppermute x6, waiting for transfers between devices: 0.02 us -> 3.52 us  [on_device(): tops = [top] + [lax.ppermute(top, 'leaf', ring(k)) for k in (1, 2, 3)]]
    all_to_all x2, waiting for transfers between devices: 3.78 us -> 1.51 us  [on_device(): got = lax.all_to_all(spread, 'mid', 0, 0)]
    ppermute x6, waiting for transfers between devices: 4.35 us -> 2.3 us  [on_device(): lax.ppermute(m, 'leaf', ring(k))]
    pallas_call x15 -> x11, Pallas kernels: 40.8 us -> 40 us  [call(): pl.pallas_call(body, out_shape=out, in_specs=[VMEM] * len(operands), out_...]
  transfers between devices with their start and end apart: 16 -> 16, of which waited for: 6 -> 7; matrix products, arithmetic and copies ran while one was open for 0% -> 0% of each run, Pallas kernels for 26% -> 31%
where the time goes in v3:
time: 103 us; the launch traced here: 102 us
  starting transfers between devices  40.8 us (40%)
  Pallas kernels  40 us (39%)
  local copies, waits for them, and re-layouts  12 us (12%)
  waiting for transfers between devices  8.98 us (9%)
    pallas_call x11, Pallas kernels, call(): pl.pallas_call(body, out_shape=out, in_specs=[VMEM] * len(operands), out_...  40 us
    all_to_all x2, starting transfers between devices, on_device(): got = lax.all_to_all(spread, 'mid', 0, 0)  16.9 us
    unnamed x52, local copies, waits for them, and re-layouts  12 us
    ppermute x6, starting transfers between devices, on_device(): lax.ppermute(m, 'leaf', ring(k))  10.7 us
    ppermute x2, starting transfers between devices, on_device(): s2 = lax.ppermute(s2, 'top', [(0, 1), (1, 0)])  7.95 us
    ppermute x6, starting transfers between devices, on_device(): tops = [top] + [lax.ppermute(top, 'leaf', ring(k)) for k in (1, 2, 3)]  5.24 us
    ppermute x6, waiting for transfers between devices, on_device(): tops = [top] + [lax.ppermute(top, 'leaf', ring(k)) for k in (1, 2, 3)]  3.52 us
    ppermute x6, waiting for transfers between devices, on_device(): lax.ppermute(m, 'leaf', ring(k))  2.3 us
  transfers between devices with their start and end apart: 16, of which 7 were waited for; matrix products, arithmetic and copies ran while one was open for 0% of the time, Pallas kernels for 31%

profile of v3, /device:TPU:1, one launch (start us, length us, event | category | flops | bytes accessed | tf_op | source)
XLA Modules:
  0.0 102.1 jit_solution(3614805554047392088)
XLA Ops:
  0.0 2.9 %first.1 = (f32[64,128]{1,0:T(8,128)}, f32[32,128]{1,0:T(8,128)}, f32[96,128]{1,0:T(8,128)}, f32[96,128]{1,0:T(8,128)}, f32[96,128]{1,0:T(8,128)}) custom-call(f32[64,2304]{1,0:T(8,128)} %bitcast.1, f32[2304,128]{1,0:T(8,128)} %refs_9_.1, f32[1,64,64]{2,1,0:T(8,128)} %leaf_ref.3, f32[1,64,64]{2,1,0:T(8,128)} %mid_ref.3), custom_call_target="tpu_custom_call" | custom-call | tf_op jit(solution)/shard_map/first/pallas_call | solution.py:287
  2.9 2.1 %collective-permute-start = (f32[96,128]{1,0:T(8,128)}, f32[96,128]{1,0:T(8,128)S(1)}, u32[]{:S(2)}, u32[]{:S(2)}) collective-permute-start(f32[96,128]{1,0:T(8,128)} %get-tuple-element.32), channel_id=1, source_target_pairs={{0,1},{1,2},{2,3},{3,0},{4,5},{5,6},{6,7},{7,4},{8,9},{9,10},{10,1... | collective-permute-start | bytes 147464 | tf_op jit(solution)/shard_map/ppermute | solution.py:364
  5.0 2.6 %collective-permute-start.1 = (f32[96,128]{1,0:T(8,128)}, f32[96,128]{1,0:T(8,128)S(1)}, u32[]{:S(2)}, u32[]{:S(2)}) collective-permute-start(f32[96,128]{1,0:T(8,128)} %get-tuple-element.33), channel_id=1, source_target_pairs={{0,2},{1,3},{2,0},{3,1},{4,6},{5,7},{6,4},{7,5},{8,10},{9,11},{10,... | collective-permute-start | bytes 147464 | tf_op jit(solution)/shard_map/ppermute | solution.py:364
  7.6 1.1 %collective-permute-start.2 = (f32[96,128]{1,0:T(8,128)}, f32[96,128]{1,0:T(8,128)S(1)}, u32[]{:S(2)}, u32[]{:S(2)}) collective-permute-start(f32[96,128]{1,0:T(8,128)} %get-tuple-element.34), channel_id=1, source_target_pairs={{0,3},{1,0},{2,1},{3,2},{4,7},{5,4},{6,5},{7,6},{8,11},{9,8},{10,9... | collective-permute-start | bytes 147464 | tf_op jit(solution)/shard_map/ppermute | solution.py:364
  8.7 3.8 %prepare.1 = (f32[2304,8]{1,0:T(8,128)}, bf16[2304,128]{1,0:T(8,128)(2,1)}, bf16[128,2048]{1,0:T(8,128)(2,1)}, bf16[128,320]{1,0:T(8,128)(2,1)}) custom-call(f32[3,2304]{1,0:T(4,128)} %coords_ref.5, s32[1,2304]{1,0:T(1,128)} %order_ref.1, f32[64,2304]{1,0:T(8,128)} %bitcast.2, f32[1,64,64]{2,1,0:T(8,128)} %leaf_ref.3, f32[1,64,64]{2,1,0:T(8,128)} %mid_ref.3, ...), custom_call_target="tpu_custom_call" | custom-call | tf_op jit(solution)/shard_map/prepare/pallas_call | solution.py:287
  12.5 0.0 collective-permute-done.m1_ref.refs_1_
  12.6 0.0 collective-permute-done.1.m2_ref.refs_2_
  12.6 0.0 copy-start.13
  12.6 0.0 collective-permute-done.2.m3_ref.refs_3_
  12.6 0.0 copy-done.20
  12.6 0.0 copy-start.15
  12.6 0.9 middle.2
  13.5 0.0 copy-done.13
  13.5 0.0 copy-done.15
  13.5 11.0 %all-to-all-start = ((f32[32,32,128]{2,1,0:T(8,128)}), f32[32,32,128]{2,1,0:T(8,128)S(1)}, u32[]{:S(2)}, u32[]{:S(2)}) async-start(f32[32,32,128]{2,1,0:T(8,128)} %middle.2), calls=%async_computation | async-start | bytes 1048576 | tf_op jit(solution)/shard_map/all_to_all | solution.py:366
  24.5 0.0 copy-done.1
  24.5 0.0 copy-done.17
  24.5 0.0 copy-start.22
  24.5 1.3 %copy-done.22 = f32[2304,8]{1,0:T(8,128)S(1)} copy-done((f32[2304,8]{1,0:T(8,128)S(1)}, f32[2304,8]{1,0:T(8,128)}, u32[]{:S(2)}) %copy-start.22) | copy-done | bytes 73752
  25.8 11.3 %near.2.refs_0_ = f32[2304,128]{1,0:T(8,128)S(1)} custom-call(f32[3,2304]{1,0:T(4,128)S(1)} %copy-done.17, f32[2304,8]{1,0:T(8,128)S(1)} %copy-done.22, f32[2304,128]{1,0:T(8,128)S(1)} %copy-done.1), custom_call_target="tpu_custom_call" | custom-call | flops 4076863488 | bytes 3538944 | tf_op jit(solution)/shard_map/near/pallas_call | solution.py:287
  37.1 0.0 copy-start.4
  37.1 1.0 %copy-done.4 = f32[2304,128]{1,0:T(8,128)} copy-done((f32[2304,128]{1,0:T(8,128)}, f32[2304,128]{1,0:T(8,128)S(1)}, u32[]{:S(2)}) %copy-start.4) | copy-done | bytes 1179672
  38.1 1.5 %all-to-all-done.got_ref = f32[32,32,128]{2,1,0:T(8,128)S(1)} async-done(((f32[32,32,128]{2,1,0:T(8,128)}), f32[32,32,128]{2,1,0:T(8,128)S(1)}, u32[]{:S(2)}, u32[]{:S(2)}) %all-to-all-start) | async-done | bytes 524320 | tf_op jit(solution)/shard_map/all_to_all | solution.py:366
  39.7 0.0 copy-done.3
  39.7 0.5 couple.2
  40.1 3.8 %collective-permute-start.3 = (f32[16,128]{1,0:T(8,128)S(1)}, f32[16,128]{1,0:T(8,128)S(1)}, u32[]{:S(2)}, u32[]{:S(2)}) collective-permute-start(f32[16,128]{1,0:T(8,128)S(1)} %get-tuple-element.41), channel_id=1, source_target_pairs={{0,128},{128,0},{1,129},{129,1},{2,130},{130,2},{3,131},{131,3},{4... | collective-permute-start | bytes 24584 | tf_op jit(solution)/shard_map/ppermute | solution.py:376
  43.9 0.8 collective-permute-done.3
  44.8 0.7 collective-permute-start.6
  45.5 1.6 %collective-permute-start.5 = (f32[32,128]{1,0:T(8,128)S(1)}, f32[32,128]{1,0:T(8,128)S(1)}, u32[]{:S(2)}, u32[]{:S(2)}) collective-permute-start(f32[32,128]{1,0:T(8,128)S(1)} %constant_dynamic-update-slice_fusion.refs_5_), channel_id=1, source_target_pairs={{0,2},{1,3},{2,0},{3,1},{4,6},{5,7},{6,4},{7,5},{8,10},{9,11},{10,... | collective-permute-start | bytes 49160 | tf_op jit(solution)/shard_map/ppermute | solution.py:378
  47.0 0.0 collective-permute-start.4
  47.0 1.3 %copy-done.21 = s32[2304,128]{1,0:T(8,128)S(1)} copy-done((s32[2304,128]{1,0:T(8,128)S(1)}, s32[2304,128]{1,0:T(8,128)}, u32[]{:S(2)}) %copy-start.21) | copy-done | bytes 1179672
  48.3 1.3 %copy-done.23 = f32[2304,8]{1,0:T(8,128)S(1)} copy-done((f32[2304,8]{1,0:T(8,128)S(1)}, f32[2304,8]{1,0:T(8,128)}, u32[]{:S(2)}) %copy-start.23) | copy-done | bytes 73752
  49.6 4.8 %targets.1.refs_10_ = f32[2304,128]{1,0:T(8,128)S(1)} custom-call(f32[2304,8]{1,0:T(8,128)S(1)} %copy-done.23, s32[2304,128]{1,0:T(8,128)S(1)} %copy-done.21), custom_call_target="tpu_custom_call" | custom-call | flops 1358954496 | bytes 2359296 | tf_op jit(solution)/shard_map/targets/pallas_call | solution.py:287
  54.3 0.0 collective-permute-done.6.refs_8_
  54.3 0.0 collective-permute-done.5.refs_7_
  54.4 0.0 collective-permute-done.4.refs_6_
  54.4 1.5 %update.1 = (f32[2304,128]{1,0:T(8,128)S(1)}, f32[32,128]{1,0:T(8,128)S(1)}, f32[96,128]{1,0:T(8,128)S(1)}, f32[96,128]{1,0:T(8,128)S(1)}, f32[96,128]{1,0:T(8,128)S(1)}) custom-call(f32[2304,128]{1,0:T(8,128)S(1)} %copy-done.5, f32[96,128]{1,0:T(8,128)S(1)} %collective-permute-done.m1_ref.refs_1_, f32[96,128]{1,0:T(8,128)S(1)} %copy-done.14, ...), custom_call_target="tpu_custom_call" | custom-call | tf_op jit(solution)/shard_map/update/pallas_call | solution.py:287
  56.0 1.0 %copy-done.6 = f32[2304,128]{1,0:T(8,128)} copy-done((f32[2304,128]{1,0:T(8,128)}, f32[2304,128]{1,0:T(8,128)S(1)}, u32[]{:S(2)}) %copy-start.6) | copy-done | bytes 1179672
  57.0 1.1 %collective-permute-start.7 = (f32[96,128]{1,0:T(8,128)S(1)}, f32[96,128]{1,0:T(8,128)S(1)}, u32[]{:S(2)}, u32[]{:S(2)}) collective-permute-start(f32[96,128]{1,0:T(8,128)S(1)} %get-tuple-element.45), channel_id=1, source_target_pairs={{0,1},{1,2},{2,3},{3,0},{4,5},{5,6},{6,7},{7,4},{8,9},{9,10},{10,1... | collective-permute-start | bytes 147464 | tf_op jit(solution)/shard_map/ppermute | solution.py:364
  58.1 2.8 %collective-permute-start.8 = (f32[96,128]{1,0:T(8,128)S(1)}, f32[96,128]{1,0:T(8,128)S(1)}, u32[]{:S(2)}, u32[]{:S(2)}) collective-permute-start(f32[96,128]{1,0:T(8,128)S(1)} %get-tuple-element.46), channel_id=1, source_target_pairs={{0,2},{1,3},{2,0},{3,1},{4,6},{5,7},{6,4},{7,5},{8,10},{9,11},{10,... | collective-permute-start | bytes 147464 | tf_op jit(solution)/shard_map/ppermute | solution.py:364
  60.9 1.0 %collective-permute-start.9 = (f32[96,128]{1,0:T(8,128)S(1)}, f32[96,128]{1,0:T(8,128)S(1)}, u32[]{:S(2)}, u32[]{:S(2)}) collective-permute-start(f32[96,128]{1,0:T(8,128)S(1)} %get-tuple-element.47), channel_id=1, source_target_pairs={{0,3},{1,0},{2,1},{3,2},{4,7},{5,4},{6,5},{7,6},{8,11},{9,8},{10,9... | collective-permute-start | bytes 147464 | tf_op jit(solution)/shard_map/ppermute | solution.py:364
  61.9 0.0 collective-permute-done.7.m1_ref.refs_1_
  61.9 1.1 %collective-permute-done.8.m2_ref.refs_2_ = f32[96,128]{1,0:T(8,128)S(1)} collective-permute-done((f32[96,128]{1,0:T(8,128)S(1)}, f32[96,128]{1,0:T(8,128)S(1)}, u32[]{:S(2)}, u32[]{:S(2)}) %collective-permute-start.8) | collective-permute-done | bytes 49184 | tf_op jit(solution)/shard_map/ppermute | solution.py:364
  63.0 1.2 %collective-permute-done.9.m3_ref.refs_3_ = f32[96,128]{1,0:T(8,128)S(1)} collective-permute-done((f32[96,128]{1,0:T(8,128)S(1)}, f32[96,128]{1,0:T(8,128)S(1)}, u32[]{:S(2)}, u32[]{:S(2)}) %collective-permute-start.9) | collective-permute-done | bytes 49184 | tf_op jit(solution)/shard_map/ppermute | solution.py:364
  64.2 0.9 middle.3
  65.1 5.8 %all-to-all-start.1 = ((f32[32,32,128]{2,1,0:T(8,128)}), f32[32,32,128]{2,1,0:T(8,128)S(1)}, u32[]{:S(2)}, u32[]{:S(2)}) async-start(f32[32,32,128]{2,1,0:T(8,128)} %middle.3), calls=%async_computation.1 | async-start | bytes 1048576 | tf_op jit(solution)/shard_map/all_to_all | solution.py:366
  70.9 1.3 %copy-done.7 = f32[2304,128]{1,0:T(8,128)S(1)} copy-done((f32[2304,128]{1,0:T(8,128)S(1)}, f32[2304,128]{1,0:T(8,128)}, u32[]{:S(2)}) %copy-start.7) | copy-done | bytes 1179672
  72.2 1.3 %copy-done.24 = f32[2304,8]{1,0:T(8,128)S(1)} copy-done((f32[2304,8]{1,0:T(8,128)S(1)}, f32[2304,8]{1,0:T(8,128)}, u32[]{:S(2)}) %copy-start.24) | copy-done | bytes 73752
  73.5 11.3 %near.3.refs_0_ = f32[2304,128]{1,0:T(8,128)S(1)} custom-call(f32[3,2304]{1,0:T(4,128)S(1)} %copy-done.18, f32[2304,8]{1,0:T(8,128)S(1)} %copy-done.24, f32[2304,128]{1,0:T(8,128)S(1)} %copy-done.7), custom_call_target="tpu_custom_call" | custom-call | flops 4076863488 | bytes 3538944 | tf_op jit(solution)/shard_map/near/pallas_call | solution.py:287
  84.8 0.0 copy-start.9
  84.8 1.0 copy-done.9
  85.8 0.0 all-to-all-done.1.got_ref
  85.8 0.5 couple.3
  86.3 4.2 %collective-permute-start.10 = (f32[16,128]{1,0:T(8,128)S(1)}, f32[16,128]{1,0:T(8,128)S(1)}, u32[]{:S(2)}, u32[]{:S(2)}) collective-permute-start(f32[16,128]{1,0:T(8,128)S(1)} %get-tuple-element.52), channel_id=1, source_target_pairs={{0,128},{128,0},{1,129},{129,1},{2,130},{130,2},{3,131},{131,3},{4... | collective-permute-start | bytes 24584 | tf_op jit(solution)/shard_map/ppermute | solution.py:376
  90.5 0.8 collective-permute-done.10
  91.3 2.4 %collective-permute-start.13 = (f32[32,128]{1,0:T(8,128)S(1)}, f32[32,128]{1,0:T(8,128)S(1)}, u32[]{:S(2)}, u32[]{:S(2)}) collective-permute-start(f32[32,128]{1,0:T(8,128)S(1)} %constant_dynamic-update-slice_fusion.2.refs_5_), channel_id=1, source_target_pairs={{0,3},{1,0},{2,1},{3,2},{4,7},{5,4},{6,5},{7,6},{8,11},{9,8},{10,9... | collective-permute-start | bytes 49160 | tf_op jit(solution)/shard_map/ppermute | solution.py:378
  93.7 0.0 collective-permute-start.12
  93.7 0.6 collective-permute-start.11
  94.3 0.3 collective-permute-done.13.refs_8_
  94.6 3.2 %collective-permute-done.12.refs_7_ = f32[32,128]{1,0:T(8,128)S(1)} collective-permute-done((f32[32,128]{1,0:T(8,128)S(1)}, f32[32,128]{1,0:T(8,128)S(1)}, u32[]{:S(2)}, u32[]{:S(2)}) %collective-permute-start.12) | collective-permute-done | bytes 16416 | tf_op jit(solution)/shard_map/ppermute | solution.py:378
  97.8 0.0 collective-permute-done.11.refs_6_
  97.8 1.3 %copy-done.8 = f32[2304,128]{1,0:T(8,128)S(1)} copy-done((f32[2304,128]{1,0:T(8,128)S(1)}, f32[2304,128]{1,0:T(8,128)}, u32[]{:S(2)}) %copy-start.8) | copy-done | bytes 1179672
  99.1 1.3 %copy-done.10 = f32[2304,128]{1,0:T(8,128)S(1)} copy-done((f32[2304,128]{1,0:T(8,128)S(1)}, f32[2304,128]{1,0:T(8,128)}, u32[]{:S(2)}) %copy-start.10) | copy-done | bytes 1179672
  100.3 1.8 %last.1 = f32[2304,128]{1,0:T(8,128)} custom-call(f32[2304,128]{1,0:T(8,128)S(1)} %copy-done.10, f32[96,128]{1,0:T(8,128)S(1)} %collective-permute-done.7.m1_ref.refs_1_, f32[96,128]{1,0:T(8,128)S(1)} %collective-permute-done.8.m2_ref.refs_2_, f32[96,128]{1,0:T(8,128)S(1)} %collective-permute-done.9.m3_ref.refs_3_, bf16[128,320]{1,0:T(8,128)(2,1)S(1)} %copy-done.12, ...), custom_call_target="tpu_custom_call" | custom-call | tf_op jit(solution)/shard_map/last/pallas_call | solution.py:287
  (33 shorter events, 0.1 us)
Async XLA Ops:
  2.9 9.7 %copy-start.20 = (f32[32,128]{1,0:T(8,128)S(1)}, f32[32,128]{1,0:T(8,128)}, u32[]{:S(2)}) copy-start(f32[32,128]{1,0:T(8,128)} %get-tuple-element.31.own_ref) | copy-start | bytes 49156
  2.9 9.7 %collective-permute-start = (f32[96,128]{1,0:T(8,128)}, f32[96,128]{1,0:T(8,128)S(1)}, u32[]{:S(2)}, u32[]{:S(2)}) collective-permute-start(f32[96,128]{1,0:T(8,128)} %get-tuple-element.32), channel_id=1, source_target_pairs={{0,1},{1,2},{2,3},{3,0},{4,5},{5,6},{6,7},{7,4},{8,9},{9,10},{10,1... | collective-permute-start | bytes 147464 | tf_op jit(solution)/shard_map/ppermute | solution.py:364
  5.0 7.6 %collective-permute-start.1 = (f32[96,128]{1,0:T(8,128)}, f32[96,128]{1,0:T(8,128)S(1)}, u32[]{:S(2)}, u32[]{:S(2)}) collective-permute-start(f32[96,128]{1,0:T(8,128)} %get-tuple-element.33), channel_id=1, source_target_pairs={{0,2},{1,3},{2,0},{3,1},{4,6},{5,7},{6,4},{7,5},{8,10},{9,11},{10,... | collective-permute-start | bytes 147464 | tf_op jit(solution)/shard_map/ppermute | solution.py:364
  7.6 5.0 %collective-permute-start.2 = (f32[96,128]{1,0:T(8,128)}, f32[96,128]{1,0:T(8,128)S(1)}, u32[]{:S(2)}, u32[]{:S(2)}) collective-permute-start(f32[96,128]{1,0:T(8,128)} %get-tuple-element.34), channel_id=1, source_target_pairs={{0,3},{1,0},{2,1},{3,2},{4,7},{5,4},{6,5},{7,6},{8,11},{9,8},{10,9... | collective-permute-start | bytes 147464 | tf_op jit(solution)/shard_map/ppermute | solution.py:364
  12.5 12.0 %copy-start.1 = (f32[2304,128]{1,0:T(8,128)S(1)}, f32[2304,128]{1,0:T(8,128)}, u32[]{:S(2)}) copy-start(f32[2304,128]{1,0:T(8,128)} %refs_9_.1) | copy-start | bytes 3538948
  12.5 12.0 %copy-start.17 = (f32[3,2304]{1,0:T(4,128)S(1)}, f32[3,2304]{1,0:T(4,128)}, u32[]{:S(2)}) copy-start(f32[3,2304]{1,0:T(4,128)} %coords_ref.5) | copy-start | bytes 82948
  12.6 0.9 copy-start.13
  12.6 0.9 copy-start.15
  13.5 26.2 %all-to-all-start = ((f32[32,32,128]{2,1,0:T(8,128)}), f32[32,32,128]{2,1,0:T(8,128)S(1)}, u32[]{:S(2)}, u32[]{:S(2)}) async-start(f32[32,32,128]{2,1,0:T(8,128)} %middle.2), calls=%async_computation | async-start | bytes 1048576 | tf_op jit(solution)/shard_map/all_to_all | solution.py:366
  24.5 1.3 %copy-start.22 = (f32[2304,8]{1,0:T(8,128)S(1)}, f32[2304,8]{1,0:T(8,128)}, u32[]{:S(2)}) copy-start(f32[2304,8]{1,0:T(8,128)} %get-tuple-element.35.columns_ref) | copy-start | bytes 221188
  25.8 13.9 %copy-start.3 = (bf16[128,2048]{1,0:T(8,128)(2,1)S(1)}, bf16[128,2048]{1,0:T(8,128)(2,1)}, u32[]{:S(2)}) copy-start(bf16[128,2048]{1,0:T(8,128)(2,1)} %get-tuple-element.39.couple_ref) | copy-start | bytes 1572868
  37.1 1.0 %copy-start.4 = (f32[2304,128]{1,0:T(8,128)}, f32[2304,128]{1,0:T(8,128)S(1)}, u32[]{:S(2)}) copy-start(f32[2304,128]{1,0:T(8,128)S(1)} %near.2.refs_0_) | copy-start | bytes 3538948
  40.1 4.6 %collective-permute-start.3 = (f32[16,128]{1,0:T(8,128)S(1)}, f32[16,128]{1,0:T(8,128)S(1)}, u32[]{:S(2)}, u32[]{:S(2)}) collective-permute-start(f32[16,128]{1,0:T(8,128)S(1)} %get-tuple-element.41), channel_id=1, source_target_pairs={{0,128},{128,0},{1,129},{129,1},{2,130},{130,2},{3,131},{131,3},{4... | collective-permute-start | bytes 24584 | tf_op jit(solution)/shard_map/ppermute | solution.py:376
  44.7 9.6 %copy-start = (f32[2304,64]{0,1:T(8,128)S(1)}, f32[2304,64]{0,1:T(8,128)}, u32[]{:S(2)}) copy-start(f32[2304,64]{0,1:T(8,128)} %param.14) | copy-start | bytes 1769476
  44.7 9.7 %copy-start.2 = (bf16[2304,128]{1,0:T(8,128)(2,1)S(1)}, bf16[2304,128]{1,0:T(8,128)(2,1)}, u32[]{:S(2)}) copy-start(bf16[2304,128]{1,0:T(8,128)(2,1)} %get-tuple-element.42.refs_11_) | copy-start | bytes 1769476
  44.7 9.7 %copy-start.5 = (f32[2304,128]{1,0:T(8,128)S(1)}, f32[2304,128]{1,0:T(8,128)}, u32[]{:S(2)}) copy-start(f32[2304,128]{1,0:T(8,128)} %copy-done.4) | copy-start | bytes 3538948
  44.7 9.7 %copy-start.11 = (bf16[128,320]{1,0:T(8,128)(2,1)S(1)}, bf16[128,320]{1,0:T(8,128)(2,1)}, u32[]{:S(2)}) copy-start(bf16[128,320]{1,0:T(8,128)(2,1)} %get-tuple-element.37.refs_4_) | copy-start | bytes 245764
  44.7 9.7 %copy-start.14 = (f32[96,128]{1,0:T(8,128)S(1)}, f32[96,128]{1,0:T(8,128)}, u32[]{:S(2)}) copy-start(f32[96,128]{1,0:T(8,128)} %copy-done.13) | copy-start | bytes 147460
  44.7 9.7 %copy-start.16 = (f32[96,128]{1,0:T(8,128)S(1)}, f32[96,128]{1,0:T(8,128)}, u32[]{:S(2)}) copy-start(f32[96,128]{1,0:T(8,128)} %copy-done.15) | copy-start | bytes 147460
  44.8 9.7 %copy-start.19 = (f32[64,128]{1,0:T(8,128)S(1)}, f32[64,128]{1,0:T(8,128)}, u32[]{:S(2)}) copy-start(f32[64,128]{1,0:T(8,128)} %get-tuple-element.43.refs_13_) | copy-start | bytes 98308
  44.8 9.6 %collective-permute-start.6 = (f32[32,128]{1,0:T(8,128)S(1)}, f32[32,128]{1,0:T(8,128)S(1)}, u32[]{:S(2)}, u32[]{:S(2)}) collective-permute-start(f32[32,128]{1,0:T(8,128)S(1)} %constant_dynamic-update-slice_fusion.refs_5_), channel_id=1, source_target_pairs={{0,3},{1,0},{2,1},{3,2},{4,7},{5,4},{6,5},{7,6},{8,11},{9,8},{10,9... | collective-permute-start | bytes 49160 | tf_op jit(solution)/shard_map/ppermute | solution.py:378
  45.5 8.9 %collective-permute-start.5 = (f32[32,128]{1,0:T(8,128)S(1)}, f32[32,128]{1,0:T(8,128)S(1)}, u32[]{:S(2)}, u32[]{:S(2)}) collective-permute-start(f32[32,128]{1,0:T(8,128)S(1)} %constant_dynamic-update-slice_fusion.refs_5_), channel_id=1, source_target_pairs={{0,2},{1,3},{2,0},{3,1},{4,6},{5,7},{6,4},{7,5},{8,10},{9,11},{10,... | collective-permute-start | bytes 49160 | tf_op jit(solution)/shard_map/ppermute | solution.py:378
  47.0 7.3 %collective-permute-start.4 = (f32[32,128]{1,0:T(8,128)S(1)}, f32[32,128]{1,0:T(8,128)S(1)}, u32[]{:S(2)}, u32[]{:S(2)}) collective-permute-start(f32[32,128]{1,0:T(8,128)S(1)} %constant_dynamic-update-slice_fusion.refs_5_), channel_id=1, source_target_pairs={{0,1},{1,2},{2,3},{3,0},{4,5},{5,6},{6,7},{7,4},{8,9},{9,10},{10,1... | collective-permute-start | bytes 49160 | tf_op jit(solution)/shard_map/ppermute | solution.py:378
  47.0 1.3 %copy-start.21 = (s32[2304,128]{1,0:T(8,128)S(1)}, s32[2304,128]{1,0:T(8,128)}, u32[]{:S(2)}) copy-start(s32[2304,128]{1,0:T(8,128)} %labels_ref.1) | copy-start | bytes 3538948
  48.3 1.3 %copy-start.23 = (f32[2304,8]{1,0:T(8,128)S(1)}, f32[2304,8]{1,0:T(8,128)}, u32[]{:S(2)}) copy-start(f32[2304,8]{1,0:T(8,128)} %get-tuple-element.35.columns_ref) | copy-start | bytes 221188
  56.0 1.0 %copy-start.6 = (f32[2304,128]{1,0:T(8,128)}, f32[2304,128]{1,0:T(8,128)S(1)}, u32[]{:S(2)}) copy-start(f32[2304,128]{1,0:T(8,128)S(1)} %get-tuple-element.48.w_ref.refs_9_) | copy-start | bytes 3538948
  57.0 13.9 %copy-start.18 = (f32[3,2304]{1,0:T(4,128)S(1)}, f32[3,2304]{1,0:T(4,128)}, u32[]{:S(2)}) copy-start(f32[3,2304]{1,0:T(4,128)} %coords_ref.5) | copy-start | bytes 82948
  57.0 4.9 %collective-permute-start.7 = (f32[96,128]{1,0:T(8,128)S(1)}, f32[96,128]{1,0:T(8,128)S(1)}, u32[]{:S(2)}, u32[]{:S(2)}) collective-permute-start(f32[96,128]{1,0:T(8,128)S(1)} %get-tuple-element.45), channel_id=1, source_target_pairs={{0,1},{1,2},{2,3},{3,0},{4,5},{5,6},{6,7},{7,4},{8,9},{9,10},{10,1... | collective-permute-start | bytes 147464 | tf_op jit(solution)/shard_map/ppermute | solution.py:364
  58.1 4.9 %collective-permute-start.8 = (f32[96,128]{1,0:T(8,128)S(1)}, f32[96,128]{1,0:T(8,128)S(1)}, u32[]{:S(2)}, u32[]{:S(2)}) collective-permute-start(f32[96,128]{1,0:T(8,128)S(1)} %get-tuple-element.46), channel_id=1, source_target_pairs={{0,2},{1,3},{2,0},{3,1},{4,6},{5,7},{6,4},{7,5},{8,10},{9,11},{10,... | collective-permute-start | bytes 147464 | tf_op jit(solution)/shard_map/ppermute | solution.py:364
  60.9 3.3 %collective-permute-start.9 = (f32[96,128]{1,0:T(8,128)S(1)}, f32[96,128]{1,0:T(8,128)S(1)}, u32[]{:S(2)}, u32[]{:S(2)}) collective-permute-start(f32[96,128]{1,0:T(8,128)S(1)} %get-tuple-element.47), channel_id=1, source_target_pairs={{0,3},{1,0},{2,1},{3,2},{4,7},{5,4},{6,5},{7,6},{8,11},{9,8},{10,9... | collective-permute-start | bytes 147464 | tf_op jit(solution)/shard_map/ppermute | solution.py:364
  65.1 20.7 %all-to-all-start.1 = ((f32[32,32,128]{2,1,0:T(8,128)}), f32[32,32,128]{2,1,0:T(8,128)S(1)}, u32[]{:S(2)}, u32[]{:S(2)}) async-start(f32[32,32,128]{2,1,0:T(8,128)} %middle.3), calls=%async_computation.1 | async-start | bytes 1048576 | tf_op jit(solution)/shard_map/all_to_all | solution.py:366
  70.9 1.3 %copy-start.7 = (f32[2304,128]{1,0:T(8,128)S(1)}, f32[2304,128]{1,0:T(8,128)}, u32[]{:S(2)}) copy-start(f32[2304,128]{1,0:T(8,128)} %copy-done.6) | copy-start | bytes 3538948
  72.2 1.3 %copy-start.24 = (f32[2304,8]{1,0:T(8,128)S(1)}, f32[2304,8]{1,0:T(8,128)}, u32[]{:S(2)}) copy-start(f32[2304,8]{1,0:T(8,128)} %get-tuple-element.35.columns_ref) | copy-start | bytes 221188
  73.5 24.3 %copy-start.12 = (bf16[128,320]{1,0:T(8,128)(2,1)S(1)}, bf16[128,320]{1,0:T(8,128)(2,1)}, u32[]{:S(2)}) copy-start(bf16[128,320]{1,0:T(8,128)(2,1)} %get-tuple-element.37.refs_4_) | copy-start | bytes 245764
  84.8 1.0 copy-start.9
  86.3 5.0 %collective-permute-start.10 = (f32[16,128]{1,0:T(8,128)S(1)}, f32[16,128]{1,0:T(8,128)S(1)}, u32[]{:S(2)}, u32[]{:S(2)}) collective-permute-start(f32[16,128]{1,0:T(8,128)S(1)} %get-tuple-element.52), channel_id=1, source_target_pairs={{0,128},{128,0},{1,129},{129,1},{2,130},{130,2},{3,131},{131,3},{4... | collective-permute-start | bytes 24584 | tf_op jit(solution)/shard_map/ppermute | solution.py:376
  91.3 3.3 %collective-permute-start.13 = (f32[32,128]{1,0:T(8,128)S(1)}, f32[32,128]{1,0:T(8,128)S(1)}, u32[]{:S(2)}, u32[]{:S(2)}) collective-permute-start(f32[32,128]{1,0:T(8,128)S(1)} %constant_dynamic-update-slice_fusion.2.refs_5_), channel_id=1, source_target_pairs={{0,3},{1,0},{2,1},{3,2},{4,7},{5,4},{6,5},{7,6},{8,11},{9,8},{10,9... | collective-permute-start | bytes 49160 | tf_op jit(solution)/shard_map/ppermute | solution.py:378
  93.7 4.1 %collective-permute-start.12 = (f32[32,128]{1,0:T(8,128)S(1)}, f32[32,128]{1,0:T(8,128)S(1)}, u32[]{:S(2)}, u32[]{:S(2)}) collective-permute-start(f32[32,128]{1,0:T(8,128)S(1)} %constant_dynamic-update-slice_fusion.2.refs_5_), channel_id=1, source_target_pairs={{0,2},{1,3},{2,0},{3,1},{4,6},{5,7},{6,4},{7,5},{8,10},{9,11},{10,... | collective-permute-start | bytes 49160 | tf_op jit(solution)/shard_map/ppermute | solution.py:378
  93.7 4.1 %collective-permute-start.11 = (f32[32,128]{1,0:T(8,128)S(1)}, f32[32,128]{1,0:T(8,128)S(1)}, u32[]{:S(2)}, u32[]{:S(2)}) collective-permute-start(f32[32,128]{1,0:T(8,128)S(1)} %constant_dynamic-update-slice_fusion.2.refs_5_), channel_id=1, source_target_pairs={{0,1},{1,2},{2,3},{3,0},{4,5},{5,6},{6,7},{7,4},{8,9},{9,10},{10,1... | collective-permute-start | bytes 49160 | tf_op jit(solution)/shard_map/ppermute | solution.py:378
  97.8 1.3 %copy-start.8 = (f32[2304,128]{1,0:T(8,128)S(1)}, f32[2304,128]{1,0:T(8,128)}, u32[]{:S(2)}) copy-start(f32[2304,128]{1,0:T(8,128)} %copy-done.6) | copy-start | bytes 3538948
  99.1 1.3 %copy-start.10 = (f32[2304,128]{1,0:T(8,128)S(1)}, f32[2304,128]{1,0:T(8,128)}, u32[]{:S(2)}) copy-start(f32[2304,128]{1,0:T(8,128)} %copy-done.9) | copy-start | bytes 3538948

commit v4 on v3

--- a/solution.py
+++ b/solution.py
@@ -21,8 +21,10 @@
 LOG2E = math.log2(math.e)
 BLOCK = 256
 REACH = 5
+BITS = 8
 TILE = 32
 VMEM = pl.BlockSpec(memory_space=pltpu.VMEM)
+HBM = pl.BlockSpec(memory_space=pltpu.HBM)
 
 
 def split(x):
@@ -114,13 +116,10 @@
 
 
 def prepare_body(
-    coords_ref, order_ref, basis_t_ref, leaf_ref, mid_ref, couple_leaf_ref, couple_mid_ref,
-    couple_top_ref, columns_ref, bcat_ref, couple_ref, down_ref,
+    basis_t_ref, leaf_ref, mid_ref, couple_leaf_ref, couple_mid_ref, couple_top_ref,
+    bcat_ref, couple_ref, down_ref,
 ):
-    n = coords_ref.shape[1]
-    order = order_ref[...].astype(F32)
-    rows = jnp.concatenate([coords_ref[...] * LOG2E, order, jnp.zeros((4, n), F32)], axis=0)
-    columns_ref[...] = rows.T
+    n = basis_t_ref.shape[1]
     for j in range(n // BLOCK):
         cols = slice(j * BLOCK, (j + 1) * BLOCK)
         bcat_ref[cols, :] = wide(basis_t_ref[:, cols].T)
@@ -137,36 +136,49 @@
     down_ref[...] = tall(jnp.concatenate([*siblings, leaf_ref[0], from_top], axis=1))
 
 
-def targets_body(columns_ref, labels_ref, out_ref, labels16_ref):
+def targets_body(order_ref, labels_ref, out_ref):
     n = labels_ref.shape[0]
-    labels16_ref[...] = labels_ref[...].astype(BF16)
-    lane = lax.broadcasted_iota(jnp.int32, (BLOCK, n), 1).astype(F32)
-
-    def rows(i, carry):
-        at = pl.ds(pl.multiple_of(i * BLOCK, BLOCK), BLOCK)
-        chosen = jnp.where(columns_ref[at, 3:4] == lane, 1.0, 0.0).astype(BF16)
-        out_ref[at, :] = jnp.dot(chosen, labels16_ref[...], preferred_element_type=F32)
-        return carry
-
-    lax.fori_loop(0, n // BLOCK, rows, 0)
-
-
-def near_body(scale, coords_ref, columns_ref, w_ref, near_ref, k_ref, sum_ref, own_ref, points_ref, wt_ref):
-    n = w_ref.shape[0]
+    group = n // BITS
+    packed = jnp.zeros((group, OUT), F32)
+    for g in range(BITS):
+        packed = packed + labels_ref[g * group : (g + 1) * group, :].astype(F32) * float(1 << g)
+    packed = packed.astype(BF16)
+    order = order_ref[...]
+    which = jnp.zeros_like(order)
+    place = jnp.ones(order.shape, F32)
+    for g in range(1, BITS):
+        beyond = order >= g * group
+        which = jnp.where(beyond, g * group, which)
+        place = jnp.where(beyond, 1.0 / (1 << g), place)
+    rows = jnp.concatenate([(order - which).astype(F32), place, jnp.zeros((6, n), F32)], axis=0)
+    lane = lax.broadcasted_iota(jnp.int32, (BLOCK, group), 1).astype(F32)
+    for j in range(n // BLOCK):
+        at = slice(j * BLOCK, (j + 1) * BLOCK)
+        columns = rows[:, at].T
+        chosen = jnp.where(columns[:, 0:1] == lane, 1.0, 0.0).astype(BF16)
+        value = jnp.dot(chosen, packed, preferred_element_type=F32) * columns[:, 1:2]
+        value = jnp.floor(value)
+        out_ref[at, :] = value - 2.0 * jnp.floor(0.5 * value)
+
+
+def near_body(
+    scale, coords_ref, w_hbm, near_hbm, k_ref, sum_ref, own_ref, points_ref, wt_ref, w_ref, near_ref, w_sem, near_sem
+):
+    n = w_hbm.shape[0]
     blocks = n // BLOCK
     wrap = (REACH - 1) * BLOCK
-    for j in range(blocks):
-        cols = slice(j * BLOCK, (j + 1) * BLOCK)
-        wt_ref[:, cols] = tall(w_ref[cols, :].T)
-    points_ref[:, 0:n] = coords_ref[...] * LOG2E
+    fetch = pltpu.make_async_copy(w_hbm, w_ref, w_sem)
+    fetch.start()
+    points_ref[0:3, 0:n] = coords_ref[...] * LOG2E
+    points_ref[3:, 0:n] = jnp.zeros((5, n), F32)
     points_ref[:, n:] = points_ref[:, 0:wrap]
-    wt_ref[:, n:] = wt_ref[:, 0:wrap]
     sum_ref[...] = jnp.zeros_like(sum_ref)
 
     def place(i):
         at = pl.multiple_of(i * BLOCK, BLOCK)
+        columns = points_ref[:, pl.ds(at, BLOCK)].T
         for k in range(3):
-            own_ref[k] = jnp.broadcast_to(columns_ref[pl.ds(at, BLOCK), k : k + 1], (BLOCK, OUT))
+            own_ref[k] = jnp.broadcast_to(columns[:, k : k + 1], (BLOCK, OUT))
         return at
 
     def build(at, slot, d):
@@ -215,6 +227,11 @@
     first = place(0)
     for d in range(REACH):
         build(first, 0, d)
+    fetch.wait()
+    for j in range(blocks):
+        cols = slice(j * BLOCK, (j + 1) * BLOCK)
+        wt_ref[:, cols] = tall(w_ref[cols, :].T)
+    wt_ref[:, n:] = wt_ref[:, 0:wrap]
     lax.fori_loop(0, (blocks - 1) // 2, pair, 0)
     last = (blocks - 1) * BLOCK
     finish(last, [use(last, 0, 0, 1), use(last, 0, 1, REACH - 1)])
@@ -224,6 +241,10 @@
         if j < REACH - 1:
             total = total + sum_ref[:, n + j * BLOCK : n + (j + 1) * BLOCK]
         near_ref[cols, :] = total.T * scale
+        pltpu.make_async_copy(near_ref.at[cols], near_hbm.at[cols], near_sem.at[j]).start()
+    for j in range(blocks):
+        cols = slice(j * BLOCK, (j + 1) * BLOCK)
+        pltpu.make_async_copy(near_ref.at[cols], near_hbm.at[cols], near_sem.at[j]).wait()
 
 
 def middle_body(own_ref, m1_ref, m2_ref, m3_ref, out_ref):
@@ -241,11 +262,25 @@
     s2_ref[...] = s2
 
 
-def update_body(*refs):
-    near_ref, messages, down_ref, tops = refs[0], refs[1:4], refs[4], refs[5:9]
+def update_body(last, *refs):
+    near_hbm, messages, down_ref, tops = refs[0], refs[1:4], refs[4], refs[5:9]
     w_ref, targets_ref, bcat_ref = refs[9:12]
-    last = len(refs) == 13
-    outs = refs[12:] if last else refs[14:]
+    if last:
+        out_hbm, near_ref, near_sem, out_ref, out_sem, w_own, w_sem = refs[12:]
+    else:
+        basis_t_ref, up_ref, out_hbm, own_ref = refs[12:16]
+        message_refs = refs[16:19]
+        near_ref, near_sem, out_ref, out_sem, whl_ref = refs[19:]
+    blocks = [slice(j, j + BLOCK) for j in range(0, near_ref.shape[0], BLOCK)]
+    loads = []
+    for j, rows in enumerate(blocks):
+        loads.append([pltpu.make_async_copy(near_hbm.at[rows], near_ref.at[rows], near_sem.at[j])])
+        if last:
+            loads[j].append(pltpu.make_async_copy(w_ref.at[rows], w_own.at[rows], w_sem.at[j]))
+        for load in loads[j]:
+            load.start()
+    if last:
+        w_ref = w_own
     own = lax.axis_index("leaf")
     quarters = [lax.rem(own + N_LEAF - k, N_LEAF) for k in range(N_LEAF)]
     g1 = unpack_quarters([ref[0:QROWS, :] for ref in tops], quarters)
@@ -256,19 +291,23 @@
     rhs = jnp.concatenate(
         [jnp.concatenate([hi, lo], axis=1), jnp.concatenate([hi, jnp.zeros_like(lo)], axis=1)], axis=0
     )
-    w_out = outs[0]
-    for j in range(w_ref.shape[0] // BLOCK):
-        rows = slice(j * BLOCK, (j + 1) * BLOCK)
+    sends = []
+    for j, rows in enumerate(blocks):
         f = jnp.dot(bcat_ref[rows, :], rhs, preferred_element_type=F32)
+        for load in loads[j]:
+            load.wait()
         f = near_ref[rows, :] + (f[:, :OUT] + f[:, OUT:])
         new = w_ref[rows, :] - ((0.5 * jnp.tanh(0.5 * f) + 0.5) - targets_ref[rows, :])
-        w_out[rows, :] = new
+        out_ref[rows, :] = new
         if not last:
-            outs[-1][rows, :] = wide(new)
+            whl_ref[rows, :] = wide(new)
+        sends.append(pltpu.make_async_copy(out_ref.at[rows], out_hbm.at[rows], out_sem.at[j]))
+        sends[j].start()
     if not last:
-        basis_t_ref, up_ref = refs[12:14]
-        s0 = dot3(tall(basis_t_ref[...]), outs[-1][...])
-        emit_messages(s0, up_ref[...], outs[1], outs[2:5])
+        s0 = dot3(tall(basis_t_ref[...]), whl_ref[...])
+        emit_messages(s0, up_ref[...], own_ref, message_refs)
+    for send in sends:
+        send.wait()
 
 
 def params(mib):
@@ -283,12 +322,17 @@
     return [(i, (i + k) % N_LEAF) for i in range(N_LEAF)]
 
 
-def call(body, out, operands, mib, name, scratch=(), work=(0, 0, 0)):
+def call(body, out, operands, mib, name, scratch=(), work=(0, 0, 0), far_in=(), far_out=()):
+    out = [pltpu.HBM(o.shape, o.dtype) if i in far_out else o for i, o in enumerate(out)]
+    operands = [
+        pltpu.with_memory_space_constraint(x, pltpu.HBM) if i in far_in else x
+        for i, x in enumerate(operands)
+    ]
     return pl.pallas_call(
         body,
         out_shape=out,
-        in_specs=[VMEM] * len(operands),
-        out_specs=jax.tree.map(lambda _: VMEM, out),
+        in_specs=[HBM if i in far_in else VMEM for i in range(len(operands))],
+        out_specs=[HBM if i in far_out else VMEM for i in range(len(out))],
         scratch_shapes=scratch,
         compiler_params=params(mib),
         cost_estimate=pl.CostEstimate(flops=work[0], bytes_accessed=work[1], transcendentals=work[2]),
@@ -311,6 +355,7 @@
     n = weights.shape[0]
     scale = 4.0 / math.sqrt(n)
     basis_t = basis.T
+    wide_n = n + (REACH - 1) * BLOCK
     message_shapes = [shape(2 * QROWS, OUT)] + [shape(RANK + 2 * QROWS, OUT)] * 3
 
     up, own, *messages = call(
@@ -320,49 +365,53 @@
         58,
         "first",
     )
-    columns, bcat, couple, down = call(
+    bcat, couple, down = call(
         prepare_body,
         [
-            shape(n, 8),
             shape(n, 2 * RANK, dtype=BF16),
             shape(2 * RANK, N_MID * RANK, dtype=BF16),
             shape(2 * RANK, 5 * RANK, dtype=BF16),
         ],
-        (coords, order, basis_t, transfer_leaf, transfer_mid, couple_leaf, couple_mid, couple_top),
+        (basis_t, transfer_leaf, transfer_mid, couple_leaf, couple_mid, couple_top),
         58,
         "prepare",
     )
-    targets = call(
+    (targets,) = call(
         targets_body,
-        shape(n, OUT),
-        (columns, labels),
+        [shape(n, OUT)],
+        (order, labels),
         12,
         "targets",
-        [pltpu.VMEM((n, OUT), BF16)],
-        (n * n * 2 * OUT, n * OUT * 8, 0),
-    )
-    own, columns = lax.optimization_barrier((own, columns))
+        work=(n * n // BITS * 2 * OUT, n * OUT * 8, 0),
+    )
+    own, couple = lax.optimization_barrier((own, couple))
 
     current = weights
     for step in range(STEPS):
         last = step == STEPS - 1
-        near = call(
+        (near,) = call(
             functools.partial(near_body, scale),
-            shape(n, OUT),
-            (coords, columns, current),
+            [shape(n, OUT)],
+            (coords, current),
             20,
             "near",
             [
                 pltpu.VMEM((2, 2, BLOCK, REACH * BLOCK), BF16),
-                pltpu.VMEM((OUT, n + (REACH - 1) * BLOCK), F32),
+                pltpu.VMEM((OUT, wide_n), F32),
                 pltpu.VMEM((3, BLOCK, OUT), F32),
-                pltpu.VMEM((3, n + (REACH - 1) * BLOCK), F32),
-                pltpu.VMEM((2 * OUT, n + (REACH - 1) * BLOCK), BF16),
+                pltpu.VMEM((8, wide_n), F32),
+                pltpu.VMEM((2 * OUT, wide_n), BF16),
+                pltpu.VMEM((n, OUT), F32),
+                pltpu.VMEM((n, OUT), F32),
+                pltpu.SemaphoreType.DMA,
+                pltpu.SemaphoreType.DMA((n // BLOCK,)),
             ],
             (6 * n * n * OUT, n * OUT * 12, n * n),
+            (1,),
+            (0,),
         )
         messages = [lax.ppermute(m, "leaf", ring(k)) for k, m in enumerate(messages, 1)]
-        spread = call(middle_body, shape(N_MID, 2 * QROWS, OUT), (own, *messages), 4, "middle")
+        (spread,) = call(middle_body, [shape(N_MID, 2 * QROWS, OUT)], (own, *messages), 4, "middle")
         got = lax.all_to_all(spread, "mid", 0, 0)
         got, near = lax.optimization_barrier((got, near))
         g1, s2 = call(
@@ -377,16 +426,22 @@
         top = jnp.concatenate([g1, s2], axis=0)
         tops = [top] + [lax.ppermute(top, "leaf", ring(k)) for k in (1, 2, 3)]
         far = (near, *messages, down, *tops, current, targets, bcat)
+        rows_buffer = [pltpu.VMEM((n, OUT), F32), pltpu.SemaphoreType.DMA((n // BLOCK,))]
+        body = functools.partial(update_body, last)
         if last:
-            current = call(update_body, shape(n, OUT), far, 8, "last")
+            (current,) = call(
+                body, [shape(n, OUT)], far, 12, "last", rows_buffer * 3, far_in=(0, 9), far_out=(0,)
+            )
         else:
             current, own, *messages = call(
-                update_body,
+                body,
                 [shape(n, OUT), *message_shapes],
                 (*far, basis_t, up),
-                12,
+                16,
                 "update",
-                [pltpu.VMEM((n, 2 * OUT), BF16)],
+                rows_buffer * 2 + [pltpu.VMEM((n, 2 * OUT), BF16)],
+                far_in=(0,),
+                far_out=(0,),
             )
     return current
 

time: 103 us -> 98.8 us (0.959)
  local copies, waits for them, and re-layouts: 12 us -> 1.31 us
  Pallas kernels: 40 us -> 44 us
  waiting for transfers between devices: 8.98 us -> 11.5 us
    unnamed x52 -> x34, local copies, waits for them, and re-layouts: 12 us -> 1.3 us
    pallas_call x11, Pallas kernels: 40 us -> 44 us  [call(): pl.pallas_call(body, out_shape=out, in_specs=[HBM if i in far_in else VME...]
    ppermute x6, waiting for transfers between devices: 3.52 us -> 5.96 us  [on_device(): tops = [top] + [lax.ppermute(top, 'leaf', ring(k)) for k in (1, 2, 3)]]
    ppermute x2, starting transfers between devices: 7.95 us -> 9.72 us  [on_device(): s2 = lax.ppermute(s2, 'top', [(0, 1), (1, 0)])]
    ppermute x6, starting transfers between devices: 10.7 us -> 9.2 us  [on_device(): lax.ppermute(m, 'leaf', ring(k))]
  transfers between devices with their start and end apart: 16 -> 16, of which waited for: 7 -> 9; matrix products, arithmetic and copies ran while one was open for 0% -> 0% of each run, Pallas kernels for 31% -> 31%
where the time goes in v4:
time: 98.8 us; the launch traced here: 98.4 us
  Pallas kernels  44 us (45%)
  starting transfers between devices  41.3 us (42%)
  waiting for transfers between devices  11.5 us (12%)
  local copies, waits for them, and re-layouts  1.31 us (1%)
    pallas_call x11, Pallas kernels, call(): pl.pallas_call(body, out_shape=out, in_specs=[HBM if i in far_in else VME...  44 us
    all_to_all x2, starting transfers between devices, on_device(): got = lax.all_to_all(spread, 'mid', 0, 0)  16.9 us
    ppermute x2, starting transfers between devices, on_device(): s2 = lax.ppermute(s2, 'top', [(0, 1), (1, 0)])  9.72 us
    ppermute x6, starting transfers between devices, on_device(): lax.ppermute(m, 'leaf', ring(k))  9.2 us
    ppermute x6, waiting for transfers between devices, on_device(): tops = [top] + [lax.ppermute(top, 'leaf', ring(k)) for k in (1, 2, 3)]  5.96 us
    ppermute x6, starting transfers between devices, on_device(): tops = [top] + [lax.ppermute(top, 'leaf', ring(k)) for k in (1, 2, 3)]  5.39 us
  transfers between devices with their start and end apart: 16, of which 9 were waited for; matrix products, arithmetic and copies ran while one was open for 0% of the time, Pallas kernels for 31%

profile of v4, /device:TPU:1, one launch (start us, length us, event | category | flops | bytes accessed | tf_op | source)
XLA Modules:
  0.0 98.4 jit_solution(14985381076043530197)
XLA Ops:
  0.0 2.8 %first.1 = (f32[64,128]{1,0:T(8,128)}, f32[32,128]{1,0:T(8,128)}, f32[96,128]{1,0:T(8,128)}, f32[96,128]{1,0:T(8,128)}, f32[96,128]{1,0:T(8,128)}) custom-call(f32[64,2304]{1,0:T(8,128)} %bitcast.1, f32[2304,128]{1,0:T(8,128)} %refs_9_.1, f32[1,64,64]{2,1,0:T(8,128)} %leaf_ref.3, f32[1,64,64]{2,1,0:T(8,128)} %mid_ref.3), custom_call_target="tpu_custom_call" | custom-call | tf_op jit(solution)/shard_map/first/pallas_call | solution.py:331
  2.8 2.1 %collective-permute-start = (f32[96,128]{1,0:T(8,128)}, f32[96,128]{1,0:T(8,128)S(1)}, u32[]{:S(2)}, u32[]{:S(2)}) collective-permute-start(f32[96,128]{1,0:T(8,128)} %get-tuple-element.31), channel_id=1, source_target_pairs={{0,1},{1,2},{2,3},{3,0},{4,5},{5,6},{6,7},{7,4},{8,9},{9,10},{10,1... | collective-permute-start | bytes 147464 | tf_op jit(solution)/shard_map/ppermute | solution.py:413
  5.0 2.6 %collective-permute-start.1 = (f32[96,128]{1,0:T(8,128)}, f32[96,128]{1,0:T(8,128)S(1)}, u32[]{:S(2)}, u32[]{:S(2)}) collective-permute-start(f32[96,128]{1,0:T(8,128)} %get-tuple-element.32), channel_id=1, source_target_pairs={{0,2},{1,3},{2,0},{3,1},{4,6},{5,7},{6,4},{7,5},{8,10},{9,11},{10,... | collective-permute-start | bytes 147464 | tf_op jit(solution)/shard_map/ppermute | solution.py:413
  7.6 1.1 %collective-permute-start.2 = (f32[96,128]{1,0:T(8,128)}, f32[96,128]{1,0:T(8,128)S(1)}, u32[]{:S(2)}, u32[]{:S(2)}) collective-permute-start(f32[96,128]{1,0:T(8,128)} %get-tuple-element.33), channel_id=1, source_target_pairs={{0,3},{1,0},{2,1},{3,2},{4,7},{5,4},{6,5},{7,6},{8,11},{9,8},{10,9... | collective-permute-start | bytes 147464 | tf_op jit(solution)/shard_map/ppermute | solution.py:413
  8.7 3.1 %prepare.1 = (bf16[2304,128]{1,0:T(8,128)(2,1)}, bf16[128,2048]{1,0:T(8,128)(2,1)}, bf16[128,320]{1,0:T(8,128)(2,1)}) custom-call(f32[64,2304]{1,0:T(8,128)} %bitcast.2, f32[1,64,64]{2,1,0:T(8,128)} %leaf_ref.3, f32[1,64,64]{2,1,0:T(8,128)} %mid_ref.3, f32[1,4,64,64]{3,2,1,0:T(8,128)} %couple_leaf_ref.1, f32[1,32,64,64]{3,2,1,0:T(8,128)} %couple_mid_ref.1, ...), custom_call_target="tpu_custom_call" | custom-call | tf_op jit(solution)/shard_map/prepare/pallas_call | solution.py:331
  11.8 0.0 collective-permute-done.m1_ref.refs_1_
  11.8 0.0 collective-permute-done.1.m2_ref.refs_2_
  11.8 0.0 collective-permute-done.2.m3_ref.refs_3_
  11.8 0.0 copy-done.12
  11.8 0.9 middle.2
  12.7 0.6 copy-done.7
  13.3 0.6 copy-done.9
  13.9 11.0 %all-to-all-start = ((f32[32,32,128]{2,1,0:T(8,128)}), f32[32,32,128]{2,1,0:T(8,128)S(1)}, u32[]{:S(2)}, u32[]{:S(2)}) async-start(f32[32,32,128]{2,1,0:T(8,128)} %middle.2), calls=%async_computation | async-start | bytes 1048576 | tf_op jit(solution)/shard_map/all_to_all | solution.py:415
  25.0 0.0 copy-done.14
  25.0 0.0 copy-start.3
  25.0 0.0 copy-start.4
  25.0 0.0 copy-start.13
  25.0 13.2 %near.2.refs_0_ = f32[2304,128]{1,0:T(8,128)} custom-call(f32[3,2304]{1,0:T(4,128)S(1)} %copy-done.14, f32[2304,128]{1,0:T(8,128)} %refs_9_.1), custom_call_target="tpu_custom_call" | custom-call | flops 4076863488 | bytes 3538944 | tf_op jit(solution)/shard_map/near/pallas_call | solution.py:331
  38.2 1.9 %all-to-all-done.got_ref = f32[32,32,128]{2,1,0:T(8,128)S(1)} async-done(((f32[32,32,128]{2,1,0:T(8,128)}), f32[32,32,128]{2,1,0:T(8,128)S(1)}, u32[]{:S(2)}, u32[]{:S(2)}) %all-to-all-start) | async-done | bytes 524320 | tf_op jit(solution)/shard_map/all_to_all | solution.py:415
  40.1 0.0 copy-done.3
  40.1 0.5 couple.2
  40.6 3.8 %collective-permute-start.3 = (f32[16,128]{1,0:T(8,128)S(1)}, f32[16,128]{1,0:T(8,128)S(1)}, u32[]{:S(2)}, u32[]{:S(2)}) collective-permute-start(f32[16,128]{1,0:T(8,128)S(1)} %get-tuple-element.39), channel_id=1, source_target_pairs={{0,128},{128,0},{1,129},{129,1},{2,130},{130,2},{3,131},{131,3},{4... | collective-permute-start | bytes 24584 | tf_op jit(solution)/shard_map/ppermute | solution.py:425
  44.4 0.8 collective-permute-done.3
  45.2 1.4 %collective-permute-start.6 = (f32[32,128]{1,0:T(8,128)S(1)}, f32[32,128]{1,0:T(8,128)S(1)}, u32[]{:S(2)}, u32[]{:S(2)}) collective-permute-start(f32[32,128]{1,0:T(8,128)S(1)} %constant_dynamic-update-slice_fusion.refs_5_), channel_id=1, source_target_pairs={{0,3},{1,0},{2,1},{3,2},{4,7},{5,4},{6,5},{7,6},{8,11},{9,8},{10,9... | collective-permute-start | bytes 49160 | tf_op jit(solution)/shard_map/ppermute | solution.py:427
  46.6 0.8 collective-permute-start.5
  47.5 0.0 collective-permute-start.4
  47.5 0.0 copy-done.4
  47.5 0.0 copy-done.13
  47.5 1.4 %targets.1.refs_10_ = f32[2304,128]{1,0:T(8,128)S(1)} custom-call(s32[1,2304]{1,0:T(1,128)S(1)} %copy-done.13, s32[2304,128]{1,0:T(8,128)S(1)} %copy-done.4), custom_call_target="tpu_custom_call" | custom-call | flops 169869312 | bytes 2359296 | tf_op jit(solution)/shard_map/targets/pallas_call | solution.py:331
  48.9 0.0 collective-permute-done.6.refs_8_
  48.9 1.9 %collective-permute-done.5.refs_7_ = f32[32,128]{1,0:T(8,128)S(1)} collective-permute-done((f32[32,128]{1,0:T(8,128)S(1)}, f32[32,128]{1,0:T(8,128)S(1)}, u32[]{:S(2)}, u32[]{:S(2)}) %collective-permute-start.5) | collective-permute-done | bytes 16416 | tf_op jit(solution)/shard_map/ppermute | solution.py:427
  50.7 0.5 collective-permute-done.4.refs_6_
  51.3 0.0 copy-done.5
  51.3 0.0 copy-done.8
  51.3 0.0 copy-done.10
  51.3 0.0 copy-done.11
  51.3 0.0 copy-done
  51.3 0.0 copy-done.1
  51.3 0.0 copy-done.2
  51.3 4.1 %update.1 = (f32[2304,128]{1,0:T(8,128)}, f32[32,128]{1,0:T(8,128)S(1)}, f32[96,128]{1,0:T(8,128)S(1)}, f32[96,128]{1,0:T(8,128)S(1)}, f32[96,128]{1,0:T(8,128)S(1)}) custom-call(f32[2304,128]{1,0:T(8,128)} %near.2.refs_0_, f32[96,128]{1,0:T(8,128)S(1)} %collective-permute-done.m1_ref.refs_1_, f32[96,128]{1,0:T(8,128)S(1)} %copy-done.8, ...), custom_call_target="tpu_custom_call" | custom-call | tf_op jit(solution)/shard_map/update/pallas_call | solution.py:331
  55.4 0.0 copy-start.15
  55.4 0.1 collective-permute-start.7
  55.5 1.9 %collective-permute-start.8 = (f32[96,128]{1,0:T(8,128)S(1)}, f32[96,128]{1,0:T(8,128)S(1)}, u32[]{:S(2)}, u32[]{:S(2)}) collective-permute-start(f32[96,128]{1,0:T(8,128)S(1)} %get-tuple-element.44), channel_id=1, source_target_pairs={{0,2},{1,3},{2,0},{3,1},{4,6},{5,7},{6,4},{7,5},{8,10},{9,11},{10,... | collective-permute-start | bytes 147464 | tf_op jit(solution)/shard_map/ppermute | solution.py:413
  57.4 1.4 %collective-permute-start.9 = (f32[96,128]{1,0:T(8,128)S(1)}, f32[96,128]{1,0:T(8,128)S(1)}, u32[]{:S(2)}, u32[]{:S(2)}) collective-permute-start(f32[96,128]{1,0:T(8,128)S(1)} %get-tuple-element.45), channel_id=1, source_target_pairs={{0,3},{1,0},{2,1},{3,2},{4,7},{5,4},{6,5},{7,6},{8,11},{9,8},{10,9... | collective-permute-start | bytes 147464 | tf_op jit(solution)/shard_map/ppermute | solution.py:413
  58.8 1.4 %collective-permute-done.7.m1_ref.refs_1_ = f32[96,128]{1,0:T(8,128)S(1)} collective-permute-done((f32[96,128]{1,0:T(8,128)S(1)}, f32[96,128]{1,0:T(8,128)S(1)}, u32[]{:S(2)}, u32[]{:S(2)}) %collective-permute-start.7) | collective-permute-done | bytes 49184 | tf_op jit(solution)/shard_map/ppermute | solution.py:413
  60.2 0.0 collective-permute-done.8.m2_ref.refs_2_
  60.2 0.6 collective-permute-done.9.m3_ref.refs_3_
  60.8 0.9 middle.3
  61.6 5.9 %all-to-all-start.1 = ((f32[32,32,128]{2,1,0:T(8,128)}), f32[32,32,128]{2,1,0:T(8,128)S(1)}, u32[]{:S(2)}, u32[]{:S(2)}) async-start(f32[32,32,128]{2,1,0:T(8,128)} %middle.3), calls=%async_computation.1 | async-start | bytes 1048576 | tf_op jit(solution)/shard_map/all_to_all | solution.py:415
  67.5 0.0 copy-done.15
  67.5 0.0 copy-start.6
  67.6 13.1 %near.3.refs_0_ = f32[2304,128]{1,0:T(8,128)} custom-call(f32[3,2304]{1,0:T(4,128)S(1)} %copy-done.15, f32[2304,128]{1,0:T(8,128)} %get-tuple-element.46.w_hbm.refs_9_), custom_call_target="tpu_custom_call" | custom-call | flops 4076863488 | bytes 3538944 | tf_op jit(solution)/shard_map/near/pallas_call | solution.py:331
  80.6 0.0 all-to-all-done.1.got_ref
  80.7 0.5 couple.3
  81.1 6.0 %collective-permute-start.10 = (f32[16,128]{1,0:T(8,128)S(1)}, f32[16,128]{1,0:T(8,128)S(1)}, u32[]{:S(2)}, u32[]{:S(2)}) collective-permute-start(f32[16,128]{1,0:T(8,128)S(1)} %get-tuple-element.50), channel_id=1, source_target_pairs={{0,128},{128,0},{1,129},{129,1},{2,130},{130,2},{3,131},{131,3},{4... | collective-permute-start | bytes 24584 | tf_op jit(solution)/shard_map/ppermute | solution.py:425
  87.1 0.8 collective-permute-done.10
  87.9 2.5 %collective-permute-start.13 = (f32[32,128]{1,0:T(8,128)S(1)}, f32[32,128]{1,0:T(8,128)S(1)}, u32[]{:S(2)}, u32[]{:S(2)}) collective-permute-start(f32[32,128]{1,0:T(8,128)S(1)} %constant_dynamic-update-slice_fusion.2.refs_5_), channel_id=1, source_target_pairs={{0,3},{1,0},{2,1},{3,2},{4,7},{5,4},{6,5},{7,6},{8,11},{9,8},{10,9... | collective-permute-start | bytes 49160 | tf_op jit(solution)/shard_map/ppermute | solution.py:427
  90.5 0.2 collective-permute-start.12
  90.7 0.4 collective-permute-start.11
  91.1 0.3 collective-permute-done.13.refs_8_
  91.3 3.3 %collective-permute-done.12.refs_7_ = f32[32,128]{1,0:T(8,128)S(1)} collective-permute-done((f32[32,128]{1,0:T(8,128)S(1)}, f32[32,128]{1,0:T(8,128)S(1)}, u32[]{:S(2)}, u32[]{:S(2)}) %collective-permute-start.12) | collective-permute-done | bytes 16416 | tf_op jit(solution)/shard_map/ppermute | solution.py:427
  94.6 0.0 collective-permute-done.11.refs_6_
  94.6 0.0 copy-done.6
  94.6 3.6 %last.1 = f32[2304,128]{1,0:T(8,128)} custom-call(f32[2304,128]{1,0:T(8,128)} %near.3.refs_0_, f32[96,128]{1,0:T(8,128)S(1)} %collective-permute-done.7.m1_ref.refs_1_, f32[96,128]{1,0:T(8,128)S(1)} %collective-permute-done.8.m2_ref.refs_2_, f32[96,128]{1,0:T(8,128)S(1)} %collective-permute-done.9.m3_ref.refs_3_, bf16[128,320]{1,0:T(8,128)(2,1)S(1)} %copy-done.6, ...), custom_call_target="tpu_custom_call" | custom-call | tf_op jit(solution)/shard_map/last/pallas_call | solution.py:331
  (15 shorter events, 0.0 us)
Async XLA Ops:
  2.8 9.0 %copy-start.12 = (f32[32,128]{1,0:T(8,128)S(1)}, f32[32,128]{1,0:T(8,128)}, u32[]{:S(2)}) copy-start(f32[32,128]{1,0:T(8,128)} %get-tuple-element.30.own_ref) | copy-start | bytes 49156
  2.8 9.0 %collective-permute-start = (f32[96,128]{1,0:T(8,128)}, f32[96,128]{1,0:T(8,128)S(1)}, u32[]{:S(2)}, u32[]{:S(2)}) collective-permute-start(f32[96,128]{1,0:T(8,128)} %get-tuple-element.31), channel_id=1, source_target_pairs={{0,1},{1,2},{2,3},{3,0},{4,5},{5,6},{6,7},{7,4},{8,9},{9,10},{10,1... | collective-permute-start | bytes 147464 | tf_op jit(solution)/shard_map/ppermute | solution.py:413
  5.0 6.8 %collective-permute-start.1 = (f32[96,128]{1,0:T(8,128)}, f32[96,128]{1,0:T(8,128)S(1)}, u32[]{:S(2)}, u32[]{:S(2)}) collective-permute-start(f32[96,128]{1,0:T(8,128)} %get-tuple-element.32), channel_id=1, source_target_pairs={{0,2},{1,3},{2,0},{3,1},{4,6},{5,7},{6,4},{7,5},{8,10},{9,11},{10,... | collective-permute-start | bytes 147464 | tf_op jit(solution)/shard_map/ppermute | solution.py:413
  7.6 4.2 %collective-permute-start.2 = (f32[96,128]{1,0:T(8,128)}, f32[96,128]{1,0:T(8,128)S(1)}, u32[]{:S(2)}, u32[]{:S(2)}) collective-permute-start(f32[96,128]{1,0:T(8,128)} %get-tuple-element.33), channel_id=1, source_target_pairs={{0,3},{1,0},{2,1},{3,2},{4,7},{5,4},{6,5},{7,6},{8,11},{9,8},{10,9... | collective-permute-start | bytes 147464 | tf_op jit(solution)/shard_map/ppermute | solution.py:413
  11.8 13.2 %copy-start.14 = (f32[3,2304]{1,0:T(4,128)S(1)}, f32[3,2304]{1,0:T(4,128)}, u32[]{:S(2)}) copy-start(f32[3,2304]{1,0:T(4,128)} %coords_ref.3) | copy-start | bytes 82948
  12.7 0.6 copy-start.7
  13.3 0.6 copy-start.9
  13.9 26.2 %all-to-all-start = ((f32[32,32,128]{2,1,0:T(8,128)}), f32[32,32,128]{2,1,0:T(8,128)S(1)}, u32[]{:S(2)}, u32[]{:S(2)}) async-start(f32[32,32,128]{2,1,0:T(8,128)} %middle.2), calls=%async_computation | async-start | bytes 1048576 | tf_op jit(solution)/shard_map/all_to_all | solution.py:415
  25.0 15.1 %copy-start.3 = (bf16[128,2048]{1,0:T(8,128)(2,1)S(1)}, bf16[128,2048]{1,0:T(8,128)(2,1)}, u32[]{:S(2)}) copy-start(bf16[128,2048]{1,0:T(8,128)(2,1)} %get-tuple-element.37.couple_ref) | copy-start | bytes 1572868
  25.0 22.5 %copy-start.4 = (s32[2304,128]{1,0:T(8,128)S(1)}, s32[2304,128]{1,0:T(8,128)}, u32[]{:S(2)}) copy-start(s32[2304,128]{1,0:T(8,128)} %labels_ref.1) | copy-start | bytes 3538948
  25.0 22.5 %copy-start.13 = (s32[1,2304]{1,0:T(1,128)S(1)}, s32[1,2304]{1,0:T(1,128)}, u32[]{:S(2)}) copy-start(s32[1,2304]{1,0:T(1,128)} %order_ref.1) | copy-start | bytes 27652
  40.1 11.1 %copy-start.5 = (bf16[128,320]{1,0:T(8,128)(2,1)S(1)}, bf16[128,320]{1,0:T(8,128)(2,1)}, u32[]{:S(2)}) copy-start(bf16[128,320]{1,0:T(8,128)(2,1)} %get-tuple-element.35.refs_4_) | copy-start | bytes 245764
  40.1 11.1 %copy-start.8 = (f32[96,128]{1,0:T(8,128)S(1)}, f32[96,128]{1,0:T(8,128)}, u32[]{:S(2)}) copy-start(f32[96,128]{1,0:T(8,128)} %copy-done.7) | copy-start | bytes 147460
  40.1 11.1 %copy-start.10 = (f32[96,128]{1,0:T(8,128)S(1)}, f32[96,128]{1,0:T(8,128)}, u32[]{:S(2)}) copy-start(f32[96,128]{1,0:T(8,128)} %copy-done.9) | copy-start | bytes 147460
  40.6 4.6 %collective-permute-start.3 = (f32[16,128]{1,0:T(8,128)S(1)}, f32[16,128]{1,0:T(8,128)S(1)}, u32[]{:S(2)}, u32[]{:S(2)}) collective-permute-start(f32[16,128]{1,0:T(8,128)S(1)} %get-tuple-element.39), channel_id=1, source_target_pairs={{0,128},{128,0},{1,129},{129,1},{2,130},{130,2},{3,131},{131,3},{4... | collective-permute-start | bytes 24584 | tf_op jit(solution)/shard_map/ppermute | solution.py:425
  44.4 6.9 %copy-start.11 = (f32[64,128]{1,0:T(8,128)S(1)}, f32[64,128]{1,0:T(8,128)}, u32[]{:S(2)}) copy-start(f32[64,128]{1,0:T(8,128)} %get-tuple-element.41.refs_13_) | copy-start | bytes 98308
  45.2 6.1 %copy-start = (f32[2304,64]{0,1:T(8,128)S(1)}, f32[2304,64]{0,1:T(8,128)}, u32[]{:S(2)}) copy-start(f32[2304,64]{0,1:T(8,128)} %param.14) | copy-start | bytes 1769476
  45.2 6.1 %copy-start.1 = (f32[2304,128]{1,0:T(8,128)S(1)}, f32[2304,128]{1,0:T(8,128)}, u32[]{:S(2)}) copy-start(f32[2304,128]{1,0:T(8,128)} %refs_9_.1) | copy-start | bytes 3538948
  45.2 6.1 %copy-start.2 = (bf16[2304,128]{1,0:T(8,128)(2,1)S(1)}, bf16[2304,128]{1,0:T(8,128)(2,1)}, u32[]{:S(2)}) copy-start(bf16[2304,128]{1,0:T(8,128)(2,1)} %get-tuple-element.40.refs_11_) | copy-start | bytes 1769476
  45.2 3.7 %collective-permute-start.6 = (f32[32,128]{1,0:T(8,128)S(1)}, f32[32,128]{1,0:T(8,128)S(1)}, u32[]{:S(2)}, u32[]{:S(2)}) collective-permute-start(f32[32,128]{1,0:T(8,128)S(1)} %constant_dynamic-update-slice_fusion.refs_5_), channel_id=1, source_target_pairs={{0,3},{1,0},{2,1},{3,2},{4,7},{5,4},{6,5},{7,6},{8,11},{9,8},{10,9... | collective-permute-start | bytes 49160 | tf_op jit(solution)/shard_map/ppermute | solution.py:427
  46.6 4.1 %collective-permute-start.5 = (f32[32,128]{1,0:T(8,128)S(1)}, f32[32,128]{1,0:T(8,128)S(1)}, u32[]{:S(2)}, u32[]{:S(2)}) collective-permute-start(f32[32,128]{1,0:T(8,128)S(1)} %constant_dynamic-update-slice_fusion.refs_5_), channel_id=1, source_target_pairs={{0,2},{1,3},{2,0},{3,1},{4,6},{5,7},{6,4},{7,5},{8,10},{9,11},{10,... | collective-permute-start | bytes 49160 | tf_op jit(solution)/shard_map/ppermute | solution.py:427
  47.5 3.8 %collective-permute-start.4 = (f32[32,128]{1,0:T(8,128)S(1)}, f32[32,128]{1,0:T(8,128)S(1)}, u32[]{:S(2)}, u32[]{:S(2)}) collective-permute-start(f32[32,128]{1,0:T(8,128)S(1)} %constant_dynamic-update-slice_fusion.refs_5_), channel_id=1, source_target_pairs={{0,1},{1,2},{2,3},{3,0},{4,5},{5,6},{6,7},{7,4},{8,9},{9,10},{10,1... | collective-permute-start | bytes 49160 | tf_op jit(solution)/shard_map/ppermute | solution.py:427
  55.4 12.1 %copy-start.15 = (f32[3,2304]{1,0:T(4,128)S(1)}, f32[3,2304]{1,0:T(4,128)}, u32[]{:S(2)}) copy-start(f32[3,2304]{1,0:T(4,128)} %coords_ref.3) | copy-start | bytes 82948
  55.4 4.8 %collective-permute-start.7 = (f32[96,128]{1,0:T(8,128)S(1)}, f32[96,128]{1,0:T(8,128)S(1)}, u32[]{:S(2)}, u32[]{:S(2)}) collective-permute-start(f32[96,128]{1,0:T(8,128)S(1)} %get-tuple-element.43), channel_id=1, source_target_pairs={{0,1},{1,2},{2,3},{3,0},{4,5},{5,6},{6,7},{7,4},{8,9},{9,10},{10,1... | collective-permute-start | bytes 147464 | tf_op jit(solution)/shard_map/ppermute | solution.py:413
  55.5 4.7 %collective-permute-start.8 = (f32[96,128]{1,0:T(8,128)S(1)}, f32[96,128]{1,0:T(8,128)S(1)}, u32[]{:S(2)}, u32[]{:S(2)}) collective-permute-start(f32[96,128]{1,0:T(8,128)S(1)} %get-tuple-element.44), channel_id=1, source_target_pairs={{0,2},{1,3},{2,0},{3,1},{4,6},{5,7},{6,4},{7,5},{8,10},{9,11},{10,... | collective-permute-start | bytes 147464 | tf_op jit(solution)/shard_map/ppermute | solution.py:413
  57.4 3.4 %collective-permute-start.9 = (f32[96,128]{1,0:T(8,128)S(1)}, f32[96,128]{1,0:T(8,128)S(1)}, u32[]{:S(2)}, u32[]{:S(2)}) collective-permute-start(f32[96,128]{1,0:T(8,128)S(1)} %get-tuple-element.45), channel_id=1, source_target_pairs={{0,3},{1,0},{2,1},{3,2},{4,7},{5,4},{6,5},{7,6},{8,11},{9,8},{10,9... | collective-permute-start | bytes 147464 | tf_op jit(solution)/shard_map/ppermute | solution.py:413
  61.6 19.0 %all-to-all-start.1 = ((f32[32,32,128]{2,1,0:T(8,128)}), f32[32,32,128]{2,1,0:T(8,128)S(1)}, u32[]{:S(2)}, u32[]{:S(2)}) async-start(f32[32,32,128]{2,1,0:T(8,128)} %middle.3), calls=%async_computation.1 | async-start | bytes 1048576 | tf_op jit(solution)/shard_map/all_to_all | solution.py:415
  67.5 27.1 %copy-start.6 = (bf16[128,320]{1,0:T(8,128)(2,1)S(1)}, bf16[128,320]{1,0:T(8,128)(2,1)}, u32[]{:S(2)}) copy-start(bf16[128,320]{1,0:T(8,128)(2,1)} %get-tuple-element.35.refs_4_) | copy-start | bytes 245764
  81.1 6.8 %collective-permute-start.10 = (f32[16,128]{1,0:T(8,128)S(1)}, f32[16,128]{1,0:T(8,128)S(1)}, u32[]{:S(2)}, u32[]{:S(2)}) collective-permute-start(f32[16,128]{1,0:T(8,128)S(1)} %get-tuple-element.50), channel_id=1, source_target_pairs={{0,128},{128,0},{1,129},{129,1},{2,130},{130,2},{3,131},{131,3},{4... | collective-permute-start | bytes 24584 | tf_op jit(solution)/shard_map/ppermute | solution.py:425
  87.9 3.4 %collective-permute-start.13 = (f32[32,128]{1,0:T(8,128)S(1)}, f32[32,128]{1,0:T(8,128)S(1)}, u32[]{:S(2)}, u32[]{:S(2)}) collective-permute-start(f32[32,128]{1,0:T(8,128)S(1)} %constant_dynamic-update-slice_fusion.2.refs_5_), channel_id=1, source_target_pairs={{0,3},{1,0},{2,1},{3,2},{4,7},{5,4},{6,5},{7,6},{8,11},{9,8},{10,9... | collective-permute-start | bytes 49160 | tf_op jit(solution)/shard_map/ppermute | solution.py:427
  90.5 4.2 %collective-permute-start.12 = (f32[32,128]{1,0:T(8,128)S(1)}, f32[32,128]{1,0:T(8,128)S(1)}, u32[]{:S(2)}, u32[]{:S(2)}) collective-permute-start(f32[32,128]{1,0:T(8,128)S(1)} %constant_dynamic-update-slice_fusion.2.refs_5_), channel_id=1, source_target_pairs={{0,2},{1,3},{2,0},{3,1},{4,6},{5,7},{6,4},{7,5},{8,10},{9,11},{10,... | collective-permute-start | bytes 49160 | tf_op jit(solution)/shard_map/ppermute | solution.py:427
  90.7 4.0 %collective-permute-start.11 = (f32[32,128]{1,0:T(8,128)S(1)}, f32[32,128]{1,0:T(8,128)S(1)}, u32[]{:S(2)}, u32[]{:S(2)}) collective-permute-start(f32[32,128]{1,0:T(8,128)S(1)} %constant_dynamic-update-slice_fusion.2.refs_5_), channel_id=1, source_target_pairs={{0,1},{1,2},{2,3},{3,0},{4,5},{5,6},{6,7},{7,4},{8,9},{9,10},{10,1... | collective-permute-start | bytes 49160 | tf_op jit(solution)/shard_map/ppermute | solution.py:427

commit v5 on v4

--- a/solution.py
+++ b/solution.py
@@ -22,6 +22,7 @@
 BLOCK = 256
 REACH = 5
 BITS = 8
+GROUP = 3
 TILE = 32
 VMEM = pl.BlockSpec(memory_space=pltpu.VMEM)
 HBM = pl.BlockSpec(memory_space=pltpu.HBM)
@@ -136,13 +137,11 @@
     down_ref[...] = tall(jnp.concatenate([*siblings, leaf_ref[0], from_top], axis=1))
 
 
-def targets_body(order_ref, labels_ref, out_ref):
+def targets_body(order_ref, labels_hbm, out_ref, labels_ref, sem):
     n = labels_ref.shape[0]
     group = n // BITS
-    packed = jnp.zeros((group, OUT), F32)
-    for g in range(BITS):
-        packed = packed + labels_ref[g * group : (g + 1) * group, :].astype(F32) * float(1 << g)
-    packed = packed.astype(BF16)
+    fetch = pltpu.make_async_copy(labels_hbm, labels_ref, sem)
+    fetch.start()
     order = order_ref[...]
     which = jnp.zeros_like(order)
     place = jnp.ones(order.shape, F32)
@@ -151,6 +150,11 @@
         which = jnp.where(beyond, g * group, which)
         place = jnp.where(beyond, 1.0 / (1 << g), place)
     rows = jnp.concatenate([(order - which).astype(F32), place, jnp.zeros((6, n), F32)], axis=0)
+    fetch.wait()
+    packed = jnp.zeros((group, OUT), F32)
+    for g in range(BITS):
+        packed = packed + labels_ref[g * group : (g + 1) * group, :].astype(F32) * float(1 << g)
+    packed = packed.astype(BF16)
     lane = lax.broadcasted_iota(jnp.int32, (BLOCK, group), 1).astype(F32)
     for j in range(n // BLOCK):
         at = slice(j * BLOCK, (j + 1) * BLOCK)
@@ -162,7 +166,8 @@
 
 
 def near_body(
-    scale, coords_ref, w_hbm, near_hbm, k_ref, sum_ref, own_ref, points_ref, wt_ref, w_ref, near_ref, w_sem, near_sem
+    scale, coords_ref, w_hbm, near_hbm, k_ref, sum_ref, own_ref, points_ref, wt_ref, w_ref, near_ref, w_sem, near_sem,
+    columns_ref,
 ):
     n = w_hbm.shape[0]
     blocks = n // BLOCK
@@ -174,12 +179,15 @@
     points_ref[:, n:] = points_ref[:, 0:wrap]
     sum_ref[...] = jnp.zeros_like(sum_ref)
 
-    def place(i):
-        at = pl.multiple_of(i * BLOCK, BLOCK)
-        columns = points_ref[:, pl.ds(at, BLOCK)].T
+    for j in range(blocks):
+        cols = slice(j * BLOCK, (j + 1) * BLOCK)
+        columns_ref[cols, :] = points_ref[:, cols].T
+
+    def place(i, slot):
         for k in range(3):
-            own_ref[k] = jnp.broadcast_to(columns[:, k : k + 1], (BLOCK, OUT))
-        return at
+            own_ref[slot, k] = jnp.broadcast_to(
+                columns_ref[pl.ds(pl.multiple_of(i * BLOCK, BLOCK), BLOCK), k : k + 1], (BLOCK, OUT)
+            )
 
     def build(at, slot, d):
         for cols in (slice(c, c + OUT) for c in range(d * BLOCK, (d + 1) * BLOCK, OUT)):
@@ -188,7 +196,7 @@
                 sub = slice(t * TILE, (t + 1) * TILE)
                 diff_sq = None
                 for k in range(3):
-                    delta = own_ref[k, sub, :] - other[k]
+                    delta = own_ref[slot, k, sub, :] - other[k]
                     diff_sq = delta * delta if diff_sq is None else diff_sq + delta * delta
                 dist = diff_sq * lax.rsqrt(jnp.maximum(diff_sq, 1e-37))
                 k_ref[slot, 0, sub, cols], k_ref[slot, 1, sub, cols] = split(jnp.exp2(-dist))
@@ -215,7 +223,8 @@
     def pair(p, carry):
         for slot in range(2):
             prev = pl.multiple_of((2 * p + slot) * BLOCK, BLOCK)
-            at = place(2 * p + slot + 1)
+            at = pl.multiple_of(prev + BLOCK, BLOCK)
+            place(lax.rem(2 * p + slot + 2, blocks), slot)
             total = None
             for d in range(REACH):
                 part = use(prev, slot, d, 1)
@@ -224,9 +233,10 @@
             finish(prev, [total])
         return carry
 
-    first = place(0)
+    place(0, 0)
+    place(1, 1)
     for d in range(REACH):
-        build(first, 0, d)
+        build(0, 0, d)
     fetch.wait()
     for j in range(blocks):
         cols = slice(j * BLOCK, (j + 1) * BLOCK)
@@ -235,16 +245,19 @@
     lax.fori_loop(0, (blocks - 1) // 2, pair, 0)
     last = (blocks - 1) * BLOCK
     finish(last, [use(last, 0, 0, 1), use(last, 0, 1, REACH - 1)])
+    sends = []
     for j in range(blocks):
         cols = slice(j * BLOCK, (j + 1) * BLOCK)
         total = sum_ref[:, cols]
         if j < REACH - 1:
             total = total + sum_ref[:, n + j * BLOCK : n + (j + 1) * BLOCK]
         near_ref[cols, :] = total.T * scale
-        pltpu.make_async_copy(near_ref.at[cols], near_hbm.at[cols], near_sem.at[j]).start()
-    for j in range(blocks):
-        cols = slice(j * BLOCK, (j + 1) * BLOCK)
-        pltpu.make_async_copy(near_ref.at[cols], near_hbm.at[cols], near_sem.at[j]).wait()
+        if j % GROUP == GROUP - 1:
+            part = slice((j + 1 - GROUP) * BLOCK, (j + 1) * BLOCK)
+            sends.append(pltpu.make_async_copy(near_ref.at[part], near_hbm.at[part], near_sem.at[j // GROUP]))
+            sends[-1].start()
+    for send in sends:
+        send.wait()
 
 
 def middle_body(own_ref, m1_ref, m2_ref, m3_ref, out_ref):
@@ -272,36 +285,37 @@
         message_refs = refs[16:19]
         near_ref, near_sem, out_ref, out_sem, whl_ref = refs[19:]
     blocks = [slice(j, j + BLOCK) for j in range(0, near_ref.shape[0], BLOCK)]
-    loads = []
-    for j, rows in enumerate(blocks):
-        loads.append([pltpu.make_async_copy(near_hbm.at[rows], near_ref.at[rows], near_sem.at[j])])
-        if last:
-            loads[j].append(pltpu.make_async_copy(w_ref.at[rows], w_own.at[rows], w_sem.at[j]))
-        for load in loads[j]:
-            load.start()
+    parts = [slice(j, j + GROUP * BLOCK) for j in range(0, near_ref.shape[0], GROUP * BLOCK)]
+    loads = [pltpu.make_async_copy(near_hbm.at[p], near_ref.at[p], near_sem.at[j]) for j, p in enumerate(parts)]
     if last:
+        loads += [pltpu.make_async_copy(w_ref.at[p], w_own.at[p], w_sem.at[j]) for j, p in enumerate(parts)]
         w_ref = w_own
+    for load in loads:
+        load.start()
     own = lax.axis_index("leaf")
     quarters = [lax.rem(own + N_LEAF - k, N_LEAF) for k in range(N_LEAF)]
     g1 = unpack_quarters([ref[0:QROWS, :] for ref in tops], quarters)
     s2 = unpack_quarters([ref[QROWS:, :] for ref in tops], quarters)
-    parts = [ref[0:RANK, :] for ref in messages] + [g1, s2]
-    g0 = dot3(down_ref[...], wide(jnp.concatenate(parts, axis=0)))
+    skeletons = [ref[0:RANK, :] for ref in messages] + [g1, s2]
+    g0 = dot3(down_ref[...], wide(jnp.concatenate(skeletons, axis=0)))
     hi, lo = split(g0)
     rhs = jnp.concatenate(
         [jnp.concatenate([hi, lo], axis=1), jnp.concatenate([hi, jnp.zeros_like(lo)], axis=1)], axis=0
     )
+    for rows in blocks:
+        f = jnp.dot(bcat_ref[rows, :], rhs, preferred_element_type=F32)
+        out_ref[rows, :] = f[:, :OUT] + f[:, OUT:]
+    for load in loads:
+        load.wait()
     sends = []
-    for j, rows in enumerate(blocks):
-        f = jnp.dot(bcat_ref[rows, :], rhs, preferred_element_type=F32)
-        for load in loads[j]:
-            load.wait()
-        f = near_ref[rows, :] + (f[:, :OUT] + f[:, OUT:])
-        new = w_ref[rows, :] - ((0.5 * jnp.tanh(0.5 * f) + 0.5) - targets_ref[rows, :])
-        out_ref[rows, :] = new
-        if not last:
-            whl_ref[rows, :] = wide(new)
-        sends.append(pltpu.make_async_copy(out_ref.at[rows], out_hbm.at[rows], out_sem.at[j]))
+    for j, part in enumerate(parts):
+        for rows in blocks[j * GROUP : (j + 1) * GROUP]:
+            f = near_ref[rows, :] + out_ref[rows, :]
+            new = w_ref[rows, :] - ((0.5 * jnp.tanh(0.5 * f) + 0.5) - targets_ref[rows, :])
+            out_ref[rows, :] = new
+            if not last:
+                whl_ref[rows, :] = wide(new)
+        sends.append(pltpu.make_async_copy(out_ref.at[part], out_hbm.at[part], out_sem.at[j]))
         sends[j].start()
     if not last:
         s0 = dot3(tall(basis_t_ref[...]), whl_ref[...])
@@ -355,6 +369,7 @@
     n = weights.shape[0]
     scale = 4.0 / math.sqrt(n)
     basis_t = basis.T
+    groups = n // (GROUP * BLOCK)
     wide_n = n + (REACH - 1) * BLOCK
     message_shapes = [shape(2 * QROWS, OUT)] + [shape(RANK + 2 * QROWS, OUT)] * 3
 
@@ -382,7 +397,9 @@
         (order, labels),
         12,
         "targets",
-        work=(n * n // BITS * 2 * OUT, n * OUT * 8, 0),
+        [pltpu.VMEM((n, OUT), jnp.int32), pltpu.SemaphoreType.DMA],
+        (n * n // BITS * 2 * OUT, n * OUT * 8, 0),
+        far_in=(1,),
     )
     own, couple = lax.optimization_barrier((own, couple))
 
@@ -398,13 +415,14 @@
             [
                 pltpu.VMEM((2, 2, BLOCK, REACH * BLOCK), BF16),
                 pltpu.VMEM((OUT, wide_n), F32),
-                pltpu.VMEM((3, BLOCK, OUT), F32),
+                pltpu.VMEM((2, 3, BLOCK, OUT), F32),
                 pltpu.VMEM((8, wide_n), F32),
                 pltpu.VMEM((2 * OUT, wide_n), BF16),
                 pltpu.VMEM((n, OUT), F32),
                 pltpu.VMEM((n, OUT), F32),
                 pltpu.SemaphoreType.DMA,
-                pltpu.SemaphoreType.DMA((n // BLOCK,)),
+                pltpu.SemaphoreType.DMA((groups,)),
+                pltpu.VMEM((n, 8), F32),
             ],
             (6 * n * n * OUT, n * OUT * 12, n * n),
             (1,),
@@ -426,7 +444,7 @@
         top = jnp.concatenate([g1, s2], axis=0)
         tops = [top] + [lax.ppermute(top, "leaf", ring(k)) for k in (1, 2, 3)]
         far = (near, *messages, down, *tops, current, targets, bcat)
-        rows_buffer = [pltpu.VMEM((n, OUT), F32), pltpu.SemaphoreType.DMA((n // BLOCK,))]
+        rows_buffer = [pltpu.VMEM((n, OUT), F32), pltpu.SemaphoreType.DMA((groups,))]
         body = functools.partial(update_body, last)
         if last:
             (current,) = call(

time: 98.8 us -> 97 us (0.982)
  local copies, waits for them, and re-layouts: 1.31 us -> 0.04 us
    unnamed x34 -> x20, local copies, waits for them, and re-layouts: 1.3 us -> 0.04 us
    ppermute x6, waiting for transfers between devices: 5.96 us -> 4.78 us  [on_device(): tops = [top] + [lax.ppermute(top, 'leaf', ring(k)) for k in (1, 2, 3)]]
  transfers between devices with their start and end apart: 16 -> 16, of which waited for: 9 -> 11; matrix products, arithmetic and copies ran while one was open for 0% -> 0% of each run, Pallas kernels for 31% -> 33%
where the time goes in v5:
time: 97 us; the launch traced here: 96.6 us
  Pallas kernels  44.6 us (46%)
  starting transfers between devices  40.4 us (42%)
  waiting for transfers between devices  11.2 us (12%)
    pallas_call x11, Pallas kernels, call(): pl.pallas_call(body, out_shape=out, in_specs=[HBM if i in far_in else VME...  44.6 us
    all_to_all x2, starting transfers between devices, on_device(): got = lax.all_to_all(spread, 'mid', 0, 0)  17.4 us
    ppermute x6, starting transfers between devices, on_device(): lax.ppermute(m, 'leaf', ring(k))  9.73 us
    ppermute x2, starting transfers between devices, on_device(): s2 = lax.ppermute(s2, 'top', [(0, 1), (1, 0)])  8.76 us
    ppermute x6, waiting for transfers between devices, on_device(): tops = [top] + [lax.ppermute(top, 'leaf', ring(k)) for k in (1, 2, 3)]  4.78 us
    ppermute x6, starting transfers between devices, on_device(): tops = [top] + [lax.ppermute(top, 'leaf', ring(k)) for k in (1, 2, 3)]  4.54 us
    all_to_all x2, waiting for transfers between devices, on_device(): got = lax.all_to_all(spread, 'mid', 0, 0)  2.85 us
  transfers between devices with their start and end apart: 16, of which 11 were waited for; matrix products, arithmetic and copies ran while one was open for 0% of the time, Pallas kernels for 33%

profile of v5, /device:TPU:1, one launch (start us, length us, event | category | flops | bytes accessed | tf_op | source)
XLA Modules:
  0.0 96.6 jit_solution(7128748123789415916)
XLA Ops:
  0.0 2.8 %first.1 = (f32[64,128]{1,0:T(8,128)}, f32[32,128]{1,0:T(8,128)}, f32[96,128]{1,0:T(8,128)}, f32[96,128]{1,0:T(8,128)}, f32[96,128]{1,0:T(8,128)}) custom-call(f32[64,2304]{1,0:T(8,128)} %bitcast.1, f32[2304,128]{1,0:T(8,128)} %refs_9_.1, f32[1,64,64]{2,1,0:T(8,128)} %leaf_ref.3, f32[1,64,64]{2,1,0:T(8,128)} %mid_ref.3), custom_call_target="tpu_custom_call" | custom-call | tf_op jit(solution)/shard_map/first/pallas_call | solution.py:345
  2.8 0.0 copy-start.6
  2.8 2.1 %collective-permute-start = (f32[96,128]{1,0:T(8,128)}, f32[96,128]{1,0:T(8,128)S(1)}, u32[]{:S(2)}, u32[]{:S(2)}) collective-permute-start(f32[96,128]{1,0:T(8,128)} %get-tuple-element.31), channel_id=1, source_target_pairs={{0,1},{1,2},{2,3},{3,0},{4,5},{5,6},{6,7},{7,4},{8,9},{9,10},{10,1... | collective-permute-start | bytes 147464 | tf_op jit(solution)/shard_map/ppermute | solution.py:431
  5.0 2.6 %collective-permute-start.1 = (f32[96,128]{1,0:T(8,128)}, f32[96,128]{1,0:T(8,128)S(1)}, u32[]{:S(2)}, u32[]{:S(2)}) collective-permute-start(f32[96,128]{1,0:T(8,128)} %get-tuple-element.32), channel_id=1, source_target_pairs={{0,2},{1,3},{2,0},{3,1},{4,6},{5,7},{6,4},{7,5},{8,10},{9,11},{10,... | collective-permute-start | bytes 147464 | tf_op jit(solution)/shard_map/ppermute | solution.py:431
  7.6 1.1 %collective-permute-start.2 = (f32[96,128]{1,0:T(8,128)}, f32[96,128]{1,0:T(8,128)S(1)}, u32[]{:S(2)}, u32[]{:S(2)}) collective-permute-start(f32[96,128]{1,0:T(8,128)} %get-tuple-element.33), channel_id=1, source_target_pairs={{0,3},{1,0},{2,1},{3,2},{4,7},{5,4},{6,5},{7,6},{8,11},{9,8},{10,9... | collective-permute-start | bytes 147464 | tf_op jit(solution)/shard_map/ppermute | solution.py:431
  8.7 3.2 %prepare.1 = (bf16[2304,128]{1,0:T(8,128)(2,1)}, bf16[128,2048]{1,0:T(8,128)(2,1)}, bf16[128,320]{1,0:T(8,128)(2,1)}) custom-call(f32[64,2304]{1,0:T(8,128)} %bitcast.2, f32[1,64,64]{2,1,0:T(8,128)} %leaf_ref.3, f32[1,64,64]{2,1,0:T(8,128)} %mid_ref.3, f32[1,4,64,64]{3,2,1,0:T(8,128)} %couple_leaf_ref.1, f32[1,32,64,64]{3,2,1,0:T(8,128)} %couple_mid_ref.1, ...), custom_call_target="tpu_custom_call" | custom-call | tf_op jit(solution)/shard_map/prepare/pallas_call | solution.py:345
  11.8 0.0 copy-start.8
  11.8 0.0 collective-permute-done.m1_ref.refs_1_
  11.8 0.0 collective-permute-done.1.m2_ref.refs_2_
  11.8 0.0 collective-permute-done.2.m3_ref.refs_3_
  11.8 0.0 copy-done.6
  11.9 0.9 middle.2
  12.7 11.0 %all-to-all-start = ((f32[32,32,128]{2,1,0:T(8,128)}), f32[32,32,128]{2,1,0:T(8,128)S(1)}, u32[]{:S(2)}, u32[]{:S(2)}) async-start(f32[32,32,128]{2,1,0:T(8,128)} %middle.2), calls=%async_computation | async-start | bytes 1048576 | tf_op jit(solution)/shard_map/all_to_all | solution.py:433
  23.7 0.0 copy-done.8
  23.8 0.0 copy-start.3
  23.8 0.0 copy-start.7
  23.8 13.1 %near.2.refs_0_ = f32[2304,128]{1,0:T(8,128)} custom-call(f32[3,2304]{1,0:T(4,128)S(1)} %copy-done.8, f32[2304,128]{1,0:T(8,128)} %refs_9_.1), custom_call_target="tpu_custom_call" | custom-call | flops 4076863488 | bytes 3538944 | tf_op jit(solution)/shard_map/near/pallas_call | solution.py:345
  36.9 2.0 %all-to-all-done.got_ref = f32[32,32,128]{2,1,0:T(8,128)S(1)} async-done(((f32[32,32,128]{2,1,0:T(8,128)}), f32[32,32,128]{2,1,0:T(8,128)S(1)}, u32[]{:S(2)}, u32[]{:S(2)}) %all-to-all-start) | async-done | bytes 524320 | tf_op jit(solution)/shard_map/all_to_all | solution.py:433
  38.9 0.0 copy-done.3
  38.9 0.0 copy-start.4
  38.9 0.5 couple.2
  39.4 3.8 %collective-permute-start.3 = (f32[16,128]{1,0:T(8,128)S(1)}, f32[16,128]{1,0:T(8,128)S(1)}, u32[]{:S(2)}, u32[]{:S(2)}) collective-permute-start(f32[16,128]{1,0:T(8,128)S(1)} %get-tuple-element.39), channel_id=1, source_target_pairs={{0,128},{128,0},{1,129},{129,1},{2,130},{130,2},{3,131},{131,3},{4... | collective-permute-start | bytes 24584 | tf_op jit(solution)/shard_map/ppermute | solution.py:443
  43.1 0.0 copy-start.5
  43.1 0.8 collective-permute-done.3
  44.0 0.0 copy-start
  44.0 0.0 copy-start.1
  44.0 0.0 copy-start.2
  44.0 1.4 %collective-permute-start.6 = (f32[32,128]{1,0:T(8,128)S(1)}, f32[32,128]{1,0:T(8,128)S(1)}, u32[]{:S(2)}, u32[]{:S(2)}) collective-permute-start(f32[32,128]{1,0:T(8,128)S(1)} %constant_dynamic-update-slice_fusion.refs_5_), channel_id=1, source_target_pairs={{0,3},{1,0},{2,1},{3,2},{4,7},{5,4},{6,5},{7,6},{8,11},{9,8},{10,9... | collective-permute-start | bytes 49160 | tf_op jit(solution)/shard_map/ppermute | solution.py:445
  45.4 0.8 collective-permute-start.5
  46.2 0.0 collective-permute-start.4
  46.2 0.0 copy-done.7
  46.2 2.6 %targets.1.refs_10_ = f32[2304,128]{1,0:T(8,128)S(1)} custom-call(s32[1,2304]{1,0:T(1,128)S(1)} %copy-done.7, s32[2304,128]{1,0:T(8,128)} %labels_hbm.1), custom_call_target="tpu_custom_call" | custom-call | flops 169869312 | bytes 2359296 | tf_op jit(solution)/shard_map/targets/pallas_call | solution.py:345
  48.9 0.0 collective-permute-done.6.refs_8_
  48.9 0.6 collective-permute-done.5.refs_7_
  49.5 0.5 collective-permute-done.4.refs_6_
  50.0 0.0 copy-done.4
  50.0 0.0 copy-done.5
  50.0 0.0 copy-done
  50.0 0.0 copy-done.1
  50.1 0.0 copy-done.2
  50.1 3.9 %update.1 = (f32[2304,128]{1,0:T(8,128)}, f32[32,128]{1,0:T(8,128)S(1)}, f32[96,128]{1,0:T(8,128)S(1)}, f32[96,128]{1,0:T(8,128)S(1)}, f32[96,128]{1,0:T(8,128)S(1)}) custom-call(f32[2304,128]{1,0:T(8,128)} %near.2.refs_0_, f32[96,128]{1,0:T(8,128)S(1)} %collective-permute-done.m1_ref.refs_1_, f32[96,128]{1,0:T(8,128)S(1)} %collective-permute-done.1.m2_ref.refs_2_, ...), custom_call_target="tpu_custom_call" | custom-call | tf_op jit(solution)/shard_map/update/pallas_call | solution.py:345
  53.9 0.8 collective-permute-start.7
  54.7 2.0 %collective-permute-start.8 = (f32[96,128]{1,0:T(8,128)S(1)}, f32[96,128]{1,0:T(8,128)S(1)}, u32[]{:S(2)}, u32[]{:S(2)}) collective-permute-start(f32[96,128]{1,0:T(8,128)S(1)} %get-tuple-element.44), channel_id=1, source_target_pairs={{0,2},{1,3},{2,0},{3,1},{4,6},{5,7},{6,4},{7,5},{8,10},{9,11},{10,... | collective-permute-start | bytes 147464 | tf_op jit(solution)/shard_map/ppermute | solution.py:431
  56.8 1.1 %collective-permute-start.9 = (f32[96,128]{1,0:T(8,128)S(1)}, f32[96,128]{1,0:T(8,128)S(1)}, u32[]{:S(2)}, u32[]{:S(2)}) collective-permute-start(f32[96,128]{1,0:T(8,128)S(1)} %get-tuple-element.45), channel_id=1, source_target_pairs={{0,3},{1,0},{2,1},{3,2},{4,7},{5,4},{6,5},{7,6},{8,11},{9,8},{10,9... | collective-permute-start | bytes 147464 | tf_op jit(solution)/shard_map/ppermute | solution.py:431
  57.9 0.3 collective-permute-done.7.m1_ref.refs_1_
  58.2 1.0 %collective-permute-done.8.m2_ref.refs_2_ = f32[96,128]{1,0:T(8,128)S(1)} collective-permute-done((f32[96,128]{1,0:T(8,128)S(1)}, f32[96,128]{1,0:T(8,128)S(1)}, u32[]{:S(2)}, u32[]{:S(2)}) %collective-permute-start.8) | collective-permute-done | bytes 49184 | tf_op jit(solution)/shard_map/ppermute | solution.py:431
  59.2 0.5 collective-permute-done.9.m3_ref.refs_3_
  59.7 0.9 middle.3
  60.6 6.3 %all-to-all-start.1 = ((f32[32,32,128]{2,1,0:T(8,128)}), f32[32,32,128]{2,1,0:T(8,128)S(1)}, u32[]{:S(2)}, u32[]{:S(2)}) async-start(f32[32,32,128]{2,1,0:T(8,128)} %middle.3), calls=%async_computation.1 | async-start | bytes 1048576 | tf_op jit(solution)/shard_map/all_to_all | solution.py:433
  66.9 13.2 %near.3.refs_0_ = f32[2304,128]{1,0:T(8,128)} custom-call(f32[3,2304]{1,0:T(4,128)S(1)} %copy-done.8, f32[2304,128]{1,0:T(8,128)} %get-tuple-element.46.w_hbm.refs_9_), custom_call_target="tpu_custom_call" | custom-call | flops 4076863488 | bytes 3538944 | tf_op jit(solution)/shard_map/near/pallas_call | solution.py:345
  80.1 0.9 all-to-all-done.1.got_ref
  81.0 0.5 couple.3
  81.5 5.0 %collective-permute-start.10 = (f32[16,128]{1,0:T(8,128)S(1)}, f32[16,128]{1,0:T(8,128)S(1)}, u32[]{:S(2)}, u32[]{:S(2)}) collective-permute-start(f32[16,128]{1,0:T(8,128)S(1)} %get-tuple-element.50), channel_id=1, source_target_pairs={{0,128},{128,0},{1,129},{129,1},{2,130},{130,2},{3,131},{131,3},{4... | collective-permute-start | bytes 24584 | tf_op jit(solution)/shard_map/ppermute | solution.py:443
  86.5 0.8 collective-permute-done.10
  87.3 1.7 %collective-permute-start.13 = (f32[32,128]{1,0:T(8,128)S(1)}, f32[32,128]{1,0:T(8,128)S(1)}, u32[]{:S(2)}, u32[]{:S(2)}) collective-permute-start(f32[32,128]{1,0:T(8,128)S(1)} %constant_dynamic-update-slice_fusion.2.refs_5_), channel_id=1, source_target_pairs={{0,3},{1,0},{2,1},{3,2},{4,7},{5,4},{6,5},{7,6},{8,11},{9,8},{10,9... | collective-permute-start | bytes 49160 | tf_op jit(solution)/shard_map/ppermute | solution.py:445
  89.0 0.3 collective-permute-start.12
  89.3 0.3 collective-permute-start.11
  89.6 0.3 collective-permute-done.13.refs_8_
  89.9 3.3 %collective-permute-done.12.refs_7_ = f32[32,128]{1,0:T(8,128)S(1)} collective-permute-done((f32[32,128]{1,0:T(8,128)S(1)}, f32[32,128]{1,0:T(8,128)S(1)}, u32[]{:S(2)}, u32[]{:S(2)}) %collective-permute-start.12) | collective-permute-done | bytes 16416 | tf_op jit(solution)/shard_map/ppermute | solution.py:445
  93.2 0.0 collective-permute-done.11.refs_6_
  93.3 3.1 %last.1 = f32[2304,128]{1,0:T(8,128)} custom-call(f32[2304,128]{1,0:T(8,128)} %near.3.refs_0_, f32[96,128]{1,0:T(8,128)S(1)} %collective-permute-done.7.m1_ref.refs_1_, f32[96,128]{1,0:T(8,128)S(1)} %collective-permute-done.8.m2_ref.refs_2_, f32[96,128]{1,0:T(8,128)S(1)} %collective-permute-done.9.m3_ref.refs_3_, bf16[128,320]{1,0:T(8,128)(2,1)S(1)} %copy-done.4, ...), custom_call_target="tpu_custom_call" | custom-call | tf_op jit(solution)/shard_map/last/pallas_call | solution.py:345
  (4 shorter events, 0.0 us)
Async XLA Ops:
  2.8 9.0 %copy-start.6 = (f32[32,128]{1,0:T(8,128)S(1)}, f32[32,128]{1,0:T(8,128)}, u32[]{:S(2)}) copy-start(f32[32,128]{1,0:T(8,128)} %get-tuple-element.30.own_ref) | copy-start | bytes 49156
  2.8 9.0 %collective-permute-start = (f32[96,128]{1,0:T(8,128)}, f32[96,128]{1,0:T(8,128)S(1)}, u32[]{:S(2)}, u32[]{:S(2)}) collective-permute-start(f32[96,128]{1,0:T(8,128)} %get-tuple-element.31), channel_id=1, source_target_pairs={{0,1},{1,2},{2,3},{3,0},{4,5},{5,6},{6,7},{7,4},{8,9},{9,10},{10,1... | collective-permute-start | bytes 147464 | tf_op jit(solution)/shard_map/ppermute | solution.py:431
  5.0 6.9 %collective-permute-start.1 = (f32[96,128]{1,0:T(8,128)}, f32[96,128]{1,0:T(8,128)S(1)}, u32[]{:S(2)}, u32[]{:S(2)}) collective-permute-start(f32[96,128]{1,0:T(8,128)} %get-tuple-element.32), channel_id=1, source_target_pairs={{0,2},{1,3},{2,0},{3,1},{4,6},{5,7},{6,4},{7,5},{8,10},{9,11},{10,... | collective-permute-start | bytes 147464 | tf_op jit(solution)/shard_map/ppermute | solution.py:431
  7.6 4.2 %collective-permute-start.2 = (f32[96,128]{1,0:T(8,128)}, f32[96,128]{1,0:T(8,128)S(1)}, u32[]{:S(2)}, u32[]{:S(2)}) collective-permute-start(f32[96,128]{1,0:T(8,128)} %get-tuple-element.33), channel_id=1, source_target_pairs={{0,3},{1,0},{2,1},{3,2},{4,7},{5,4},{6,5},{7,6},{8,11},{9,8},{10,9... | collective-permute-start | bytes 147464 | tf_op jit(solution)/shard_map/ppermute | solution.py:431
  11.8 11.9 %copy-start.8 = (f32[3,2304]{1,0:T(4,128)S(1)}, f32[3,2304]{1,0:T(4,128)}, u32[]{:S(2)}) copy-start(f32[3,2304]{1,0:T(4,128)} %coords_ref.3) | copy-start | bytes 82948
  12.7 26.2 %all-to-all-start = ((f32[32,32,128]{2,1,0:T(8,128)}), f32[32,32,128]{2,1,0:T(8,128)S(1)}, u32[]{:S(2)}, u32[]{:S(2)}) async-start(f32[32,32,128]{2,1,0:T(8,128)} %middle.2), calls=%async_computation | async-start | bytes 1048576 | tf_op jit(solution)/shard_map/all_to_all | solution.py:433
  23.8 15.1 %copy-start.3 = (bf16[128,2048]{1,0:T(8,128)(2,1)S(1)}, bf16[128,2048]{1,0:T(8,128)(2,1)}, u32[]{:S(2)}) copy-start(bf16[128,2048]{1,0:T(8,128)(2,1)} %get-tuple-element.37.couple_ref) | copy-start | bytes 1572868
  23.8 22.5 %copy-start.7 = (s32[1,2304]{1,0:T(1,128)S(1)}, s32[1,2304]{1,0:T(1,128)}, u32[]{:S(2)}) copy-start(s32[1,2304]{1,0:T(1,128)} %order_ref.1) | copy-start | bytes 27652
  38.9 11.1 %copy-start.4 = (bf16[128,320]{1,0:T(8,128)(2,1)S(1)}, bf16[128,320]{1,0:T(8,128)(2,1)}, u32[]{:S(2)}) copy-start(bf16[128,320]{1,0:T(8,128)(2,1)} %get-tuple-element.35.refs_4_) | copy-start | bytes 245764
  39.4 4.6 %collective-permute-start.3 = (f32[16,128]{1,0:T(8,128)S(1)}, f32[16,128]{1,0:T(8,128)S(1)}, u32[]{:S(2)}, u32[]{:S(2)}) collective-permute-start(f32[16,128]{1,0:T(8,128)S(1)} %get-tuple-element.39), channel_id=1, source_target_pairs={{0,128},{128,0},{1,129},{129,1},{2,130},{130,2},{3,131},{131,3},{4... | collective-permute-start | bytes 24584 | tf_op jit(solution)/shard_map/ppermute | solution.py:443
  43.1 6.9 %copy-start.5 = (f32[64,128]{1,0:T(8,128)S(1)}, f32[64,128]{1,0:T(8,128)}, u32[]{:S(2)}) copy-start(f32[64,128]{1,0:T(8,128)} %get-tuple-element.41.refs_13_) | copy-start | bytes 98308
  44.0 6.1 %copy-start = (f32[2304,64]{0,1:T(8,128)S(1)}, f32[2304,64]{0,1:T(8,128)}, u32[]{:S(2)}) copy-start(f32[2304,64]{0,1:T(8,128)} %param.14) | copy-start | bytes 1769476
  44.0 6.1 %copy-start.1 = (f32[2304,128]{1,0:T(8,128)S(1)}, f32[2304,128]{1,0:T(8,128)}, u32[]{:S(2)}) copy-start(f32[2304,128]{1,0:T(8,128)} %refs_9_.1) | copy-start | bytes 3538948
  44.0 6.1 %copy-start.2 = (bf16[2304,128]{1,0:T(8,128)(2,1)S(1)}, bf16[2304,128]{1,0:T(8,128)(2,1)}, u32[]{:S(2)}) copy-start(bf16[2304,128]{1,0:T(8,128)(2,1)} %get-tuple-element.40.refs_11_) | copy-start | bytes 1769476
  44.0 4.9 %collective-permute-start.6 = (f32[32,128]{1,0:T(8,128)S(1)}, f32[32,128]{1,0:T(8,128)S(1)}, u32[]{:S(2)}, u32[]{:S(2)}) collective-permute-start(f32[32,128]{1,0:T(8,128)S(1)} %constant_dynamic-update-slice_fusion.refs_5_), channel_id=1, source_target_pairs={{0,3},{1,0},{2,1},{3,2},{4,7},{5,4},{6,5},{7,6},{8,11},{9,8},{10,9... | collective-permute-start | bytes 49160 | tf_op jit(solution)/shard_map/ppermute | solution.py:445
  45.4 4.1 %collective-permute-start.5 = (f32[32,128]{1,0:T(8,128)S(1)}, f32[32,128]{1,0:T(8,128)S(1)}, u32[]{:S(2)}, u32[]{:S(2)}) collective-permute-start(f32[32,128]{1,0:T(8,128)S(1)} %constant_dynamic-update-slice_fusion.refs_5_), channel_id=1, source_target_pairs={{0,2},{1,3},{2,0},{3,1},{4,6},{5,7},{6,4},{7,5},{8,10},{9,11},{10,... | collective-permute-start | bytes 49160 | tf_op jit(solution)/shard_map/ppermute | solution.py:445
  46.2 3.8 %collective-permute-start.4 = (f32[32,128]{1,0:T(8,128)S(1)}, f32[32,128]{1,0:T(8,128)S(1)}, u32[]{:S(2)}, u32[]{:S(2)}) collective-permute-start(f32[32,128]{1,0:T(8,128)S(1)} %constant_dynamic-update-slice_fusion.refs_5_), channel_id=1, source_target_pairs={{0,1},{1,2},{2,3},{3,0},{4,5},{5,6},{6,7},{7,4},{8,9},{9,10},{10,1... | collective-permute-start | bytes 49160 | tf_op jit(solution)/shard_map/ppermute | solution.py:445
  53.9 4.2 %collective-permute-start.7 = (f32[96,128]{1,0:T(8,128)S(1)}, f32[96,128]{1,0:T(8,128)S(1)}, u32[]{:S(2)}, u32[]{:S(2)}) collective-permute-start(f32[96,128]{1,0:T(8,128)S(1)} %get-tuple-element.43), channel_id=1, source_target_pairs={{0,1},{1,2},{2,3},{3,0},{4,5},{5,6},{6,7},{7,4},{8,9},{9,10},{10,1... | collective-permute-start | bytes 147464 | tf_op jit(solution)/shard_map/ppermute | solution.py:431
  54.7 4.4 %collective-permute-start.8 = (f32[96,128]{1,0:T(8,128)S(1)}, f32[96,128]{1,0:T(8,128)S(1)}, u32[]{:S(2)}, u32[]{:S(2)}) collective-permute-start(f32[96,128]{1,0:T(8,128)S(1)} %get-tuple-element.44), channel_id=1, source_target_pairs={{0,2},{1,3},{2,0},{3,1},{4,6},{5,7},{6,4},{7,5},{8,10},{9,11},{10,... | collective-permute-start | bytes 147464 | tf_op jit(solution)/shard_map/ppermute | solution.py:431
  56.8 2.9 %collective-permute-start.9 = (f32[96,128]{1,0:T(8,128)S(1)}, f32[96,128]{1,0:T(8,128)S(1)}, u32[]{:S(2)}, u32[]{:S(2)}) collective-permute-start(f32[96,128]{1,0:T(8,128)S(1)} %get-tuple-element.45), channel_id=1, source_target_pairs={{0,3},{1,0},{2,1},{3,2},{4,7},{5,4},{6,5},{7,6},{8,11},{9,8},{10,9... | collective-permute-start | bytes 147464 | tf_op jit(solution)/shard_map/ppermute | solution.py:431
  60.6 20.4 %all-to-all-start.1 = ((f32[32,32,128]{2,1,0:T(8,128)}), f32[32,32,128]{2,1,0:T(8,128)S(1)}, u32[]{:S(2)}, u32[]{:S(2)}) async-start(f32[32,32,128]{2,1,0:T(8,128)} %middle.3), calls=%async_computation.1 | async-start | bytes 1048576 | tf_op jit(solution)/shard_map/all_to_all | solution.py:433
  81.5 5.8 %collective-permute-start.10 = (f32[16,128]{1,0:T(8,128)S(1)}, f32[16,128]{1,0:T(8,128)S(1)}, u32[]{:S(2)}, u32[]{:S(2)}) collective-permute-start(f32[16,128]{1,0:T(8,128)S(1)} %get-tuple-element.50), channel_id=1, source_target_pairs={{0,128},{128,0},{1,129},{129,1},{2,130},{130,2},{3,131},{131,3},{4... | collective-permute-start | bytes 24584 | tf_op jit(solution)/shard_map/ppermute | solution.py:443
  87.3 2.6 %collective-permute-start.13 = (f32[32,128]{1,0:T(8,128)S(1)}, f32[32,128]{1,0:T(8,128)S(1)}, u32[]{:S(2)}, u32[]{:S(2)}) collective-permute-start(f32[32,128]{1,0:T(8,128)S(1)} %constant_dynamic-update-slice_fusion.2.refs_5_), channel_id=1, source_target_pairs={{0,3},{1,0},{2,1},{3,2},{4,7},{5,4},{6,5},{7,6},{8,11},{9,8},{10,9... | collective-permute-start | bytes 49160 | tf_op jit(solution)/shard_map/ppermute | solution.py:445
  89.0 4.2 %collective-permute-start.12 = (f32[32,128]{1,0:T(8,128)S(1)}, f32[32,128]{1,0:T(8,128)S(1)}, u32[]{:S(2)}, u32[]{:S(2)}) collective-permute-start(f32[32,128]{1,0:T(8,128)S(1)} %constant_dynamic-update-slice_fusion.2.refs_5_), channel_id=1, source_target_pairs={{0,2},{1,3},{2,0},{3,1},{4,6},{5,7},{6,4},{7,5},{8,10},{9,11},{10,... | collective-permute-start | bytes 49160 | tf_op jit(solution)/shard_map/ppermute | solution.py:445
  89.3 4.0 %collective-permute-start.11 = (f32[32,128]{1,0:T(8,128)S(1)}, f32[32,128]{1,0:T(8,128)S(1)}, u32[]{:S(2)}, u32[]{:S(2)}) collective-permute-start(f32[32,128]{1,0:T(8,128)S(1)} %constant_dynamic-update-slice_fusion.2.refs_5_), channel_id=1, source_target_pairs={{0,1},{1,2},{2,3},{3,0},{4,5},{5,6},{6,7},{7,4},{8,9},{9,10},{10,1... | collective-permute-start | bytes 49160 | tf_op jit(solution)/shard_map/ppermute | solution.py:445

commit v6 on v5

--- a/solution.py
+++ b/solution.py
@@ -137,12 +137,9 @@
     down_ref[...] = tall(jnp.concatenate([*siblings, leaf_ref[0], from_top], axis=1))
 
 
-def targets_body(order_ref, labels_hbm, out_ref, labels_ref, sem):
+def permuted_labels(order, labels_ref):
     n = labels_ref.shape[0]
     group = n // BITS
-    fetch = pltpu.make_async_copy(labels_hbm, labels_ref, sem)
-    fetch.start()
-    order = order_ref[...]
     which = jnp.zeros_like(order)
     place = jnp.ones(order.shape, F32)
     for g in range(1, BITS):
@@ -150,29 +147,73 @@
         which = jnp.where(beyond, g * group, which)
         place = jnp.where(beyond, 1.0 / (1 << g), place)
     rows = jnp.concatenate([(order - which).astype(F32), place, jnp.zeros((6, n), F32)], axis=0)
-    fetch.wait()
     packed = jnp.zeros((group, OUT), F32)
     for g in range(BITS):
         packed = packed + labels_ref[g * group : (g + 1) * group, :].astype(F32) * float(1 << g)
     packed = packed.astype(BF16)
     lane = lax.broadcasted_iota(jnp.int32, (BLOCK, group), 1).astype(F32)
     for j in range(n // BLOCK):
-        at = slice(j * BLOCK, (j + 1) * BLOCK)
-        columns = rows[:, at].T
+        columns = rows[:, j * BLOCK : (j + 1) * BLOCK].T
         chosen = jnp.where(columns[:, 0:1] == lane, 1.0, 0.0).astype(BF16)
         value = jnp.dot(chosen, packed, preferred_element_type=F32) * columns[:, 1:2]
         value = jnp.floor(value)
-        out_ref[at, :] = value - 2.0 * jnp.floor(0.5 * value)
+        yield value - 2.0 * jnp.floor(0.5 * value)
+
+
+def finish_body(scale, *refs):
+    first = len(refs) == 13
+    if first:
+        sum_hbm, w_hbm, order_ref, labels_hbm, near_ref, base_ref, targets_hbm = refs[:7]
+        sum_ref, w_ref, labels_ref, targets_ref, sems, sent = refs[7:13]
+        pairs = [(labels_hbm, labels_ref), (w_hbm, w_ref), (sum_hbm, sum_ref)]
+    else:
+        sum_hbm, w_hbm, targets_hbm, near_ref, base_ref, sum_ref, w_ref, targets_ref, sems = refs
+        pairs = [(sum_hbm, sum_ref), (w_hbm, w_ref), (targets_hbm, targets_ref)]
+    loads = [pltpu.make_async_copy(a, b, sems.at[i]) for i, (a, b) in enumerate(pairs)]
+    for load in loads:
+        load.start()
+    n = near_ref.shape[0]
+    blocks = [slice(j, j + BLOCK) for j in range(0, n, BLOCK)]
+    if first:
+        loads[0].wait()
+        for rows, found in zip(blocks, permuted_labels(order_ref[...], labels_ref)):
+            targets_ref[rows, :] = found
+        send = pltpu.make_async_copy(targets_ref, targets_hbm, sent)
+        send.start()
+    for load in loads[1:] if first else loads:
+        load.wait()
+    for rows in blocks:
+        base_ref[rows, :] = w_ref[rows, :] + targets_ref[rows, :]
+        near_ref[rows, :] = sum_ref[:, rows].T * scale
+    if first:
+        send.wait()
+
+
+def turn_body(w_hbm, wt_hbm, w_ref, wt_ref, w_sem, wt_sem):
+    n = w_hbm.shape[0]
+    parts = [slice(j, j + GROUP * BLOCK) for j in range(0, n, GROUP * BLOCK)]
+    loads = [pltpu.make_async_copy(w_hbm.at[p], w_ref.at[p], w_sem.at[j]) for j, p in enumerate(parts)]
+    sends = [
+        pltpu.make_async_copy(wt_ref.at[:, p], wt_hbm.at[:, p], wt_sem.at[j]) for j, p in enumerate(parts)
+    ]
+    for load in loads:
+        load.start()
+    for part, load, send in zip(parts, loads, sends):
+        load.wait()
+        for j in range(part.start, part.stop, BLOCK):
+            wt_ref[:, j : j + BLOCK] = tall(w_ref[j : j + BLOCK, :].T)
+        send.start()
+    for send in sends:
+        send.wait()
 
 
 def near_body(
-    scale, coords_ref, w_hbm, near_hbm, k_ref, sum_ref, own_ref, points_ref, wt_ref, w_ref, near_ref, w_sem, near_sem,
-    columns_ref,
+    turned, coords_ref, w_hbm, near_hbm, k_ref, sum_ref, own_ref, points_ref, wt_ref, columns_ref, w_sem, near_sem, *w_own
 ):
-    n = w_hbm.shape[0]
+    n = coords_ref.shape[1]
     blocks = n // BLOCK
     wrap = (REACH - 1) * BLOCK
-    fetch = pltpu.make_async_copy(w_hbm, w_ref, w_sem)
+    fetch = pltpu.make_async_copy(w_hbm, wt_ref.at[:, 0:n] if turned else w_own[0], w_sem)
     fetch.start()
     points_ref[0:3, 0:n] = coords_ref[...] * LOG2E
     points_ref[3:, 0:n] = jnp.zeros((5, n), F32)
@@ -238,24 +279,22 @@
     for d in range(REACH):
         build(0, 0, d)
     fetch.wait()
-    for j in range(blocks):
-        cols = slice(j * BLOCK, (j + 1) * BLOCK)
-        wt_ref[:, cols] = tall(w_ref[cols, :].T)
+    if not turned:
+        for j in range(blocks):
+            cols = slice(j * BLOCK, (j + 1) * BLOCK)
+            wt_ref[:, cols] = tall(w_own[0][cols, :].T)
     wt_ref[:, n:] = wt_ref[:, 0:wrap]
     lax.fori_loop(0, (blocks - 1) // 2, pair, 0)
     last = (blocks - 1) * BLOCK
+    parts = [slice(wrap, last), slice(0, wrap), slice(last, n)]
+    sends = [
+        pltpu.make_async_copy(sum_ref.at[:, p], near_hbm.at[:, p], near_sem.at[j]) for j, p in enumerate(parts)
+    ]
+    sends[0].start()
     finish(last, [use(last, 0, 0, 1), use(last, 0, 1, REACH - 1)])
-    sends = []
-    for j in range(blocks):
-        cols = slice(j * BLOCK, (j + 1) * BLOCK)
-        total = sum_ref[:, cols]
-        if j < REACH - 1:
-            total = total + sum_ref[:, n + j * BLOCK : n + (j + 1) * BLOCK]
-        near_ref[cols, :] = total.T * scale
-        if j % GROUP == GROUP - 1:
-            part = slice((j + 1 - GROUP) * BLOCK, (j + 1) * BLOCK)
-            sends.append(pltpu.make_async_copy(near_ref.at[part], near_hbm.at[part], near_sem.at[j // GROUP]))
-            sends[-1].start()
+    sum_ref[:, 0:wrap] += sum_ref[:, n:]
+    sends[1].start()
+    sends[2].start()
     for send in sends:
         send.wait()
 
@@ -276,22 +315,16 @@
 
 
 def update_body(last, *refs):
-    near_hbm, messages, down_ref, tops = refs[0], refs[1:4], refs[4], refs[5:9]
-    w_ref, targets_ref, bcat_ref = refs[9:12]
+    near_ref, messages, down_ref, tops = refs[0], refs[1:4], refs[4], refs[5:9]
+    base_ref, bcat_ref = refs[9:11]
     if last:
-        out_hbm, near_ref, near_sem, out_ref, out_sem, w_own, w_sem = refs[12:]
+        out_hbm, out_ref, out_sem = refs[11:]
     else:
-        basis_t_ref, up_ref, out_hbm, own_ref = refs[12:16]
-        message_refs = refs[16:19]
-        near_ref, near_sem, out_ref, out_sem, whl_ref = refs[19:]
-    blocks = [slice(j, j + BLOCK) for j in range(0, near_ref.shape[0], BLOCK)]
-    parts = [slice(j, j + GROUP * BLOCK) for j in range(0, near_ref.shape[0], GROUP * BLOCK)]
-    loads = [pltpu.make_async_copy(near_hbm.at[p], near_ref.at[p], near_sem.at[j]) for j, p in enumerate(parts)]
-    if last:
-        loads += [pltpu.make_async_copy(w_ref.at[p], w_own.at[p], w_sem.at[j]) for j, p in enumerate(parts)]
-        w_ref = w_own
-    for load in loads:
-        load.start()
+        basis_t_ref, up_ref, out_hbm, own_ref = refs[11:15]
+        message_refs = refs[15:18]
+        out_ref, out_sem, whl_ref = refs[18:]
+    blocks = [slice(j, j + BLOCK) for j in range(0, base_ref.shape[0], BLOCK)]
+    parts = [slice(j, j + GROUP * BLOCK) for j in range(0, base_ref.shape[0], GROUP * BLOCK)]
     own = lax.axis_index("leaf")
     quarters = [lax.rem(own + N_LEAF - k, N_LEAF) for k in range(N_LEAF)]
     g1 = unpack_quarters([ref[0:QROWS, :] for ref in tops], quarters)
@@ -302,16 +335,12 @@
     rhs = jnp.concatenate(
         [jnp.concatenate([hi, lo], axis=1), jnp.concatenate([hi, jnp.zeros_like(lo)], axis=1)], axis=0
     )
-    for rows in blocks:
-        f = jnp.dot(bcat_ref[rows, :], rhs, preferred_element_type=F32)
-        out_ref[rows, :] = f[:, :OUT] + f[:, OUT:]
-    for load in loads:
-        load.wait()
     sends = []
     for j, part in enumerate(parts):
         for rows in blocks[j * GROUP : (j + 1) * GROUP]:
-            f = near_ref[rows, :] + out_ref[rows, :]
-            new = w_ref[rows, :] - ((0.5 * jnp.tanh(0.5 * f) + 0.5) - targets_ref[rows, :])
+            f = jnp.dot(bcat_ref[rows, :], rhs, preferred_element_type=F32)
+            f = near_ref[rows, :] + (f[:, :OUT] + f[:, OUT:])
+            new = base_ref[rows, :] - (0.5 * jnp.tanh(0.5 * f) + 0.5)
             out_ref[rows, :] = new
             if not last:
                 whl_ref[rows, :] = wide(new)
@@ -391,25 +420,35 @@
         58,
         "prepare",
     )
-    (targets,) = call(
-        targets_body,
-        [shape(n, OUT)],
-        (order, labels),
-        12,
-        "targets",
-        [pltpu.VMEM((n, OUT), jnp.int32), pltpu.SemaphoreType.DMA],
-        (n * n // BITS * 2 * OUT, n * OUT * 8, 0),
-        far_in=(1,),
-    )
     own, couple = lax.optimization_barrier((own, couple))
 
     current = weights
     for step in range(STEPS):
         last = step == STEPS - 1
-        (near,) = call(
-            functools.partial(near_body, scale),
-            [shape(n, OUT)],
-            (coords, current),
+        if step:
+            (w_near,) = call(
+                turn_body,
+                [shape(2 * OUT, n, dtype=BF16)],
+                (current,),
+                8,
+                "turn",
+                [
+                    pltpu.VMEM((n, OUT), F32),
+                    pltpu.VMEM((2 * OUT, n), BF16),
+                    pltpu.SemaphoreType.DMA((groups,)),
+                    pltpu.SemaphoreType.DMA((groups,)),
+                ],
+                (0, n * OUT * 8, 0),
+                (0,),
+                (0,),
+            )
+            own, w_near = lax.optimization_barrier((own, w_near))
+        else:
+            w_near = current
+        (near_t,) = call(
+            functools.partial(near_body, bool(step)),
+            [shape(OUT, n)],
+            (coords, w_near),
             20,
             "near",
             [
@@ -418,12 +457,11 @@
                 pltpu.VMEM((2, 3, BLOCK, OUT), F32),
                 pltpu.VMEM((8, wide_n), F32),
                 pltpu.VMEM((2 * OUT, wide_n), BF16),
-                pltpu.VMEM((n, OUT), F32),
-                pltpu.VMEM((n, OUT), F32),
+                pltpu.VMEM((n, 8), F32),
                 pltpu.SemaphoreType.DMA,
-                pltpu.SemaphoreType.DMA((groups,)),
-                pltpu.VMEM((n, 8), F32),
-            ],
+                pltpu.SemaphoreType.DMA((3,)),
+            ]
+            + ([] if step else [pltpu.VMEM((n, OUT), F32)]),
             (6 * n * n * OUT, n * OUT * 12, n * n),
             (1,),
             (0,),
@@ -431,7 +469,7 @@
         messages = [lax.ppermute(m, "leaf", ring(k)) for k, m in enumerate(messages, 1)]
         (spread,) = call(middle_body, [shape(N_MID, 2 * QROWS, OUT)], (own, *messages), 4, "middle")
         got = lax.all_to_all(spread, "mid", 0, 0)
-        got, near = lax.optimization_barrier((got, near))
+        got, near_t = lax.optimization_barrier((got, near_t))
         g1, s2 = call(
             couple_body,
             [shape(QROWS, OUT)] * 2,
@@ -443,22 +481,51 @@
         s2 = lax.ppermute(s2, "top", [(0, 1), (1, 0)])
         top = jnp.concatenate([g1, s2], axis=0)
         tops = [top] + [lax.ppermute(top, "leaf", ring(k)) for k in (1, 2, 3)]
-        far = (near, *messages, down, *tops, current, targets, bcat)
+        kept = [pltpu.VMEM((OUT, n), F32), pltpu.VMEM((n, OUT), F32)]
+        if step:
+            near, base = call(
+                functools.partial(finish_body, scale),
+                [shape(n, OUT)] * 2,
+                (near_t, current, targets),
+                8,
+                "finish",
+                [*kept, pltpu.VMEM((n, OUT), F32), pltpu.SemaphoreType.DMA((3,))],
+                (n * OUT, n * OUT * 20, 0),
+                (0, 1, 2),
+            )
+        else:
+            near, base, targets = call(
+                functools.partial(finish_body, scale),
+                [shape(n, OUT)] * 3,
+                (near_t, current, order, labels),
+                12,
+                "finish",
+                [
+                    *kept,
+                    pltpu.VMEM((n, OUT), jnp.int32),
+                    pltpu.VMEM((n, OUT), F32),
+                    pltpu.SemaphoreType.DMA((3,)),
+                    pltpu.SemaphoreType.DMA,
+                ],
+                (n * n // BITS * 2 * OUT, n * OUT * 24, 0),
+                (0, 1, 3),
+                (2,),
+            )
+        far = (near, *messages, down, *tops, base, bcat)
         rows_buffer = [pltpu.VMEM((n, OUT), F32), pltpu.SemaphoreType.DMA((groups,))]
         body = functools.partial(update_body, last)
         if last:
             (current,) = call(
-                body, [shape(n, OUT)], far, 12, "last", rows_buffer * 3, far_in=(0, 9), far_out=(0,)
+                body, [shape(n, OUT)], far, 8, "last", rows_buffer, far_out=(0,)
             )
         else:
             current, own, *messages = call(
                 body,
                 [shape(n, OUT), *message_shapes],
                 (*far, basis_t, up),
-                16,
+                12,
                 "update",
-                rows_buffer * 2 + [pltpu.VMEM((n, 2 * OUT), BF16)],
-                far_in=(0,),
+                [*rows_buffer, pltpu.VMEM((n, 2 * OUT), BF16)],
                 far_out=(0,),
             )
     return current

time: 97 us -> 94.7 us (0.976)
  waiting for transfers between devices: 11.2 us -> 6.83 us
  Pallas kernels: 44.6 us -> 46.7 us
    ppermute x6, waiting for transfers between devices: 4.78 us -> 1.19 us  [on_device(): tops = [top] + [lax.ppermute(top, 'leaf', ring(k)) for k in (1, 2, 3)]]
    pallas_call x11 -> x13, Pallas kernels: 44.6 us -> 46.7 us  [call(): pl.pallas_call(body, out_shape=out, in_specs=[HBM if i in far_in else VME...]
    ppermute x6, waiting for transfers between devices: 1.88 us -> 0.02 us  [on_device(): lax.ppermute(m, 'leaf', ring(k))]
    all_to_all x2, waiting for transfers between devices: 2.85 us -> 3.97 us  [on_device(): got = lax.all_to_all(spread, 'mid', 0, 0)]
    ppermute x6, starting transfers between devices: 9.73 us -> 10.8 us  [on_device(): lax.ppermute(m, 'leaf', ring(k))]
  transfers between devices with their start and end apart: 16 -> 16, of which waited for: 11 -> 6; matrix products, arithmetic and copies ran while one was open for 0% -> 0% of each run, Pallas kernels for 33% -> 40%
where the time goes in v6:
time: 94.7 us; the launch traced here: 94.3 us
  Pallas kernels  46.7 us (49%)
  starting transfers between devices  40.4 us (43%)
  waiting for transfers between devices  6.83 us (7%)
    pallas_call x13, Pallas kernels, call(): pl.pallas_call(body, out_shape=out, in_specs=[HBM if i in far_in else VME...  46.7 us
    all_to_all x2, starting transfers between devices, on_device(): got = lax.all_to_all(spread, 'mid', 0, 0)  16.7 us
    ppermute x6, starting transfers between devices, on_device(): lax.ppermute(m, 'leaf', ring(k))  10.8 us
    ppermute x2, starting transfers between devices, on_device(): s2 = lax.ppermute(s2, 'top', [(0, 1), (1, 0)])  8.37 us
    ppermute x6, starting transfers between devices, on_device(): tops = [top] + [lax.ppermute(top, 'leaf', ring(k)) for k in (1, 2, 3)]  4.54 us
    all_to_all x2, waiting for transfers between devices, on_device(): got = lax.all_to_all(spread, 'mid', 0, 0)  3.97 us
  transfers between devices with their start and end apart: 16, of which 6 were waited for; matrix products, arithmetic and copies ran while one was open for 0% of the time, Pallas kernels for 40%

profile of v6, /device:TPU:1, one launch (start us, length us, event | category | flops | bytes accessed | tf_op | source)
XLA Modules:
  0.0 94.3 jit_solution(7759919398647023280)
XLA Ops:
  0.0 2.8 %first.1 = (f32[64,128]{1,0:T(8,128)}, f32[32,128]{1,0:T(8,128)}, f32[96,128]{1,0:T(8,128)}, f32[96,128]{1,0:T(8,128)}, f32[96,128]{1,0:T(8,128)}) custom-call(f32[64,2304]{1,0:T(8,128)} %bitcast.1, f32[2304,128]{1,0:T(8,128)} %refs_1_.1, f32[1,64,64]{2,1,0:T(8,128)} %leaf_ref.3, f32[1,64,64]{2,1,0:T(8,128)} %mid_ref.3), custom_call_target="tpu_custom_call" | custom-call | tf_op jit(solution)/shard_map/first/pallas_call | solution.py:374
  2.8 0.0 copy-start.5
  2.8 2.1 %collective-permute-start = (f32[96,128]{1,0:T(8,128)}, f32[96,128]{1,0:T(8,128)S(1)}, u32[]{:S(2)}, u32[]{:S(2)}) collective-permute-start(f32[96,128]{1,0:T(8,128)} %get-tuple-element.38), channel_id=1, source_target_pairs={{0,1},{1,2},{2,3},{3,0},{4,5},{5,6},{6,7},{7,4},{8,9},{9,10},{10,1... | collective-permute-start | bytes 147464 | tf_op jit(solution)/shard_map/ppermute | solution.py:469
  5.0 2.6 %collective-permute-start.1 = (f32[96,128]{1,0:T(8,128)}, f32[96,128]{1,0:T(8,128)S(1)}, u32[]{:S(2)}, u32[]{:S(2)}) collective-permute-start(f32[96,128]{1,0:T(8,128)} %get-tuple-element.39), channel_id=1, source_target_pairs={{0,2},{1,3},{2,0},{3,1},{4,6},{5,7},{6,4},{7,5},{8,10},{9,11},{10,... | collective-permute-start | bytes 147464 | tf_op jit(solution)/shard_map/ppermute | solution.py:469
  7.6 1.1 %collective-permute-start.2 = (f32[96,128]{1,0:T(8,128)}, f32[96,128]{1,0:T(8,128)S(1)}, u32[]{:S(2)}, u32[]{:S(2)}) collective-permute-start(f32[96,128]{1,0:T(8,128)} %get-tuple-element.40), channel_id=1, source_target_pairs={{0,3},{1,0},{2,1},{3,2},{4,7},{5,4},{6,5},{7,6},{8,11},{9,8},{10,9... | collective-permute-start | bytes 147464 | tf_op jit(solution)/shard_map/ppermute | solution.py:469
  8.7 3.1 %prepare.1 = (bf16[2304,128]{1,0:T(8,128)(2,1)}, bf16[128,2048]{1,0:T(8,128)(2,1)}, bf16[128,320]{1,0:T(8,128)(2,1)}) custom-call(f32[64,2304]{1,0:T(8,128)} %bitcast.2, f32[1,64,64]{2,1,0:T(8,128)} %leaf_ref.3, f32[1,64,64]{2,1,0:T(8,128)} %mid_ref.3, f32[1,4,64,64]{3,2,1,0:T(8,128)} %couple_leaf_ref.1, f32[1,32,64,64]{3,2,1,0:T(8,128)} %couple_mid_ref.1, ...), custom_call_target="tpu_custom_call" | custom-call | tf_op jit(solution)/shard_map/prepare/pallas_call | solution.py:374
  11.8 0.0 copy-start.7
  11.8 0.0 collective-permute-done.m1_ref.refs_1_
  11.8 0.0 collective-permute-done.1.m2_ref.refs_2_
  11.8 0.0 collective-permute-done.2.m3_ref.refs_3_
  11.8 0.0 copy-done.5
  11.8 0.9 middle.2
  12.7 11.0 %all-to-all-start = ((f32[32,32,128]{2,1,0:T(8,128)}), f32[32,32,128]{2,1,0:T(8,128)S(1)}, u32[]{:S(2)}, u32[]{:S(2)}) async-start(f32[32,32,128]{2,1,0:T(8,128)} %middle.2), calls=%async_computation | async-start | bytes 1048576 | tf_op jit(solution)/shard_map/all_to_all | solution.py:471
  23.8 0.0 copy-done.7
  23.8 0.0 copy-start.2
  23.8 0.0 copy-start.6
  23.8 12.9 %near.2.refs_0_ = f32[128,2304]{1,0:T(8,128)} custom-call(f32[3,2304]{1,0:T(4,128)S(1)} %copy-done.7, f32[2304,128]{1,0:T(8,128)} %refs_1_.1), custom_call_target="tpu_custom_call" | custom-call | flops 4076863488 | bytes 3538944 | tf_op jit(solution)/shard_map/near/pallas_call | solution.py:374
  36.7 2.2 %all-to-all-done.got_ref = f32[32,32,128]{2,1,0:T(8,128)S(1)} async-done(((f32[32,32,128]{2,1,0:T(8,128)}), f32[32,32,128]{2,1,0:T(8,128)S(1)}, u32[]{:S(2)}, u32[]{:S(2)}) %all-to-all-start) | async-done | bytes 524320 | tf_op jit(solution)/shard_map/all_to_all | solution.py:471
  38.9 0.0 copy-done.2
  38.9 0.5 couple.2
  39.4 3.8 %collective-permute-start.3 = (f32[16,128]{1,0:T(8,128)S(1)}, f32[16,128]{1,0:T(8,128)S(1)}, u32[]{:S(2)}, u32[]{:S(2)}) collective-permute-start(f32[16,128]{1,0:T(8,128)S(1)} %get-tuple-element.47), channel_id=1, source_target_pairs={{0,128},{128,0},{1,129},{129,1},{2,130},{130,2},{3,131},{131,3},{4... | collective-permute-start | bytes 24584 | tf_op jit(solution)/shard_map/ppermute | solution.py:481
  43.1 0.8 collective-permute-done.3
  44.0 0.0 copy-start
  44.0 0.0 copy-start.1
  44.0 0.0 copy-start.3
  44.0 0.0 copy-start.4
  44.0 1.4 %collective-permute-start.6 = (f32[32,128]{1,0:T(8,128)S(1)}, f32[32,128]{1,0:T(8,128)S(1)}, u32[]{:S(2)}, u32[]{:S(2)}) collective-permute-start(f32[32,128]{1,0:T(8,128)S(1)} %constant_dynamic-update-slice_fusion.refs_5_), channel_id=1, source_target_pairs={{0,3},{1,0},{2,1},{3,2},{4,7},{5,4},{6,5},{7,6},{8,11},{9,8},{10,9... | collective-permute-start | bytes 49160 | tf_op jit(solution)/shard_map/ppermute | solution.py:483
  45.4 0.8 collective-permute-start.5
  46.2 0.0 collective-permute-start.4
  46.3 0.0 copy-done.6
  46.3 3.8 %finish.2 = (f32[2304,128]{1,0:T(8,128)S(1)}, f32[2304,128]{1,0:T(8,128)S(1)}, f32[2304,128]{1,0:T(8,128)}) custom-call(f32[128,2304]{1,0:T(8,128)} %near.2.refs_0_, f32[2304,128]{1,0:T(8,128)} %refs_1_.1, s32[1,2304]{1,0:T(1,128)S(1)} %copy-done.6, s32[2304,128]{1,0:T(8,128)} %refs_3_.1), custom_call_target="tpu_custom_call" | custom-call | flops 169869312 | bytes 7077888 | tf_op jit(solution)/shard_map/finish/pallas_call | solution.py:374
  50.0 0.0 collective-permute-done.6.refs_8_
  50.0 0.0 collective-permute-done.5.refs_7_
  50.1 0.0 collective-permute-done.4.refs_6_
  50.1 0.0 copy-done
  50.1 0.0 copy-done.1
  50.1 0.0 copy-done.3
  50.1 0.0 copy-done.4
  50.1 2.2 %update.1 = (f32[2304,128]{1,0:T(8,128)}, f32[32,128]{1,0:T(8,128)S(1)}, f32[96,128]{1,0:T(8,128)S(1)}, f32[96,128]{1,0:T(8,128)S(1)}, f32[96,128]{1,0:T(8,128)S(1)}) custom-call(f32[2304,128]{1,0:T(8,128)S(1)} %get-tuple-element.42.refs_0_, f32[96,128]{1,0:T(8,128)S(1)} %collective-permute-done.m1_ref.refs_1_, ...), custom_call_target="tpu_custom_call" | custom-call | tf_op jit(solution)/shard_map/update/pallas_call | solution.py:374
  52.3 1.9 %collective-permute-start.7 = (f32[96,128]{1,0:T(8,128)S(1)}, f32[96,128]{1,0:T(8,128)S(1)}, u32[]{:S(2)}, u32[]{:S(2)}) collective-permute-start(f32[96,128]{1,0:T(8,128)S(1)} %get-tuple-element.54), channel_id=1, source_target_pairs={{0,1},{1,2},{2,3},{3,0},{4,5},{5,6},{6,7},{7,4},{8,9},{9,10},{10,1... | collective-permute-start | bytes 147464 | tf_op jit(solution)/shard_map/ppermute | solution.py:469
  54.2 2.0 %collective-permute-start.8 = (f32[96,128]{1,0:T(8,128)S(1)}, f32[96,128]{1,0:T(8,128)S(1)}, u32[]{:S(2)}, u32[]{:S(2)}) collective-permute-start(f32[96,128]{1,0:T(8,128)S(1)} %get-tuple-element.55), channel_id=1, source_target_pairs={{0,2},{1,3},{2,0},{3,1},{4,6},{5,7},{6,4},{7,5},{8,10},{9,11},{10,... | collective-permute-start | bytes 147464 | tf_op jit(solution)/shard_map/ppermute | solution.py:469
  56.2 1.1 %collective-permute-start.9 = (f32[96,128]{1,0:T(8,128)S(1)}, f32[96,128]{1,0:T(8,128)S(1)}, u32[]{:S(2)}, u32[]{:S(2)}) collective-permute-start(f32[96,128]{1,0:T(8,128)S(1)} %get-tuple-element.56), channel_id=1, source_target_pairs={{0,3},{1,0},{2,1},{3,2},{4,7},{5,4},{6,5},{7,6},{8,11},{9,8},{10,9... | collective-permute-start | bytes 147464 | tf_op jit(solution)/shard_map/ppermute | solution.py:469
  57.3 2.3 %turn.1.w_hbm = bf16[256,2304]{1,0:T(8,128)(2,1)} custom-call(f32[2304,128]{1,0:T(8,128)} %get-tuple-element.52.w_hbm.refs_1_), custom_call_target="tpu_custom_call" | custom-call | bytes 2359296 | tf_op jit(solution)/shard_map/turn/pallas_call | solution.py:374
  59.6 0.0 collective-permute-done.7.m1_ref.refs_1_
  59.6 0.0 collective-permute-done.8.m2_ref.refs_2_
  59.7 0.0 collective-permute-done.9.m3_ref.refs_3_
  59.7 0.9 middle.3
  60.5 5.6 %all-to-all-start.1 = ((f32[32,32,128]{2,1,0:T(8,128)}), f32[32,32,128]{2,1,0:T(8,128)S(1)}, u32[]{:S(2)}, u32[]{:S(2)}) async-start(f32[32,32,128]{2,1,0:T(8,128)} %middle.3), calls=%async_computation.1 | async-start | bytes 1048576 | tf_op jit(solution)/shard_map/all_to_all | solution.py:471
  66.2 12.7 %near.3.refs_0_ = f32[128,2304]{1,0:T(8,128)} custom-call(f32[3,2304]{1,0:T(4,128)S(1)} %copy-done.7, bf16[256,2304]{1,0:T(8,128)(2,1)} %turn.1.w_hbm), custom_call_target="tpu_custom_call" | custom-call | flops 4076863488 | bytes 3538944 | tf_op jit(solution)/shard_map/near/pallas_call | solution.py:374
  78.8 1.8 %all-to-all-done.1.got_ref = f32[32,32,128]{2,1,0:T(8,128)S(1)} async-done(((f32[32,32,128]{2,1,0:T(8,128)}), f32[32,32,128]{2,1,0:T(8,128)S(1)}, u32[]{:S(2)}, u32[]{:S(2)}) %all-to-all-start.1) | async-done | bytes 524320 | tf_op jit(solution)/shard_map/all_to_all | solution.py:471
  80.6 0.5 couple.3
  81.1 4.6 %collective-permute-start.10 = (f32[16,128]{1,0:T(8,128)S(1)}, f32[16,128]{1,0:T(8,128)S(1)}, u32[]{:S(2)}, u32[]{:S(2)}) collective-permute-start(f32[16,128]{1,0:T(8,128)S(1)} %get-tuple-element.63), channel_id=1, source_target_pairs={{0,128},{128,0},{1,129},{129,1},{2,130},{130,2},{3,131},{131,3},{4... | collective-permute-start | bytes 24584 | tf_op jit(solution)/shard_map/ppermute | solution.py:481
  85.7 0.8 collective-permute-done.10
  86.5 1.7 %collective-permute-start.13 = (f32[32,128]{1,0:T(8,128)S(1)}, f32[32,128]{1,0:T(8,128)S(1)}, u32[]{:S(2)}, u32[]{:S(2)}) collective-permute-start(f32[32,128]{1,0:T(8,128)S(1)} %constant_dynamic-update-slice_fusion.2.refs_5_), channel_id=1, source_target_pairs={{0,3},{1,0},{2,1},{3,2},{4,7},{5,4},{6,5},{7,6},{8,11},{9,8},{10,9... | collective-permute-start | bytes 49160 | tf_op jit(solution)/shard_map/ppermute | solution.py:483
  88.2 0.3 collective-permute-start.12
  88.6 0.2 collective-permute-start.11
  88.8 2.5 %finish.3 = (f32[2304,128]{1,0:T(8,128)S(1)}, f32[2304,128]{1,0:T(8,128)S(1)}) custom-call(f32[128,2304]{1,0:T(8,128)} %near.3.refs_0_, f32[2304,128]{1,0:T(8,128)} %get-tuple-element.52.w_hbm.refs_1_, f32[2304,128]{1,0:T(8,128)} %get-tuple-element.59.refs_2_), custom_call_target="tpu_custom_call" | custom-call | flops 294912 | bytes 5898240 | tf_op jit(solution)/shard_map/finish/pallas_call | solution.py:374
  91.3 0.0 collective-permute-done.13.refs_8_
  91.3 1.0 %collective-permute-done.12.refs_7_ = f32[32,128]{1,0:T(8,128)S(1)} collective-permute-done((f32[32,128]{1,0:T(8,128)S(1)}, f32[32,128]{1,0:T(8,128)S(1)}, u32[]{:S(2)}, u32[]{:S(2)}) %collective-permute-start.12) | collective-permute-done | bytes 16416 | tf_op jit(solution)/shard_map/ppermute | solution.py:483
  92.3 0.2 collective-permute-done.11.refs_6_
  92.5 1.6 %last.1 = f32[2304,128]{1,0:T(8,128)} custom-call(f32[2304,128]{1,0:T(8,128)S(1)} %get-tuple-element.60.refs_0_, f32[96,128]{1,0:T(8,128)S(1)} %collective-permute-done.7.m1_ref.refs_1_, f32[96,128]{1,0:T(8,128)S(1)} %collective-permute-done.8.m2_ref.refs_2_, f32[96,128]{1,0:T(8,128)S(1)} %collective-permute-done.9.m3_ref.refs_3_, ...), custom_call_target="tpu_custom_call" | custom-call | tf_op jit(solution)/shard_map/last/pallas_call | solution.py:374
  (4 shorter events, 0.0 us)
Async XLA Ops:
  2.8 9.0 %copy-start.5 = (f32[32,128]{1,0:T(8,128)S(1)}, f32[32,128]{1,0:T(8,128)}, u32[]{:S(2)}) copy-start(f32[32,128]{1,0:T(8,128)} %get-tuple-element.37.own_ref) | copy-start | bytes 49156
  2.8 9.0 %collective-permute-start = (f32[96,128]{1,0:T(8,128)}, f32[96,128]{1,0:T(8,128)S(1)}, u32[]{:S(2)}, u32[]{:S(2)}) collective-permute-start(f32[96,128]{1,0:T(8,128)} %get-tuple-element.38), channel_id=1, source_target_pairs={{0,1},{1,2},{2,3},{3,0},{4,5},{5,6},{6,7},{7,4},{8,9},{9,10},{10,1... | collective-permute-start | bytes 147464 | tf_op jit(solution)/shard_map/ppermute | solution.py:469
  5.0 6.8 %collective-permute-start.1 = (f32[96,128]{1,0:T(8,128)}, f32[96,128]{1,0:T(8,128)S(1)}, u32[]{:S(2)}, u32[]{:S(2)}) collective-permute-start(f32[96,128]{1,0:T(8,128)} %get-tuple-element.39), channel_id=1, source_target_pairs={{0,2},{1,3},{2,0},{3,1},{4,6},{5,7},{6,4},{7,5},{8,10},{9,11},{10,... | collective-permute-start | bytes 147464 | tf_op jit(solution)/shard_map/ppermute | solution.py:469
  7.6 4.2 %collective-permute-start.2 = (f32[96,128]{1,0:T(8,128)}, f32[96,128]{1,0:T(8,128)S(1)}, u32[]{:S(2)}, u32[]{:S(2)}) collective-permute-start(f32[96,128]{1,0:T(8,128)} %get-tuple-element.40), channel_id=1, source_target_pairs={{0,3},{1,0},{2,1},{3,2},{4,7},{5,4},{6,5},{7,6},{8,11},{9,8},{10,9... | collective-permute-start | bytes 147464 | tf_op jit(solution)/shard_map/ppermute | solution.py:469
  11.8 12.0 %copy-start.7 = (f32[3,2304]{1,0:T(4,128)S(1)}, f32[3,2304]{1,0:T(4,128)}, u32[]{:S(2)}) copy-start(f32[3,2304]{1,0:T(4,128)} %coords_ref.3) | copy-start | bytes 82948
  12.7 26.2 %all-to-all-start = ((f32[32,32,128]{2,1,0:T(8,128)}), f32[32,32,128]{2,1,0:T(8,128)S(1)}, u32[]{:S(2)}, u32[]{:S(2)}) async-start(f32[32,32,128]{2,1,0:T(8,128)} %middle.2), calls=%async_computation | async-start | bytes 1048576 | tf_op jit(solution)/shard_map/all_to_all | solution.py:471
  23.8 15.1 %copy-start.2 = (bf16[128,2048]{1,0:T(8,128)(2,1)S(1)}, bf16[128,2048]{1,0:T(8,128)(2,1)}, u32[]{:S(2)}) copy-start(bf16[128,2048]{1,0:T(8,128)(2,1)} %get-tuple-element.45.couple_ref) | copy-start | bytes 1572868
  23.8 22.5 %copy-start.6 = (s32[1,2304]{1,0:T(1,128)S(1)}, s32[1,2304]{1,0:T(1,128)}, u32[]{:S(2)}) copy-start(s32[1,2304]{1,0:T(1,128)} %refs_2_.1) | copy-start | bytes 27652
  39.4 4.6 %collective-permute-start.3 = (f32[16,128]{1,0:T(8,128)S(1)}, f32[16,128]{1,0:T(8,128)S(1)}, u32[]{:S(2)}, u32[]{:S(2)}) collective-permute-start(f32[16,128]{1,0:T(8,128)S(1)} %get-tuple-element.47), channel_id=1, source_target_pairs={{0,128},{128,0},{1,129},{129,1},{2,130},{130,2},{3,131},{131,3},{4... | collective-permute-start | bytes 24584 | tf_op jit(solution)/shard_map/ppermute | solution.py:481
  44.0 6.1 %copy-start = (f32[2304,64]{0,1:T(8,128)S(1)}, f32[2304,64]{0,1:T(8,128)}, u32[]{:S(2)}) copy-start(f32[2304,64]{0,1:T(8,128)} %param.14) | copy-start | bytes 1769476
  44.0 6.1 %copy-start.1 = (bf16[2304,128]{1,0:T(8,128)(2,1)S(1)}, bf16[2304,128]{1,0:T(8,128)(2,1)}, u32[]{:S(2)}) copy-start(bf16[2304,128]{1,0:T(8,128)(2,1)} %get-tuple-element.49.refs_10_) | copy-start | bytes 1769476
  44.0 6.1 %copy-start.3 = (bf16[128,320]{1,0:T(8,128)(2,1)S(1)}, bf16[128,320]{1,0:T(8,128)(2,1)}, u32[]{:S(2)}) copy-start(bf16[128,320]{1,0:T(8,128)(2,1)} %get-tuple-element.43.refs_4_) | copy-start | bytes 245764
  44.0 6.1 %copy-start.4 = (f32[64,128]{1,0:T(8,128)S(1)}, f32[64,128]{1,0:T(8,128)}, u32[]{:S(2)}) copy-start(f32[64,128]{1,0:T(8,128)} %get-tuple-element.50.refs_12_) | copy-start | bytes 98308
  44.0 6.1 %collective-permute-start.6 = (f32[32,128]{1,0:T(8,128)S(1)}, f32[32,128]{1,0:T(8,128)S(1)}, u32[]{:S(2)}, u32[]{:S(2)}) collective-permute-start(f32[32,128]{1,0:T(8,128)S(1)} %constant_dynamic-update-slice_fusion.refs_5_), channel_id=1, source_target_pairs={{0,3},{1,0},{2,1},{3,2},{4,7},{5,4},{6,5},{7,6},{8,11},{9,8},{10,9... | collective-permute-start | bytes 49160 | tf_op jit(solution)/shard_map/ppermute | solution.py:483
  45.4 4.6 %collective-permute-start.5 = (f32[32,128]{1,0:T(8,128)S(1)}, f32[32,128]{1,0:T(8,128)S(1)}, u32[]{:S(2)}, u32[]{:S(2)}) collective-permute-start(f32[32,128]{1,0:T(8,128)S(1)} %constant_dynamic-update-slice_fusion.refs_5_), channel_id=1, source_target_pairs={{0,2},{1,3},{2,0},{3,1},{4,6},{5,7},{6,4},{7,5},{8,10},{9,11},{10,... | collective-permute-start | bytes 49160 | tf_op jit(solution)/shard_map/ppermute | solution.py:483
  46.2 3.8 %collective-permute-start.4 = (f32[32,128]{1,0:T(8,128)S(1)}, f32[32,128]{1,0:T(8,128)S(1)}, u32[]{:S(2)}, u32[]{:S(2)}) collective-permute-start(f32[32,128]{1,0:T(8,128)S(1)} %constant_dynamic-update-slice_fusion.refs_5_), channel_id=1, source_target_pairs={{0,1},{1,2},{2,3},{3,0},{4,5},{5,6},{6,7},{7,4},{8,9},{9,10},{10,1... | collective-permute-start | bytes 49160 | tf_op jit(solution)/shard_map/ppermute | solution.py:483
  52.3 7.3 %collective-permute-start.7 = (f32[96,128]{1,0:T(8,128)S(1)}, f32[96,128]{1,0:T(8,128)S(1)}, u32[]{:S(2)}, u32[]{:S(2)}) collective-permute-start(f32[96,128]{1,0:T(8,128)S(1)} %get-tuple-element.54), channel_id=1, source_target_pairs={{0,1},{1,2},{2,3},{3,0},{4,5},{5,6},{6,7},{7,4},{8,9},{9,10},{10,1... | collective-permute-start | bytes 147464 | tf_op jit(solution)/shard_map/ppermute | solution.py:469
  54.2 5.5 %collective-permute-start.8 = (f32[96,128]{1,0:T(8,128)S(1)}, f32[96,128]{1,0:T(8,128)S(1)}, u32[]{:S(2)}, u32[]{:S(2)}) collective-permute-start(f32[96,128]{1,0:T(8,128)S(1)} %get-tuple-element.55), channel_id=1, source_target_pairs={{0,2},{1,3},{2,0},{3,1},{4,6},{5,7},{6,4},{7,5},{8,10},{9,11},{10,... | collective-permute-start | bytes 147464 | tf_op jit(solution)/shard_map/ppermute | solution.py:469
  56.2 3.4 %collective-permute-start.9 = (f32[96,128]{1,0:T(8,128)S(1)}, f32[96,128]{1,0:T(8,128)S(1)}, u32[]{:S(2)}, u32[]{:S(2)}) collective-permute-start(f32[96,128]{1,0:T(8,128)S(1)} %get-tuple-element.56), channel_id=1, source_target_pairs={{0,3},{1,0},{2,1},{3,2},{4,7},{5,4},{6,5},{7,6},{8,11},{9,8},{10,9... | collective-permute-start | bytes 147464 | tf_op jit(solution)/shard_map/ppermute | solution.py:469
  60.5 20.1 %all-to-all-start.1 = ((f32[32,32,128]{2,1,0:T(8,128)}), f32[32,32,128]{2,1,0:T(8,128)S(1)}, u32[]{:S(2)}, u32[]{:S(2)}) async-start(f32[32,32,128]{2,1,0:T(8,128)} %middle.3), calls=%async_computation.1 | async-start | bytes 1048576 | tf_op jit(solution)/shard_map/all_to_all | solution.py:471
  81.1 5.4 %collective-permute-start.10 = (f32[16,128]{1,0:T(8,128)S(1)}, f32[16,128]{1,0:T(8,128)S(1)}, u32[]{:S(2)}, u32[]{:S(2)}) collective-permute-start(f32[16,128]{1,0:T(8,128)S(1)} %get-tuple-element.63), channel_id=1, source_target_pairs={{0,128},{128,0},{1,129},{129,1},{2,130},{130,2},{3,131},{131,3},{4... | collective-permute-start | bytes 24584 | tf_op jit(solution)/shard_map/ppermute | solution.py:481
  86.5 4.8 %collective-permute-start.13 = (f32[32,128]{1,0:T(8,128)S(1)}, f32[32,128]{1,0:T(8,128)S(1)}, u32[]{:S(2)}, u32[]{:S(2)}) collective-permute-start(f32[32,128]{1,0:T(8,128)S(1)} %constant_dynamic-update-slice_fusion.2.refs_5_), channel_id=1, source_target_pairs={{0,3},{1,0},{2,1},{3,2},{4,7},{5,4},{6,5},{7,6},{8,11},{9,8},{10,9... | collective-permute-start | bytes 49160 | tf_op jit(solution)/shard_map/ppermute | solution.py:483
  88.2 4.1 %collective-permute-start.12 = (f32[32,128]{1,0:T(8,128)S(1)}, f32[32,128]{1,0:T(8,128)S(1)}, u32[]{:S(2)}, u32[]{:S(2)}) collective-permute-start(f32[32,128]{1,0:T(8,128)S(1)} %constant_dynamic-update-slice_fusion.2.refs_5_), channel_id=1, source_target_pairs={{0,2},{1,3},{2,0},{3,1},{4,6},{5,7},{6,4},{7,5},{8,10},{9,11},{10,... | collective-permute-start | bytes 49160 | tf_op jit(solution)/shard_map/ppermute | solution.py:483
  88.6 3.9 %collective-permute-start.11 = (f32[32,128]{1,0:T(8,128)S(1)}, f32[32,128]{1,0:T(8,128)S(1)}, u32[]{:S(2)}, u32[]{:S(2)}) collective-permute-start(f32[32,128]{1,0:T(8,128)S(1)} %constant_dynamic-update-slice_fusion.2.refs_5_), channel_id=1, source_target_pairs={{0,1},{1,2},{2,3},{3,0},{4,5},{5,6},{6,7},{7,4},{8,9},{9,10},{10,1... | collective-permute-start | bytes 49160 | tf_op jit(solution)/shard_map/ppermute | solution.py:483

commit v7 on v6

--- a/solution.py
+++ b/solution.py
@@ -23,6 +23,7 @@
 REACH = 5
 BITS = 8
 GROUP = 3
+DEPTH = 3
 TILE = 32
 VMEM = pl.BlockSpec(memory_space=pltpu.VMEM)
 HBM = pl.BlockSpec(memory_space=pltpu.HBM)
@@ -207,19 +208,58 @@
         send.wait()
 
 
-def near_body(
-    turned, coords_ref, w_hbm, near_hbm, k_ref, sum_ref, own_ref, points_ref, wt_ref, columns_ref, w_sem, near_sem, *w_own
+def product(w, hi, lo, contract):
+    dims = (((1,), (contract,)), ((), ()))
+    a = lax.dot_general(w, hi, dims, preferred_element_type=F32)
+    b = lax.dot_general(w[:OUT], lo, dims, preferred_element_type=F32)
+    return a[:OUT] + (a[OUT:] + b)
+
+
+def use_block(wt_ref, k_ref, sum_ref, at, slot, d, count):
+    cols = slice(d * BLOCK, (d + count) * BLOCK)
+    where = pl.ds(at + d * BLOCK, count * BLOCK)
+    hi, lo = k_ref[slot, 0, :, cols], k_ref[slot, 1, :, cols]
+    part = product(wt_ref[:, where], hi, lo, 1)
+    if d:
+        sum_ref[:, where] += product(wt_ref[:, pl.ds(at, BLOCK)], hi, lo, 0)
+    return part
+
+
+def use_row(wt_ref, k_ref, sum_ref, at, slot):
+    part = use_block(wt_ref, k_ref, sum_ref, at, slot, 0, 1)
+    part = part + use_block(wt_ref, k_ref, sum_ref, at, slot, 1, REACH - 1)
+    sum_ref[:, pl.ds(at, BLOCK)] += part
+
+
+def send_sums(sum_ref, near_hbm, near_sem, use_last):
+    n = near_hbm.shape[1]
+    wrap, last = (REACH - 1) * BLOCK, n - BLOCK
+    parts = [slice(wrap, last), slice(0, wrap), slice(last, n)]
+    sends = [
+        pltpu.make_async_copy(sum_ref.at[:, p], near_hbm.at[:, p], near_sem.at[j]) for j, p in enumerate(parts)
+    ]
+    sends[0].start()
+    use_last()
+    sum_ref[:, 0:wrap] += sum_ref[:, n:]
+    sends[1].start()
+    sends[2].start()
+    for send in sends:
+        send.wait()
+
+
+def build_body(
+    coords_ref, w_hbm, near_hbm, k_hbm, k_ref, sum_ref, own_ref, points_ref, wt_ref, columns_ref, w_ref, w_sem, near_sem,
+    k_sem,
 ):
     n = coords_ref.shape[1]
     blocks = n // BLOCK
     wrap = (REACH - 1) * BLOCK
-    fetch = pltpu.make_async_copy(w_hbm, wt_ref.at[:, 0:n] if turned else w_own[0], w_sem)
+    fetch = pltpu.make_async_copy(w_hbm, w_ref, w_sem)
     fetch.start()
     points_ref[0:3, 0:n] = coords_ref[...] * LOG2E
     points_ref[3:, 0:n] = jnp.zeros((5, n), F32)
     points_ref[:, n:] = points_ref[:, 0:wrap]
     sum_ref[...] = jnp.zeros_like(sum_ref)
-
     for j in range(blocks):
         cols = slice(j * BLOCK, (j + 1) * BLOCK)
         columns_ref[cols, :] = points_ref[:, cols].T
@@ -242,61 +282,84 @@
                 dist = diff_sq * lax.rsqrt(jnp.maximum(diff_sq, 1e-37))
                 k_ref[slot, 0, sub, cols], k_ref[slot, 1, sub, cols] = split(jnp.exp2(-dist))
 
-    def product(w, hi, lo, contract):
-        dims = (((1,), (contract,)), ((), ()))
-        a = lax.dot_general(w, hi, dims, preferred_element_type=F32)
-        b = lax.dot_general(w[:OUT], lo, dims, preferred_element_type=F32)
-        return a[:OUT] + (a[OUT:] + b)
-
-    def use(at, slot, d, count):
-        cols = slice(d * BLOCK, (d + count) * BLOCK)
-        where = pl.ds(at + d * BLOCK, count * BLOCK)
-        part = product(wt_ref[:, where], k_ref[slot, 0, :, cols], k_ref[slot, 1, :, cols], 1)
-        if d:
-            sum_ref[:, where] += product(
-                wt_ref[:, pl.ds(at, BLOCK)], k_ref[slot, 0, :, cols], k_ref[slot, 1, :, cols], 0
-            )
-        return part
-
-    def finish(at, parts):
-        sum_ref[:, pl.ds(at, BLOCK)] += functools.reduce(jnp.add, parts)
-
-    def pair(p, carry):
-        for slot in range(2):
-            prev = pl.multiple_of((2 * p + slot) * BLOCK, BLOCK)
-            at = pl.multiple_of(prev + BLOCK, BLOCK)
-            place(lax.rem(2 * p + slot + 2, blocks), slot)
-            total = None
-            for d in range(REACH):
-                part = use(prev, slot, d, 1)
-                total = part if total is None else total + part
-                build(at, 1 - slot, d)
-            finish(prev, [total])
-        return carry
+    def keep(i, slot):
+        return pltpu.make_async_copy(k_ref.at[slot], k_hbm.at[i], k_sem.at[slot])
+
+    def step(i, slot, free):
+        prev = pl.multiple_of(i * BLOCK, BLOCK)
+        at = pl.multiple_of(prev + BLOCK, BLOCK)
+        if not free:
+            keep(i - 1, 1 - slot).wait()
+        place(lax.rem(i + 2, blocks), slot)
+        total = None
+        for d in range(REACH):
+            part = use_block(wt_ref, k_ref, sum_ref, prev, slot, d, 1)
+            total = part if total is None else total + part
+            build(at, 1 - slot, d)
+        sum_ref[:, pl.ds(prev, BLOCK)] += total
+        keep(i + 1, 1 - slot).start()
 
     place(0, 0)
     place(1, 1)
     for d in range(REACH):
         build(0, 0, d)
+    keep(0, 0).start()
     fetch.wait()
-    if not turned:
-        for j in range(blocks):
-            cols = slice(j * BLOCK, (j + 1) * BLOCK)
-            wt_ref[:, cols] = tall(w_own[0][cols, :].T)
+    for j in range(blocks):
+        cols = slice(j * BLOCK, (j + 1) * BLOCK)
+        wt_ref[:, cols] = tall(w_ref[cols, :].T)
     wt_ref[:, n:] = wt_ref[:, 0:wrap]
-    lax.fori_loop(0, (blocks - 1) // 2, pair, 0)
-    last = (blocks - 1) * BLOCK
-    parts = [slice(wrap, last), slice(0, wrap), slice(last, n)]
-    sends = [
-        pltpu.make_async_copy(sum_ref.at[:, p], near_hbm.at[:, p], near_sem.at[j]) for j, p in enumerate(parts)
-    ]
-    sends[0].start()
-    finish(last, [use(last, 0, 0, 1), use(last, 0, 1, REACH - 1)])
-    sum_ref[:, 0:wrap] += sum_ref[:, n:]
-    sends[1].start()
-    sends[2].start()
-    for send in sends:
-        send.wait()
+    step(0, 0, True)
+    step(1, 1, False)
+
+    def pair(p, carry):
+        step(2 * p, 0, False)
+        step(2 * p + 1, 1, False)
+        return carry
+
+    lax.fori_loop(1, (blocks - 1) // 2, pair, 0)
+    send_sums(
+        sum_ref, near_hbm, near_sem, lambda: use_row(wt_ref, k_ref, sum_ref, (blocks - 1) * BLOCK, 0)
+    )
+    keep(blocks - 2, 1).wait()
+    keep(blocks - 1, 0).wait()
+
+
+def near_body(w_hbm, k_hbm, near_hbm, k_ref, sum_ref, wt_ref, w_sem, near_sem, k_sem):
+    n = w_hbm.shape[1]
+    blocks = n // BLOCK
+
+    def load(i, slot):
+        return pltpu.make_async_copy(k_hbm.at[i], k_ref.at[slot], k_sem.at[slot])
+
+    fetch = pltpu.make_async_copy(w_hbm, wt_ref.at[:, 0:n], w_sem)
+    fetch.start()
+    for i in range(DEPTH - 1):
+        load(i, i).start()
+    sum_ref[...] = jnp.zeros_like(sum_ref)
+    fetch.wait()
+    wt_ref[:, n:] = wt_ref[:, 0 : (REACH - 1) * BLOCK]
+
+    def several(p, carry):
+        for slot in range(DEPTH):
+            i = DEPTH * p + slot
+            load(i + DEPTH - 1, (slot + DEPTH - 1) % DEPTH).start()
+            load(i, slot).wait()
+            use_row(wt_ref, k_ref, sum_ref, pl.multiple_of(i * BLOCK, BLOCK), slot)
+        return carry
+
+    lax.fori_loop(0, blocks // DEPTH - 1, several, 0)
+    for i in range(blocks - DEPTH, blocks - 1):
+        slot = i % DEPTH
+        if i + DEPTH - 1 < blocks:
+            load(i + DEPTH - 1, (slot + DEPTH - 1) % DEPTH).start()
+        load(i, slot).wait()
+        use_row(wt_ref, k_ref, sum_ref, i * BLOCK, slot)
+    load(blocks - 1, (blocks - 1) % DEPTH).wait()
+    send_sums(
+        sum_ref, near_hbm, near_sem,
+        lambda: use_row(wt_ref, k_ref, sum_ref, (blocks - 1) * BLOCK, (blocks - 1) % DEPTH),
+    )
 
 
 def middle_body(own_ref, m1_ref, m2_ref, m3_ref, out_ref):
@@ -425,8 +488,11 @@
     current = weights
     for step in range(STEPS):
         last = step == STEPS - 1
+        row_blocks = n // BLOCK
+        sums = pltpu.VMEM((OUT, wide_n), F32)
+        turned = pltpu.VMEM((2 * OUT, wide_n), BF16)
         if step:
-            (w_near,) = call(
+            (w_turned,) = call(
                 turn_body,
                 [shape(2 * OUT, n, dtype=BF16)],
                 (current,),
@@ -442,30 +508,48 @@
                 (0,),
                 (0,),
             )
-            own, w_near = lax.optimization_barrier((own, w_near))
+            own, w_turned = lax.optimization_barrier((own, w_turned))
+            (near_t,) = call(
+                near_body,
+                [shape(OUT, n)],
+                (w_turned, kept_blocks),
+                20,
+                "near",
+                [
+                    pltpu.VMEM((DEPTH, 2, BLOCK, REACH * BLOCK), BF16),
+                    sums,
+                    turned,
+                    pltpu.SemaphoreType.DMA,
+                    pltpu.SemaphoreType.DMA((3,)),
+                    pltpu.SemaphoreType.DMA((DEPTH,)),
+                ],
+                (6 * n * n * OUT, n * OUT * 12 + n * n * 2, 0),
+                (0, 1),
+                (0,),
+            )
         else:
-            w_near = current
-        (near_t,) = call(
-            functools.partial(near_body, bool(step)),
-            [shape(OUT, n)],
-            (coords, w_near),
-            20,
-            "near",
-            [
-                pltpu.VMEM((2, 2, BLOCK, REACH * BLOCK), BF16),
-                pltpu.VMEM((OUT, wide_n), F32),
-                pltpu.VMEM((2, 3, BLOCK, OUT), F32),
-                pltpu.VMEM((8, wide_n), F32),
-                pltpu.VMEM((2 * OUT, wide_n), BF16),
-                pltpu.VMEM((n, 8), F32),
-                pltpu.SemaphoreType.DMA,
-                pltpu.SemaphoreType.DMA((3,)),
-            ]
-            + ([] if step else [pltpu.VMEM((n, OUT), F32)]),
-            (6 * n * n * OUT, n * OUT * 12, n * n),
-            (1,),
-            (0,),
-        )
+            near_t, kept_blocks = call(
+                build_body,
+                [shape(OUT, n), shape(row_blocks, 2, BLOCK, REACH * BLOCK, dtype=BF16)],
+                (coords, current),
+                20,
+                "build",
+                [
+                    pltpu.VMEM((2, 2, BLOCK, REACH * BLOCK), BF16),
+                    sums,
+                    pltpu.VMEM((2, 3, BLOCK, OUT), F32),
+                    pltpu.VMEM((8, wide_n), F32),
+                    turned,
+                    pltpu.VMEM((n, 8), F32),
+                    pltpu.VMEM((n, OUT), F32),
+                    pltpu.SemaphoreType.DMA,
+                    pltpu.SemaphoreType.DMA((3,)),
+                    pltpu.SemaphoreType.DMA((2,)),
+                ],
+                (6 * n * n * OUT, n * OUT * 12, n * n),
+                (1,),
+                (0, 1),
+            )
         messages = [lax.ppermute(m, "leaf", ring(k)) for k, m in enumerate(messages, 1)]
         (spread,) = call(middle_body, [shape(N_MID, 2 * QROWS, OUT)], (own, *messages), 4, "middle")
         got = lax.all_to_all(spread, "mid", 0, 0)

time: 94.7 us -> 97.8 us (1.033)
  starting transfers between devices: 40.4 us -> 42.7 us
    all_to_all x2, starting transfers between devices: 16.7 us -> 19.5 us  [on_device(): got = lax.all_to_all(spread, 'mid', 0, 0)]
  transfers between devices with their start and end apart: 16 -> 16, of which waited for: 6 -> 5; matrix products, arithmetic and copies ran while one was open for 0% -> 0% of each run, Pallas kernels for 40% -> 39%
where the time goes in v7:
time: 97.8 us; the launch traced here: 97.4 us
  Pallas kernels  47.5 us (49%)
  starting transfers between devices  42.7 us (44%)
  waiting for transfers between devices  6.76 us (7%)
    pallas_call x13, Pallas kernels, call(): pl.pallas_call(body, out_shape=out, in_specs=[HBM if i in far_in else VME...  47.5 us
    all_to_all x2, starting transfers between devices, on_device(): got = lax.all_to_all(spread, 'mid', 0, 0)  19.5 us
    ppermute x6, starting transfers between devices, on_device(): lax.ppermute(m, 'leaf', ring(k))  10.8 us
    ppermute x2, starting transfers between devices, on_device(): s2 = lax.ppermute(s2, 'top', [(0, 1), (1, 0)])  7.84 us
    ppermute x6, starting transfers between devices, on_device(): tops = [top] + [lax.ppermute(top, 'leaf', ring(k)) for k in (1, 2, 3)]  4.52 us
    all_to_all x2, waiting for transfers between devices, on_device(): got = lax.all_to_all(spread, 'mid', 0, 0)  3.91 us
  transfers between devices with their start and end apart: 16, of which 5 were waited for; matrix products, arithmetic and copies ran while one was open for 0% of the time, Pallas kernels for 39%

profile of v7, /device:TPU:1, one launch (start us, length us, event | category | flops | bytes accessed | tf_op | source)
XLA Modules:
  0.0 97.4 jit_solution(13645576821895051179)
XLA Ops:
  0.0 2.8 %first.1 = (f32[64,128]{1,0:T(8,128)}, f32[32,128]{1,0:T(8,128)}, f32[96,128]{1,0:T(8,128)}, f32[96,128]{1,0:T(8,128)}, f32[96,128]{1,0:T(8,128)}) custom-call(f32[64,2304]{1,0:T(8,128)} %bitcast.1, f32[2304,128]{1,0:T(8,128)} %refs_1_.1, f32[1,64,64]{2,1,0:T(8,128)} %leaf_ref.3, f32[1,64,64]{2,1,0:T(8,128)} %mid_ref.3), custom_call_target="tpu_custom_call" | custom-call | tf_op jit(solution)/shard_map/first/pallas_call | solution.py:437
  2.8 0.0 copy-start.5
  2.8 2.1 %collective-permute-start = (f32[96,128]{1,0:T(8,128)}, f32[96,128]{1,0:T(8,128)S(1)}, u32[]{:S(2)}, u32[]{:S(2)}) collective-permute-start(f32[96,128]{1,0:T(8,128)} %get-tuple-element.40), channel_id=1, source_target_pairs={{0,1},{1,2},{2,3},{3,0},{4,5},{5,6},{6,7},{7,4},{8,9},{9,10},{10,1... | collective-permute-start | bytes 147464 | tf_op jit(solution)/shard_map/ppermute | solution.py:553
  5.0 2.6 %collective-permute-start.1 = (f32[96,128]{1,0:T(8,128)}, f32[96,128]{1,0:T(8,128)S(1)}, u32[]{:S(2)}, u32[]{:S(2)}) collective-permute-start(f32[96,128]{1,0:T(8,128)} %get-tuple-element.41), channel_id=1, source_target_pairs={{0,2},{1,3},{2,0},{3,1},{4,6},{5,7},{6,4},{7,5},{8,10},{9,11},{10,... | collective-permute-start | bytes 147464 | tf_op jit(solution)/shard_map/ppermute | solution.py:553
  7.6 1.1 %collective-permute-start.2 = (f32[96,128]{1,0:T(8,128)}, f32[96,128]{1,0:T(8,128)S(1)}, u32[]{:S(2)}, u32[]{:S(2)}) collective-permute-start(f32[96,128]{1,0:T(8,128)} %get-tuple-element.42), channel_id=1, source_target_pairs={{0,3},{1,0},{2,1},{3,2},{4,7},{5,4},{6,5},{7,6},{8,11},{9,8},{10,9... | collective-permute-start | bytes 147464 | tf_op jit(solution)/shard_map/ppermute | solution.py:553
  8.7 3.1 %prepare.1 = (bf16[2304,128]{1,0:T(8,128)(2,1)}, bf16[128,2048]{1,0:T(8,128)(2,1)}, bf16[128,320]{1,0:T(8,128)(2,1)}) custom-call(f32[64,2304]{1,0:T(8,128)} %bitcast.2, f32[1,64,64]{2,1,0:T(8,128)} %leaf_ref.3, f32[1,64,64]{2,1,0:T(8,128)} %mid_ref.3, f32[1,4,64,64]{3,2,1,0:T(8,128)} %couple_leaf_ref.1, f32[1,32,64,64]{3,2,1,0:T(8,128)} %couple_mid_ref.1, ...), custom_call_target="tpu_custom_call" | custom-call | tf_op jit(solution)/shard_map/prepare/pallas_call | solution.py:437
  11.8 0.0 copy-start.7
  11.8 0.0 collective-permute-done.m1_ref.refs_1_
  11.8 0.0 collective-permute-done.1.m2_ref.refs_2_
  11.8 0.0 collective-permute-done.2.m3_ref.refs_3_
  11.8 0.0 copy-done.5
  11.8 0.9 middle.2
  12.7 11.0 %all-to-all-start = ((f32[32,32,128]{2,1,0:T(8,128)}), f32[32,32,128]{2,1,0:T(8,128)S(1)}, u32[]{:S(2)}, u32[]{:S(2)}) async-start(f32[32,32,128]{2,1,0:T(8,128)} %middle.2), calls=%async_computation | async-start | bytes 1048576 | tf_op jit(solution)/shard_map/all_to_all | solution.py:555
  23.8 0.0 copy-done.7
  23.8 0.0 copy-start.2
  23.8 0.0 copy-start.6
  23.8 15.8 %build.1 = (f32[128,2304]{1,0:T(8,128)}, bf16[9,2,256,1280]{3,2,1,0:T(8,128)(2,1)}) custom-call(f32[3,2304]{1,0:T(4,128)S(1)} %copy-done.7, f32[2304,128]{1,0:T(8,128)} %refs_1_.1), custom_call_target="tpu_custom_call" | custom-call | flops 4076863488 | bytes 3538944 | tf_op jit(solution)/shard_map/build/pallas_call | solution.py:437
  39.6 0.0 all-to-all-done.got_ref
  39.6 0.0 copy-done.2
  39.6 0.5 couple.2
  40.1 3.3 %collective-permute-start.3 = (f32[16,128]{1,0:T(8,128)S(1)}, f32[16,128]{1,0:T(8,128)S(1)}, u32[]{:S(2)}, u32[]{:S(2)}) collective-permute-start(f32[16,128]{1,0:T(8,128)S(1)} %get-tuple-element.50), channel_id=1, source_target_pairs={{0,128},{128,0},{1,129},{129,1},{2,130},{130,2},{3,131},{131,3},{4... | collective-permute-start | bytes 24584 | tf_op jit(solution)/shard_map/ppermute | solution.py:565
  43.3 0.8 collective-permute-done.3
  44.2 0.0 copy-start
  44.2 0.0 copy-start.1
  44.2 0.0 copy-start.3
  44.2 0.0 copy-start.4
  44.2 1.5 %collective-permute-start.6 = (f32[32,128]{1,0:T(8,128)S(1)}, f32[32,128]{1,0:T(8,128)S(1)}, u32[]{:S(2)}, u32[]{:S(2)}) collective-permute-start(f32[32,128]{1,0:T(8,128)S(1)} %constant_dynamic-update-slice_fusion.refs_5_), channel_id=1, source_target_pairs={{0,3},{1,0},{2,1},{3,2},{4,7},{5,4},{6,5},{7,6},{8,11},{9,8},{10,9... | collective-permute-start | bytes 49160 | tf_op jit(solution)/shard_map/ppermute | solution.py:567
  45.6 0.8 collective-permute-start.5
  46.4 0.0 collective-permute-start.4
  46.4 0.0 copy-done.6
  46.4 3.8 %finish.2 = (f32[2304,128]{1,0:T(8,128)S(1)}, f32[2304,128]{1,0:T(8,128)S(1)}, f32[2304,128]{1,0:T(8,128)}) custom-call(f32[128,2304]{1,0:T(8,128)} %get-tuple-element.44.refs_0_, f32[2304,128]{1,0:T(8,128)} %refs_1_.1, s32[1,2304]{1,0:T(1,128)S(1)} %copy-done.6, s32[2304,128]{1,0:T(8,128)} %refs_3_.1), custom_call_target="tpu_custom_call" | custom-call | flops 169869312 | bytes 7077888 | tf_op jit(solution)/shard_map/finish/pallas_call | solution.py:437
  50.3 0.0 collective-permute-done.6.refs_8_
  50.3 0.0 collective-permute-done.5.refs_7_
  50.3 0.0 collective-permute-done.4.refs_6_
  50.3 0.0 copy-done
  50.3 0.0 copy-done.1
  50.3 0.0 copy-done.3
  50.4 0.0 copy-done.4
  50.4 2.2 %update.1 = (f32[2304,128]{1,0:T(8,128)}, f32[32,128]{1,0:T(8,128)S(1)}, f32[96,128]{1,0:T(8,128)S(1)}, f32[96,128]{1,0:T(8,128)S(1)}, f32[96,128]{1,0:T(8,128)S(1)}) custom-call(f32[2304,128]{1,0:T(8,128)S(1)} %get-tuple-element.45.refs_0_, f32[96,128]{1,0:T(8,128)S(1)} %collective-permute-done.m1_ref.refs_1_, ...), custom_call_target="tpu_custom_call" | custom-call | tf_op jit(solution)/shard_map/update/pallas_call | solution.py:437
  52.5 1.9 %collective-permute-start.7 = (f32[96,128]{1,0:T(8,128)S(1)}, f32[96,128]{1,0:T(8,128)S(1)}, u32[]{:S(2)}, u32[]{:S(2)}) collective-permute-start(f32[96,128]{1,0:T(8,128)S(1)} %get-tuple-element.57), channel_id=1, source_target_pairs={{0,1},{1,2},{2,3},{3,0},{4,5},{5,6},{6,7},{7,4},{8,9},{9,10},{10,1... | collective-permute-start | bytes 147464 | tf_op jit(solution)/shard_map/ppermute | solution.py:553
  54.5 2.0 %collective-permute-start.8 = (f32[96,128]{1,0:T(8,128)S(1)}, f32[96,128]{1,0:T(8,128)S(1)}, u32[]{:S(2)}, u32[]{:S(2)}) collective-permute-start(f32[96,128]{1,0:T(8,128)S(1)} %get-tuple-element.58), channel_id=1, source_target_pairs={{0,2},{1,3},{2,0},{3,1},{4,6},{5,7},{6,4},{7,5},{8,10},{9,11},{10,... | collective-permute-start | bytes 147464 | tf_op jit(solution)/shard_map/ppermute | solution.py:553
  56.5 1.1 %collective-permute-start.9 = (f32[96,128]{1,0:T(8,128)S(1)}, f32[96,128]{1,0:T(8,128)S(1)}, u32[]{:S(2)}, u32[]{:S(2)}) collective-permute-start(f32[96,128]{1,0:T(8,128)S(1)} %get-tuple-element.59), channel_id=1, source_target_pairs={{0,3},{1,0},{2,1},{3,2},{4,7},{5,4},{6,5},{7,6},{8,11},{9,8},{10,9... | collective-permute-start | bytes 147464 | tf_op jit(solution)/shard_map/ppermute | solution.py:553
  57.5 2.3 %turn.1.w_hbm = bf16[256,2304]{1,0:T(8,128)(2,1)} custom-call(f32[2304,128]{1,0:T(8,128)} %get-tuple-element.55.w_hbm.refs_1_), custom_call_target="tpu_custom_call" | custom-call | bytes 2359296 | tf_op jit(solution)/shard_map/turn/pallas_call | solution.py:437
  59.9 0.0 collective-permute-done.7.m1_ref.refs_1_
  59.9 0.0 collective-permute-done.8.m2_ref.refs_2_
  59.9 0.0 collective-permute-done.9.m3_ref.refs_3_
  59.9 0.9 middle.3
  60.8 8.5 %all-to-all-start.1 = ((f32[32,32,128]{2,1,0:T(8,128)}), f32[32,32,128]{2,1,0:T(8,128)S(1)}, u32[]{:S(2)}, u32[]{:S(2)}) async-start(f32[32,32,128]{2,1,0:T(8,128)} %middle.3), calls=%async_computation.1 | async-start | bytes 1048576 | tf_op jit(solution)/shard_map/all_to_all | solution.py:555
  69.3 10.6 %near.1.refs_0_ = f32[128,2304]{1,0:T(8,128)} custom-call(bf16[256,2304]{1,0:T(8,128)(2,1)} %turn.1.w_hbm, bf16[9,2,256,1280]{3,2,1,0:T(8,128)(2,1)} %get-tuple-element.61.k_hbm), custom_call_target="tpu_custom_call" | custom-call | flops 4076863488 | bytes 14155776 | tf_op jit(solution)/shard_map/near/pallas_call | solution.py:437
  79.9 3.9 %all-to-all-done.1.got_ref = f32[32,32,128]{2,1,0:T(8,128)S(1)} async-done(((f32[32,32,128]{2,1,0:T(8,128)}), f32[32,32,128]{2,1,0:T(8,128)S(1)}, u32[]{:S(2)}, u32[]{:S(2)}) %all-to-all-start.1) | async-done | bytes 524320 | tf_op jit(solution)/shard_map/all_to_all | solution.py:555
  83.8 0.5 couple.3
  84.3 4.6 %collective-permute-start.10 = (f32[16,128]{1,0:T(8,128)S(1)}, f32[16,128]{1,0:T(8,128)S(1)}, u32[]{:S(2)}, u32[]{:S(2)}) collective-permute-start(f32[16,128]{1,0:T(8,128)S(1)} %get-tuple-element.67), channel_id=1, source_target_pairs={{0,128},{128,0},{1,129},{129,1},{2,130},{130,2},{3,131},{131,3},{4... | collective-permute-start | bytes 24584 | tf_op jit(solution)/shard_map/ppermute | solution.py:565
  88.9 0.8 collective-permute-done.10
  89.7 1.7 %collective-permute-start.13 = (f32[32,128]{1,0:T(8,128)S(1)}, f32[32,128]{1,0:T(8,128)S(1)}, u32[]{:S(2)}, u32[]{:S(2)}) collective-permute-start(f32[32,128]{1,0:T(8,128)S(1)} %constant_dynamic-update-slice_fusion.2.refs_5_), channel_id=1, source_target_pairs={{0,3},{1,0},{2,1},{3,2},{4,7},{5,4},{6,5},{7,6},{8,11},{9,8},{10,9... | collective-permute-start | bytes 49160 | tf_op jit(solution)/shard_map/ppermute | solution.py:567
  91.4 0.3 collective-permute-start.12
  91.7 0.3 collective-permute-start.11
  92.0 2.5 %finish.3 = (f32[2304,128]{1,0:T(8,128)S(1)}, f32[2304,128]{1,0:T(8,128)S(1)}) custom-call(f32[128,2304]{1,0:T(8,128)} %near.1.refs_0_, f32[2304,128]{1,0:T(8,128)} %get-tuple-element.55.w_hbm.refs_1_, f32[2304,128]{1,0:T(8,128)} %get-tuple-element.63.refs_2_), custom_call_target="tpu_custom_call" | custom-call | flops 294912 | bytes 5898240 | tf_op jit(solution)/shard_map/finish/pallas_call | solution.py:437
  94.5 0.0 collective-permute-done.13.refs_8_
  94.5 1.0 %collective-permute-done.12.refs_7_ = f32[32,128]{1,0:T(8,128)S(1)} collective-permute-done((f32[32,128]{1,0:T(8,128)S(1)}, f32[32,128]{1,0:T(8,128)S(1)}, u32[]{:S(2)}, u32[]{:S(2)}) %collective-permute-start.12) | collective-permute-done | bytes 16416 | tf_op jit(solution)/shard_map/ppermute | solution.py:567
  95.5 0.2 collective-permute-done.11.refs_6_
  95.6 1.6 %last.1 = f32[2304,128]{1,0:T(8,128)} custom-call(f32[2304,128]{1,0:T(8,128)S(1)} %get-tuple-element.64.refs_0_, f32[96,128]{1,0:T(8,128)S(1)} %collective-permute-done.7.m1_ref.refs_1_, f32[96,128]{1,0:T(8,128)S(1)} %collective-permute-done.8.m2_ref.refs_2_, f32[96,128]{1,0:T(8,128)S(1)} %collective-permute-done.9.m3_ref.refs_3_, ...), custom_call_target="tpu_custom_call" | custom-call | tf_op jit(solution)/shard_map/last/pallas_call | solution.py:437
  (4 shorter events, 0.0 us)
Async XLA Ops:
  2.8 9.0 %copy-start.5 = (f32[32,128]{1,0:T(8,128)S(1)}, f32[32,128]{1,0:T(8,128)}, u32[]{:S(2)}) copy-start(f32[32,128]{1,0:T(8,128)} %get-tuple-element.39.own_ref) | copy-start | bytes 49156
  2.8 8.9 %collective-permute-start = (f32[96,128]{1,0:T(8,128)}, f32[96,128]{1,0:T(8,128)S(1)}, u32[]{:S(2)}, u32[]{:S(2)}) collective-permute-start(f32[96,128]{1,0:T(8,128)} %get-tuple-element.40), channel_id=1, source_target_pairs={{0,1},{1,2},{2,3},{3,0},{4,5},{5,6},{6,7},{7,4},{8,9},{9,10},{10,1... | collective-permute-start | bytes 147464 | tf_op jit(solution)/shard_map/ppermute | solution.py:553
  5.0 6.8 %collective-permute-start.1 = (f32[96,128]{1,0:T(8,128)}, f32[96,128]{1,0:T(8,128)S(1)}, u32[]{:S(2)}, u32[]{:S(2)}) collective-permute-start(f32[96,128]{1,0:T(8,128)} %get-tuple-element.41), channel_id=1, source_target_pairs={{0,2},{1,3},{2,0},{3,1},{4,6},{5,7},{6,4},{7,5},{8,10},{9,11},{10,... | collective-permute-start | bytes 147464 | tf_op jit(solution)/shard_map/ppermute | solution.py:553
  7.6 4.2 %collective-permute-start.2 = (f32[96,128]{1,0:T(8,128)}, f32[96,128]{1,0:T(8,128)S(1)}, u32[]{:S(2)}, u32[]{:S(2)}) collective-permute-start(f32[96,128]{1,0:T(8,128)} %get-tuple-element.42), channel_id=1, source_target_pairs={{0,3},{1,0},{2,1},{3,2},{4,7},{5,4},{6,5},{7,6},{8,11},{9,8},{10,9... | collective-permute-start | bytes 147464 | tf_op jit(solution)/shard_map/ppermute | solution.py:553
  11.8 12.0 %copy-start.7 = (f32[3,2304]{1,0:T(4,128)S(1)}, f32[3,2304]{1,0:T(4,128)}, u32[]{:S(2)}) copy-start(f32[3,2304]{1,0:T(4,128)} %coords_ref.1) | copy-start | bytes 82948
  12.7 26.9 %all-to-all-start = ((f32[32,32,128]{2,1,0:T(8,128)}), f32[32,32,128]{2,1,0:T(8,128)S(1)}, u32[]{:S(2)}, u32[]{:S(2)}) async-start(f32[32,32,128]{2,1,0:T(8,128)} %middle.2), calls=%async_computation | async-start | bytes 1048576 | tf_op jit(solution)/shard_map/all_to_all | solution.py:555
  23.8 15.8 %copy-start.2 = (bf16[128,2048]{1,0:T(8,128)(2,1)S(1)}, bf16[128,2048]{1,0:T(8,128)(2,1)}, u32[]{:S(2)}) copy-start(bf16[128,2048]{1,0:T(8,128)(2,1)} %get-tuple-element.48.couple_ref) | copy-start | bytes 1572868
  23.8 22.7 %copy-start.6 = (s32[1,2304]{1,0:T(1,128)S(1)}, s32[1,2304]{1,0:T(1,128)}, u32[]{:S(2)}) copy-start(s32[1,2304]{1,0:T(1,128)} %refs_2_.1) | copy-start | bytes 27652
  40.1 4.1 %collective-permute-start.3 = (f32[16,128]{1,0:T(8,128)S(1)}, f32[16,128]{1,0:T(8,128)S(1)}, u32[]{:S(2)}, u32[]{:S(2)}) collective-permute-start(f32[16,128]{1,0:T(8,128)S(1)} %get-tuple-element.50), channel_id=1, source_target_pairs={{0,128},{128,0},{1,129},{129,1},{2,130},{130,2},{3,131},{131,3},{4... | collective-permute-start | bytes 24584 | tf_op jit(solution)/shard_map/ppermute | solution.py:565
  44.2 6.2 %copy-start = (f32[2304,64]{0,1:T(8,128)S(1)}, f32[2304,64]{0,1:T(8,128)}, u32[]{:S(2)}) copy-start(f32[2304,64]{0,1:T(8,128)} %param.14) | copy-start | bytes 1769476
  44.2 6.2 %copy-start.1 = (bf16[2304,128]{1,0:T(8,128)(2,1)S(1)}, bf16[2304,128]{1,0:T(8,128)(2,1)}, u32[]{:S(2)}) copy-start(bf16[2304,128]{1,0:T(8,128)(2,1)} %get-tuple-element.52.refs_10_) | copy-start | bytes 1769476
  44.2 6.2 %copy-start.3 = (bf16[128,320]{1,0:T(8,128)(2,1)S(1)}, bf16[128,320]{1,0:T(8,128)(2,1)}, u32[]{:S(2)}) copy-start(bf16[128,320]{1,0:T(8,128)(2,1)} %get-tuple-element.46.refs_4_) | copy-start | bytes 245764
  44.2 6.2 %copy-start.4 = (f32[64,128]{1,0:T(8,128)S(1)}, f32[64,128]{1,0:T(8,128)}, u32[]{:S(2)}) copy-start(f32[64,128]{1,0:T(8,128)} %get-tuple-element.53.refs_12_) | copy-start | bytes 98308
  44.2 6.1 %collective-permute-start.6 = (f32[32,128]{1,0:T(8,128)S(1)}, f32[32,128]{1,0:T(8,128)S(1)}, u32[]{:S(2)}, u32[]{:S(2)}) collective-permute-start(f32[32,128]{1,0:T(8,128)S(1)} %constant_dynamic-update-slice_fusion.refs_5_), channel_id=1, source_target_pairs={{0,3},{1,0},{2,1},{3,2},{4,7},{5,4},{6,5},{7,6},{8,11},{9,8},{10,9... | collective-permute-start | bytes 49160 | tf_op jit(solution)/shard_map/ppermute | solution.py:567
  45.6 4.7 %collective-permute-start.5 = (f32[32,128]{1,0:T(8,128)S(1)}, f32[32,128]{1,0:T(8,128)S(1)}, u32[]{:S(2)}, u32[]{:S(2)}) collective-permute-start(f32[32,128]{1,0:T(8,128)S(1)} %constant_dynamic-update-slice_fusion.refs_5_), channel_id=1, source_target_pairs={{0,2},{1,3},{2,0},{3,1},{4,6},{5,7},{6,4},{7,5},{8,10},{9,11},{10,... | collective-permute-start | bytes 49160 | tf_op jit(solution)/shard_map/ppermute | solution.py:567
  46.4 3.9 %collective-permute-start.4 = (f32[32,128]{1,0:T(8,128)S(1)}, f32[32,128]{1,0:T(8,128)S(1)}, u32[]{:S(2)}, u32[]{:S(2)}) collective-permute-start(f32[32,128]{1,0:T(8,128)S(1)} %constant_dynamic-update-slice_fusion.refs_5_), channel_id=1, source_target_pairs={{0,1},{1,2},{2,3},{3,0},{4,5},{5,6},{6,7},{7,4},{8,9},{9,10},{10,1... | collective-permute-start | bytes 49160 | tf_op jit(solution)/shard_map/ppermute | solution.py:567
  52.5 7.4 %collective-permute-start.7 = (f32[96,128]{1,0:T(8,128)S(1)}, f32[96,128]{1,0:T(8,128)S(1)}, u32[]{:S(2)}, u32[]{:S(2)}) collective-permute-start(f32[96,128]{1,0:T(8,128)S(1)} %get-tuple-element.57), channel_id=1, source_target_pairs={{0,1},{1,2},{2,3},{3,0},{4,5},{5,6},{6,7},{7,4},{8,9},{9,10},{10,1... | collective-permute-start | bytes 147464 | tf_op jit(solution)/shard_map/ppermute | solution.py:553
  54.5 5.4 %collective-permute-start.8 = (f32[96,128]{1,0:T(8,128)S(1)}, f32[96,128]{1,0:T(8,128)S(1)}, u32[]{:S(2)}, u32[]{:S(2)}) collective-permute-start(f32[96,128]{1,0:T(8,128)S(1)} %get-tuple-element.58), channel_id=1, source_target_pairs={{0,2},{1,3},{2,0},{3,1},{4,6},{5,7},{6,4},{7,5},{8,10},{9,11},{10,... | collective-permute-start | bytes 147464 | tf_op jit(solution)/shard_map/ppermute | solution.py:553
  56.5 3.4 %collective-permute-start.9 = (f32[96,128]{1,0:T(8,128)S(1)}, f32[96,128]{1,0:T(8,128)S(1)}, u32[]{:S(2)}, u32[]{:S(2)}) collective-permute-start(f32[96,128]{1,0:T(8,128)S(1)} %get-tuple-element.59), channel_id=1, source_target_pairs={{0,3},{1,0},{2,1},{3,2},{4,7},{5,4},{6,5},{7,6},{8,11},{9,8},{10,9... | collective-permute-start | bytes 147464 | tf_op jit(solution)/shard_map/ppermute | solution.py:553
  60.8 23.0 %all-to-all-start.1 = ((f32[32,32,128]{2,1,0:T(8,128)}), f32[32,32,128]{2,1,0:T(8,128)S(1)}, u32[]{:S(2)}, u32[]{:S(2)}) async-start(f32[32,32,128]{2,1,0:T(8,128)} %middle.3), calls=%async_computation.1 | async-start | bytes 1048576 | tf_op jit(solution)/shard_map/all_to_all | solution.py:555
  84.3 5.4 %collective-permute-start.10 = (f32[16,128]{1,0:T(8,128)S(1)}, f32[16,128]{1,0:T(8,128)S(1)}, u32[]{:S(2)}, u32[]{:S(2)}) collective-permute-start(f32[16,128]{1,0:T(8,128)S(1)} %get-tuple-element.67), channel_id=1, source_target_pairs={{0,128},{128,0},{1,129},{129,1},{2,130},{130,2},{3,131},{131,3},{4... | collective-permute-start | bytes 24584 | tf_op jit(solution)/shard_map/ppermute | solution.py:565
  89.7 4.8 %collective-permute-start.13 = (f32[32,128]{1,0:T(8,128)S(1)}, f32[32,128]{1,0:T(8,128)S(1)}, u32[]{:S(2)}, u32[]{:S(2)}) collective-permute-start(f32[32,128]{1,0:T(8,128)S(1)} %constant_dynamic-update-slice_fusion.2.refs_5_), channel_id=1, source_target_pairs={{0,3},{1,0},{2,1},{3,2},{4,7},{5,4},{6,5},{7,6},{8,11},{9,8},{10,9... | collective-permute-start | bytes 49160 | tf_op jit(solution)/shard_map/ppermute | solution.py:567
  91.4 4.1 %collective-permute-start.12 = (f32[32,128]{1,0:T(8,128)S(1)}, f32[32,128]{1,0:T(8,128)S(1)}, u32[]{:S(2)}, u32[]{:S(2)}) collective-permute-start(f32[32,128]{1,0:T(8,128)S(1)} %constant_dynamic-update-slice_fusion.2.refs_5_), channel_id=1, source_target_pairs={{0,2},{1,3},{2,0},{3,1},{4,6},{5,7},{6,4},{7,5},{8,10},{9,11},{10,... | collective-permute-start | bytes 49160 | tf_op jit(solution)/shard_map/ppermute | solution.py:567
  91.7 4.0 %collective-permute-start.11 = (f32[32,128]{1,0:T(8,128)S(1)}, f32[32,128]{1,0:T(8,128)S(1)}, u32[]{:S(2)}, u32[]{:S(2)}) collective-permute-start(f32[32,128]{1,0:T(8,128)S(1)} %constant_dynamic-update-slice_fusion.2.refs_5_), channel_id=1, source_target_pairs={{0,1},{1,2},{2,3},{3,0},{4,5},{5,6},{6,7},{7,4},{8,9},{9,10},{10,1... | collective-permute-start | bytes 49160 | tf_op jit(solution)/shard_map/ppermute | solution.py:567

commit v8 on v6

--- a/solution.py
+++ b/solution.py
@@ -109,37 +109,62 @@
         ref[RANK:, :] = quarter(lax.rem(own + k, N_LEAF))
 
 
-def first_body(basis_t_ref, w_ref, leaf_ref, mid_ref, up_ref, own_ref, *message_refs):
+def first_body(basis_t_hbm, w_hbm, leaf_ref, mid_ref, up_ref, own_ref, *refs):
+    message_refs, (basis_t_ref, w_ref, basis_sem, w_sem) = refs[:3], refs[3:]
+    n = w_hbm.shape[0]
+    parts = [slice(j, j + GROUP * BLOCK) for j in range(0, n, GROUP * BLOCK)]
+    basis = pltpu.make_async_copy(basis_t_hbm, basis_t_ref, basis_sem)
+    loads = [pltpu.make_async_copy(w_hbm.at[p], w_ref.at[p], w_sem.at[j]) for j, p in enumerate(parts)]
+    for load in (basis, *loads):
+        load.start()
     through = jnp.dot(leaf_ref[0], mid_ref[0], precision=HP, preferred_element_type=F32)
     up_ref[...] = jnp.concatenate([leaf_ref[0], through], axis=1)
-    s0 = dot3(tall(basis_t_ref[...]), wide(w_ref[...]))
+    basis.wait()
+    s0 = None
+    for part, load in zip(parts, loads):
+        load.wait()
+        term = dot3(tall(basis_t_ref[:, part]), wide(w_ref[part, :]))
+        s0 = term if s0 is None else s0 + term
     emit_messages(s0, up_ref[...], own_ref, message_refs)
 
 
 def prepare_body(
-    basis_t_ref, leaf_ref, mid_ref, couple_leaf_ref, couple_mid_ref, couple_top_ref,
-    bcat_ref, couple_ref, down_ref,
+    basis_t_hbm, leaf_ref, mid_ref, couple_leaf_ref, couple_mid_hbm, couple_top_ref, bcat_hbm, couple_hbm, down_ref,
+    basis_t_ref, couple_mid_ref, bcat_ref, couple_ref, sems,
 ):
     n = basis_t_ref.shape[1]
-    for j in range(n // BLOCK):
-        cols = slice(j * BLOCK, (j + 1) * BLOCK)
-        bcat_ref[cols, :] = wide(basis_t_ref[:, cols].T)
+    blocks_in = pltpu.make_async_copy(couple_mid_hbm, couple_mid_ref, sems.at[0])
+    basis_in = pltpu.make_async_copy(basis_t_hbm, basis_t_ref, sems.at[1])
+    couple_out = pltpu.make_async_copy(couple_ref, couple_hbm, sems.at[2])
+    bcat_out = pltpu.make_async_copy(bcat_ref, bcat_hbm, sems.at[3])
+    blocks_in.start()
+    basis_in.start()
     own_mid, own_leaf = lax.axis_index("mid"), lax.axis_index("leaf")
+    blocks_in.wait()
     for m in range(N_MID // 2):
         pair = [
             jnp.where(own_mid == i, 0.0, couple_mid_ref[0, i]) for i in (2 * m, 2 * m + 1)
         ]
         couple_ref[:, m * OUT : (m + 1) * OUT] = tall(jnp.concatenate(pair, axis=1))
+    couple_out.start()
+    basis_in.wait()
+    for j in range(n // BLOCK):
+        cols = slice(j * BLOCK, (j + 1) * BLOCK)
+        bcat_ref[cols, :] = wide(basis_t_ref[:, cols].T)
+    bcat_out.start()
     other = 1 - lax.axis_index("top")
     from_top = jnp.dot(mid_ref[0], couple_top_ref[0, other], precision=HP, preferred_element_type=F32)
     from_top = jnp.dot(leaf_ref[0], from_top, precision=HP, preferred_element_type=F32)
     siblings = [couple_leaf_ref[0, lax.rem(own_leaf + N_LEAF - k, N_LEAF)] for k in (1, 2, 3)]
     down_ref[...] = tall(jnp.concatenate([*siblings, leaf_ref[0], from_top], axis=1))
-
-
-def permuted_labels(order, labels_ref):
+    couple_out.wait()
+    bcat_out.wait()
+
+
+def permute_labels(order, fetch, labels_ref, chosen_ref, bit_ref, out_ref):
     n = labels_ref.shape[0]
     group = n // BITS
+    blocks = [slice(j, j + BLOCK) for j in range(0, n, BLOCK)]
     which = jnp.zeros_like(order)
     place = jnp.ones(order.shape, F32)
     for g in range(1, BITS):
@@ -147,25 +172,28 @@
         which = jnp.where(beyond, g * group, which)
         place = jnp.where(beyond, 1.0 / (1 << g), place)
     rows = jnp.concatenate([(order - which).astype(F32), place, jnp.zeros((6, n), F32)], axis=0)
+    lane = lax.broadcasted_iota(jnp.int32, (BLOCK, group), 1).astype(F32)
+    for at in blocks:
+        columns = rows[:, at].T
+        chosen_ref[at, :] = jnp.where(columns[:, 0:1] == lane, 1.0, 0.0).astype(BF16)
+        bit_ref[at, :] = columns
+    fetch.wait()
     packed = jnp.zeros((group, OUT), F32)
     for g in range(BITS):
         packed = packed + labels_ref[g * group : (g + 1) * group, :].astype(F32) * float(1 << g)
     packed = packed.astype(BF16)
-    lane = lax.broadcasted_iota(jnp.int32, (BLOCK, group), 1).astype(F32)
-    for j in range(n // BLOCK):
-        columns = rows[:, j * BLOCK : (j + 1) * BLOCK].T
-        chosen = jnp.where(columns[:, 0:1] == lane, 1.0, 0.0).astype(BF16)
-        value = jnp.dot(chosen, packed, preferred_element_type=F32) * columns[:, 1:2]
+    for at in blocks:
+        value = jnp.dot(chosen_ref[at, :], packed, preferred_element_type=F32) * bit_ref[at, 1:2]
         value = jnp.floor(value)
-        yield value - 2.0 * jnp.floor(0.5 * value)
+        out_ref[at, :] = value - 2.0 * jnp.floor(0.5 * value)
 
 
 def finish_body(scale, *refs):
-    first = len(refs) == 13
+    first = len(refs) == 15
     if first:
         sum_hbm, w_hbm, order_ref, labels_hbm, near_ref, base_ref, targets_hbm = refs[:7]
-        sum_ref, w_ref, labels_ref, targets_ref, sems, sent = refs[7:13]
-        pairs = [(labels_hbm, labels_ref), (w_hbm, w_ref), (sum_hbm, sum_ref)]
+        sum_ref, w_ref, labels_ref, targets_ref, chosen_ref, bit_ref, sems, sent = refs[7:]
+        pairs = [(labels_hbm, labels_ref), (sum_hbm, sum_ref), (w_hbm, w_ref)]
     else:
         sum_hbm, w_hbm, targets_hbm, near_ref, base_ref, sum_ref, w_ref, targets_ref, sems = refs
         pairs = [(sum_hbm, sum_ref), (w_hbm, w_ref), (targets_hbm, targets_ref)]
@@ -175,16 +203,17 @@
     n = near_ref.shape[0]
     blocks = [slice(j, j + BLOCK) for j in range(0, n, BLOCK)]
     if first:
-        loads[0].wait()
-        for rows, found in zip(blocks, permuted_labels(order_ref[...], labels_ref)):
-            targets_ref[rows, :] = found
+        permute_labels(order_ref[...], loads[0], labels_ref, chosen_ref, bit_ref, targets_ref)
         send = pltpu.make_async_copy(targets_ref, targets_hbm, sent)
         send.start()
-    for load in loads[1:] if first else loads:
+        loads = loads[1:]
+    loads[0].wait()
+    for rows in blocks:
+        near_ref[rows, :] = sum_ref[:, rows].T * scale
+    for load in loads[1:]:
         load.wait()
     for rows in blocks:
         base_ref[rows, :] = w_ref[rows, :] + targets_ref[rows, :]
-        near_ref[rows, :] = sum_ref[:, rows].T * scale
     if first:
         send.wait()
 
@@ -408,6 +437,13 @@
         (basis_t, weights, transfer_leaf, transfer_mid),
         58,
         "first",
+        [
+            pltpu.VMEM((RANK, n), F32),
+            pltpu.VMEM((n, OUT), F32),
+            pltpu.SemaphoreType.DMA,
+            pltpu.SemaphoreType.DMA((groups,)),
+        ],
+        far_in=(0, 1),
     )
     bcat, couple, down = call(
         prepare_body,
@@ -419,6 +455,15 @@
         (basis_t, transfer_leaf, transfer_mid, couple_leaf, couple_mid, couple_top),
         58,
         "prepare",
+        [
+            pltpu.VMEM((RANK, n), F32),
+            pltpu.VMEM((1, N_MID, RANK, RANK), F32),
+            pltpu.VMEM((n, 2 * RANK), BF16),
+            pltpu.VMEM((2 * RANK, N_MID * RANK), BF16),
+            pltpu.SemaphoreType.DMA((4,)),
+        ],
+        far_in=(0, 4),
+        far_out=(0, 1),
     )
     own, couple = lax.optimization_barrier((own, couple))
 
@@ -498,12 +543,14 @@
                 functools.partial(finish_body, scale),
                 [shape(n, OUT)] * 3,
                 (near_t, current, order, labels),
-                12,
+                16,
                 "finish",
                 [
                     *kept,
                     pltpu.VMEM((n, OUT), jnp.int32),
                     pltpu.VMEM((n, OUT), F32),
+                    pltpu.VMEM((n, n // BITS), BF16),
+                    pltpu.VMEM((n, 8), F32),
                     pltpu.SemaphoreType.DMA((3,)),
                     pltpu.SemaphoreType.DMA,
                 ],

time: 94.7 us -> 96.7 us (1.021)
  Pallas kernels: 46.7 us -> 48.2 us
    pallas_call x13, Pallas kernels: 46.7 us -> 48.2 us  [call(): pl.pallas_call(body, out_shape=out, in_specs=[HBM if i in far_in else VME...]
  transfers between devices with their start and end apart: 16 -> 16, of which waited for: 6 -> 7; matrix products, arithmetic and copies ran while one was open for 0% -> 0% of each run, Pallas kernels for 40% -> 39%
where the time goes in v8:
time: 96.7 us; the launch traced here: 96.2 us
  Pallas kernels  48.2 us (50%)
  starting transfers between devices  40.2 us (42%)
  waiting for transfers between devices  7.39 us (8%)
    pallas_call x13, Pallas kernels, call(): pl.pallas_call(body, out_shape=out, in_specs=[HBM if i in far_in else VME...  48.2 us
    all_to_all x2, starting transfers between devices, on_device(): got = lax.all_to_all(spread, 'mid', 0, 0)  16.5 us
    ppermute x6, starting transfers between devices, on_device(): lax.ppermute(m, 'leaf', ring(k))  10.4 us
    ppermute x2, starting transfers between devices, on_device(): s2 = lax.ppermute(s2, 'top', [(0, 1), (1, 0)])  8.63 us
    ppermute x6, starting transfers between devices, on_device(): tops = [top] + [lax.ppermute(top, 'leaf', ring(k)) for k in (1, 2, 3)]  4.62 us
    all_to_all x2, waiting for transfers between devices, on_device(): got = lax.all_to_all(spread, 'mid', 0, 0)  3.69 us
    ppermute x6, waiting for transfers between devices, on_device(): tops = [top] + [lax.ppermute(top, 'leaf', ring(k)) for k in (1, 2, 3)]  2.03 us
  transfers between devices with their start and end apart: 16, of which 7 were waited for; matrix products, arithmetic and copies ran while one was open for 0% of the time, Pallas kernels for 39%

profile of v8, /device:TPU:1, one launch (start us, length us, event | category | flops | bytes accessed | tf_op | source)
XLA Modules:
  0.0 96.2 jit_solution(11200004793662692001)
XLA Ops:
  0.0 3.9 %first.1 = (f32[64,128]{1,0:T(8,128)}, f32[32,128]{1,0:T(8,128)}, f32[96,128]{1,0:T(8,128)}, f32[96,128]{1,0:T(8,128)}, f32[96,128]{1,0:T(8,128)}) custom-call(f32[64,2304]{1,0:T(8,128)} %bitcast.1, f32[2304,128]{1,0:T(8,128)} %refs_1_.1, f32[1,64,64]{2,1,0:T(8,128)} %leaf_ref.3, f32[1,64,64]{2,1,0:T(8,128)} %mid_ref.3), custom_call_target="tpu_custom_call" | custom-call | tf_op jit(solution)/shard_map/first/pallas_call | solution.py:403
  3.9 0.0 copy-start.5
  3.9 2.2 %collective-permute-start = (f32[96,128]{1,0:T(8,128)}, f32[96,128]{1,0:T(8,128)S(1)}, u32[]{:S(2)}, u32[]{:S(2)}) collective-permute-start(f32[96,128]{1,0:T(8,128)} %get-tuple-element.38), channel_id=1, source_target_pairs={{0,1},{1,2},{2,3},{3,0},{4,5},{5,6},{6,7},{7,4},{8,9},{9,10},{10,1... | collective-permute-start | bytes 147464 | tf_op jit(solution)/shard_map/ppermute | solution.py:514
  6.1 2.6 %collective-permute-start.1 = (f32[96,128]{1,0:T(8,128)}, f32[96,128]{1,0:T(8,128)S(1)}, u32[]{:S(2)}, u32[]{:S(2)}) collective-permute-start(f32[96,128]{1,0:T(8,128)} %get-tuple-element.39), channel_id=1, source_target_pairs={{0,2},{1,3},{2,0},{3,1},{4,6},{5,7},{6,4},{7,5},{8,10},{9,11},{10,... | collective-permute-start | bytes 147464 | tf_op jit(solution)/shard_map/ppermute | solution.py:514
  8.7 1.1 %collective-permute-start.2 = (f32[96,128]{1,0:T(8,128)}, f32[96,128]{1,0:T(8,128)S(1)}, u32[]{:S(2)}, u32[]{:S(2)}) collective-permute-start(f32[96,128]{1,0:T(8,128)} %get-tuple-element.40), channel_id=1, source_target_pairs={{0,3},{1,0},{2,1},{3,2},{4,7},{5,4},{6,5},{7,6},{8,11},{9,8},{10,9... | collective-permute-start | bytes 147464 | tf_op jit(solution)/shard_map/ppermute | solution.py:514
  9.8 4.4 %prepare.1 = (bf16[2304,128]{1,0:T(8,128)(2,1)}, bf16[128,2048]{1,0:T(8,128)(2,1)}, bf16[128,320]{1,0:T(8,128)(2,1)}) custom-call(f32[64,2304]{1,0:T(8,128)} %bitcast.2, f32[1,64,64]{2,1,0:T(8,128)} %leaf_ref.3, f32[1,64,64]{2,1,0:T(8,128)} %mid_ref.3, f32[1,4,64,64]{3,2,1,0:T(8,128)} %couple_leaf_ref.1, f32[1,32,64,64]{3,2,1,0:T(8,128)} %couple_mid_hbm.1, ...), custom_call_target="tpu_custom_call" | custom-call | tf_op jit(solution)/shard_map/prepare/pallas_call | solution.py:403
  14.2 0.0 copy-start.7
  14.3 0.0 collective-permute-done.m1_ref.refs_1_
  14.3 0.0 collective-permute-done.1.m2_ref.refs_2_
  14.3 0.0 collective-permute-done.2.m3_ref.refs_3_
  14.3 0.0 copy-done.5
  14.3 0.9 middle.2
  15.2 11.0 %all-to-all-start = ((f32[32,32,128]{2,1,0:T(8,128)}), f32[32,32,128]{2,1,0:T(8,128)S(1)}, u32[]{:S(2)}, u32[]{:S(2)}) async-start(f32[32,32,128]{2,1,0:T(8,128)} %middle.2), calls=%async_computation | async-start | bytes 1048576 | tf_op jit(solution)/shard_map/all_to_all | solution.py:516
  26.2 0.0 copy-done.7
  26.2 0.0 copy-start.2
  26.2 0.0 copy-start.6
  26.3 12.9 %near.2.refs_0_ = f32[128,2304]{1,0:T(8,128)} custom-call(f32[3,2304]{1,0:T(4,128)S(1)} %copy-done.7, f32[2304,128]{1,0:T(8,128)} %refs_1_.1), custom_call_target="tpu_custom_call" | custom-call | flops 4076863488 | bytes 3538944 | tf_op jit(solution)/shard_map/near/pallas_call | solution.py:403
  39.2 2.2 %all-to-all-done.got_ref = f32[32,32,128]{2,1,0:T(8,128)S(1)} async-done(((f32[32,32,128]{2,1,0:T(8,128)}), f32[32,32,128]{2,1,0:T(8,128)S(1)}, u32[]{:S(2)}, u32[]{:S(2)}) %all-to-all-start) | async-done | bytes 524320 | tf_op jit(solution)/shard_map/all_to_all | solution.py:516
  41.4 0.0 copy-done.2
  41.4 0.5 couple.2
  41.9 3.7 %collective-permute-start.3 = (f32[16,128]{1,0:T(8,128)S(1)}, f32[16,128]{1,0:T(8,128)S(1)}, u32[]{:S(2)}, u32[]{:S(2)}) collective-permute-start(f32[16,128]{1,0:T(8,128)S(1)} %get-tuple-element.47), channel_id=1, source_target_pairs={{0,128},{128,0},{1,129},{129,1},{2,130},{130,2},{3,131},{131,3},{4... | collective-permute-start | bytes 24584 | tf_op jit(solution)/shard_map/ppermute | solution.py:526
  45.6 0.8 collective-permute-done.3
  46.4 0.0 copy-start
  46.4 0.0 copy-start.1
  46.4 0.0 copy-start.3
  46.4 0.0 copy-start.4
  46.5 0.3 collective-permute-start.6
  46.7 2.0 %collective-permute-start.5 = (f32[32,128]{1,0:T(8,128)S(1)}, f32[32,128]{1,0:T(8,128)S(1)}, u32[]{:S(2)}, u32[]{:S(2)}) collective-permute-start(f32[32,128]{1,0:T(8,128)S(1)} %constant_dynamic-update-slice_fusion.refs_5_), channel_id=1, source_target_pairs={{0,2},{1,3},{2,0},{3,1},{4,6},{5,7},{6,4},{7,5},{8,10},{9,11},{10,... | collective-permute-start | bytes 49160 | tf_op jit(solution)/shard_map/ppermute | solution.py:528
  48.7 0.0 collective-permute-start.4
  48.7 0.0 copy-done.6
  48.7 3.3 %finish.2 = (f32[2304,128]{1,0:T(8,128)S(1)}, f32[2304,128]{1,0:T(8,128)S(1)}, f32[2304,128]{1,0:T(8,128)}) custom-call(f32[128,2304]{1,0:T(8,128)} %near.2.refs_0_, f32[2304,128]{1,0:T(8,128)} %refs_1_.1, s32[1,2304]{1,0:T(1,128)S(1)} %copy-done.6, s32[2304,128]{1,0:T(8,128)} %refs_3_.1), custom_call_target="tpu_custom_call" | custom-call | flops 169869312 | bytes 7077888 | tf_op jit(solution)/shard_map/finish/pallas_call | solution.py:403
  52.0 0.0 collective-permute-done.6.refs_8_
  52.0 0.0 collective-permute-done.5.refs_7_
  52.0 0.5 collective-permute-done.4.refs_6_
  52.5 0.0 copy-done
  52.5 0.0 copy-done.1
  52.5 0.0 copy-done.3
  52.5 0.0 copy-done.4
  52.5 2.2 %update.1 = (f32[2304,128]{1,0:T(8,128)}, f32[32,128]{1,0:T(8,128)S(1)}, f32[96,128]{1,0:T(8,128)S(1)}, f32[96,128]{1,0:T(8,128)S(1)}, f32[96,128]{1,0:T(8,128)S(1)}) custom-call(f32[2304,128]{1,0:T(8,128)S(1)} %get-tuple-element.42.refs_0_, f32[96,128]{1,0:T(8,128)S(1)} %collective-permute-done.m1_ref.refs_1_, ...), custom_call_target="tpu_custom_call" | custom-call | tf_op jit(solution)/shard_map/update/pallas_call | solution.py:403
  54.7 0.3 collective-permute-start.7
  55.0 3.2 %collective-permute-start.8 = (f32[96,128]{1,0:T(8,128)S(1)}, f32[96,128]{1,0:T(8,128)S(1)}, u32[]{:S(2)}, u32[]{:S(2)}) collective-permute-start(f32[96,128]{1,0:T(8,128)S(1)} %get-tuple-element.55), channel_id=1, source_target_pairs={{0,2},{1,3},{2,0},{3,1},{4,6},{5,7},{6,4},{7,5},{8,10},{9,11},{10,... | collective-permute-start | bytes 147464 | tf_op jit(solution)/shard_map/ppermute | solution.py:514
  58.2 1.1 %collective-permute-start.9 = (f32[96,128]{1,0:T(8,128)S(1)}, f32[96,128]{1,0:T(8,128)S(1)}, u32[]{:S(2)}, u32[]{:S(2)}) collective-permute-start(f32[96,128]{1,0:T(8,128)S(1)} %get-tuple-element.56), channel_id=1, source_target_pairs={{0,3},{1,0},{2,1},{3,2},{4,7},{5,4},{6,5},{7,6},{8,11},{9,8},{10,9... | collective-permute-start | bytes 147464 | tf_op jit(solution)/shard_map/ppermute | solution.py:514
  59.3 2.3 %turn.1.w_hbm = bf16[256,2304]{1,0:T(8,128)(2,1)} custom-call(f32[2304,128]{1,0:T(8,128)} %get-tuple-element.52.w_hbm.refs_1_), custom_call_target="tpu_custom_call" | custom-call | bytes 2359296 | tf_op jit(solution)/shard_map/turn/pallas_call | solution.py:403
  61.6 0.0 collective-permute-done.7.m1_ref.refs_1_
  61.7 0.0 collective-permute-done.8.m2_ref.refs_2_
  61.7 0.0 collective-permute-done.9.m3_ref.refs_3_
  61.7 0.9 middle.3
  62.5 5.5 %all-to-all-start.1 = ((f32[32,32,128]{2,1,0:T(8,128)}), f32[32,32,128]{2,1,0:T(8,128)S(1)}, u32[]{:S(2)}, u32[]{:S(2)}) async-start(f32[32,32,128]{2,1,0:T(8,128)} %middle.3), calls=%async_computation.1 | async-start | bytes 1048576 | tf_op jit(solution)/shard_map/all_to_all | solution.py:516
  68.0 12.7 %near.3.refs_0_ = f32[128,2304]{1,0:T(8,128)} custom-call(f32[3,2304]{1,0:T(4,128)S(1)} %copy-done.7, bf16[256,2304]{1,0:T(8,128)(2,1)} %turn.1.w_hbm), custom_call_target="tpu_custom_call" | custom-call | flops 4076863488 | bytes 3538944 | tf_op jit(solution)/shard_map/near/pallas_call | solution.py:403
  80.7 1.5 %all-to-all-done.1.got_ref = f32[32,32,128]{2,1,0:T(8,128)S(1)} async-done(((f32[32,32,128]{2,1,0:T(8,128)}), f32[32,32,128]{2,1,0:T(8,128)S(1)}, u32[]{:S(2)}, u32[]{:S(2)}) %all-to-all-start.1) | async-done | bytes 524320 | tf_op jit(solution)/shard_map/all_to_all | solution.py:516
  82.2 0.5 couple.3
  82.7 4.9 %collective-permute-start.10 = (f32[16,128]{1,0:T(8,128)S(1)}, f32[16,128]{1,0:T(8,128)S(1)}, u32[]{:S(2)}, u32[]{:S(2)}) collective-permute-start(f32[16,128]{1,0:T(8,128)S(1)} %get-tuple-element.63), channel_id=1, source_target_pairs={{0,128},{128,0},{1,129},{129,1},{2,130},{130,2},{3,131},{131,3},{4... | collective-permute-start | bytes 24584 | tf_op jit(solution)/shard_map/ppermute | solution.py:526
  87.6 0.8 collective-permute-done.10
  88.4 1.8 %collective-permute-start.13 = (f32[32,128]{1,0:T(8,128)S(1)}, f32[32,128]{1,0:T(8,128)S(1)}, u32[]{:S(2)}, u32[]{:S(2)}) collective-permute-start(f32[32,128]{1,0:T(8,128)S(1)} %constant_dynamic-update-slice_fusion.2.refs_5_), channel_id=1, source_target_pairs={{0,3},{1,0},{2,1},{3,2},{4,7},{5,4},{6,5},{7,6},{8,11},{9,8},{10,9... | collective-permute-start | bytes 49160 | tf_op jit(solution)/shard_map/ppermute | solution.py:528
  90.2 0.4 collective-permute-start.12
  90.6 0.2 collective-permute-start.11
  90.7 2.1 %finish.3 = (f32[2304,128]{1,0:T(8,128)S(1)}, f32[2304,128]{1,0:T(8,128)S(1)}) custom-call(f32[128,2304]{1,0:T(8,128)} %near.3.refs_0_, f32[2304,128]{1,0:T(8,128)} %get-tuple-element.52.w_hbm.refs_1_, f32[2304,128]{1,0:T(8,128)} %get-tuple-element.59.refs_2_), custom_call_target="tpu_custom_call" | custom-call | flops 294912 | bytes 5898240 | tf_op jit(solution)/shard_map/finish/pallas_call | solution.py:403
  92.9 0.0 collective-permute-done.13.refs_8_
  92.9 1.4 %collective-permute-done.12.refs_7_ = f32[32,128]{1,0:T(8,128)S(1)} collective-permute-done((f32[32,128]{1,0:T(8,128)S(1)}, f32[32,128]{1,0:T(8,128)S(1)}, u32[]{:S(2)}, u32[]{:S(2)}) %collective-permute-start.12) | collective-permute-done | bytes 16416 | tf_op jit(solution)/shard_map/ppermute | solution.py:528
  94.3 0.2 collective-permute-done.11.refs_6_
  94.4 1.6 %last.1 = f32[2304,128]{1,0:T(8,128)} custom-call(f32[2304,128]{1,0:T(8,128)S(1)} %get-tuple-element.60.refs_0_, f32[96,128]{1,0:T(8,128)S(1)} %collective-permute-done.7.m1_ref.refs_1_, f32[96,128]{1,0:T(8,128)S(1)} %collective-permute-done.8.m2_ref.refs_2_, f32[96,128]{1,0:T(8,128)S(1)} %collective-permute-done.9.m3_ref.refs_3_, ...), custom_call_target="tpu_custom_call" | custom-call | tf_op jit(solution)/shard_map/last/pallas_call | solution.py:403
  (4 shorter events, 0.0 us)
Async XLA Ops:
  3.9 10.4 %copy-start.5 = (f32[32,128]{1,0:T(8,128)S(1)}, f32[32,128]{1,0:T(8,128)}, u32[]{:S(2)}) copy-start(f32[32,128]{1,0:T(8,128)} %get-tuple-element.37.own_ref) | copy-start | bytes 49156
  3.9 10.4 %collective-permute-start = (f32[96,128]{1,0:T(8,128)}, f32[96,128]{1,0:T(8,128)S(1)}, u32[]{:S(2)}, u32[]{:S(2)}) collective-permute-start(f32[96,128]{1,0:T(8,128)} %get-tuple-element.38), channel_id=1, source_target_pairs={{0,1},{1,2},{2,3},{3,0},{4,5},{5,6},{6,7},{7,4},{8,9},{9,10},{10,1... | collective-permute-start | bytes 147464 | tf_op jit(solution)/shard_map/ppermute | solution.py:514
  6.1 8.2 %collective-permute-start.1 = (f32[96,128]{1,0:T(8,128)}, f32[96,128]{1,0:T(8,128)S(1)}, u32[]{:S(2)}, u32[]{:S(2)}) collective-permute-start(f32[96,128]{1,0:T(8,128)} %get-tuple-element.39), channel_id=1, source_target_pairs={{0,2},{1,3},{2,0},{3,1},{4,6},{5,7},{6,4},{7,5},{8,10},{9,11},{10,... | collective-permute-start | bytes 147464 | tf_op jit(solution)/shard_map/ppermute | solution.py:514
  8.7 5.6 %collective-permute-start.2 = (f32[96,128]{1,0:T(8,128)}, f32[96,128]{1,0:T(8,128)S(1)}, u32[]{:S(2)}, u32[]{:S(2)}) collective-permute-start(f32[96,128]{1,0:T(8,128)} %get-tuple-element.40), channel_id=1, source_target_pairs={{0,3},{1,0},{2,1},{3,2},{4,7},{5,4},{6,5},{7,6},{8,11},{9,8},{10,9... | collective-permute-start | bytes 147464 | tf_op jit(solution)/shard_map/ppermute | solution.py:514
  14.2 12.0 %copy-start.7 = (f32[3,2304]{1,0:T(4,128)S(1)}, f32[3,2304]{1,0:T(4,128)}, u32[]{:S(2)}) copy-start(f32[3,2304]{1,0:T(4,128)} %coords_ref.3) | copy-start | bytes 82948
  15.2 26.2 %all-to-all-start = ((f32[32,32,128]{2,1,0:T(8,128)}), f32[32,32,128]{2,1,0:T(8,128)S(1)}, u32[]{:S(2)}, u32[]{:S(2)}) async-start(f32[32,32,128]{2,1,0:T(8,128)} %middle.2), calls=%async_computation | async-start | bytes 1048576 | tf_op jit(solution)/shard_map/all_to_all | solution.py:516
  26.2 15.1 %copy-start.2 = (bf16[128,2048]{1,0:T(8,128)(2,1)S(1)}, bf16[128,2048]{1,0:T(8,128)(2,1)}, u32[]{:S(2)}) copy-start(bf16[128,2048]{1,0:T(8,128)(2,1)} %get-tuple-element.45.couple_ref) | copy-start | bytes 1572868
  26.2 22.5 %copy-start.6 = (s32[1,2304]{1,0:T(1,128)S(1)}, s32[1,2304]{1,0:T(1,128)}, u32[]{:S(2)}) copy-start(s32[1,2304]{1,0:T(1,128)} %refs_2_.1) | copy-start | bytes 27652
  41.9 4.6 %collective-permute-start.3 = (f32[16,128]{1,0:T(8,128)S(1)}, f32[16,128]{1,0:T(8,128)S(1)}, u32[]{:S(2)}, u32[]{:S(2)}) collective-permute-start(f32[16,128]{1,0:T(8,128)S(1)} %get-tuple-element.47), channel_id=1, source_target_pairs={{0,128},{128,0},{1,129},{129,1},{2,130},{130,2},{3,131},{131,3},{4... | collective-permute-start | bytes 24584 | tf_op jit(solution)/shard_map/ppermute | solution.py:526
  46.4 6.1 %copy-start = (f32[2304,64]{0,1:T(8,128)S(1)}, f32[2304,64]{0,1:T(8,128)}, u32[]{:S(2)}) copy-start(f32[2304,64]{0,1:T(8,128)} %param.14) | copy-start | bytes 1769476
  46.4 6.1 %copy-start.1 = (bf16[2304,128]{1,0:T(8,128)(2,1)S(1)}, bf16[2304,128]{1,0:T(8,128)(2,1)}, u32[]{:S(2)}) copy-start(bf16[2304,128]{1,0:T(8,128)(2,1)} %get-tuple-element.49.refs_10_) | copy-start | bytes 1769476
  46.4 6.1 %copy-start.3 = (bf16[128,320]{1,0:T(8,128)(2,1)S(1)}, bf16[128,320]{1,0:T(8,128)(2,1)}, u32[]{:S(2)}) copy-start(bf16[128,320]{1,0:T(8,128)(2,1)} %get-tuple-element.43.refs_4_) | copy-start | bytes 245764
  46.4 6.1 %copy-start.4 = (f32[64,128]{1,0:T(8,128)S(1)}, f32[64,128]{1,0:T(8,128)}, u32[]{:S(2)}) copy-start(f32[64,128]{1,0:T(8,128)} %get-tuple-element.50.refs_12_) | copy-start | bytes 98308
  46.5 5.6 %collective-permute-start.6 = (f32[32,128]{1,0:T(8,128)S(1)}, f32[32,128]{1,0:T(8,128)S(1)}, u32[]{:S(2)}, u32[]{:S(2)}) collective-permute-start(f32[32,128]{1,0:T(8,128)S(1)} %constant_dynamic-update-slice_fusion.refs_5_), channel_id=1, source_target_pairs={{0,3},{1,0},{2,1},{3,2},{4,7},{5,4},{6,5},{7,6},{8,11},{9,8},{10,9... | collective-permute-start | bytes 49160 | tf_op jit(solution)/shard_map/ppermute | solution.py:528
  46.7 5.3 %collective-permute-start.5 = (f32[32,128]{1,0:T(8,128)S(1)}, f32[32,128]{1,0:T(8,128)S(1)}, u32[]{:S(2)}, u32[]{:S(2)}) collective-permute-start(f32[32,128]{1,0:T(8,128)S(1)} %constant_dynamic-update-slice_fusion.refs_5_), channel_id=1, source_target_pairs={{0,2},{1,3},{2,0},{3,1},{4,6},{5,7},{6,4},{7,5},{8,10},{9,11},{10,... | collective-permute-start | bytes 49160 | tf_op jit(solution)/shard_map/ppermute | solution.py:528
  48.7 3.8 %collective-permute-start.4 = (f32[32,128]{1,0:T(8,128)S(1)}, f32[32,128]{1,0:T(8,128)S(1)}, u32[]{:S(2)}, u32[]{:S(2)}) collective-permute-start(f32[32,128]{1,0:T(8,128)S(1)} %constant_dynamic-update-slice_fusion.refs_5_), channel_id=1, source_target_pairs={{0,1},{1,2},{2,3},{3,0},{4,5},{5,6},{6,7},{7,4},{8,9},{9,10},{10,1... | collective-permute-start | bytes 49160 | tf_op jit(solution)/shard_map/ppermute | solution.py:528
  54.7 6.9 %collective-permute-start.7 = (f32[96,128]{1,0:T(8,128)S(1)}, f32[96,128]{1,0:T(8,128)S(1)}, u32[]{:S(2)}, u32[]{:S(2)}) collective-permute-start(f32[96,128]{1,0:T(8,128)S(1)} %get-tuple-element.54), channel_id=1, source_target_pairs={{0,1},{1,2},{2,3},{3,0},{4,5},{5,6},{6,7},{7,4},{8,9},{9,10},{10,1... | collective-permute-start | bytes 147464 | tf_op jit(solution)/shard_map/ppermute | solution.py:514
  55.0 6.7 %collective-permute-start.8 = (f32[96,128]{1,0:T(8,128)S(1)}, f32[96,128]{1,0:T(8,128)S(1)}, u32[]{:S(2)}, u32[]{:S(2)}) collective-permute-start(f32[96,128]{1,0:T(8,128)S(1)} %get-tuple-element.55), channel_id=1, source_target_pairs={{0,2},{1,3},{2,0},{3,1},{4,6},{5,7},{6,4},{7,5},{8,10},{9,11},{10,... | collective-permute-start | bytes 147464 | tf_op jit(solution)/shard_map/ppermute | solution.py:514
  58.2 3.4 %collective-permute-start.9 = (f32[96,128]{1,0:T(8,128)S(1)}, f32[96,128]{1,0:T(8,128)S(1)}, u32[]{:S(2)}, u32[]{:S(2)}) collective-permute-start(f32[96,128]{1,0:T(8,128)S(1)} %get-tuple-element.56), channel_id=1, source_target_pairs={{0,3},{1,0},{2,1},{3,2},{4,7},{5,4},{6,5},{7,6},{8,11},{9,8},{10,9... | collective-permute-start | bytes 147464 | tf_op jit(solution)/shard_map/ppermute | solution.py:514
  62.5 19.7 %all-to-all-start.1 = ((f32[32,32,128]{2,1,0:T(8,128)}), f32[32,32,128]{2,1,0:T(8,128)S(1)}, u32[]{:S(2)}, u32[]{:S(2)}) async-start(f32[32,32,128]{2,1,0:T(8,128)} %middle.3), calls=%async_computation.1 | async-start | bytes 1048576 | tf_op jit(solution)/shard_map/all_to_all | solution.py:516
  82.7 5.7 %collective-permute-start.10 = (f32[16,128]{1,0:T(8,128)S(1)}, f32[16,128]{1,0:T(8,128)S(1)}, u32[]{:S(2)}, u32[]{:S(2)}) collective-permute-start(f32[16,128]{1,0:T(8,128)S(1)} %get-tuple-element.63), channel_id=1, source_target_pairs={{0,128},{128,0},{1,129},{129,1},{2,130},{130,2},{3,131},{131,3},{4... | collective-permute-start | bytes 24584 | tf_op jit(solution)/shard_map/ppermute | solution.py:526
  88.4 4.5 %collective-permute-start.13 = (f32[32,128]{1,0:T(8,128)S(1)}, f32[32,128]{1,0:T(8,128)S(1)}, u32[]{:S(2)}, u32[]{:S(2)}) collective-permute-start(f32[32,128]{1,0:T(8,128)S(1)} %constant_dynamic-update-slice_fusion.2.refs_5_), channel_id=1, source_target_pairs={{0,3},{1,0},{2,1},{3,2},{4,7},{5,4},{6,5},{7,6},{8,11},{9,8},{10,9... | collective-permute-start | bytes 49160 | tf_op jit(solution)/shard_map/ppermute | solution.py:528
  90.2 4.1 %collective-permute-start.12 = (f32[32,128]{1,0:T(8,128)S(1)}, f32[32,128]{1,0:T(8,128)S(1)}, u32[]{:S(2)}, u32[]{:S(2)}) collective-permute-start(f32[32,128]{1,0:T(8,128)S(1)} %constant_dynamic-update-slice_fusion.2.refs_5_), channel_id=1, source_target_pairs={{0,2},{1,3},{2,0},{3,1},{4,6},{5,7},{6,4},{7,5},{8,10},{9,11},{10,... | collective-permute-start | bytes 49160 | tf_op jit(solution)/shard_map/ppermute | solution.py:528
  90.6 3.9 %collective-permute-start.11 = (f32[32,128]{1,0:T(8,128)S(1)}, f32[32,128]{1,0:T(8,128)S(1)}, u32[]{:S(2)}, u32[]{:S(2)}) collective-permute-start(f32[32,128]{1,0:T(8,128)S(1)} %constant_dynamic-update-slice_fusion.2.refs_5_), channel_id=1, source_target_pairs={{0,1},{1,2},{2,3},{3,0},{4,5},{5,6},{6,7},{7,4},{8,9},{9,10},{10,1... | collective-permute-start | bytes 49160 | tf_op jit(solution)/shard_map/ppermute | solution.py:528

commit v9 on v6

--- a/solution.py
+++ b/solution.py
@@ -137,9 +137,15 @@
     down_ref[...] = tall(jnp.concatenate([*siblings, leaf_ref[0], from_top], axis=1))
 
 
-def permuted_labels(order, labels_ref):
+def thirds(rows):
+    size = -(-rows // 48) * 16
+    return [slice(j, min(j + size, rows)) for j in range(0, rows, size)]
+
+
+def permute_labels(order, fetch, labels_ref, chosen_ref, bit_ref, out_ref):
     n = labels_ref.shape[0]
     group = n // BITS
+    blocks = [slice(j, j + BLOCK) for j in range(0, n, BLOCK)]
     which = jnp.zeros_like(order)
     place = jnp.ones(order.shape, F32)
     for g in range(1, BITS):
@@ -147,44 +153,53 @@
         which = jnp.where(beyond, g * group, which)
         place = jnp.where(beyond, 1.0 / (1 << g), place)
     rows = jnp.concatenate([(order - which).astype(F32), place, jnp.zeros((6, n), F32)], axis=0)
+    lane = lax.broadcasted_iota(jnp.int32, (BLOCK, group), 1).astype(F32)
+    for at in blocks:
+        columns = rows[:, at].T
+        chosen_ref[at, :] = jnp.where(columns[:, 0:1] == lane, 1.0, 0.0).astype(BF16)
+        bit_ref[at, :] = columns
+    for load in fetch:
+        load.wait()
     packed = jnp.zeros((group, OUT), F32)
     for g in range(BITS):
         packed = packed + labels_ref[g * group : (g + 1) * group, :].astype(F32) * float(1 << g)
     packed = packed.astype(BF16)
-    lane = lax.broadcasted_iota(jnp.int32, (BLOCK, group), 1).astype(F32)
-    for j in range(n // BLOCK):
-        columns = rows[:, j * BLOCK : (j + 1) * BLOCK].T
-        chosen = jnp.where(columns[:, 0:1] == lane, 1.0, 0.0).astype(BF16)
-        value = jnp.dot(chosen, packed, preferred_element_type=F32) * columns[:, 1:2]
+    for at in blocks:
+        value = jnp.dot(chosen_ref[at, :], packed, preferred_element_type=F32) * bit_ref[at, 1:2]
         value = jnp.floor(value)
-        yield value - 2.0 * jnp.floor(0.5 * value)
+        out_ref[at, :] = value - 2.0 * jnp.floor(0.5 * value)
 
 
 def finish_body(scale, *refs):
-    first = len(refs) == 13
+    first = len(refs) == 15
     if first:
         sum_hbm, w_hbm, order_ref, labels_hbm, near_ref, base_ref, targets_hbm = refs[:7]
-        sum_ref, w_ref, labels_ref, targets_ref, sems, sent = refs[7:13]
-        pairs = [(labels_hbm, labels_ref), (w_hbm, w_ref), (sum_hbm, sum_ref)]
+        sum_ref, w_ref, labels_ref, targets_ref, chosen_ref, bit_ref, sems, sent = refs[7:]
+        pairs = [(labels_hbm, labels_ref), (sum_hbm, sum_ref), (w_hbm, w_ref)]
     else:
         sum_hbm, w_hbm, targets_hbm, near_ref, base_ref, sum_ref, w_ref, targets_ref, sems = refs
         pairs = [(sum_hbm, sum_ref), (w_hbm, w_ref), (targets_hbm, targets_ref)]
-    loads = [pltpu.make_async_copy(a, b, sems.at[i]) for i, (a, b) in enumerate(pairs)]
-    for load in loads:
+    loads = [
+        [pltpu.make_async_copy(a.at[p], b.at[p], sems.at[i, j]) for j, p in enumerate(thirds(a.shape[0]))]
+        for i, (a, b) in enumerate(pairs)
+    ]
+    for load in sum(loads, []):
         load.start()
     n = near_ref.shape[0]
     blocks = [slice(j, j + BLOCK) for j in range(0, n, BLOCK)]
     if first:
-        loads[0].wait()
-        for rows, found in zip(blocks, permuted_labels(order_ref[...], labels_ref)):
-            targets_ref[rows, :] = found
+        permute_labels(order_ref[...], loads[0], labels_ref, chosen_ref, bit_ref, targets_ref)
         send = pltpu.make_async_copy(targets_ref, targets_hbm, sent)
         send.start()
-    for load in loads[1:] if first else loads:
+        loads = loads[1:]
+    for load in loads[0]:
+        load.wait()
+    for rows in blocks:
+        near_ref[rows, :] = sum_ref[:, rows].T * scale
+    for load in sum(loads[1:], []):
         load.wait()
     for rows in blocks:
         base_ref[rows, :] = w_ref[rows, :] + targets_ref[rows, :]
-        near_ref[rows, :] = sum_ref[:, rows].T * scale
     if first:
         send.wait()
 
@@ -344,8 +359,9 @@
             out_ref[rows, :] = new
             if not last:
                 whl_ref[rows, :] = wide(new)
-        sends.append(pltpu.make_async_copy(out_ref.at[part], out_hbm.at[part], out_sem.at[j]))
-        sends[j].start()
+        for i, rows in enumerate(blocks[j * GROUP : (j + 1) * GROUP], j * GROUP):
+            sends.append(pltpu.make_async_copy(out_ref.at[rows], out_hbm.at[rows], out_sem.at[i]))
+            sends[i].start()
     if not last:
         s0 = dot3(tall(basis_t_ref[...]), whl_ref[...])
         emit_messages(s0, up_ref[...], own_ref, message_refs)
@@ -489,7 +505,7 @@
                 (near_t, current, targets),
                 8,
                 "finish",
-                [*kept, pltpu.VMEM((n, OUT), F32), pltpu.SemaphoreType.DMA((3,))],
+                [*kept, pltpu.VMEM((n, OUT), F32), pltpu.SemaphoreType.DMA((3, 3))],
                 (n * OUT, n * OUT * 20, 0),
                 (0, 1, 2),
             )
@@ -498,13 +514,15 @@
                 functools.partial(finish_body, scale),
                 [shape(n, OUT)] * 3,
                 (near_t, current, order, labels),
-                12,
+                16,
                 "finish",
                 [
                     *kept,
                     pltpu.VMEM((n, OUT), jnp.int32),
                     pltpu.VMEM((n, OUT), F32),
-                    pltpu.SemaphoreType.DMA((3,)),
+                    pltpu.VMEM((n, n // BITS), BF16),
+                    pltpu.VMEM((n, 8), F32),
+                    pltpu.SemaphoreType.DMA((3, 3)),
                     pltpu.SemaphoreType.DMA,
                 ],
                 (n * n // BITS * 2 * OUT, n * OUT * 24, 0),
@@ -512,7 +530,7 @@
                 (2,),
             )
         far = (near, *messages, down, *tops, base, bcat)
-        rows_buffer = [pltpu.VMEM((n, OUT), F32), pltpu.SemaphoreType.DMA((groups,))]
+        rows_buffer = [pltpu.VMEM((n, OUT), F32), pltpu.SemaphoreType.DMA((n // BLOCK,))]
         body = functools.partial(update_body, last)
         if last:
             (current,) = call(

time: 94.7 us -> 94.4 us (level)
  transfers between devices with their start and end apart: 16 -> 16, of which waited for: 6 -> 7; matrix products, arithmetic and copies ran while one was open for 0% -> 0% of each run, Pallas kernels for 40% -> 39%
where the time goes in v9:
time: 94.4 us; the launch traced here: 93.9 us
  Pallas kernels  46 us (49%)
  starting transfers between devices  40 us (42%)
  waiting for transfers between devices  7.58 us (8%)
    pallas_call x13, Pallas kernels, call(): pl.pallas_call(body, out_shape=out, in_specs=[HBM if i in far_in else VME...  46 us
    all_to_all x2, starting transfers between devices, on_device(): got = lax.all_to_all(spread, 'mid', 0, 0)  16.7 us
    ppermute x6, starting transfers between devices, on_device(): lax.ppermute(m, 'leaf', ring(k))  10.4 us
    ppermute x2, starting transfers between devices, on_device(): s2 = lax.ppermute(s2, 'top', [(0, 1), (1, 0)])  8.41 us
    ppermute x6, starting transfers between devices, on_device(): tops = [top] + [lax.ppermute(top, 'leaf', ring(k)) for k in (1, 2, 3)]  4.55 us
    all_to_all x2, waiting for transfers between devices, on_device(): got = lax.all_to_all(spread, 'mid', 0, 0)  3.92 us
    ppermute x6, waiting for transfers between devices, on_device(): tops = [top] + [lax.ppermute(top, 'leaf', ring(k)) for k in (1, 2, 3)]  1.99 us
  transfers between devices with their start and end apart: 16, of which 7 were waited for; matrix products, arithmetic and copies ran while one was open for 0% of the time, Pallas kernels for 39%

profile of v9, /device:TPU:1, one launch (start us, length us, event | category | flops | bytes accessed | tf_op | source)
XLA Modules:
  0.0 93.9 jit_solution(15262909425427190041)
XLA Ops:
  0.0 2.8 %first.1 = (f32[64,128]{1,0:T(8,128)}, f32[32,128]{1,0:T(8,128)}, f32[96,128]{1,0:T(8,128)}, f32[96,128]{1,0:T(8,128)}, f32[96,128]{1,0:T(8,128)}) custom-call(f32[64,2304]{1,0:T(8,128)} %bitcast.1, f32[2304,128]{1,0:T(8,128)} %refs_1_.1, f32[1,64,64]{2,1,0:T(8,128)} %leaf_ref.3, f32[1,64,64]{2,1,0:T(8,128)} %mid_ref.3), custom_call_target="tpu_custom_call" | custom-call | tf_op jit(solution)/shard_map/first/pallas_call | solution.py:390
  2.8 0.0 copy-start.5
  2.8 2.1 %collective-permute-start = (f32[96,128]{1,0:T(8,128)}, f32[96,128]{1,0:T(8,128)S(1)}, u32[]{:S(2)}, u32[]{:S(2)}) collective-permute-start(f32[96,128]{1,0:T(8,128)} %get-tuple-element.38), channel_id=1, source_target_pairs={{0,1},{1,2},{2,3},{3,0},{4,5},{5,6},{6,7},{7,4},{8,9},{9,10},{10,1... | collective-permute-start | bytes 147464 | tf_op jit(solution)/shard_map/ppermute | solution.py:485
  5.0 2.6 %collective-permute-start.1 = (f32[96,128]{1,0:T(8,128)}, f32[96,128]{1,0:T(8,128)S(1)}, u32[]{:S(2)}, u32[]{:S(2)}) collective-permute-start(f32[96,128]{1,0:T(8,128)} %get-tuple-element.39), channel_id=1, source_target_pairs={{0,2},{1,3},{2,0},{3,1},{4,6},{5,7},{6,4},{7,5},{8,10},{9,11},{10,... | collective-permute-start | bytes 147464 | tf_op jit(solution)/shard_map/ppermute | solution.py:485
  7.6 1.1 %collective-permute-start.2 = (f32[96,128]{1,0:T(8,128)}, f32[96,128]{1,0:T(8,128)S(1)}, u32[]{:S(2)}, u32[]{:S(2)}) collective-permute-start(f32[96,128]{1,0:T(8,128)} %get-tuple-element.40), channel_id=1, source_target_pairs={{0,3},{1,0},{2,1},{3,2},{4,7},{5,4},{6,5},{7,6},{8,11},{9,8},{10,9... | collective-permute-start | bytes 147464 | tf_op jit(solution)/shard_map/ppermute | solution.py:485
  8.7 3.1 %prepare.1 = (bf16[2304,128]{1,0:T(8,128)(2,1)}, bf16[128,2048]{1,0:T(8,128)(2,1)}, bf16[128,320]{1,0:T(8,128)(2,1)}) custom-call(f32[64,2304]{1,0:T(8,128)} %bitcast.2, f32[1,64,64]{2,1,0:T(8,128)} %leaf_ref.3, f32[1,64,64]{2,1,0:T(8,128)} %mid_ref.3, f32[1,4,64,64]{3,2,1,0:T(8,128)} %couple_leaf_ref.1, f32[1,32,64,64]{3,2,1,0:T(8,128)} %couple_mid_ref.1, ...), custom_call_target="tpu_custom_call" | custom-call | tf_op jit(solution)/shard_map/prepare/pallas_call | solution.py:390
  11.8 0.0 copy-start.7
  11.8 0.0 collective-permute-done.m1_ref.refs_1_
  11.8 0.0 collective-permute-done.1.m2_ref.refs_2_
  11.8 0.0 collective-permute-done.2.m3_ref.refs_3_
  11.8 0.0 copy-done.5
  11.8 0.9 middle.2
  12.7 11.0 %all-to-all-start = ((f32[32,32,128]{2,1,0:T(8,128)}), f32[32,32,128]{2,1,0:T(8,128)S(1)}, u32[]{:S(2)}, u32[]{:S(2)}) async-start(f32[32,32,128]{2,1,0:T(8,128)} %middle.2), calls=%async_computation | async-start | bytes 1048576 | tf_op jit(solution)/shard_map/all_to_all | solution.py:487
  23.8 0.0 copy-done.7
  23.8 0.0 copy-start.2
  23.8 0.0 copy-start.6
  23.8 12.9 %near.2.refs_0_ = f32[128,2304]{1,0:T(8,128)} custom-call(f32[3,2304]{1,0:T(4,128)S(1)} %copy-done.7, f32[2304,128]{1,0:T(8,128)} %refs_1_.1), custom_call_target="tpu_custom_call" | custom-call | flops 4076863488 | bytes 3538944 | tf_op jit(solution)/shard_map/near/pallas_call | solution.py:390
  36.7 2.2 %all-to-all-done.got_ref = f32[32,32,128]{2,1,0:T(8,128)S(1)} async-done(((f32[32,32,128]{2,1,0:T(8,128)}), f32[32,32,128]{2,1,0:T(8,128)S(1)}, u32[]{:S(2)}, u32[]{:S(2)}) %all-to-all-start) | async-done | bytes 524320 | tf_op jit(solution)/shard_map/all_to_all | solution.py:487
  38.9 0.0 copy-done.2
  38.9 0.5 couple.2
  39.4 3.8 %collective-permute-start.3 = (f32[16,128]{1,0:T(8,128)S(1)}, f32[16,128]{1,0:T(8,128)S(1)}, u32[]{:S(2)}, u32[]{:S(2)}) collective-permute-start(f32[16,128]{1,0:T(8,128)S(1)} %get-tuple-element.47), channel_id=1, source_target_pairs={{0,128},{128,0},{1,129},{129,1},{2,130},{130,2},{3,131},{131,3},{4... | collective-permute-start | bytes 24584 | tf_op jit(solution)/shard_map/ppermute | solution.py:497
  43.1 0.8 collective-permute-done.3
  44.0 0.0 copy-start
  44.0 0.0 copy-start.1
  44.0 0.0 copy-start.3
  44.0 0.0 copy-start.4
  44.0 1.4 %collective-permute-start.6 = (f32[32,128]{1,0:T(8,128)S(1)}, f32[32,128]{1,0:T(8,128)S(1)}, u32[]{:S(2)}, u32[]{:S(2)}) collective-permute-start(f32[32,128]{1,0:T(8,128)S(1)} %constant_dynamic-update-slice_fusion.refs_5_), channel_id=1, source_target_pairs={{0,3},{1,0},{2,1},{3,2},{4,7},{5,4},{6,5},{7,6},{8,11},{9,8},{10,9... | collective-permute-start | bytes 49160 | tf_op jit(solution)/shard_map/ppermute | solution.py:499
  45.4 0.8 collective-permute-start.5
  46.2 0.0 collective-permute-start.4
  46.3 0.0 copy-done.6
  46.3 3.3 %finish.2 = (f32[2304,128]{1,0:T(8,128)S(1)}, f32[2304,128]{1,0:T(8,128)S(1)}, f32[2304,128]{1,0:T(8,128)}) custom-call(f32[128,2304]{1,0:T(8,128)} %near.2.refs_0_, f32[2304,128]{1,0:T(8,128)} %refs_1_.1, s32[1,2304]{1,0:T(1,128)S(1)} %copy-done.6, s32[2304,128]{1,0:T(8,128)} %refs_3_.1), custom_call_target="tpu_custom_call" | custom-call | flops 169869312 | bytes 7077888 | tf_op jit(solution)/shard_map/finish/pallas_call | solution.py:390
  49.6 0.0 collective-permute-done.6.refs_8_
  49.6 0.0 collective-permute-done.5.refs_7_
  49.6 0.5 collective-permute-done.4.refs_6_
  50.0 0.0 copy-done
  50.1 0.0 copy-done.1
  50.1 0.0 copy-done.3
  50.1 0.0 copy-done.4
  50.1 2.2 %update.1 = (f32[2304,128]{1,0:T(8,128)}, f32[32,128]{1,0:T(8,128)S(1)}, f32[96,128]{1,0:T(8,128)S(1)}, f32[96,128]{1,0:T(8,128)S(1)}, f32[96,128]{1,0:T(8,128)S(1)}) custom-call(f32[2304,128]{1,0:T(8,128)S(1)} %get-tuple-element.42.refs_0_, f32[96,128]{1,0:T(8,128)S(1)} %collective-permute-done.m1_ref.refs_1_, ...), custom_call_target="tpu_custom_call" | custom-call | tf_op jit(solution)/shard_map/update/pallas_call | solution.py:390
  52.3 1.5 %collective-permute-start.7 = (f32[96,128]{1,0:T(8,128)S(1)}, f32[96,128]{1,0:T(8,128)S(1)}, u32[]{:S(2)}, u32[]{:S(2)}) collective-permute-start(f32[96,128]{1,0:T(8,128)S(1)} %get-tuple-element.54), channel_id=1, source_target_pairs={{0,1},{1,2},{2,3},{3,0},{4,5},{5,6},{6,7},{7,4},{8,9},{9,10},{10,1... | collective-permute-start | bytes 147464 | tf_op jit(solution)/shard_map/ppermute | solution.py:485
  53.8 2.0 %collective-permute-start.8 = (f32[96,128]{1,0:T(8,128)S(1)}, f32[96,128]{1,0:T(8,128)S(1)}, u32[]{:S(2)}, u32[]{:S(2)}) collective-permute-start(f32[96,128]{1,0:T(8,128)S(1)} %get-tuple-element.55), channel_id=1, source_target_pairs={{0,2},{1,3},{2,0},{3,1},{4,6},{5,7},{6,4},{7,5},{8,10},{9,11},{10,... | collective-permute-start | bytes 147464 | tf_op jit(solution)/shard_map/ppermute | solution.py:485
  55.8 1.1 %collective-permute-start.9 = (f32[96,128]{1,0:T(8,128)S(1)}, f32[96,128]{1,0:T(8,128)S(1)}, u32[]{:S(2)}, u32[]{:S(2)}) collective-permute-start(f32[96,128]{1,0:T(8,128)S(1)} %get-tuple-element.56), channel_id=1, source_target_pairs={{0,3},{1,0},{2,1},{3,2},{4,7},{5,4},{6,5},{7,6},{8,11},{9,8},{10,9... | collective-permute-start | bytes 147464 | tf_op jit(solution)/shard_map/ppermute | solution.py:485
  56.9 2.3 %turn.1.w_hbm = bf16[256,2304]{1,0:T(8,128)(2,1)} custom-call(f32[2304,128]{1,0:T(8,128)} %get-tuple-element.52.w_hbm.refs_1_), custom_call_target="tpu_custom_call" | custom-call | bytes 2359296 | tf_op jit(solution)/shard_map/turn/pallas_call | solution.py:390
  59.2 0.0 collective-permute-done.7.m1_ref.refs_1_
  59.2 0.0 collective-permute-done.8.m2_ref.refs_2_
  59.3 0.0 collective-permute-done.9.m3_ref.refs_3_
  59.3 0.9 middle.3
  60.1 5.6 %all-to-all-start.1 = ((f32[32,32,128]{2,1,0:T(8,128)}), f32[32,32,128]{2,1,0:T(8,128)S(1)}, u32[]{:S(2)}, u32[]{:S(2)}) async-start(f32[32,32,128]{2,1,0:T(8,128)} %middle.3), calls=%async_computation.1 | async-start | bytes 1048576 | tf_op jit(solution)/shard_map/all_to_all | solution.py:487
  65.7 12.7 %near.3.refs_0_ = f32[128,2304]{1,0:T(8,128)} custom-call(f32[3,2304]{1,0:T(4,128)S(1)} %copy-done.7, bf16[256,2304]{1,0:T(8,128)(2,1)} %turn.1.w_hbm), custom_call_target="tpu_custom_call" | custom-call | flops 4076863488 | bytes 3538944 | tf_op jit(solution)/shard_map/near/pallas_call | solution.py:390
  78.4 1.7 %all-to-all-done.1.got_ref = f32[32,32,128]{2,1,0:T(8,128)S(1)} async-done(((f32[32,32,128]{2,1,0:T(8,128)}), f32[32,32,128]{2,1,0:T(8,128)S(1)}, u32[]{:S(2)}, u32[]{:S(2)}) %all-to-all-start.1) | async-done | bytes 524320 | tf_op jit(solution)/shard_map/all_to_all | solution.py:487
  80.2 0.5 couple.3
  80.7 4.6 %collective-permute-start.10 = (f32[16,128]{1,0:T(8,128)S(1)}, f32[16,128]{1,0:T(8,128)S(1)}, u32[]{:S(2)}, u32[]{:S(2)}) collective-permute-start(f32[16,128]{1,0:T(8,128)S(1)} %get-tuple-element.63), channel_id=1, source_target_pairs={{0,128},{128,0},{1,129},{129,1},{2,130},{130,2},{3,131},{131,3},{4... | collective-permute-start | bytes 24584 | tf_op jit(solution)/shard_map/ppermute | solution.py:497
  85.3 0.8 collective-permute-done.10
  86.1 1.7 %collective-permute-start.13 = (f32[32,128]{1,0:T(8,128)S(1)}, f32[32,128]{1,0:T(8,128)S(1)}, u32[]{:S(2)}, u32[]{:S(2)}) collective-permute-start(f32[32,128]{1,0:T(8,128)S(1)} %constant_dynamic-update-slice_fusion.2.refs_5_), channel_id=1, source_target_pairs={{0,3},{1,0},{2,1},{3,2},{4,7},{5,4},{6,5},{7,6},{8,11},{9,8},{10,9... | collective-permute-start | bytes 49160 | tf_op jit(solution)/shard_map/ppermute | solution.py:499
  87.8 0.3 collective-permute-start.12
  88.2 0.2 collective-permute-start.11
  88.4 2.1 %finish.3 = (f32[2304,128]{1,0:T(8,128)S(1)}, f32[2304,128]{1,0:T(8,128)S(1)}) custom-call(f32[128,2304]{1,0:T(8,128)} %near.3.refs_0_, f32[2304,128]{1,0:T(8,128)} %get-tuple-element.52.w_hbm.refs_1_, f32[2304,128]{1,0:T(8,128)} %get-tuple-element.59.refs_2_), custom_call_target="tpu_custom_call" | custom-call | flops 294912 | bytes 5898240 | tf_op jit(solution)/shard_map/finish/pallas_call | solution.py:390
  90.6 0.0 collective-permute-done.13.refs_8_
  90.6 1.4 %collective-permute-done.12.refs_7_ = f32[32,128]{1,0:T(8,128)S(1)} collective-permute-done((f32[32,128]{1,0:T(8,128)S(1)}, f32[32,128]{1,0:T(8,128)S(1)}, u32[]{:S(2)}, u32[]{:S(2)}) %collective-permute-start.12) | collective-permute-done | bytes 16416 | tf_op jit(solution)/shard_map/ppermute | solution.py:499
  91.9 0.2 collective-permute-done.11.refs_6_
  92.1 1.7 %last.1 = f32[2304,128]{1,0:T(8,128)} custom-call(f32[2304,128]{1,0:T(8,128)S(1)} %get-tuple-element.60.refs_0_, f32[96,128]{1,0:T(8,128)S(1)} %collective-permute-done.7.m1_ref.refs_1_, f32[96,128]{1,0:T(8,128)S(1)} %collective-permute-done.8.m2_ref.refs_2_, f32[96,128]{1,0:T(8,128)S(1)} %collective-permute-done.9.m3_ref.refs_3_, ...), custom_call_target="tpu_custom_call" | custom-call | tf_op jit(solution)/shard_map/last/pallas_call | solution.py:390
  (4 shorter events, 0.0 us)
Async XLA Ops:
  2.8 9.0 %copy-start.5 = (f32[32,128]{1,0:T(8,128)S(1)}, f32[32,128]{1,0:T(8,128)}, u32[]{:S(2)}) copy-start(f32[32,128]{1,0:T(8,128)} %get-tuple-element.37.own_ref) | copy-start | bytes 49156
  2.8 9.0 %collective-permute-start = (f32[96,128]{1,0:T(8,128)}, f32[96,128]{1,0:T(8,128)S(1)}, u32[]{:S(2)}, u32[]{:S(2)}) collective-permute-start(f32[96,128]{1,0:T(8,128)} %get-tuple-element.38), channel_id=1, source_target_pairs={{0,1},{1,2},{2,3},{3,0},{4,5},{5,6},{6,7},{7,4},{8,9},{9,10},{10,1... | collective-permute-start | bytes 147464 | tf_op jit(solution)/shard_map/ppermute | solution.py:485
  5.0 6.8 %collective-permute-start.1 = (f32[96,128]{1,0:T(8,128)}, f32[96,128]{1,0:T(8,128)S(1)}, u32[]{:S(2)}, u32[]{:S(2)}) collective-permute-start(f32[96,128]{1,0:T(8,128)} %get-tuple-element.39), channel_id=1, source_target_pairs={{0,2},{1,3},{2,0},{3,1},{4,6},{5,7},{6,4},{7,5},{8,10},{9,11},{10,... | collective-permute-start | bytes 147464 | tf_op jit(solution)/shard_map/ppermute | solution.py:485
  7.6 4.2 %collective-permute-start.2 = (f32[96,128]{1,0:T(8,128)}, f32[96,128]{1,0:T(8,128)S(1)}, u32[]{:S(2)}, u32[]{:S(2)}) collective-permute-start(f32[96,128]{1,0:T(8,128)} %get-tuple-element.40), channel_id=1, source_target_pairs={{0,3},{1,0},{2,1},{3,2},{4,7},{5,4},{6,5},{7,6},{8,11},{9,8},{10,9... | collective-permute-start | bytes 147464 | tf_op jit(solution)/shard_map/ppermute | solution.py:485
  11.8 12.0 %copy-start.7 = (f32[3,2304]{1,0:T(4,128)S(1)}, f32[3,2304]{1,0:T(4,128)}, u32[]{:S(2)}) copy-start(f32[3,2304]{1,0:T(4,128)} %coords_ref.3) | copy-start | bytes 82948
  12.7 26.2 %all-to-all-start = ((f32[32,32,128]{2,1,0:T(8,128)}), f32[32,32,128]{2,1,0:T(8,128)S(1)}, u32[]{:S(2)}, u32[]{:S(2)}) async-start(f32[32,32,128]{2,1,0:T(8,128)} %middle.2), calls=%async_computation | async-start | bytes 1048576 | tf_op jit(solution)/shard_map/all_to_all | solution.py:487
  23.8 15.1 %copy-start.2 = (bf16[128,2048]{1,0:T(8,128)(2,1)S(1)}, bf16[128,2048]{1,0:T(8,128)(2,1)}, u32[]{:S(2)}) copy-start(bf16[128,2048]{1,0:T(8,128)(2,1)} %get-tuple-element.45.couple_ref) | copy-start | bytes 1572868
  23.8 22.5 %copy-start.6 = (s32[1,2304]{1,0:T(1,128)S(1)}, s32[1,2304]{1,0:T(1,128)}, u32[]{:S(2)}) copy-start(s32[1,2304]{1,0:T(1,128)} %refs_2_.1) | copy-start | bytes 27652
  39.4 4.6 %collective-permute-start.3 = (f32[16,128]{1,0:T(8,128)S(1)}, f32[16,128]{1,0:T(8,128)S(1)}, u32[]{:S(2)}, u32[]{:S(2)}) collective-permute-start(f32[16,128]{1,0:T(8,128)S(1)} %get-tuple-element.47), channel_id=1, source_target_pairs={{0,128},{128,0},{1,129},{129,1},{2,130},{130,2},{3,131},{131,3},{4... | collective-permute-start | bytes 24584 | tf_op jit(solution)/shard_map/ppermute | solution.py:497
  44.0 6.1 %copy-start = (f32[2304,64]{0,1:T(8,128)S(1)}, f32[2304,64]{0,1:T(8,128)}, u32[]{:S(2)}) copy-start(f32[2304,64]{0,1:T(8,128)} %param.14) | copy-start | bytes 1769476
  44.0 6.1 %copy-start.1 = (bf16[2304,128]{1,0:T(8,128)(2,1)S(1)}, bf16[2304,128]{1,0:T(8,128)(2,1)}, u32[]{:S(2)}) copy-start(bf16[2304,128]{1,0:T(8,128)(2,1)} %get-tuple-element.49.refs_10_) | copy-start | bytes 1769476
  44.0 6.1 %copy-start.3 = (bf16[128,320]{1,0:T(8,128)(2,1)S(1)}, bf16[128,320]{1,0:T(8,128)(2,1)}, u32[]{:S(2)}) copy-start(bf16[128,320]{1,0:T(8,128)(2,1)} %get-tuple-element.43.refs_4_) | copy-start | bytes 245764
  44.0 6.1 %copy-start.4 = (f32[64,128]{1,0:T(8,128)S(1)}, f32[64,128]{1,0:T(8,128)}, u32[]{:S(2)}) copy-start(f32[64,128]{1,0:T(8,128)} %get-tuple-element.50.refs_12_) | copy-start | bytes 98308
  44.0 5.6 %collective-permute-start.6 = (f32[32,128]{1,0:T(8,128)S(1)}, f32[32,128]{1,0:T(8,128)S(1)}, u32[]{:S(2)}, u32[]{:S(2)}) collective-permute-start(f32[32,128]{1,0:T(8,128)S(1)} %constant_dynamic-update-slice_fusion.refs_5_), channel_id=1, source_target_pairs={{0,3},{1,0},{2,1},{3,2},{4,7},{5,4},{6,5},{7,6},{8,11},{9,8},{10,9... | collective-permute-start | bytes 49160 | tf_op jit(solution)/shard_map/ppermute | solution.py:499
  45.4 4.2 %collective-permute-start.5 = (f32[32,128]{1,0:T(8,128)S(1)}, f32[32,128]{1,0:T(8,128)S(1)}, u32[]{:S(2)}, u32[]{:S(2)}) collective-permute-start(f32[32,128]{1,0:T(8,128)S(1)} %constant_dynamic-update-slice_fusion.refs_5_), channel_id=1, source_target_pairs={{0,2},{1,3},{2,0},{3,1},{4,6},{5,7},{6,4},{7,5},{8,10},{9,11},{10,... | collective-permute-start | bytes 49160 | tf_op jit(solution)/shard_map/ppermute | solution.py:499
  46.2 3.8 %collective-permute-start.4 = (f32[32,128]{1,0:T(8,128)S(1)}, f32[32,128]{1,0:T(8,128)S(1)}, u32[]{:S(2)}, u32[]{:S(2)}) collective-permute-start(f32[32,128]{1,0:T(8,128)S(1)} %constant_dynamic-update-slice_fusion.refs_5_), channel_id=1, source_target_pairs={{0,1},{1,2},{2,3},{3,0},{4,5},{5,6},{6,7},{7,4},{8,9},{9,10},{10,1... | collective-permute-start | bytes 49160 | tf_op jit(solution)/shard_map/ppermute | solution.py:499
  52.3 6.9 %collective-permute-start.7 = (f32[96,128]{1,0:T(8,128)S(1)}, f32[96,128]{1,0:T(8,128)S(1)}, u32[]{:S(2)}, u32[]{:S(2)}) collective-permute-start(f32[96,128]{1,0:T(8,128)S(1)} %get-tuple-element.54), channel_id=1, source_target_pairs={{0,1},{1,2},{2,3},{3,0},{4,5},{5,6},{6,7},{7,4},{8,9},{9,10},{10,1... | collective-permute-start | bytes 147464 | tf_op jit(solution)/shard_map/ppermute | solution.py:485
  53.8 5.5 %collective-permute-start.8 = (f32[96,128]{1,0:T(8,128)S(1)}, f32[96,128]{1,0:T(8,128)S(1)}, u32[]{:S(2)}, u32[]{:S(2)}) collective-permute-start(f32[96,128]{1,0:T(8,128)S(1)} %get-tuple-element.55), channel_id=1, source_target_pairs={{0,2},{1,3},{2,0},{3,1},{4,6},{5,7},{6,4},{7,5},{8,10},{9,11},{10,... | collective-permute-start | bytes 147464 | tf_op jit(solution)/shard_map/ppermute | solution.py:485
  55.8 3.4 %collective-permute-start.9 = (f32[96,128]{1,0:T(8,128)S(1)}, f32[96,128]{1,0:T(8,128)S(1)}, u32[]{:S(2)}, u32[]{:S(2)}) collective-permute-start(f32[96,128]{1,0:T(8,128)S(1)} %get-tuple-element.56), channel_id=1, source_target_pairs={{0,3},{1,0},{2,1},{3,2},{4,7},{5,4},{6,5},{7,6},{8,11},{9,8},{10,9... | collective-permute-start | bytes 147464 | tf_op jit(solution)/shard_map/ppermute | solution.py:485
  60.1 20.1 %all-to-all-start.1 = ((f32[32,32,128]{2,1,0:T(8,128)}), f32[32,32,128]{2,1,0:T(8,128)S(1)}, u32[]{:S(2)}, u32[]{:S(2)}) async-start(f32[32,32,128]{2,1,0:T(8,128)} %middle.3), calls=%async_computation.1 | async-start | bytes 1048576 | tf_op jit(solution)/shard_map/all_to_all | solution.py:487
  80.7 5.5 %collective-permute-start.10 = (f32[16,128]{1,0:T(8,128)S(1)}, f32[16,128]{1,0:T(8,128)S(1)}, u32[]{:S(2)}, u32[]{:S(2)}) collective-permute-start(f32[16,128]{1,0:T(8,128)S(1)} %get-tuple-element.63), channel_id=1, source_target_pairs={{0,128},{128,0},{1,129},{129,1},{2,130},{130,2},{3,131},{131,3},{4... | collective-permute-start | bytes 24584 | tf_op jit(solution)/shard_map/ppermute | solution.py:497
  86.1 4.4 %collective-permute-start.13 = (f32[32,128]{1,0:T(8,128)S(1)}, f32[32,128]{1,0:T(8,128)S(1)}, u32[]{:S(2)}, u32[]{:S(2)}) collective-permute-start(f32[32,128]{1,0:T(8,128)S(1)} %constant_dynamic-update-slice_fusion.2.refs_5_), channel_id=1, source_target_pairs={{0,3},{1,0},{2,1},{3,2},{4,7},{5,4},{6,5},{7,6},{8,11},{9,8},{10,9... | collective-permute-start | bytes 49160 | tf_op jit(solution)/shard_map/ppermute | solution.py:499
  87.8 4.1 %collective-permute-start.12 = (f32[32,128]{1,0:T(8,128)S(1)}, f32[32,128]{1,0:T(8,128)S(1)}, u32[]{:S(2)}, u32[]{:S(2)}) collective-permute-start(f32[32,128]{1,0:T(8,128)S(1)} %constant_dynamic-update-slice_fusion.2.refs_5_), channel_id=1, source_target_pairs={{0,2},{1,3},{2,0},{3,1},{4,6},{5,7},{6,4},{7,5},{8,10},{9,11},{10,... | collective-permute-start | bytes 49160 | tf_op jit(solution)/shard_map/ppermute | solution.py:499
  88.2 3.9 %collective-permute-start.11 = (f32[32,128]{1,0:T(8,128)S(1)}, f32[32,128]{1,0:T(8,128)S(1)}, u32[]{:S(2)}, u32[]{:S(2)}) collective-permute-start(f32[32,128]{1,0:T(8,128)S(1)} %constant_dynamic-update-slice_fusion.2.refs_5_), channel_id=1, source_target_pairs={{0,1},{1,2},{2,3},{3,0},{4,5},{5,6},{6,7},{7,4},{8,9},{9,10},{10,1... | collective-permute-start | bytes 49160 | tf_op jit(solution)/shard_map/ppermute | solution.py:499

commit v10 on v9

--- a/solution.py
+++ b/solution.py
@@ -204,22 +204,21 @@
         send.wait()
 
 
-def turn_body(w_hbm, wt_hbm, w_ref, wt_ref, w_sem, wt_sem):
-    n = w_hbm.shape[0]
+def turn_body(w_ref, wt_hbm, w_hbm, wt_ref, wt_sem, w_sem):
+    n = w_ref.shape[0]
     parts = [slice(j, j + GROUP * BLOCK) for j in range(0, n, GROUP * BLOCK)]
-    loads = [pltpu.make_async_copy(w_hbm.at[p], w_ref.at[p], w_sem.at[j]) for j, p in enumerate(parts)]
     sends = [
         pltpu.make_async_copy(wt_ref.at[:, p], wt_hbm.at[:, p], wt_sem.at[j]) for j, p in enumerate(parts)
     ]
-    for load in loads:
-        load.start()
-    for part, load, send in zip(parts, loads, sends):
-        load.wait()
+    copies = [pltpu.make_async_copy(w_ref.at[p], w_hbm.at[p], w_sem.at[j]) for j, p in enumerate(parts)]
+    for copy in copies:
+        copy.start()
+    for part, send in zip(parts, sends):
         for j in range(part.start, part.stop, BLOCK):
             wt_ref[:, j : j + BLOCK] = tall(w_ref[j : j + BLOCK, :].T)
         send.start()
-    for send in sends:
-        send.wait()
+    for copy in copies + sends:
+        copy.wait()
 
 
 def near_body(
@@ -335,9 +334,9 @@
     if last:
         out_hbm, out_ref, out_sem = refs[11:]
     else:
-        basis_t_ref, up_ref, out_hbm, own_ref = refs[11:15]
+        basis_t_ref, up_ref, out_ref, own_ref = refs[11:15]
         message_refs = refs[15:18]
-        out_ref, out_sem, whl_ref = refs[18:]
+        (whl_ref,) = refs[18:]
     blocks = [slice(j, j + BLOCK) for j in range(0, base_ref.shape[0], BLOCK)]
     parts = [slice(j, j + GROUP * BLOCK) for j in range(0, base_ref.shape[0], GROUP * BLOCK)]
     own = lax.axis_index("leaf")
@@ -359,7 +358,7 @@
             out_ref[rows, :] = new
             if not last:
                 whl_ref[rows, :] = wide(new)
-        for i, rows in enumerate(blocks[j * GROUP : (j + 1) * GROUP], j * GROUP):
+        for i, rows in enumerate(blocks[j * GROUP : (j + 1) * GROUP] if last else [], j * GROUP):
             sends.append(pltpu.make_async_copy(out_ref.at[rows], out_hbm.at[rows], out_sem.at[i]))
             sends[i].start()
     if not last:
@@ -442,21 +441,19 @@
     for step in range(STEPS):
         last = step == STEPS - 1
         if step:
-            (w_near,) = call(
+            w_near, current = call(
                 turn_body,
-                [shape(2 * OUT, n, dtype=BF16)],
+                [shape(2 * OUT, n, dtype=BF16), shape(n, OUT)],
                 (current,),
                 8,
                 "turn",
                 [
-                    pltpu.VMEM((n, OUT), F32),
                     pltpu.VMEM((2 * OUT, n), BF16),
                     pltpu.SemaphoreType.DMA((groups,)),
                     pltpu.SemaphoreType.DMA((groups,)),
                 ],
-                (0, n * OUT * 8, 0),
-                (0,),
-                (0,),
+                (0, n * OUT * 12, 0),
+                far_out=(0, 1),
             )
             own, w_near = lax.optimization_barrier((own, w_near))
         else:
@@ -543,8 +540,7 @@
                 (*far, basis_t, up),
                 12,
                 "update",
-                [*rows_buffer, pltpu.VMEM((n, 2 * OUT), BF16)],
-                far_out=(0,),
+                [pltpu.VMEM((n, 2 * OUT), BF16)],
             )
     return current
 

time: 94.4 us -> 93.5 us (level)
  Pallas kernels: 46 us -> 44.3 us
    pallas_call x13, Pallas kernels: 46 us -> 44.3 us  [call(): pl.pallas_call(body, out_shape=out, in_specs=[HBM if i in far_in else VME...]
  transfers between devices with their start and end apart: 16 -> 16, of which waited for: 7 -> 7; matrix products, arithmetic and copies ran while one was open for 0% -> 0% of each run, Pallas kernels for 39% -> 38%
where the time goes in v10:
time: 93.5 us; the launch traced here: 93.1 us
  Pallas kernels  44.3 us (47%)
  starting transfers between devices  40.2 us (43%)
  waiting for transfers between devices  8.31 us (9%)
    pallas_call x13, Pallas kernels, call(): pl.pallas_call(body, out_shape=out, in_specs=[HBM if i in far_in else VME...  44.3 us
    all_to_all x2, starting transfers between devices, on_device(): got = lax.all_to_all(spread, 'mid', 0, 0)  16.9 us
    ppermute x6, starting transfers between devices, on_device(): lax.ppermute(m, 'leaf', ring(k))  10.4 us
    ppermute x2, starting transfers between devices, on_device(): s2 = lax.ppermute(s2, 'top', [(0, 1), (1, 0)])  8.35 us
    ppermute x6, starting transfers between devices, on_device(): tops = [top] + [lax.ppermute(top, 'leaf', ring(k)) for k in (1, 2, 3)]  4.52 us
    all_to_all x2, waiting for transfers between devices, on_device(): got = lax.all_to_all(spread, 'mid', 0, 0)  4.03 us
    ppermute x6, waiting for transfers between devices, on_device(): tops = [top] + [lax.ppermute(top, 'leaf', ring(k)) for k in (1, 2, 3)]  1.93 us
  transfers between devices with their start and end apart: 16, of which 7 were waited for; matrix products, arithmetic and copies ran while one was open for 0% of the time, Pallas kernels for 38%

profile of v10, /device:TPU:1, one launch (start us, length us, event | category | flops | bytes accessed | tf_op | source)
XLA Modules:
  0.0 93.1 jit_solution(13435473394491717879)
XLA Ops:
  0.0 2.8 %first.1 = (f32[64,128]{1,0:T(8,128)}, f32[32,128]{1,0:T(8,128)}, f32[96,128]{1,0:T(8,128)}, f32[96,128]{1,0:T(8,128)}, f32[96,128]{1,0:T(8,128)}) custom-call(f32[64,2304]{1,0:T(8,128)} %bitcast.1, f32[2304,128]{1,0:T(8,128)} %refs_1_.1, f32[1,64,64]{2,1,0:T(8,128)} %leaf_ref.3, f32[1,64,64]{2,1,0:T(8,128)} %mid_ref.3), custom_call_target="tpu_custom_call" | custom-call | tf_op jit(solution)/shard_map/first/pallas_call | solution.py:389
  2.8 0.0 copy-start.5
  2.8 2.1 %collective-permute-start = (f32[96,128]{1,0:T(8,128)}, f32[96,128]{1,0:T(8,128)S(1)}, u32[]{:S(2)}, u32[]{:S(2)}) collective-permute-start(f32[96,128]{1,0:T(8,128)} %get-tuple-element.40), channel_id=1, source_target_pairs={{0,1},{1,2},{2,3},{3,0},{4,5},{5,6},{6,7},{7,4},{8,9},{9,10},{10,1... | collective-permute-start | bytes 147464 | tf_op jit(solution)/shard_map/ppermute | solution.py:482
  5.0 2.6 %collective-permute-start.1 = (f32[96,128]{1,0:T(8,128)}, f32[96,128]{1,0:T(8,128)S(1)}, u32[]{:S(2)}, u32[]{:S(2)}) collective-permute-start(f32[96,128]{1,0:T(8,128)} %get-tuple-element.41), channel_id=1, source_target_pairs={{0,2},{1,3},{2,0},{3,1},{4,6},{5,7},{6,4},{7,5},{8,10},{9,11},{10,... | collective-permute-start | bytes 147464 | tf_op jit(solution)/shard_map/ppermute | solution.py:482
  7.6 1.1 %collective-permute-start.2 = (f32[96,128]{1,0:T(8,128)}, f32[96,128]{1,0:T(8,128)S(1)}, u32[]{:S(2)}, u32[]{:S(2)}) collective-permute-start(f32[96,128]{1,0:T(8,128)} %get-tuple-element.42), channel_id=1, source_target_pairs={{0,3},{1,0},{2,1},{3,2},{4,7},{5,4},{6,5},{7,6},{8,11},{9,8},{10,9... | collective-permute-start | bytes 147464 | tf_op jit(solution)/shard_map/ppermute | solution.py:482
  8.7 3.1 %prepare.1 = (bf16[2304,128]{1,0:T(8,128)(2,1)}, bf16[128,2048]{1,0:T(8,128)(2,1)}, bf16[128,320]{1,0:T(8,128)(2,1)}) custom-call(f32[64,2304]{1,0:T(8,128)} %bitcast.2, f32[1,64,64]{2,1,0:T(8,128)} %leaf_ref.3, f32[1,64,64]{2,1,0:T(8,128)} %mid_ref.3, f32[1,4,64,64]{3,2,1,0:T(8,128)} %couple_leaf_ref.1, f32[1,32,64,64]{3,2,1,0:T(8,128)} %couple_mid_ref.1, ...), custom_call_target="tpu_custom_call" | custom-call | tf_op jit(solution)/shard_map/prepare/pallas_call | solution.py:389
  11.8 0.0 copy-start.7
  11.8 0.0 collective-permute-done.m1_ref.refs_1_
  11.8 0.0 collective-permute-done.1.m2_ref.refs_2_
  11.8 0.0 collective-permute-done.2.m3_ref.refs_3_
  11.8 0.0 copy-done.5
  11.8 0.9 middle.2
  12.7 11.0 %all-to-all-start = ((f32[32,32,128]{2,1,0:T(8,128)}), f32[32,32,128]{2,1,0:T(8,128)S(1)}, u32[]{:S(2)}, u32[]{:S(2)}) async-start(f32[32,32,128]{2,1,0:T(8,128)} %middle.2), calls=%async_computation | async-start | bytes 1048576 | tf_op jit(solution)/shard_map/all_to_all | solution.py:484
  23.7 0.0 copy-done.7
  23.8 0.0 copy-start.2
  23.8 0.0 copy-start.6
  23.8 12.9 %near.2.refs_0_ = f32[128,2304]{1,0:T(8,128)} custom-call(f32[3,2304]{1,0:T(4,128)S(1)} %copy-done.7, f32[2304,128]{1,0:T(8,128)} %refs_1_.1), custom_call_target="tpu_custom_call" | custom-call | flops 4076863488 | bytes 3538944 | tf_op jit(solution)/shard_map/near/pallas_call | solution.py:389
  36.7 2.2 %all-to-all-done.got_ref = f32[32,32,128]{2,1,0:T(8,128)S(1)} async-done(((f32[32,32,128]{2,1,0:T(8,128)}), f32[32,32,128]{2,1,0:T(8,128)S(1)}, u32[]{:S(2)}, u32[]{:S(2)}) %all-to-all-start) | async-done | bytes 524320 | tf_op jit(solution)/shard_map/all_to_all | solution.py:484
  38.9 0.0 copy-done.2
  38.9 0.5 couple.2
  39.4 3.8 %collective-permute-start.3 = (f32[16,128]{1,0:T(8,128)S(1)}, f32[16,128]{1,0:T(8,128)S(1)}, u32[]{:S(2)}, u32[]{:S(2)}) collective-permute-start(f32[16,128]{1,0:T(8,128)S(1)} %get-tuple-element.49), channel_id=1, source_target_pairs={{0,128},{128,0},{1,129},{129,1},{2,130},{130,2},{3,131},{131,3},{4... | collective-permute-start | bytes 24584 | tf_op jit(solution)/shard_map/ppermute | solution.py:494
  43.1 0.8 collective-permute-done.3
  44.0 0.0 copy-start
  44.0 0.0 copy-start.1
  44.0 0.0 copy-start.3
  44.0 0.0 copy-start.4
  44.0 1.4 %collective-permute-start.6 = (f32[32,128]{1,0:T(8,128)S(1)}, f32[32,128]{1,0:T(8,128)S(1)}, u32[]{:S(2)}, u32[]{:S(2)}) collective-permute-start(f32[32,128]{1,0:T(8,128)S(1)} %constant_dynamic-update-slice_fusion.refs_5_), channel_id=1, source_target_pairs={{0,3},{1,0},{2,1},{3,2},{4,7},{5,4},{6,5},{7,6},{8,11},{9,8},{10,9... | collective-permute-start | bytes 49160 | tf_op jit(solution)/shard_map/ppermute | solution.py:496
  45.4 0.8 collective-permute-start.5
  46.2 0.0 collective-permute-start.4
  46.2 0.0 copy-done.6
  46.2 3.3 %finish.2 = (f32[2304,128]{1,0:T(8,128)S(1)}, f32[2304,128]{1,0:T(8,128)S(1)}, f32[2304,128]{1,0:T(8,128)}) custom-call(f32[128,2304]{1,0:T(8,128)} %near.2.refs_0_, f32[2304,128]{1,0:T(8,128)} %refs_1_.1, s32[1,2304]{1,0:T(1,128)S(1)} %copy-done.6, s32[2304,128]{1,0:T(8,128)} %refs_3_.1), custom_call_target="tpu_custom_call" | custom-call | flops 169869312 | bytes 7077888 | tf_op jit(solution)/shard_map/finish/pallas_call | solution.py:389
  49.6 0.0 collective-permute-done.6.refs_8_
  49.6 0.0 collective-permute-done.5.refs_7_
  49.6 0.4 collective-permute-done.4.refs_6_
  50.0 0.0 copy-done
  50.0 0.0 copy-done.1
  50.0 0.0 copy-done.3
  50.0 0.0 copy-done.4
  50.1 1.5 %update.1 = (f32[2304,128]{1,0:T(8,128)S(1)}, f32[32,128]{1,0:T(8,128)S(1)}, f32[96,128]{1,0:T(8,128)S(1)}, f32[96,128]{1,0:T(8,128)S(1)}, f32[96,128]{1,0:T(8,128)S(1)}) custom-call(f32[2304,128]{1,0:T(8,128)S(1)} %get-tuple-element.44.refs_0_, f32[96,128]{1,0:T(8,128)S(1)} %collective-permute-done.m1_ref.refs_1_, ...), custom_call_target="tpu_custom_call" | custom-call | tf_op jit(solution)/shard_map/update/pallas_call | solution.py:389
  51.5 1.5 %collective-permute-start.7 = (f32[96,128]{1,0:T(8,128)S(1)}, f32[96,128]{1,0:T(8,128)S(1)}, u32[]{:S(2)}, u32[]{:S(2)}) collective-permute-start(f32[96,128]{1,0:T(8,128)S(1)} %get-tuple-element.57), channel_id=1, source_target_pairs={{0,1},{1,2},{2,3},{3,0},{4,5},{5,6},{6,7},{7,4},{8,9},{9,10},{10,1... | collective-permute-start | bytes 147464 | tf_op jit(solution)/shard_map/ppermute | solution.py:482
  53.0 2.0 %collective-permute-start.8 = (f32[96,128]{1,0:T(8,128)S(1)}, f32[96,128]{1,0:T(8,128)S(1)}, u32[]{:S(2)}, u32[]{:S(2)}) collective-permute-start(f32[96,128]{1,0:T(8,128)S(1)} %get-tuple-element.58), channel_id=1, source_target_pairs={{0,2},{1,3},{2,0},{3,1},{4,6},{5,7},{6,4},{7,5},{8,10},{9,11},{10,... | collective-permute-start | bytes 147464 | tf_op jit(solution)/shard_map/ppermute | solution.py:482
  55.1 1.1 %collective-permute-start.9 = (f32[96,128]{1,0:T(8,128)S(1)}, f32[96,128]{1,0:T(8,128)S(1)}, u32[]{:S(2)}, u32[]{:S(2)}) collective-permute-start(f32[96,128]{1,0:T(8,128)S(1)} %get-tuple-element.59), channel_id=1, source_target_pairs={{0,3},{1,0},{2,1},{3,2},{4,7},{5,4},{6,5},{7,6},{8,11},{9,8},{10,9... | collective-permute-start | bytes 147464 | tf_op jit(solution)/shard_map/ppermute | solution.py:482
  56.1 1.4 %turn.1 = (bf16[256,2304]{1,0:T(8,128)(2,1)}, f32[2304,128]{1,0:T(8,128)}) custom-call(f32[2304,128]{1,0:T(8,128)S(1)} %get-tuple-element.54.w_ref), custom_call_target="tpu_custom_call" | custom-call | bytes 3538944 | tf_op jit(solution)/shard_map/turn/pallas_call | solution.py:389
  57.6 0.0 collective-permute-done.7.m1_ref.refs_1_
  57.6 0.0 collective-permute-done.8.m2_ref.refs_2_
  57.6 0.7 collective-permute-done.9.m3_ref.refs_3_
  58.3 0.8 middle.3
  59.1 5.9 %all-to-all-start.1 = ((f32[32,32,128]{2,1,0:T(8,128)}), f32[32,32,128]{2,1,0:T(8,128)S(1)}, u32[]{:S(2)}, u32[]{:S(2)}) async-start(f32[32,32,128]{2,1,0:T(8,128)} %middle.3), calls=%async_computation.1 | async-start | bytes 1048576 | tf_op jit(solution)/shard_map/all_to_all | solution.py:484
  65.0 12.6 %near.3.refs_0_ = f32[128,2304]{1,0:T(8,128)} custom-call(f32[3,2304]{1,0:T(4,128)S(1)} %copy-done.7, bf16[256,2304]{1,0:T(8,128)(2,1)} %get-tuple-element.60.w_hbm), custom_call_target="tpu_custom_call" | custom-call | flops 4076863488 | bytes 3538944 | tf_op jit(solution)/shard_map/near/pallas_call | solution.py:389
  77.6 1.9 %all-to-all-done.1.got_ref = f32[32,32,128]{2,1,0:T(8,128)S(1)} async-done(((f32[32,32,128]{2,1,0:T(8,128)}), f32[32,32,128]{2,1,0:T(8,128)S(1)}, u32[]{:S(2)}, u32[]{:S(2)}) %all-to-all-start.1) | async-done | bytes 524320 | tf_op jit(solution)/shard_map/all_to_all | solution.py:484
  79.5 0.5 couple.3
  80.0 4.6 %collective-permute-start.10 = (f32[16,128]{1,0:T(8,128)S(1)}, f32[16,128]{1,0:T(8,128)S(1)}, u32[]{:S(2)}, u32[]{:S(2)}) collective-permute-start(f32[16,128]{1,0:T(8,128)S(1)} %get-tuple-element.67), channel_id=1, source_target_pairs={{0,128},{128,0},{1,129},{129,1},{2,130},{130,2},{3,131},{131,3},{4... | collective-permute-start | bytes 24584 | tf_op jit(solution)/shard_map/ppermute | solution.py:494
  84.6 0.8 collective-permute-done.10
  85.4 1.7 %collective-permute-start.13 = (f32[32,128]{1,0:T(8,128)S(1)}, f32[32,128]{1,0:T(8,128)S(1)}, u32[]{:S(2)}, u32[]{:S(2)}) collective-permute-start(f32[32,128]{1,0:T(8,128)S(1)} %constant_dynamic-update-slice_fusion.2.refs_5_), channel_id=1, source_target_pairs={{0,3},{1,0},{2,1},{3,2},{4,7},{5,4},{6,5},{7,6},{8,11},{9,8},{10,9... | collective-permute-start | bytes 49160 | tf_op jit(solution)/shard_map/ppermute | solution.py:496
  87.1 0.2 collective-permute-start.12
  87.3 0.3 collective-permute-start.11
  87.7 2.1 %finish.3 = (f32[2304,128]{1,0:T(8,128)S(1)}, f32[2304,128]{1,0:T(8,128)S(1)}) custom-call(f32[128,2304]{1,0:T(8,128)} %near.3.refs_0_, f32[2304,128]{1,0:T(8,128)} %get-tuple-element.62.refs_1_, f32[2304,128]{1,0:T(8,128)} %get-tuple-element.63.refs_2_), custom_call_target="tpu_custom_call" | custom-call | flops 294912 | bytes 5898240 | tf_op jit(solution)/shard_map/finish/pallas_call | solution.py:389
  89.8 0.0 collective-permute-done.13.refs_8_
  89.8 1.5 %collective-permute-done.12.refs_7_ = f32[32,128]{1,0:T(8,128)S(1)} collective-permute-done((f32[32,128]{1,0:T(8,128)S(1)}, f32[32,128]{1,0:T(8,128)S(1)}, u32[]{:S(2)}, u32[]{:S(2)}) %collective-permute-start.12) | collective-permute-done | bytes 16416 | tf_op jit(solution)/shard_map/ppermute | solution.py:496
  91.3 0.0 collective-permute-done.11.refs_6_
  91.3 1.7 %last.1 = f32[2304,128]{1,0:T(8,128)} custom-call(f32[2304,128]{1,0:T(8,128)S(1)} %get-tuple-element.64.refs_0_, f32[96,128]{1,0:T(8,128)S(1)} %collective-permute-done.7.m1_ref.refs_1_, f32[96,128]{1,0:T(8,128)S(1)} %collective-permute-done.8.m2_ref.refs_2_, f32[96,128]{1,0:T(8,128)S(1)} %collective-permute-done.9.m3_ref.refs_3_, ...), custom_call_target="tpu_custom_call" | custom-call | tf_op jit(solution)/shard_map/last/pallas_call | solution.py:389
  (4 shorter events, 0.0 us)
Async XLA Ops:
  2.8 9.0 %copy-start.5 = (f32[32,128]{1,0:T(8,128)S(1)}, f32[32,128]{1,0:T(8,128)}, u32[]{:S(2)}) copy-start(f32[32,128]{1,0:T(8,128)} %get-tuple-element.39.own_ref) | copy-start | bytes 49156
  2.8 9.0 %collective-permute-start = (f32[96,128]{1,0:T(8,128)}, f32[96,128]{1,0:T(8,128)S(1)}, u32[]{:S(2)}, u32[]{:S(2)}) collective-permute-start(f32[96,128]{1,0:T(8,128)} %get-tuple-element.40), channel_id=1, source_target_pairs={{0,1},{1,2},{2,3},{3,0},{4,5},{5,6},{6,7},{7,4},{8,9},{9,10},{10,1... | collective-permute-start | bytes 147464 | tf_op jit(solution)/shard_map/ppermute | solution.py:482
  5.0 6.8 %collective-permute-start.1 = (f32[96,128]{1,0:T(8,128)}, f32[96,128]{1,0:T(8,128)S(1)}, u32[]{:S(2)}, u32[]{:S(2)}) collective-permute-start(f32[96,128]{1,0:T(8,128)} %get-tuple-element.41), channel_id=1, source_target_pairs={{0,2},{1,3},{2,0},{3,1},{4,6},{5,7},{6,4},{7,5},{8,10},{9,11},{10,... | collective-permute-start | bytes 147464 | tf_op jit(solution)/shard_map/ppermute | solution.py:482
  7.6 4.2 %collective-permute-start.2 = (f32[96,128]{1,0:T(8,128)}, f32[96,128]{1,0:T(8,128)S(1)}, u32[]{:S(2)}, u32[]{:S(2)}) collective-permute-start(f32[96,128]{1,0:T(8,128)} %get-tuple-element.42), channel_id=1, source_target_pairs={{0,3},{1,0},{2,1},{3,2},{4,7},{5,4},{6,5},{7,6},{8,11},{9,8},{10,9... | collective-permute-start | bytes 147464 | tf_op jit(solution)/shard_map/ppermute | solution.py:482
  11.8 12.0 %copy-start.7 = (f32[3,2304]{1,0:T(4,128)S(1)}, f32[3,2304]{1,0:T(4,128)}, u32[]{:S(2)}) copy-start(f32[3,2304]{1,0:T(4,128)} %coords_ref.3) | copy-start | bytes 82948
  12.7 26.2 %all-to-all-start = ((f32[32,32,128]{2,1,0:T(8,128)}), f32[32,32,128]{2,1,0:T(8,128)S(1)}, u32[]{:S(2)}, u32[]{:S(2)}) async-start(f32[32,32,128]{2,1,0:T(8,128)} %middle.2), calls=%async_computation | async-start | bytes 1048576 | tf_op jit(solution)/shard_map/all_to_all | solution.py:484
  23.8 15.1 %copy-start.2 = (bf16[128,2048]{1,0:T(8,128)(2,1)S(1)}, bf16[128,2048]{1,0:T(8,128)(2,1)}, u32[]{:S(2)}) copy-start(bf16[128,2048]{1,0:T(8,128)(2,1)} %get-tuple-element.47.couple_ref) | copy-start | bytes 1572868
  23.8 22.5 %copy-start.6 = (s32[1,2304]{1,0:T(1,128)S(1)}, s32[1,2304]{1,0:T(1,128)}, u32[]{:S(2)}) copy-start(s32[1,2304]{1,0:T(1,128)} %refs_2_.1) | copy-start | bytes 27652
  39.4 4.6 %collective-permute-start.3 = (f32[16,128]{1,0:T(8,128)S(1)}, f32[16,128]{1,0:T(8,128)S(1)}, u32[]{:S(2)}, u32[]{:S(2)}) collective-permute-start(f32[16,128]{1,0:T(8,128)S(1)} %get-tuple-element.49), channel_id=1, source_target_pairs={{0,128},{128,0},{1,129},{129,1},{2,130},{130,2},{3,131},{131,3},{4... | collective-permute-start | bytes 24584 | tf_op jit(solution)/shard_map/ppermute | solution.py:494
  44.0 6.1 %copy-start = (f32[2304,64]{0,1:T(8,128)S(1)}, f32[2304,64]{0,1:T(8,128)}, u32[]{:S(2)}) copy-start(f32[2304,64]{0,1:T(8,128)} %param.14) | copy-start | bytes 1769476
  44.0 6.1 %copy-start.1 = (bf16[2304,128]{1,0:T(8,128)(2,1)S(1)}, bf16[2304,128]{1,0:T(8,128)(2,1)}, u32[]{:S(2)}) copy-start(bf16[2304,128]{1,0:T(8,128)(2,1)} %get-tuple-element.51.refs_10_) | copy-start | bytes 1769476
  44.0 6.1 %copy-start.3 = (bf16[128,320]{1,0:T(8,128)(2,1)S(1)}, bf16[128,320]{1,0:T(8,128)(2,1)}, u32[]{:S(2)}) copy-start(bf16[128,320]{1,0:T(8,128)(2,1)} %get-tuple-element.45.refs_4_) | copy-start | bytes 245764
  44.0 6.1 %copy-start.4 = (f32[64,128]{1,0:T(8,128)S(1)}, f32[64,128]{1,0:T(8,128)}, u32[]{:S(2)}) copy-start(f32[64,128]{1,0:T(8,128)} %get-tuple-element.52.refs_12_) | copy-start | bytes 98308
  44.0 5.6 %collective-permute-start.6 = (f32[32,128]{1,0:T(8,128)S(1)}, f32[32,128]{1,0:T(8,128)S(1)}, u32[]{:S(2)}, u32[]{:S(2)}) collective-permute-start(f32[32,128]{1,0:T(8,128)S(1)} %constant_dynamic-update-slice_fusion.refs_5_), channel_id=1, source_target_pairs={{0,3},{1,0},{2,1},{3,2},{4,7},{5,4},{6,5},{7,6},{8,11},{9,8},{10,9... | collective-permute-start | bytes 49160 | tf_op jit(solution)/shard_map/ppermute | solution.py:496
  45.4 4.2 %collective-permute-start.5 = (f32[32,128]{1,0:T(8,128)S(1)}, f32[32,128]{1,0:T(8,128)S(1)}, u32[]{:S(2)}, u32[]{:S(2)}) collective-permute-start(f32[32,128]{1,0:T(8,128)S(1)} %constant_dynamic-update-slice_fusion.refs_5_), channel_id=1, source_target_pairs={{0,2},{1,3},{2,0},{3,1},{4,6},{5,7},{6,4},{7,5},{8,10},{9,11},{10,... | collective-permute-start | bytes 49160 | tf_op jit(solution)/shard_map/ppermute | solution.py:496
  46.2 3.8 %collective-permute-start.4 = (f32[32,128]{1,0:T(8,128)S(1)}, f32[32,128]{1,0:T(8,128)S(1)}, u32[]{:S(2)}, u32[]{:S(2)}) collective-permute-start(f32[32,128]{1,0:T(8,128)S(1)} %constant_dynamic-update-slice_fusion.refs_5_), channel_id=1, source_target_pairs={{0,1},{1,2},{2,3},{3,0},{4,5},{5,6},{6,7},{7,4},{8,9},{9,10},{10,1... | collective-permute-start | bytes 49160 | tf_op jit(solution)/shard_map/ppermute | solution.py:496
  51.5 6.0 %collective-permute-start.7 = (f32[96,128]{1,0:T(8,128)S(1)}, f32[96,128]{1,0:T(8,128)S(1)}, u32[]{:S(2)}, u32[]{:S(2)}) collective-permute-start(f32[96,128]{1,0:T(8,128)S(1)} %get-tuple-element.57), channel_id=1, source_target_pairs={{0,1},{1,2},{2,3},{3,0},{4,5},{5,6},{6,7},{7,4},{8,9},{9,10},{10,1... | collective-permute-start | bytes 147464 | tf_op jit(solution)/shard_map/ppermute | solution.py:482
  53.0 4.6 %collective-permute-start.8 = (f32[96,128]{1,0:T(8,128)S(1)}, f32[96,128]{1,0:T(8,128)S(1)}, u32[]{:S(2)}, u32[]{:S(2)}) collective-permute-start(f32[96,128]{1,0:T(8,128)S(1)} %get-tuple-element.58), channel_id=1, source_target_pairs={{0,2},{1,3},{2,0},{3,1},{4,6},{5,7},{6,4},{7,5},{8,10},{9,11},{10,... | collective-permute-start | bytes 147464 | tf_op jit(solution)/shard_map/ppermute | solution.py:482
  55.1 3.2 %collective-permute-start.9 = (f32[96,128]{1,0:T(8,128)S(1)}, f32[96,128]{1,0:T(8,128)S(1)}, u32[]{:S(2)}, u32[]{:S(2)}) collective-permute-start(f32[96,128]{1,0:T(8,128)S(1)} %get-tuple-element.59), channel_id=1, source_target_pairs={{0,3},{1,0},{2,1},{3,2},{4,7},{5,4},{6,5},{7,6},{8,11},{9,8},{10,9... | collective-permute-start | bytes 147464 | tf_op jit(solution)/shard_map/ppermute | solution.py:482
  59.1 20.4 %all-to-all-start.1 = ((f32[32,32,128]{2,1,0:T(8,128)}), f32[32,32,128]{2,1,0:T(8,128)S(1)}, u32[]{:S(2)}, u32[]{:S(2)}) async-start(f32[32,32,128]{2,1,0:T(8,128)} %middle.3), calls=%async_computation.1 | async-start | bytes 1048576 | tf_op jit(solution)/shard_map/all_to_all | solution.py:484
  80.0 5.4 %collective-permute-start.10 = (f32[16,128]{1,0:T(8,128)S(1)}, f32[16,128]{1,0:T(8,128)S(1)}, u32[]{:S(2)}, u32[]{:S(2)}) collective-permute-start(f32[16,128]{1,0:T(8,128)S(1)} %get-tuple-element.67), channel_id=1, source_target_pairs={{0,128},{128,0},{1,129},{129,1},{2,130},{130,2},{3,131},{131,3},{4... | collective-permute-start | bytes 24584 | tf_op jit(solution)/shard_map/ppermute | solution.py:494
  85.4 4.4 %collective-permute-start.13 = (f32[32,128]{1,0:T(8,128)S(1)}, f32[32,128]{1,0:T(8,128)S(1)}, u32[]{:S(2)}, u32[]{:S(2)}) collective-permute-start(f32[32,128]{1,0:T(8,128)S(1)} %constant_dynamic-update-slice_fusion.2.refs_5_), channel_id=1, source_target_pairs={{0,3},{1,0},{2,1},{3,2},{4,7},{5,4},{6,5},{7,6},{8,11},{9,8},{10,9... | collective-permute-start | bytes 49160 | tf_op jit(solution)/shard_map/ppermute | solution.py:496
  87.1 4.2 %collective-permute-start.12 = (f32[32,128]{1,0:T(8,128)S(1)}, f32[32,128]{1,0:T(8,128)S(1)}, u32[]{:S(2)}, u32[]{:S(2)}) collective-permute-start(f32[32,128]{1,0:T(8,128)S(1)} %constant_dynamic-update-slice_fusion.2.refs_5_), channel_id=1, source_target_pairs={{0,2},{1,3},{2,0},{3,1},{4,6},{5,7},{6,4},{7,5},{8,10},{9,11},{10,... | collective-permute-start | bytes 49160 | tf_op jit(solution)/shard_map/ppermute | solution.py:496
  87.3 4.0 %collective-permute-start.11 = (f32[32,128]{1,0:T(8,128)S(1)}, f32[32,128]{1,0:T(8,128)S(1)}, u32[]{:S(2)}, u32[]{:S(2)}) collective-permute-start(f32[32,128]{1,0:T(8,128)S(1)} %constant_dynamic-update-slice_fusion.2.refs_5_), channel_id=1, source_target_pairs={{0,1},{1,2},{2,3},{3,0},{4,5},{5,6},{6,7},{7,4},{8,9},{9,10},{10,1... | collective-permute-start | bytes 49160 | tf_op jit(solution)/shard_map/ppermute | solution.py:496

commit v11 on v10

--- a/solution.py
+++ b/solution.py
@@ -109,7 +109,14 @@
         ref[RANK:, :] = quarter(lax.rem(own + k, N_LEAF))
 
 
-def first_body(basis_t_ref, w_ref, leaf_ref, mid_ref, up_ref, own_ref, *message_refs):
+def first_body(basis_t_hbm, w_hbm, leaf_hbm, mid_hbm, up_ref, own_ref, *refs):
+    message_refs, (basis_t_ref, w_ref, leaf_ref, mid_ref, sems) = refs[:3], refs[3:]
+    pairs = [(w_hbm, w_ref), (basis_t_hbm, basis_t_ref), (leaf_hbm, leaf_ref), (mid_hbm, mid_ref)]
+    loads = [pltpu.make_async_copy(a, b, sems.at[i]) for i, (a, b) in enumerate(pairs)]
+    for load in loads:
+        load.start()
+    for load in loads[::-1]:
+        load.wait()
     through = jnp.dot(leaf_ref[0], mid_ref[0], precision=HP, preferred_element_type=F32)
     up_ref[...] = jnp.concatenate([leaf_ref[0], through], axis=1)
     s0 = dot3(tall(basis_t_ref[...]), wide(w_ref[...]))
@@ -421,8 +428,16 @@
         first_body,
         [shape(RANK, 2 * RANK), *message_shapes],
         (basis_t, weights, transfer_leaf, transfer_mid),
-        58,
+        8,
         "first",
+        [
+            pltpu.VMEM((RANK, n), F32),
+            pltpu.VMEM((n, OUT), F32),
+            pltpu.VMEM((1, RANK, RANK), F32),
+            pltpu.VMEM((1, RANK, RANK), F32),
+            pltpu.SemaphoreType.DMA((4,)),
+        ],
+        far_in=(0, 1, 2, 3),
     )
     bcat, couple, down = call(
         prepare_body,

time: 93.5 us -> 92.9 us (level)
  transfers between devices with their start and end apart: 16 -> 16, of which waited for: 7 -> 8; matrix products, arithmetic and copies ran while one was open for 0% -> 0% of each run, Pallas kernels for 38% -> 38%
where the time goes in v11:
time: 92.9 us; the launch traced here: 92.5 us
  Pallas kernels  43.7 us (47%)
  starting transfers between devices  40.4 us (43%)
  waiting for transfers between devices  8.08 us (9%)
    pallas_call x13, Pallas kernels, call(): pl.pallas_call(body, out_shape=out, in_specs=[HBM if i in far_in else VME...  43.7 us
    all_to_all x2, starting transfers between devices, on_device(): got = lax.all_to_all(spread, 'mid', 0, 0)  16.5 us
    ppermute x6, starting transfers between devices, on_device(): lax.ppermute(m, 'leaf', ring(k))  10.2 us
    ppermute x2, starting transfers between devices, on_device(): s2 = lax.ppermute(s2, 'top', [(0, 1), (1, 0)])  8.93 us
    ppermute x6, starting transfers between devices, on_device(): tops = [top] + [lax.ppermute(top, 'leaf', ring(k)) for k in (1, 2, 3)]  4.82 us
    all_to_all x2, waiting for transfers between devices, on_device(): got = lax.all_to_all(spread, 'mid', 0, 0)  3.44 us
    ppermute x6, waiting for transfers between devices, on_device(): tops = [top] + [lax.ppermute(top, 'leaf', ring(k)) for k in (1, 2, 3)]  2.28 us
  transfers between devices with their start and end apart: 16, of which 8 were waited for; matrix products, arithmetic and copies ran while one was open for 0% of the time, Pallas kernels for 38%

profile of v11, /device:TPU:1, one launch (start us, length us, event | category | flops | bytes accessed | tf_op | source)
XLA Modules:
  0.0 92.5 jit_solution(6787038052819687852)
XLA Ops:
  0.0 2.2 %first.1 = (f32[64,128]{1,0:T(8,128)S(1)}, f32[32,128]{1,0:T(8,128)S(1)}, f32[96,128]{1,0:T(8,128)S(1)}, f32[96,128]{1,0:T(8,128)S(1)}, f32[96,128]{1,0:T(8,128)S(1)}) custom-call(f32[64,2304]{1,0:T(8,128)} %bitcast.1, f32[2304,128]{1,0:T(8,128)} %refs_1_.1, f32[1,64,64]{2,1,0:T(8,128)} %leaf_ref.1, f32[1,64,64]{2,1,0:T(8,128)} %mid_ref.1), custom_call_target="tpu_custom_call" | custom-call | tf_op jit(solution)/shard_map/first/pallas_call | solution.py:396
  2.2 2.2 %collective-permute-start = (f32[96,128]{1,0:T(8,128)S(1)}, f32[96,128]{1,0:T(8,128)S(1)}, u32[]{:S(2)}, u32[]{:S(2)}) collective-permute-start(f32[96,128]{1,0:T(8,128)S(1)} %get-tuple-element.40), channel_id=1, source_target_pairs={{0,1},{1,2},{2,3},{3,0},{4,5},{5,6},{6,7},{7,4},{8,9},{9,10},{10,1... | collective-permute-start | bytes 147464 | tf_op jit(solution)/shard_map/ppermute | solution.py:497
  4.4 2.6 %collective-permute-start.1 = (f32[96,128]{1,0:T(8,128)S(1)}, f32[96,128]{1,0:T(8,128)S(1)}, u32[]{:S(2)}, u32[]{:S(2)}) collective-permute-start(f32[96,128]{1,0:T(8,128)S(1)} %get-tuple-element.41), channel_id=1, source_target_pairs={{0,2},{1,3},{2,0},{3,1},{4,6},{5,7},{6,4},{7,5},{8,10},{9,11},{10,... | collective-permute-start | bytes 147464 | tf_op jit(solution)/shard_map/ppermute | solution.py:497
  7.0 1.1 %collective-permute-start.2 = (f32[96,128]{1,0:T(8,128)S(1)}, f32[96,128]{1,0:T(8,128)S(1)}, u32[]{:S(2)}, u32[]{:S(2)}) collective-permute-start(f32[96,128]{1,0:T(8,128)S(1)} %get-tuple-element.42), channel_id=1, source_target_pairs={{0,3},{1,0},{2,1},{3,2},{4,7},{5,4},{6,5},{7,6},{8,11},{9,8},{10,9... | collective-permute-start | bytes 147464 | tf_op jit(solution)/shard_map/ppermute | solution.py:497
  8.1 3.2 %prepare.1 = (bf16[2304,128]{1,0:T(8,128)(2,1)}, bf16[128,2048]{1,0:T(8,128)(2,1)}, bf16[128,320]{1,0:T(8,128)(2,1)}) custom-call(f32[64,2304]{1,0:T(8,128)} %bitcast.2, f32[1,64,64]{2,1,0:T(8,128)} %leaf_ref.1, f32[1,64,64]{2,1,0:T(8,128)} %mid_ref.1, f32[1,4,64,64]{3,2,1,0:T(8,128)} %couple_leaf_ref.1, f32[1,32,64,64]{3,2,1,0:T(8,128)} %couple_mid_ref.1, ...), custom_call_target="tpu_custom_call" | custom-call | tf_op jit(solution)/shard_map/prepare/pallas_call | solution.py:396
  11.3 0.0 copy-start.5
  11.3 0.0 collective-permute-done.m1_ref.refs_1_
  11.3 0.0 collective-permute-done.1.m2_ref.refs_2_
  11.3 0.0 collective-permute-done.2.m3_ref.refs_3_
  11.3 0.9 middle.2
  12.2 11.0 %all-to-all-start = ((f32[32,32,128]{2,1,0:T(8,128)}), f32[32,32,128]{2,1,0:T(8,128)S(1)}, u32[]{:S(2)}, u32[]{:S(2)}) async-start(f32[32,32,128]{2,1,0:T(8,128)} %middle.2), calls=%async_computation | async-start | bytes 1048576 | tf_op jit(solution)/shard_map/all_to_all | solution.py:499
  23.2 0.0 copy-done.5
  23.2 0.0 copy-start.2
  23.2 0.0 copy-start.4
  23.3 12.9 %near.2.refs_0_ = f32[128,2304]{1,0:T(8,128)} custom-call(f32[3,2304]{1,0:T(4,128)S(1)} %copy-done.5, f32[2304,128]{1,0:T(8,128)} %refs_1_.1), custom_call_target="tpu_custom_call" | custom-call | flops 4076863488 | bytes 3538944 | tf_op jit(solution)/shard_map/near/pallas_call | solution.py:396
  36.2 2.2 %all-to-all-done.got_ref = f32[32,32,128]{2,1,0:T(8,128)S(1)} async-done(((f32[32,32,128]{2,1,0:T(8,128)}), f32[32,32,128]{2,1,0:T(8,128)S(1)}, u32[]{:S(2)}, u32[]{:S(2)}) %all-to-all-start) | async-done | bytes 524320 | tf_op jit(solution)/shard_map/all_to_all | solution.py:499
  38.4 0.0 copy-done.2
  38.4 0.5 couple.2
  38.9 3.7 %collective-permute-start.3 = (f32[16,128]{1,0:T(8,128)S(1)}, f32[16,128]{1,0:T(8,128)S(1)}, u32[]{:S(2)}, u32[]{:S(2)}) collective-permute-start(f32[16,128]{1,0:T(8,128)S(1)} %get-tuple-element.49), channel_id=1, source_target_pairs={{0,128},{128,0},{1,129},{129,1},{2,130},{130,2},{3,131},{131,3},{4... | collective-permute-start | bytes 24584 | tf_op jit(solution)/shard_map/ppermute | solution.py:509
  42.6 0.8 collective-permute-done.3
  43.4 0.0 copy-start
  43.4 0.0 copy-start.1
  43.4 0.0 copy-start.3
  43.4 1.2 %collective-permute-start.6 = (f32[32,128]{1,0:T(8,128)S(1)}, f32[32,128]{1,0:T(8,128)S(1)}, u32[]{:S(2)}, u32[]{:S(2)}) collective-permute-start(f32[32,128]{1,0:T(8,128)S(1)} %constant_dynamic-update-slice_fusion.refs_5_), channel_id=1, source_target_pairs={{0,3},{1,0},{2,1},{3,2},{4,7},{5,4},{6,5},{7,6},{8,11},{9,8},{10,9... | collective-permute-start | bytes 49160 | tf_op jit(solution)/shard_map/ppermute | solution.py:511
  44.7 1.0 %collective-permute-start.5 = (f32[32,128]{1,0:T(8,128)S(1)}, f32[32,128]{1,0:T(8,128)S(1)}, u32[]{:S(2)}, u32[]{:S(2)}) collective-permute-start(f32[32,128]{1,0:T(8,128)S(1)} %constant_dynamic-update-slice_fusion.refs_5_), channel_id=1, source_target_pairs={{0,2},{1,3},{2,0},{3,1},{4,6},{5,7},{6,4},{7,5},{8,10},{9,11},{10,... | collective-permute-start | bytes 49160 | tf_op jit(solution)/shard_map/ppermute | solution.py:511
  45.7 0.0 collective-permute-start.4
  45.7 0.0 copy-done.4
  45.7 3.3 %finish.2 = (f32[2304,128]{1,0:T(8,128)S(1)}, f32[2304,128]{1,0:T(8,128)S(1)}, f32[2304,128]{1,0:T(8,128)}) custom-call(f32[128,2304]{1,0:T(8,128)} %near.2.refs_0_, f32[2304,128]{1,0:T(8,128)} %refs_1_.1, s32[1,2304]{1,0:T(1,128)S(1)} %copy-done.4, s32[2304,128]{1,0:T(8,128)} %refs_3_.1), custom_call_target="tpu_custom_call" | custom-call | flops 169869312 | bytes 7077888 | tf_op jit(solution)/shard_map/finish/pallas_call | solution.py:396
  49.0 0.0 collective-permute-done.6.refs_8_
  49.0 0.0 collective-permute-done.5.refs_7_
  49.1 0.7 collective-permute-done.4.refs_6_
  49.8 0.0 copy-done
  49.8 0.0 copy-done.1
  49.8 0.0 copy-done.3
  49.8 1.5 %update.1 = (f32[2304,128]{1,0:T(8,128)S(1)}, f32[32,128]{1,0:T(8,128)S(1)}, f32[96,128]{1,0:T(8,128)S(1)}, f32[96,128]{1,0:T(8,128)S(1)}, f32[96,128]{1,0:T(8,128)S(1)}) custom-call(f32[2304,128]{1,0:T(8,128)S(1)} %get-tuple-element.44.refs_0_, f32[96,128]{1,0:T(8,128)S(1)} %collective-permute-done.m1_ref.refs_1_, ...), custom_call_target="tpu_custom_call" | custom-call | tf_op jit(solution)/shard_map/update/pallas_call | solution.py:396
  51.3 1.0 %collective-permute-start.7 = (f32[96,128]{1,0:T(8,128)S(1)}, f32[96,128]{1,0:T(8,128)S(1)}, u32[]{:S(2)}, u32[]{:S(2)}) collective-permute-start(f32[96,128]{1,0:T(8,128)S(1)} %get-tuple-element.57), channel_id=1, source_target_pairs={{0,1},{1,2},{2,3},{3,0},{4,5},{5,6},{6,7},{7,4},{8,9},{9,10},{10,1... | collective-permute-start | bytes 147464 | tf_op jit(solution)/shard_map/ppermute | solution.py:497
  52.3 2.2 %collective-permute-start.8 = (f32[96,128]{1,0:T(8,128)S(1)}, f32[96,128]{1,0:T(8,128)S(1)}, u32[]{:S(2)}, u32[]{:S(2)}) collective-permute-start(f32[96,128]{1,0:T(8,128)S(1)} %get-tuple-element.58), channel_id=1, source_target_pairs={{0,2},{1,3},{2,0},{3,1},{4,6},{5,7},{6,4},{7,5},{8,10},{9,11},{10,... | collective-permute-start | bytes 147464 | tf_op jit(solution)/shard_map/ppermute | solution.py:497
  54.5 1.1 %collective-permute-start.9 = (f32[96,128]{1,0:T(8,128)S(1)}, f32[96,128]{1,0:T(8,128)S(1)}, u32[]{:S(2)}, u32[]{:S(2)}) collective-permute-start(f32[96,128]{1,0:T(8,128)S(1)} %get-tuple-element.59), channel_id=1, source_target_pairs={{0,3},{1,0},{2,1},{3,2},{4,7},{5,4},{6,5},{7,6},{8,11},{9,8},{10,9... | collective-permute-start | bytes 147464 | tf_op jit(solution)/shard_map/ppermute | solution.py:497
  55.6 1.4 %turn.1 = (bf16[256,2304]{1,0:T(8,128)(2,1)}, f32[2304,128]{1,0:T(8,128)}) custom-call(f32[2304,128]{1,0:T(8,128)S(1)} %get-tuple-element.54.w_ref), custom_call_target="tpu_custom_call" | custom-call | bytes 3538944 | tf_op jit(solution)/shard_map/turn/pallas_call | solution.py:396
  57.0 0.0 collective-permute-done.7.m1_ref.refs_1_
  57.0 0.0 collective-permute-done.8.m2_ref.refs_2_
  57.1 0.7 collective-permute-done.9.m3_ref.refs_3_
  57.7 0.9 middle.3
  58.6 5.5 %all-to-all-start.1 = ((f32[32,32,128]{2,1,0:T(8,128)}), f32[32,32,128]{2,1,0:T(8,128)S(1)}, u32[]{:S(2)}, u32[]{:S(2)}) async-start(f32[32,32,128]{2,1,0:T(8,128)} %middle.3), calls=%async_computation.1 | async-start | bytes 1048576 | tf_op jit(solution)/shard_map/all_to_all | solution.py:499
  64.1 12.6 %near.3.refs_0_ = f32[128,2304]{1,0:T(8,128)} custom-call(f32[3,2304]{1,0:T(4,128)S(1)} %copy-done.5, bf16[256,2304]{1,0:T(8,128)(2,1)} %get-tuple-element.60.w_hbm), custom_call_target="tpu_custom_call" | custom-call | flops 4076863488 | bytes 3538944 | tf_op jit(solution)/shard_map/near/pallas_call | solution.py:396
  76.7 1.3 %all-to-all-done.1.got_ref = f32[32,32,128]{2,1,0:T(8,128)S(1)} async-done(((f32[32,32,128]{2,1,0:T(8,128)}), f32[32,32,128]{2,1,0:T(8,128)S(1)}, u32[]{:S(2)}, u32[]{:S(2)}) %all-to-all-start.1) | async-done | bytes 524320 | tf_op jit(solution)/shard_map/all_to_all | solution.py:499
  78.0 0.5 couple.3
  78.5 5.2 %collective-permute-start.10 = (f32[16,128]{1,0:T(8,128)S(1)}, f32[16,128]{1,0:T(8,128)S(1)}, u32[]{:S(2)}, u32[]{:S(2)}) collective-permute-start(f32[16,128]{1,0:T(8,128)S(1)} %get-tuple-element.67), channel_id=1, source_target_pairs={{0,128},{128,0},{1,129},{129,1},{2,130},{130,2},{3,131},{131,3},{4... | collective-permute-start | bytes 24584 | tf_op jit(solution)/shard_map/ppermute | solution.py:509
  83.6 0.8 collective-permute-done.10
  84.5 2.0 %collective-permute-start.13 = (f32[32,128]{1,0:T(8,128)S(1)}, f32[32,128]{1,0:T(8,128)S(1)}, u32[]{:S(2)}, u32[]{:S(2)}) collective-permute-start(f32[32,128]{1,0:T(8,128)S(1)} %constant_dynamic-update-slice_fusion.2.refs_5_), channel_id=1, source_target_pairs={{0,3},{1,0},{2,1},{3,2},{4,7},{5,4},{6,5},{7,6},{8,11},{9,8},{10,9... | collective-permute-start | bytes 49160 | tf_op jit(solution)/shard_map/ppermute | solution.py:511
  86.4 0.3 collective-permute-start.12
  86.7 0.3 collective-permute-start.11
  87.0 2.1 %finish.3 = (f32[2304,128]{1,0:T(8,128)S(1)}, f32[2304,128]{1,0:T(8,128)S(1)}) custom-call(f32[128,2304]{1,0:T(8,128)} %near.3.refs_0_, f32[2304,128]{1,0:T(8,128)} %get-tuple-element.62.refs_1_, f32[2304,128]{1,0:T(8,128)} %get-tuple-element.63.refs_2_), custom_call_target="tpu_custom_call" | custom-call | flops 294912 | bytes 5898240 | tf_op jit(solution)/shard_map/finish/pallas_call | solution.py:396
  89.2 0.0 collective-permute-done.13.refs_8_
  89.2 1.5 %collective-permute-done.12.refs_7_ = f32[32,128]{1,0:T(8,128)S(1)} collective-permute-done((f32[32,128]{1,0:T(8,128)S(1)}, f32[32,128]{1,0:T(8,128)S(1)}, u32[]{:S(2)}, u32[]{:S(2)}) %collective-permute-start.12) | collective-permute-done | bytes 16416 | tf_op jit(solution)/shard_map/ppermute | solution.py:511
  90.6 0.1 collective-permute-done.11.refs_6_
  90.7 1.7 %last.1 = f32[2304,128]{1,0:T(8,128)} custom-call(f32[2304,128]{1,0:T(8,128)S(1)} %get-tuple-element.64.refs_0_, f32[96,128]{1,0:T(8,128)S(1)} %collective-permute-done.7.m1_ref.refs_1_, f32[96,128]{1,0:T(8,128)S(1)} %collective-permute-done.8.m2_ref.refs_2_, f32[96,128]{1,0:T(8,128)S(1)} %collective-permute-done.9.m3_ref.refs_3_, ...), custom_call_target="tpu_custom_call" | custom-call | tf_op jit(solution)/shard_map/last/pallas_call | solution.py:396
  (4 shorter events, 0.0 us)
Async XLA Ops:
  2.2 9.1 %collective-permute-start = (f32[96,128]{1,0:T(8,128)S(1)}, f32[96,128]{1,0:T(8,128)S(1)}, u32[]{:S(2)}, u32[]{:S(2)}) collective-permute-start(f32[96,128]{1,0:T(8,128)S(1)} %get-tuple-element.40), channel_id=1, source_target_pairs={{0,1},{1,2},{2,3},{3,0},{4,5},{5,6},{6,7},{7,4},{8,9},{9,10},{10,1... | collective-permute-start | bytes 147464 | tf_op jit(solution)/shard_map/ppermute | solution.py:497
  4.4 6.9 %collective-permute-start.1 = (f32[96,128]{1,0:T(8,128)S(1)}, f32[96,128]{1,0:T(8,128)S(1)}, u32[]{:S(2)}, u32[]{:S(2)}) collective-permute-start(f32[96,128]{1,0:T(8,128)S(1)} %get-tuple-element.41), channel_id=1, source_target_pairs={{0,2},{1,3},{2,0},{3,1},{4,6},{5,7},{6,4},{7,5},{8,10},{9,11},{10,... | collective-permute-start | bytes 147464 | tf_op jit(solution)/shard_map/ppermute | solution.py:497
  7.0 4.2 %collective-permute-start.2 = (f32[96,128]{1,0:T(8,128)S(1)}, f32[96,128]{1,0:T(8,128)S(1)}, u32[]{:S(2)}, u32[]{:S(2)}) collective-permute-start(f32[96,128]{1,0:T(8,128)S(1)} %get-tuple-element.42), channel_id=1, source_target_pairs={{0,3},{1,0},{2,1},{3,2},{4,7},{5,4},{6,5},{7,6},{8,11},{9,8},{10,9... | collective-permute-start | bytes 147464 | tf_op jit(solution)/shard_map/ppermute | solution.py:497
  11.3 12.0 %copy-start.5 = (f32[3,2304]{1,0:T(4,128)S(1)}, f32[3,2304]{1,0:T(4,128)}, u32[]{:S(2)}) copy-start(f32[3,2304]{1,0:T(4,128)} %coords_ref.3) | copy-start | bytes 82948
  12.2 26.2 %all-to-all-start = ((f32[32,32,128]{2,1,0:T(8,128)}), f32[32,32,128]{2,1,0:T(8,128)S(1)}, u32[]{:S(2)}, u32[]{:S(2)}) async-start(f32[32,32,128]{2,1,0:T(8,128)} %middle.2), calls=%async_computation | async-start | bytes 1048576 | tf_op jit(solution)/shard_map/all_to_all | solution.py:499
  23.2 15.1 %copy-start.2 = (bf16[128,2048]{1,0:T(8,128)(2,1)S(1)}, bf16[128,2048]{1,0:T(8,128)(2,1)}, u32[]{:S(2)}) copy-start(bf16[128,2048]{1,0:T(8,128)(2,1)} %get-tuple-element.47.couple_ref) | copy-start | bytes 1572868
  23.2 22.5 %copy-start.4 = (s32[1,2304]{1,0:T(1,128)S(1)}, s32[1,2304]{1,0:T(1,128)}, u32[]{:S(2)}) copy-start(s32[1,2304]{1,0:T(1,128)} %refs_2_.1) | copy-start | bytes 27652
  38.9 4.6 %collective-permute-start.3 = (f32[16,128]{1,0:T(8,128)S(1)}, f32[16,128]{1,0:T(8,128)S(1)}, u32[]{:S(2)}, u32[]{:S(2)}) collective-permute-start(f32[16,128]{1,0:T(8,128)S(1)} %get-tuple-element.49), channel_id=1, source_target_pairs={{0,128},{128,0},{1,129},{129,1},{2,130},{130,2},{3,131},{131,3},{4... | collective-permute-start | bytes 24584 | tf_op jit(solution)/shard_map/ppermute | solution.py:509
  43.4 6.4 %copy-start = (f32[2304,64]{0,1:T(8,128)S(1)}, f32[2304,64]{0,1:T(8,128)}, u32[]{:S(2)}) copy-start(f32[2304,64]{0,1:T(8,128)} %param.14) | copy-start | bytes 1769476
  43.4 6.4 %copy-start.1 = (bf16[2304,128]{1,0:T(8,128)(2,1)S(1)}, bf16[2304,128]{1,0:T(8,128)(2,1)}, u32[]{:S(2)}) copy-start(bf16[2304,128]{1,0:T(8,128)(2,1)} %get-tuple-element.51.refs_10_) | copy-start | bytes 1769476
  43.4 6.4 %copy-start.3 = (bf16[128,320]{1,0:T(8,128)(2,1)S(1)}, bf16[128,320]{1,0:T(8,128)(2,1)}, u32[]{:S(2)}) copy-start(bf16[128,320]{1,0:T(8,128)(2,1)} %get-tuple-element.45.refs_4_) | copy-start | bytes 245764
  43.4 5.6 %collective-permute-start.6 = (f32[32,128]{1,0:T(8,128)S(1)}, f32[32,128]{1,0:T(8,128)S(1)}, u32[]{:S(2)}, u32[]{:S(2)}) collective-permute-start(f32[32,128]{1,0:T(8,128)S(1)} %constant_dynamic-update-slice_fusion.refs_5_), channel_id=1, source_target_pairs={{0,3},{1,0},{2,1},{3,2},{4,7},{5,4},{6,5},{7,6},{8,11},{9,8},{10,9... | collective-permute-start | bytes 49160 | tf_op jit(solution)/shard_map/ppermute | solution.py:511
  44.7 4.4 %collective-permute-start.5 = (f32[32,128]{1,0:T(8,128)S(1)}, f32[32,128]{1,0:T(8,128)S(1)}, u32[]{:S(2)}, u32[]{:S(2)}) collective-permute-start(f32[32,128]{1,0:T(8,128)S(1)} %constant_dynamic-update-slice_fusion.refs_5_), channel_id=1, source_target_pairs={{0,2},{1,3},{2,0},{3,1},{4,6},{5,7},{6,4},{7,5},{8,10},{9,11},{10,... | collective-permute-start | bytes 49160 | tf_op jit(solution)/shard_map/ppermute | solution.py:511
  45.7 4.1 %collective-permute-start.4 = (f32[32,128]{1,0:T(8,128)S(1)}, f32[32,128]{1,0:T(8,128)S(1)}, u32[]{:S(2)}, u32[]{:S(2)}) collective-permute-start(f32[32,128]{1,0:T(8,128)S(1)} %constant_dynamic-update-slice_fusion.refs_5_), channel_id=1, source_target_pairs={{0,1},{1,2},{2,3},{3,0},{4,5},{5,6},{6,7},{7,4},{8,9},{9,10},{10,1... | collective-permute-start | bytes 49160 | tf_op jit(solution)/shard_map/ppermute | solution.py:511
  51.3 5.7 %collective-permute-start.7 = (f32[96,128]{1,0:T(8,128)S(1)}, f32[96,128]{1,0:T(8,128)S(1)}, u32[]{:S(2)}, u32[]{:S(2)}) collective-permute-start(f32[96,128]{1,0:T(8,128)S(1)} %get-tuple-element.57), channel_id=1, source_target_pairs={{0,1},{1,2},{2,3},{3,0},{4,5},{5,6},{6,7},{7,4},{8,9},{9,10},{10,1... | collective-permute-start | bytes 147464 | tf_op jit(solution)/shard_map/ppermute | solution.py:497
  52.3 4.8 %collective-permute-start.8 = (f32[96,128]{1,0:T(8,128)S(1)}, f32[96,128]{1,0:T(8,128)S(1)}, u32[]{:S(2)}, u32[]{:S(2)}) collective-permute-start(f32[96,128]{1,0:T(8,128)S(1)} %get-tuple-element.58), channel_id=1, source_target_pairs={{0,2},{1,3},{2,0},{3,1},{4,6},{5,7},{6,4},{7,5},{8,10},{9,11},{10,... | collective-permute-start | bytes 147464 | tf_op jit(solution)/shard_map/ppermute | solution.py:497
  54.5 3.2 %collective-permute-start.9 = (f32[96,128]{1,0:T(8,128)S(1)}, f32[96,128]{1,0:T(8,128)S(1)}, u32[]{:S(2)}, u32[]{:S(2)}) collective-permute-start(f32[96,128]{1,0:T(8,128)S(1)} %get-tuple-element.59), channel_id=1, source_target_pairs={{0,3},{1,0},{2,1},{3,2},{4,7},{5,4},{6,5},{7,6},{8,11},{9,8},{10,9... | collective-permute-start | bytes 147464 | tf_op jit(solution)/shard_map/ppermute | solution.py:497
  58.6 19.4 %all-to-all-start.1 = ((f32[32,32,128]{2,1,0:T(8,128)}), f32[32,32,128]{2,1,0:T(8,128)S(1)}, u32[]{:S(2)}, u32[]{:S(2)}) async-start(f32[32,32,128]{2,1,0:T(8,128)} %middle.3), calls=%async_computation.1 | async-start | bytes 1048576 | tf_op jit(solution)/shard_map/all_to_all | solution.py:499
  78.5 6.0 %collective-permute-start.10 = (f32[16,128]{1,0:T(8,128)S(1)}, f32[16,128]{1,0:T(8,128)S(1)}, u32[]{:S(2)}, u32[]{:S(2)}) collective-permute-start(f32[16,128]{1,0:T(8,128)S(1)} %get-tuple-element.67), channel_id=1, source_target_pairs={{0,128},{128,0},{1,129},{129,1},{2,130},{130,2},{3,131},{131,3},{4... | collective-permute-start | bytes 24584 | tf_op jit(solution)/shard_map/ppermute | solution.py:509
  84.5 4.7 %collective-permute-start.13 = (f32[32,128]{1,0:T(8,128)S(1)}, f32[32,128]{1,0:T(8,128)S(1)}, u32[]{:S(2)}, u32[]{:S(2)}) collective-permute-start(f32[32,128]{1,0:T(8,128)S(1)} %constant_dynamic-update-slice_fusion.2.refs_5_), channel_id=1, source_target_pairs={{0,3},{1,0},{2,1},{3,2},{4,7},{5,4},{6,5},{7,6},{8,11},{9,8},{10,9... | collective-permute-start | bytes 49160 | tf_op jit(solution)/shard_map/ppermute | solution.py:511
  86.4 4.2 %collective-permute-start.12 = (f32[32,128]{1,0:T(8,128)S(1)}, f32[32,128]{1,0:T(8,128)S(1)}, u32[]{:S(2)}, u32[]{:S(2)}) collective-permute-start(f32[32,128]{1,0:T(8,128)S(1)} %constant_dynamic-update-slice_fusion.2.refs_5_), channel_id=1, source_target_pairs={{0,2},{1,3},{2,0},{3,1},{4,6},{5,7},{6,4},{7,5},{8,10},{9,11},{10,... | collective-permute-start | bytes 49160 | tf_op jit(solution)/shard_map/ppermute | solution.py:511
  86.7 4.0 %collective-permute-start.11 = (f32[32,128]{1,0:T(8,128)S(1)}, f32[32,128]{1,0:T(8,128)S(1)}, u32[]{:S(2)}, u32[]{:S(2)}) collective-permute-start(f32[32,128]{1,0:T(8,128)S(1)} %constant_dynamic-update-slice_fusion.2.refs_5_), channel_id=1, source_target_pairs={{0,1},{1,2},{2,3},{3,0},{4,5},{5,6},{6,7},{7,4},{8,9},{9,10},{10,1... | collective-permute-start | bytes 49160 | tf_op jit(solution)/shard_map/ppermute | solution.py:511
